TPU v7x, 32 devices: a whole 2x2x4 slice. The times are simulated.
32 devices in a mesh: groups: 2 (over y), rows: 4 (over z), segment: 2 (over x), chan: 2 (over core).
Axes of the slice: x: 2, y: 2, z: 4, core: 2. Of those that a mesh axis runs over, the one named last changes fastest.
Arguments:
- latent: bfloat16 [8, 8, 160, 384], P(('groups', 'segment'), 'rows'), parts along dimension 0, may hold values from -6 to 6
- cache_mid: bfloat16 [4, 8, 160, 384], P('groups', 'rows'), parts along dimension 0, may hold values from -6 to 6
- cache_low: bfloat16 [4, 16, 320, 192], P('groups', 'rows'), parts along dimension 0, may hold values from -6 to 6
- gain_mid: float32 [384], replicated, may hold values from 0.1 to 1.9
- gain_attn: float32 [384], replicated, may hold values from 0.1 to 1.9
- gain_low: float32 [192], replicated, may hold values from 0.1 to 1.9
- conv_mid: bfloat16 [3, 3, 3, 384, 384], P(None, None, None, None, 'chan'), may hold values from -0.0625 to 0.0625
- attn_qkv: bfloat16 [384, 1152], replicated, may hold values from -4 to 4
- attn_proj: bfloat16 [384, 384], replicated, may hold values from -0.3125 to 0.3125
- conv_up: bfloat16 [3, 3, 384, 192], P(None, None, None, 'chan'), may hold values from -0.109375 to 0.109375
- conv_low: bfloat16 [3, 3, 3, 192, 192], P(None, None, None, None, 'chan'), may hold values from -0.078125 to 0.078125
Outputs:
- decoded: bfloat16 [8, 16, 320, 192], P(('groups', 'segment'), 'rows', None, 'chan'), parts along dimension 0
There are 2 independent parts, one for each index of `groups`. A program takes and returns all parts, laid end to end along the dimension named above; an argument that names none is the same for every part. Nothing has to cross between parts.
All inputs are finite; a program needn't handle non-finite values.
Results may differ from a plain program's by a relative error of at most 0.0071.
Values may be sent and summed in bfloat16 or wider, within the bound.
No kernel may reach another device: no remote copies, remote signals or barrier semaphores. Data moves between devices by JAX's collectives and lax.ppermute only.
A program may use at most 128 MiB of HBM per device.

v0:
```python
import functools
import math

import jax
import jax.numpy as jnp
from jax import lax
from jax.experimental import pallas as pl
from jax.experimental.pallas import tpu as pltpu
from jax.sharding import PartitionSpec as P

BF16, F32 = jnp.bfloat16, jnp.float32
VMEM_LIMIT = 56 * 1024 * 1024
NT = (((1,), (1,)), ((), ()))
EPS = 1e-06


def vmem():
    return pl.BlockSpec(memory_space=pltpu.VMEM)


def smem():
    return pl.BlockSpec(memory_space=pltpu.SMEM)


def dot_nt(left, right):
    return lax.dot_general(left, right, NT, preferred_element_type=F32)


def normed(values, gain):
    mean = jnp.mean(values * values, axis=-1, keepdims=True)
    return values * lax.rsqrt(mean + EPS) * gain


def silu(values):
    return values / (1.0 + jnp.exp(-values))


def from_left(values):
    column = lax.broadcasted_iota(jnp.int32, values.shape, 0)
    return jnp.where(column == 0, 0.0, pltpu.roll(values, 1, 0))


def from_right(values):
    count = values.shape[0]
    column = lax.broadcasted_iota(jnp.int32, values.shape, 0)
    return jnp.where(column == count - 1, 0.0, pltpu.roll(values, count - 1, 0))


def mid_kernel(place, latent, halo, cache, cache_halo, gain, weights, own, passed, acc, seen, seen_cache):
    frames, rows, width, channels = latent.shape
    part = weights.shape[-2]
    past = cache.shape[0]
    taps = past + 1
    tap = pl.program_id(0)
    first = place[0] == 0

    def spread(row):
        return jnp.concatenate([from_left(row), row, from_right(row)], axis=-1).astype(BF16)

    def row_of(block, rims, f, l):
        if l == 0:
            return rims[0, f]
        if l == rows + 1:
            return rims[1, f]
        return block[f, l - 1]

    @pl.when(tap == 0)
    def _():
        for f in range(frames):
            for l in range(rows + 2):
                row = row_of(latent, halo, f, l).astype(F32)
                seen[f, l] = spread(silu(normed(row, gain[...])))
            mine = latent[f].astype(F32).reshape(rows * width, channels)
            low = mine[:, :part]
            for index in range(1, channels // part):
                low = jnp.where(place[1] == index, mine[:, index * part : (index + 1) * part], low)
            acc[f] = low
        for f in range(frames, frames + past):
            acc[f] = jnp.zeros_like(acc[f])

        @pl.when(first)
        def _():
            for f in range(past):
                for l in range(rows + 2):
                    seen_cache[f, l] = spread(row_of(cache, cache_halo, f, l).astype(F32))

    def product(block, f):
        total = None
        for dy in range(3):
            rhs = jnp.concatenate([weights[0, dy, dx] for dx in range(3)], axis=-1)
            term = dot_nt(block[f, dy : dy + rows].reshape(rows * width, 3 * channels), rhs)
            total = term if total is None else total + term
        return total

    for f in range(frames):
        acc[f + past - tap] += product(seen, f)
    for f in range(past):
        @pl.when(first & (tap <= f))
        def _(f=f):
            acc[f - tap] += product(seen_cache, f)

    @pl.when(tap == taps - 1)
    def _():
        for f in range(frames):
            own[f] = acc[f]
        passed[...] = jnp.concatenate([acc[frames + t] for t in range(past)], axis=-1).astype(BF16)


def mid_conv(place, latent, halo, cache, cache_halo, gain, weights):
    frames, rows, width, channels = latent.shape
    taps, part = weights.shape[0], weights.shape[-2]
    past = taps - 1
    return pl.pallas_call(
        mid_kernel,
        grid=(taps,),
        in_specs=[smem(), vmem(), vmem(), vmem(), vmem(), vmem(),
                  pl.BlockSpec((1, 3, 3, part, channels), lambda k: (k, 0, 0, 0, 0))],
        out_specs=[vmem(), vmem()],
        out_shape=[
            jax.ShapeDtypeStruct((frames, rows * width, part), F32),
            jax.ShapeDtypeStruct((rows * width, past * part), BF16),
        ],
        scratch_shapes=[
            pltpu.VMEM((frames + past, rows * width, part), F32),
            pltpu.VMEM((frames, rows + 2, width, 3 * channels), BF16),
            pltpu.VMEM((past, rows + 2, width, 3 * channels), BF16),
        ],
        compiler_params=pltpu.CompilerParams(vmem_limit_bytes=VMEM_LIMIT),
        name="mid_conv",
    )(place, latent, halo, cache, cache_halo, gain, weights)


def attn_kernel(place, frame, gain, qkv, proj, out, normal, keys, values):
    height, width, channels = frame.shape[1:]
    rows = out.shape[1]
    step = 2
    scale = 1.0 / (math.sqrt(channels) * math.log(2.0))

    def prepare(index, carry):
        chunk = frame[0, pl.ds(index * step, step)].reshape(step * width, channels).astype(F32)
        scaled = normed(chunk, gain[...]).astype(BF16)
        normal[pl.ds(index * step, step)] = scaled.reshape(step, width, channels)
        both = jnp.dot(scaled, qkv[:, channels:], preferred_element_type=F32).astype(BF16)
        at = pl.ds(pl.multiple_of(index * step * width, 16), step * width)
        keys[at] = both[:, :channels]
        values[at] = both[:, channels:]
        return carry

    lax.fori_loop(0, height // step, prepare, 0)
    start = place[2] * (rows - 2) - 1
    for block in range(rows // step):
        spots = [start + block * step + i for i in range(step)]
        kept = [jnp.clip(spot, 0, height - 1) for spot in spots]
        inputs = jnp.concatenate([normal[spot] for spot in kept], axis=0)
        query = jnp.dot(inputs, qkv[:, :channels], preferred_element_type=F32).astype(BF16)
        scores = dot_nt(query, keys[...]) * scale
        powers = jnp.exp2(scores - jnp.max(scores, axis=-1, keepdims=True))
        total = jnp.sum(powers, axis=-1, keepdims=True)
        mixed = jnp.dot(powers.astype(BF16), values[...], preferred_element_type=F32) / total
        branch = jnp.dot(mixed.astype(BF16), proj[...], preferred_element_type=F32)
        for i in range(step):
            inside = (spots[i] >= 0) & (spots[i] < height)
            summed = frame[0, kept[i]].astype(F32) + branch[i * width : (i + 1) * width]
            out[0, block * step + i] = jnp.where(inside, summed, 0.0).astype(BF16)


def attention(place, frame, gain, qkv, proj, rows):
    count, height, width, channels = frame.shape
    return pl.pallas_call(
        attn_kernel,
        grid=(count,),
        in_specs=[smem(), pl.BlockSpec((1, height, width, channels), lambda f: (f, 0, 0, 0)),
                  vmem(), vmem(), vmem()],
        out_specs=pl.BlockSpec((1, rows, width, channels), lambda f: (f, 0, 0, 0)),
        out_shape=jax.ShapeDtypeStruct((count, rows, width, channels), BF16),
        scratch_shapes=[
            pltpu.VMEM((height, width, channels), BF16),
            pltpu.VMEM((height * width, channels), BF16),
            pltpu.VMEM((height * width, channels), BF16),
        ],
        compiler_params=pltpu.CompilerParams(vmem_limit_bytes=VMEM_LIMIT),
        name="frame_attention",
    )(place, frame, gain, qkv, proj)


def low_kernel(place, tile, up, gain, weights, select, even, odd, own, passed, seen, upper, window, kept, acc):
    frames, ext, width, channels = tile.shape
    part = up.shape[2]
    rows = ext - 2
    high = 2 * rows
    past = even.shape[0]
    phases = own.shape[1]
    first = place[0] == 0

    def windowed(left, right):
        return jnp.concatenate([from_left(right), left, right, from_right(left)], axis=-1).astype(BF16)

    for f in range(frames):
        for l in range(ext):
            row = tile[f, l].astype(F32)
            seen[f, l] = jnp.concatenate([from_left(row), row, from_right(row)], axis=-1).astype(BF16)
        for a in range(2):
            for b in range(2):
                lanes = slice(b * channels, (b + 2) * channels)
                span = (ext - 1) * width
                top = seen[f, : ext - 1, :, lanes].reshape(span, 2 * channels)
                bottom = seen[f, 1:, :, lanes].reshape(span, 2 * channels)
                got = dot_nt(top, up[a, b, :, : 2 * channels]) + dot_nt(bottom, up[a, b, :, 2 * channels :])
                for p in range(ext - 1):
                    upper[2 * p + 1 - a, b] = got[p * width : (p + 1) * width].astype(BF16)
        for j in range(high + 2):
            sides = [upper[j, b].astype(F32) for b in range(2)]
            if 1 <= j <= high:
                kept[f, j - 1] = jnp.concatenate(sides, axis=-1).astype(BF16)
            sides = [silu(normed(side, gain[...])) for side in sides]
            if j == 0:
                sides = [jnp.where(place[2] == 0, 0.0, side) for side in sides]
            if j == high + 1:
                sides = [jnp.where(place[2] == place[3] - 1, 0.0, side) for side in sides]
            window[f, j] = windowed(*sides)

    def stacked(block, f):
        return jnp.concatenate(
            [block[f, dy : dy + high].reshape(high * width, 4 * part) for dy in range(3)], axis=-1
        )

    for f in range(frames):
        acc[f] = dot_nt(select[...], kept[f].reshape(high * width, 2 * part))
    for f in range(frames, frames + past):
        acc[f] = jnp.zeros_like(acc[f])
    for f in range(frames):
        got = dot_nt(weights[...], stacked(window, f))
        for tap in range(past + 1):
            acc[f + past - tap] += got[tap * phases : (tap + 1) * phases]
    for t in range(past):
        passed[t] = acc[frames + t].astype(BF16)

    @pl.when(first)
    def _():
        for f in range(past):
            for j in range(high + 2):
                window[0, j] = windowed(even[f, j].astype(F32), odd[f, j].astype(F32))
            got = dot_nt(weights[: (f + 1) * phases], stacked(window, 0))
            for tap in range(f + 1):
                acc[f - tap] += got[tap * phases : (tap + 1) * phases]

    for f in range(frames):
        own[f] = acc[f]


def low_stage(place, tile, up, gain, weights, select, even, odd):
    frames, ext, width, channels = tile.shape
    part = up.shape[2]
    high = 2 * (ext - 2)
    past = even.shape[0]
    phases = select.shape[0]
    return pl.pallas_call(
        low_kernel,
        in_specs=[smem()] + [vmem()] * 7,
        out_specs=[vmem(), vmem()],
        out_shape=[
            jax.ShapeDtypeStruct((frames, phases, high * width), F32),
            jax.ShapeDtypeStruct((past, phases, high * width), BF16),
        ],
        scratch_shapes=[
            pltpu.VMEM((frames, ext, width, 3 * channels), BF16),
            pltpu.VMEM((high + 2, 2, width, part), BF16),
            pltpu.VMEM((frames, high + 2, width, 4 * part), BF16),
            pltpu.VMEM((frames, high, width, 2 * part), BF16),
            pltpu.VMEM((frames + past, phases, high * width), F32),
        ],
        compiler_params=pltpu.CompilerParams(vmem_limit_bytes=VMEM_LIMIT),
        name="low_stage",
    )(place, tile, up, gain, weights, select, even, odd)


def lane_windows(high, width):
    starts = [width * i // 128 * 128 for i in range(high)]
    span = max(width * i - start + width for i, start in enumerate(starts))
    span = min(-(-span // 128) * 128, high * width)
    starts = [min(start, high * width - span) for start in starts]
    return starts, span


def weaver(high, width):
    starts, span = lane_windows(high, width)
    lane = lax.broadcasted_iota(jnp.int32, (span, 2 * width), 0)
    column = lax.broadcasted_iota(jnp.int32, (span, 2 * width), 1)
    blocks = []
    for i, start in enumerate(starts):
        pixel = lane - (width * i - start)
        blocks.append([(column == 2 * pixel + b).astype(BF16) for b in range(2)])
    return jnp.stack([jnp.concatenate(pair, axis=0) for pair in blocks])


def finish_kernel(starts, own, passed, weave, out):
    half = own.shape[1] // 2
    span = weave.shape[1] // 2
    for f in range(own.shape[0]):
        total = own[f]
        if f < passed.shape[0]:
            total = total + passed[f].astype(F32)
        total = total.astype(BF16)
        for i, start in enumerate(starts):
            lanes = slice(start, start + span)
            sides = jnp.concatenate([total[:half, lanes], total[half:, lanes]], axis=-1)
            out[f, i] = jnp.dot(sides, weave[i], preferred_element_type=F32).astype(BF16)


def finish(own, passed, weave, high, width):
    frames, phases = own.shape[:2]
    starts, _ = lane_windows(high, width)
    return pl.pallas_call(
        functools.partial(finish_kernel, starts),
        in_specs=[vmem()] * 3,
        out_specs=vmem(),
        out_shape=jax.ShapeDtypeStruct((frames, high, phases // 2, 2 * width), BF16),
        compiler_params=pltpu.CompilerParams(vmem_limit_bytes=VMEM_LIMIT),
        name="finish",
    )(own, passed, weave)


def rim_exchange(values, chan):
    rows, chans = lax.axis_size("rows"), lax.axis_size("chan")
    sent = jnp.where(chan == 0, values[:, -1], values[:, 0])
    route = [(r * chans, (r + 1) * chans) for r in range(rows - 1)]
    route += [((r + 1) * chans + 1, r * chans + 1) for r in range(rows - 1)]
    return lax.ppermute(sent, ("rows", "chan"), route)


def to_next(values):
    count = lax.axis_size("segment")
    return lax.ppermute(values, "segment", [(i, i + 1) for i in range(count - 1)])


def up_weights(conv_up):
    whole = lax.all_gather(jnp.swapaxes(conv_up, 2, 3), "chan", axis=2, tiled=True).astype(F32)

    def folded(parts, a):
        return (parts[0], parts[1] + parts[2]) if a == 0 else (parts[0] + parts[1], parts[2])

    blocks = []
    for a in range(2):
        for b in range(2):
            pieces = []
            for line in folded([whole[i] for i in range(3)], a):
                pieces += folded([line[i] for i in range(3)], b)
            blocks.append(jnp.concatenate(pieces, axis=-1))
    stacked = jnp.stack(blocks).astype(BF16)
    return stacked.reshape((2, 2) + stacked.shape[1:])


def low_weights(conv_low):
    turned = jnp.swapaxes(conv_low, 3, 4)
    columns = [turned[:, :, i] for i in range(3)]
    blank = jnp.zeros_like(columns[0])
    even = jnp.concatenate(columns + [blank], axis=-1)
    odd = jnp.concatenate([blank] + columns, axis=-1)
    both = jnp.stack([even, odd], axis=1)
    both = both.transpose(0, 1, 3, 2, 4)
    return both.reshape(both.shape[0] * 2 * both.shape[2], -1)


def body(
    latent,
    cache_mid,
    cache_low,
    gain_mid,
    gain_attn,
    gain_low,
    conv_mid,
    attn_qkv,
    attn_proj,
    conv_up,
    conv_low,
):
    chan = lax.axis_index("chan")
    row = lax.axis_index("rows")
    place = jnp.stack(
        [lax.axis_index("segment"), chan, row, jnp.int32(lax.axis_size("rows"))]
    ).astype(jnp.int32)
    frames, rows, width, channels = latent.shape
    mid_part = conv_mid.shape[-1]
    low_part = conv_low.shape[-1]
    past = conv_mid.shape[0] - 1

    rim = rim_exchange(latent, chan)
    cache_rim = rim_exchange(cache_mid, chan)
    low_rim = rim_exchange(cache_low, chan)
    up = up_weights(conv_up)
    rims = lax.all_gather(jnp.concatenate([rim, cache_rim], axis=0), "chan")
    low_rims = lax.all_gather(low_rim, "chan")

    own, passed = mid_conv(
        place, latent, rims[:, :frames], cache_mid, rims[:, frames:],
        gain_mid[None], jnp.swapaxes(conv_mid, 3, 4),
    )
    arrived = to_next(passed).astype(F32)
    added = [arrived[:, t * mid_part : (t + 1) * mid_part] for t in range(past)]
    first_part = jnp.stack(
        [own[f] + added[f] if f < past else own[f] for f in range(frames)]
    ).astype(BF16).reshape(frames, rows, width, mid_part)
    mine = lax.all_to_all(first_part, "chan", split_axis=0, concat_axis=3, tiled=True)
    frame = lax.all_gather(mine, "rows", axis=1, tiled=True)

    reached = attention(place, frame, gain_attn[None], attn_qkv, attn_proj, rows + 2)
    tile = lax.all_gather(reached, "chan", axis=0, tiled=True)

    cached = jnp.concatenate([low_rims[0][:, None], cache_low, low_rims[1][:, None]], axis=1)
    cached = cached.reshape(cached.shape[:2] + (width, 2, cached.shape[-1]))
    phase = lax.broadcasted_iota(jnp.int32, (2 * low_part, 2 * gain_low.shape[0]), 0)
    spot = lax.broadcasted_iota(jnp.int32, (2 * low_part, 2 * gain_low.shape[0]), 1)
    side, lane = phase // low_part, phase % low_part
    select = (spot == side * gain_low.shape[0] + chan * low_part + lane).astype(BF16)
    own_low, passed_low = low_stage(
        place, tile, up, gain_low[None], low_weights(conv_low), select,
        cached[:, :, :, 0], cached[:, :, :, 1],
    )
    high = 2 * rows
    out = finish(own_low, to_next(passed_low), weaver(high, width), high, width)
    return jnp.swapaxes(out, 2, 3)


def solution(mesh):
    placed = (
        P(("groups", "segment"), "rows", None, None),
        P("groups", "rows", None, None),
        P("groups", "rows", None, None),
        P(),
        P(),
        P(),
        P(None, None, None, None, "chan"),
        P(),
        P(),
        P(None, None, None, "chan"),
        P(None, None, None, None, "chan"),
    )
    return jax.shard_map(
        body,
        mesh=mesh,
        in_specs=placed,
        out_specs=P(("groups", "segment"), "rows", None, "chan"),
        check_vma=False,
    )
```

profile of v0, /device:TPU:0, one launch (start us, length us, event | category | flops | bytes accessed | tf_op | source)
XLA Modules:
  0.0 165.1 jit_solution(2660579705299866321)
XLA Ops:
  6.5 1.9 %fusion.4 = bf16[2,160,384]{2,1,0:T(8,128)(2,1)} fusion(bf16[2,2,160,384]{3,2,1,0:T(8,128)(2,1)} %cache.1, pred[]{:T(512)S(6)} %eq.34), kind=kLoop, calls=%fused_computation.58 | loop fusion | flops 122880 | bytes 737281 | tf_op jit(solution)/shard_map/jit(_where)/select_n | solution.py:325
  8.5 5.6 %collective-permute-start.1 = (bf16[2,160,384]{2,1,0:T(8,128)(2,1)}, bf16[2,160,384]{2,1,0:T(8,128)(2,1)}, u32[]{:S(2)}, u32[]{:S(2)}) collective-permute-start(bf16[2,160,384]{2,1,0:T(8,128)(2,1)} %fusion.4), channel_id=1, source_target_pairs={{0,4},{4,8},{8,12},{5,1},{9,5},{13,9},{2,6},{6,10},{10,14},{7,3},{... | collective-permute-start | bytes 737288 | tf_op jit(solution)/shard_map/ppermute | solution.py:328
  14.1 1.8 %fusion.5 = bf16[2,160,384]{2,1,0:T(8,128)(2,1)} fusion(bf16[2,2,160,384]{3,2,1,0:T(8,128)(2,1)} %latent.1, pred[]{:T(512)S(6)} %eq.34), kind=kLoop, calls=%fused_computation.60 | loop fusion | flops 122880 | bytes 737281 | tf_op jit(solution)/shard_map/jit(_where)/select_n | solution.py:325
  15.9 3.5 %collective-permute-start = (bf16[2,160,384]{2,1,0:T(8,128)(2,1)}, bf16[2,160,384]{2,1,0:T(8,128)(2,1)}, u32[]{:S(2)}, u32[]{:S(2)}) collective-permute-start(bf16[2,160,384]{2,1,0:T(8,128)(2,1)} %fusion.5), channel_id=1, source_target_pairs={{0,4},{4,8},{8,12},{5,1},{9,5},{13,9},{2,6},{6,10},{10,14},{7,3},{... | collective-permute-start | bytes 737288 | tf_op jit(solution)/shard_map/ppermute | solution.py:328
  20.2 3.5 %collective-permute-start.3 = (bf16[2,320,192]{1,2,0:T(8,128)(2,1)}, bf16[2,320,192]{1,2,0:T(8,128)(2,1)}, u32[]{:S(2)}, u32[]{:S(2)}) collective-permute-start(bf16[2,320,192]{1,2,0:T(8,128)(2,1)} %fusion.2), channel_id=1, source_target_pairs={{0,4},{4,8},{8,12},{5,1},{9,5},{13,9},{2,6},{6,10},{10,14},{7,3},{... | collective-permute-start | bytes 737288 | tf_op jit(solution)/shard_map/ppermute | solution.py:328
  29.2 2.9 %maximum_bitcast_fusion.1 = (bf16[3,1,3,96,768]{3,4,2,0,1:T(8,128)(2,1)S(1)}, bf16[3,1,3,96,768]{3,4,2,0,1:T(8,128)(2,1)S(1)}) fusion(bf16[3,3,96,192]{2,3,1,0:T(8,128)(2,1)S(1)} %broadcast_in_dim.15, bf16[3,3,96,192]{2,3,1,0:T(8,128)(2,1)S(1)} %get-tuple-element.28, bf16[3,3,96,192]{2,3,1,0:T(8,128)(2,1)S(1)} %get-tuple-element.29, ...), kind=kLoop, calls=%fused_computation.3 | loop fusion | flops 10616832 | bytes 3981312 | tf_op jit(solution)/shard_map/stack | solution.py:359
  36.3 3.5 %copy.63 = bf16[2,4,320,192]{3,1,2,0:T(4,128)(2,1)} copy(bf16[2,4,320,192]{2,3,1,0:T(8,128)(2,1)} %param.13) | data formatting | bytes 1966080 | tf_op args[2]
  39.8 1.3 broadcast_in_dim.12.gain
  41.1 1.3 broadcast_in_dim.13.gain
  42.4 5.4 %copy.59 = bf16[3,2,96,3,768]{4,3,2,1,0:T(4,128)(2,1)} copy(bf16[3,2,96,3,768]{2,4,3,0,1:T(8,128)(2,1)S(1)} %maximum_bitcast_fusion) | data formatting | bytes 5308416 | tf_op jit(solution)/shard_map/transpose | solution.py:360
  47.7 4.1 %copy.76 = bf16[72,8,3,768]{3,1,2,0:T(8,128)(2,1)} copy(bf16[72,8,3,768]{3,2,1,0:T(4,128)(2,1)} %bitcast.119) | data formatting | bytes 5308416
  52.7 1.1 pad_maximum_fusion.1
  53.8 2.5 %all-gather = bf16[8,160,384]{2,1,0:T(8,128)(2,1)S(1)} all-gather(bf16[4,160,384]{2,1,0:T(8,128)(2,1)S(1)} %pad_maximum_fusion.1), channel_id=2, replica_groups=mesh['groups'=2,'rows'=4,'segment'=2,'chan'=2] {'chan'}, dimensions={0}, use_global_device_ids=true | all-gather | bytes 1474560 | tf_op jit(solution)/shard_map/all_gather | solution.py:391
  56.3 1.1 fusion.24
  57.4 11.8 %mid_conv.1 = (f32[2,320,192]{2,1,0:T(8,128)}, bf16[320,384]{1,0:T(8,128)(2,1)}) custom-call(s32[4]{0:T(128)} %pad_add_fusion.place, bf16[2,2,160,384]{3,2,1,0:T(8,128)(2,1)} %latent.1, bf16[2,2,160,384]{3,2,1,0:T(8,128)(2,1)} %get-tuple-element.33.halo, bf16[2,2,160,384]{3,2,1,0:T(8,128)(2,1)} %cache.1, ...), custom_call_target="tpu_custom_call" | custom-call | tf_op jit(solution)/shard_map/mid_conv/pallas_call | solution.py:113
  69.2 1.4 collective-permute-start.2
  70.7 2.4 %all-gather.1 = bf16[4,320,192]{1,2,0:T(8,128)(2,1)S(1)} all-gather(bf16[2,320,192]{1,2,0:T(8,128)(2,1)} %collective-permute-done.3), channel_id=3, replica_groups=mesh['groups'=2,'rows'=4,'segment'=2,'chan'=2] {'chan'}, dimensions={0}, use_global_device_ids=true | all-gather | bytes 737280 | tf_op jit(solution)/shard_map/all_gather | solution.py:392
  73.9 1.2 copy.62
  75.1 1.0 copy_dynamic-update-slice_fusion.2
  76.1 1.9 %copy.64 = bf16[2,320,192]{2,0,1:T(2,128)(2,1)} copy(bf16[2,320,192]{1,2,0:T(8,128)(2,1)} %get-tuple-element.42) | data formatting | bytes 491520 | tf_op jit(solution)/shard_map/slice | solution.py:409
  79.0 1.4 slice_bitcast_fusion
  80.7 4.0 %all_to_all.18 = bf16[2,2,160,192]{3,2,1,0:T(8,128)(2,1)S(1)} all-to-all(bf16[2,2,160,192]{3,2,1,0:T(8,128)(2,1)S(1)} %pad_maximum_fusion.2), channel_id=1, replica_groups=mesh['groups'=2,'rows'=4,'segment'=2,'chan'=2] {'chan'}, dimensions={0} | all-to-all | bytes 491520 | tf_op jit(solution)/shard_map/all_to_all | solution.py:403
  85.3 20.9 %all_gather.23 = bf16[1,8,160,384]{3,2,0,1:T(8,128)(2,1)} all-gather(bf16[1,2,160,384]{3,2,0,1:T(8,128)(2,1)S(1)} %bitcast.130), channel_id=1, replica_groups=mesh['groups'=2,'rows'=4,'segment'=2,'chan'=2] {'rows'}, dimensions={1}, use_global_device_ids=true | all-gather | bytes 1228800 | tf_op jit(solution)/shard_map/all_gather | solution.py:404
  106.2 7.9 %frame_attention.1 = bf16[1,4,160,384]{3,2,1,0:T(8,128)(2,1)} custom-call(s32[4]{0:T(128)} %pad_add_fusion.place, bf16[1,8,160,384]{3,2,1,0:T(8,128)(2,1)} %bitcast.125, f32[1,384]{1,0:T(1,128)} %broadcast_in_dim.13.gain, bf16[384,1152]{1,0:T(8,128)(2,1)} %qkv.1, bf16[384,384]{1,0:T(8,128)(2,1)} %proj.1), custom_call_target="tpu_custom_call" | custom-call | tf_op jit(solution)/shard_map/frame_attention/pallas_call | solution.py:169
  114.1 7.1 %all_gather.24.tile = bf16[2,4,160,384]{3,2,1,0:T(8,128)(2,1)} all-gather(bf16[1,4,160,384]{3,2,1,0:T(8,128)(2,1)} %frame_attention.1), channel_id=1, replica_groups=mesh['groups'=2,'rows'=4,'segment'=2,'chan'=2] {'chan'}, dimensions={0}, use_global_device_ids=true | all-gather | bytes 1474560 | tf_op jit(solution)/shard_map/all_gather | solution.py:407
  121.2 1.5 convert_element_type.12
  123.5 1.7 %pad_maximum_fusion = bf16[4,192,1536]{2,1,0:T(8,128)(2,1)} fusion(bf16[1,192,1536]{2,1,0:T(8,128)(2,1)S(1)} %get-tuple-element.47, bf16[1,192,1536]{2,1,0:T(8,128)(2,1)S(1)} %get-tuple-element.46, bf16[1,192,1536]{2,1,0:T(8,128)(2,1)S(1)} %get-tuple-element.45, bf16[1,192,1536]{2,1,0:T(8,128)(2,1)S(1)} %get-tuple-element.44), kind=kLoop, calls=%fused_computation.2 | loop fusion | flops 3538944 | bytes 4718592 | tf_op jit(solution)/shard_map/stack | solution.py:349
  125.3 16.0 %low_stage.1 = (f32[2,192,640]{2,1,0:T(8,128)}, bf16[2,192,640]{2,1,0:T(8,128)(2,1)}) custom-call(s32[4]{0:T(128)} %pad_add_fusion.place, bf16[2,4,160,384]{3,2,1,0:T(8,128)(2,1)} %all_gather.24.tile, bf16[2,2,192,1536]{3,2,1,0:T(8,128)(2,1)} %bitcast.121, f32[1,192]{1,0:T(1,128)} %bitcast.134, bf16[576,2304]{1,0:T(8,128)(2,1)} %bitcast.120, ...), custom_call_target="tpu_custom_call" | custom-call | tf_op jit(solution)/shard_map/low_stage/pallas_call | solution.py:257
  141.2 1.3 collective-permute-start.4
  142.8 1.5 add_convert_fusion.weave
  144.3 9.8 %collective-permute-done.4.passed = bf16[2,192,640]{2,1,0:T(8,128)(2,1)S(1)} collective-permute-done((bf16[2,192,640]{2,1,0:T(8,128)(2,1)}, bf16[2,192,640]{2,1,0:T(8,128)(2,1)S(1)}, u32[]{:S(2)}, u32[]{:S(2)}) %collective-permute-start.4) | collective-permute-done | bytes 491552 | tf_op jit(solution)/shard_map/ppermute | solution.py:333
  154.9 3.3 %finish.1 = bf16[2,4,96,320]{3,2,1,0:T(8,128)(2,1)} custom-call(f32[2,192,640]{2,1,0:T(8,128)} %get-tuple-element.11.own, bf16[2,192,640]{2,1,0:T(8,128)(2,1)} %copy-done.8, bf16[4,512,320]{2,1,0:T(8,128)(2,1)} %add_convert_fusion.weave), custom_call_target="tpu_custom_call" | custom-call | tf_op jit(solution)/shard_map/finish/pallas_call | solution.py:313
  (87 shorter events, 15.6 us)
Async XLA Ops:
  6.5 12.9 %copy-start.1 = (bf16[2,4,320,192]{2,3,1,0:T(8,128)(2,1)S(1)}, bf16[2,4,320,192]{2,3,1,0:T(8,128)(2,1)}, u32[]{:S(2)}) copy-start(bf16[2,4,320,192]{2,3,1,0:T(8,128)(2,1)} %param.13) | copy-start | bytes 2949124
  6.5 22.4 %copy-start.2 = (bf16[3,3,3,192,96]{4,3,2,1,0:T(8,128)(2,1)S(1)}, bf16[3,3,3,192,96]{4,3,2,1,0:T(8,128)(2,1)}, u32[]{:S(2)}) copy-start(bf16[3,3,3,192,96]{4,3,2,1,0:T(8,128)(2,1)} %param.21) | copy-start | bytes 2985988
  6.5 114.7 %all-gather.4.cloned.1.call-start = ((), (), s32[]{:S(2)}) async-start(), calls=%async_computation.1 | async-start | bytes 1990656 | tf_op jit(solution)/shard_map/all_gather | solution.py:337
  8.5 44.2 %collective-permute-start.1 = (bf16[2,160,384]{2,1,0:T(8,128)(2,1)}, bf16[2,160,384]{2,1,0:T(8,128)(2,1)}, u32[]{:S(2)}, u32[]{:S(2)}) collective-permute-start(bf16[2,160,384]{2,1,0:T(8,128)(2,1)} %fusion.4), channel_id=1, source_target_pairs={{0,4},{4,8},{8,12},{5,1},{9,5},{13,9},{2,6},{6,10},{10,14},{7,3},{... | collective-permute-start | bytes 737288 | tf_op jit(solution)/shard_map/ppermute | solution.py:328
  15.9 36.8 %collective-permute-start = (bf16[2,160,384]{2,1,0:T(8,128)(2,1)}, bf16[2,160,384]{2,1,0:T(8,128)(2,1)}, u32[]{:S(2)}, u32[]{:S(2)}) collective-permute-start(bf16[2,160,384]{2,1,0:T(8,128)(2,1)} %fusion.5), channel_id=1, source_target_pairs={{0,4},{4,8},{8,12},{5,1},{9,5},{13,9},{2,6},{6,10},{10,14},{7,3},{... | collective-permute-start | bytes 737288 | tf_op jit(solution)/shard_map/ppermute | solution.py:328
  20.2 50.5 %collective-permute-start.3 = (bf16[2,320,192]{1,2,0:T(8,128)(2,1)}, bf16[2,320,192]{1,2,0:T(8,128)(2,1)}, u32[]{:S(2)}, u32[]{:S(2)}) collective-permute-start(bf16[2,320,192]{1,2,0:T(8,128)(2,1)} %fusion.2), channel_id=1, source_target_pairs={{0,4},{4,8},{8,12},{5,1},{9,5},{13,9},{2,6},{6,10},{10,14},{7,3},{... | collective-permute-start | bytes 737288 | tf_op jit(solution)/shard_map/ppermute | solution.py:328
  32.1 0.9 copy-start.15
  32.1 0.9 copy-start.16
  32.1 1.8 %copy-start.13 = (s32[256]{0:T(256)S(1)}, s32[256]{0:T(256)}, u32[]{:S(2)}) copy-start(s32[256]{0:T(256)} %broadcast_add_fusion.1) | copy-start | bytes 3076
  32.1 1.8 %copy-start.14 = (s32[256]{0:T(256)S(1)}, s32[256]{0:T(256)}, u32[]{:S(2)}) copy-start(s32[256]{0:T(256)} %add_multiply_fusion.1) | copy-start | bytes 3076
  32.1 2.7 %copy-start.11 = (s32[256]{0:T(256)S(1)}, s32[256]{0:T(256)}, u32[]{:S(2)}) copy-start(s32[256]{0:T(256)} %broadcast_add_fusion.2) | copy-start | bytes 3076
  32.1 2.7 %copy-start.12 = (s32[256]{0:T(256)S(1)}, s32[256]{0:T(256)}, u32[]{:S(2)}) copy-start(s32[256]{0:T(256)} %add_multiply_fusion.2) | copy-start | bytes 3076
  47.7 4.1 %copy-start.17 = (pred[192]{0:T(512)(128)(4,1)S(1)}, pred[192]{0:T(512)(128)(4,1)}, u32[]{:S(2)}) copy-start(pred[192]{0:T(512)(128)(4,1)} %get-tuple-element.50) | copy-start | bytes 580
  47.7 4.1 %copy-start.18 = (pred[192]{0:T(512)(128)(4,1)S(1)}, pred[192]{0:T(512)(128)(4,1)}, u32[]{:S(2)}) copy-start(pred[192]{0:T(512)(128)(4,1)} %get-tuple-element.51) | copy-start | bytes 580
  69.2 8.8 %copy-start = (bf16[2,4,320,192]{3,1,2,0:T(4,128)(2,1)S(1)}, bf16[2,4,320,192]{3,1,2,0:T(4,128)(2,1)}, u32[]{:S(2)}) copy-start(bf16[2,4,320,192]{3,1,2,0:T(4,128)(2,1)} %copy.63) | copy-start | bytes 2949124
  69.2 11.2 %collective-permute-start.2 = (bf16[320,384]{1,0:T(8,128)(2,1)}, bf16[320,384]{1,0:T(8,128)(2,1)S(1)}, u32[]{:S(2)}, u32[]{:S(2)}) collective-permute-start(bf16[320,384]{1,0:T(8,128)(2,1)} %get-tuple-element.10), channel_id=1, source_target_pairs={{0,2},{1,3},{4,6},{5,7},{8,10},{9,11},{12,14},{13,15},{16,18},{17,... | collective-permute-start | bytes 737288 | tf_op jit(solution)/shard_map/ppermute | solution.py:333
  78.0 1.0 copy-start.3
  79.0 1.4 copy-start.7
  125.3 17.3 %copy-start.9 = (s32[256]{0:T(256)S(1)}, s32[256]{0:T(256)}, u32[]{:S(2)}) copy-start(s32[256]{0:T(256)} %broadcast_add_fusion.3) | copy-start | bytes 3076
  125.3 17.3 %copy-start.10 = (s32[256]{0:T(256)S(1)}, s32[256]{0:T(256)}, u32[]{:S(2)}) copy-start(s32[256]{0:T(256)} %iota_multiply_fusion) | copy-start | bytes 3076
  125.3 17.6 %copy-start.4 = (pred[1,512,320]{2,1,0:T(8,128)(4,1)S(1)}, pred[1,512,320]{2,1,0:T(8,128)(4,1)}, u32[]{:S(2)}) copy-start(pred[1,512,320]{2,1,0:T(8,128)(4,1)} %add_bitcast_fusion.3) | copy-start | bytes 491524
  125.3 17.6 %copy-start.5 = (pred[1,512,320]{2,1,0:T(8,128)(4,1)S(1)}, pred[1,512,320]{2,1,0:T(8,128)(4,1)}, u32[]{:S(2)}) copy-start(pred[1,512,320]{2,1,0:T(8,128)(4,1)} %add_bitcast_fusion.2) | copy-start | bytes 491524
  125.3 17.6 %copy-start.6 = (pred[1,512,320]{2,1,0:T(8,128)(4,1)S(1)}, pred[1,512,320]{2,1,0:T(8,128)(4,1)}, u32[]{:S(2)}) copy-start(pred[1,512,320]{2,1,0:T(8,128)(4,1)} %add_bitcast_fusion.1) | copy-start | bytes 491524
  141.2 12.9 %collective-permute-start.4 = (bf16[2,192,640]{2,1,0:T(8,128)(2,1)}, bf16[2,192,640]{2,1,0:T(8,128)(2,1)S(1)}, u32[]{:S(2)}, u32[]{:S(2)}) collective-permute-start(bf16[2,192,640]{2,1,0:T(8,128)(2,1)} %get-tuple-element.12), channel_id=1, source_target_pairs={{0,2},{1,3},{4,6},{5,7},{8,10},{9,11},{12,14},{13,15},{16,18},{17,... | collective-permute-start | bytes 1474568 | tf_op jit(solution)/shard_map/ppermute | solution.py:333
  154.1 0.8 copy-start.8
Sparse Core Ops, SparseCore 0:
  19.5 7.9 all-gather.3
where the time goes:
time: 166 us; the launch traced here: 165 us
  Pallas kernels  39 us (23%)
  blocking collectives  37 us (22%)
  local copies, waits for them, and re-layouts  25.6 us (15%)
  other arithmetic  24.6 us (15%)
  starting transfers between devices  15.4 us (9%)
  between operations  13.8 us (8%)
  waiting for transfers between devices  9.84 us (6%)
    all_gather x1, blocking collectives, body(): frame = lax.all_gather(mine, 'rows', axis=1, tiled=True)  20.9 us
    pallas_call x1, Pallas kernels, low_stage(): pl.pallas_call(low_kernel, in_specs=[smem()] + [vmem()] * 7, out_specs=[v...  16 us
    ppermute x3, starting transfers between devices, rim_exchange(): return lax.ppermute(sent, ('rows', 'chan'), route)  12.6 us
    pallas_call x1, Pallas kernels, mid_conv(): pl.pallas_call(mid_kernel, grid=(taps,), in_specs=[smem(), vmem(), vmem()...  11.8 us
    unnamed x42, local copies, waits for them, and re-layouts  10.4 us
    ppermute x2, waiting for transfers between devices, to_next(): lax.ppermute(values, 'segment', [(i, i + 1) for i in range(count - 1)])  9.81 us
    pallas_call x1, Pallas kernels, attention(): pl.pallas_call(attn_kernel, grid=(count,), in_specs=[smem(), pl.BlockSpec...  7.91 us
    all_gather x1, blocking collectives, body(): tile = lax.all_gather(reached, 'chan', axis=0, tiled=True)  7.09 us
  transfers between devices with their start and end apart: 6, of which 1 were waited for; matrix products, arithmetic and copies ran while one was open for 26% of the time, Pallas kernels for 12%

commit v1 on v0

v1 whole, which is shorter than its diff:
```python
import functools
import math

import jax
import jax.numpy as jnp
from jax import lax
from jax.experimental import pallas as pl
from jax.experimental.pallas import tpu as pltpu
from jax.sharding import PartitionSpec as P

BF16, F32 = jnp.bfloat16, jnp.float32
MIB = 1024 * 1024
NT = (((1,), (1,)), ((), ()))
EPS = 1e-06


def room(need):
    return min(56 * MIB, need + 6 * MIB)


def vmem():
    return pl.BlockSpec(memory_space=pltpu.VMEM)


def smem():
    return pl.BlockSpec(memory_space=pltpu.SMEM)


def dot_nt(left, right):
    return lax.dot_general(left, right, NT, preferred_element_type=F32)


def normed(values, gain):
    mean = jnp.mean(values * values, axis=-1, keepdims=True)
    return values * lax.rsqrt(mean + EPS) * gain


def silu(values):
    return values / (1.0 + jnp.exp(-values))


def from_left(values):
    column = lax.broadcasted_iota(jnp.int32, values.shape, 0)
    return jnp.where(column == 0, 0.0, pltpu.roll(values, 1, 0))


def from_right(values):
    count = values.shape[0]
    column = lax.broadcasted_iota(jnp.int32, values.shape, 0)
    return jnp.where(column == count - 1, 0.0, pltpu.roll(values, count - 1, 0))


def rim_kernel(place, latent, cache, low, rim, cache_rim):
    frames = latent.shape[0]
    past, _, channels, columns = low.shape
    width = columns // 2
    rim[...] = latent[:, 0]
    cache_rim[:past] = cache[:, 0]
    pixel = lax.broadcasted_iota(jnp.int32, (width, columns), 0)
    column = lax.broadcasted_iota(jnp.int32, (width, columns), 1)
    for f in range(past):
        sides = [dot_nt((column == 2 * pixel + b).astype(BF16), low[f, 0]) for b in range(2)]
        cache_rim[past + f] = jnp.concatenate(sides, axis=-1).astype(BF16)


def edge_rows(place, latent, cache, low):
    frames, rows, width, channels = latent.shape
    past, high, low_channels, columns = low.shape

    def edge(count):
        return lambda i, place: (0, jnp.where(place[1] == 0, count - 1, 0), 0, 0)

    return pl.pallas_call(
        rim_kernel,
        grid_spec=pltpu.PrefetchScalarGridSpec(
            num_scalar_prefetch=1,
            grid=(1,),
            in_specs=[
                pl.BlockSpec((frames, 1, width, channels), edge(rows)),
                pl.BlockSpec((past, 1, width, channels), edge(rows)),
                pl.BlockSpec((past, 1, low_channels, columns), edge(high)),
            ],
            out_specs=[
                pl.BlockSpec((frames, width, channels), lambda i, place: (0, 0, 0)),
                pl.BlockSpec((2 * past, width, channels), lambda i, place: (0, 0, 0)),
            ],
        ),
        out_shape=[
            jax.ShapeDtypeStruct((frames, width, channels), BF16),
            jax.ShapeDtypeStruct((2 * past, width, channels), BF16),
        ],
        compiler_params=pltpu.CompilerParams(vmem_limit_bytes=room(16 * latent.nbytes)),
        name="edge_rows",
    )(place, latent, cache, low)


def weight_kernel(up, low, folded, turned):
    def fold(parts, a):
        return (parts[0], parts[1] + parts[2]) if a == 0 else (parts[0] + parts[1], parts[2])

    whole = [[up[dy, dx].astype(F32) for dx in range(3)] for dy in range(3)]
    for a in range(2):
        lines = [fold([whole[dy][dx] for dy in range(3)], a) for dx in range(3)]
        for b in range(2):
            pieces = []
            for i in range(2):
                pieces += fold([lines[dx][i] for dx in range(3)], b)
            folded[a, b] = jnp.concatenate(pieces, axis=-1).astype(BF16)
    taps, _, _, channels, part = low.shape
    first = lax.broadcasted_iota(jnp.int32, (part, part), 0)
    second = lax.broadcasted_iota(jnp.int32, (part, part), 1)
    same = (first == second).astype(BF16)
    blank = jnp.zeros((part, channels), F32)
    for k in range(taps):
        for dy in range(3):
            columns = [dot_nt(same, low[k, dy, dx]) for dx in range(3)]
            lanes = slice(dy * 4 * channels, (dy + 1) * 4 * channels)
            for b in range(2):
                row = [blank] * b + columns + [blank] * (1 - b)
                turned[(2 * k + b) * part : (2 * k + b + 1) * part, lanes] = jnp.concatenate(row, axis=-1).astype(BF16)


def weight_forms(up, low):
    taps, _, _, channels, part = low.shape
    return pl.pallas_call(
        weight_kernel,
        in_specs=[vmem()] * 2,
        out_specs=[vmem()] * 2,
        out_shape=[
            jax.ShapeDtypeStruct((2, 2, up.shape[2], 4 * up.shape[3]), BF16),
            jax.ShapeDtypeStruct((2 * taps * part, 12 * channels), BF16),
        ],
        compiler_params=pltpu.CompilerParams(vmem_limit_bytes=room(6 * up.nbytes + 6 * low.nbytes)),
        name="weight_forms",
    )(up, low)


def spread(row):
    return jnp.concatenate([from_left(row), row, from_right(row)], axis=-1).astype(BF16)


def tile_row(block, rims, f, l):
    rows = block.shape[1]
    if l == 0:
        return rims[0, f]
    if l == rows + 1:
        return rims[1, f]
    return block[f, l - 1]


def tap_rows(weights, dy):
    return jnp.concatenate([weights[0, dy, dx] for dx in range(3)], axis=-1)


def mid_kernel(past, place, latent, halo, gain, weights, own, passed, acc, seen):
    frames, rows, width, channels = latent.shape
    part = weights.shape[-2]
    size = rows * width
    tap = pl.program_id(0)

    @pl.when(tap == 0)
    def _():
        for f in range(frames):
            for l in range(rows + 2):
                row = tile_row(latent, halo, f, l).astype(F32)
                seen[f, l] = spread(silu(normed(row, gain[...])))
            mine = latent[f].astype(F32).reshape(size, channels)
            kept = mine[:, :part]
            for index in range(1, channels // part):
                kept = jnp.where(place[1] == index, mine[:, index * part : (index + 1) * part], kept)
            acc[f] = kept
        for f in range(frames, frames + past):
            acc[f] = jnp.zeros_like(acc[f])

    total = None
    for dy in range(3):
        left = jnp.concatenate(
            [seen[f, dy : dy + rows].reshape(size, 3 * channels) for f in range(frames)], axis=0
        )
        term = dot_nt(left, tap_rows(weights, dy))
        total = term if total is None else total + term
    for f in range(frames):
        acc[f + past - tap] += total[f * size : (f + 1) * size]

    @pl.when(tap == past)
    def _():
        own[...] = jnp.concatenate([acc[f] for f in range(frames)], axis=-1)
        passed[...] = jnp.concatenate([acc[frames + t] for t in range(past)], axis=-1).astype(BF16)


def mid_conv(place, latent, halo, gain, weights):
    frames, rows, width, channels = latent.shape
    taps, part = weights.shape[0], weights.shape[-2]
    past = taps - 1
    size = rows * width
    scratch = [
        pltpu.VMEM((frames + past, size, part), F32),
        pltpu.VMEM((frames, rows + 2, width, 3 * channels), BF16),
    ]
    need = 4 * latent.nbytes + 2 * weights.nbytes // taps + (frames + past) * size * 3 * part * 4
    return pl.pallas_call(
        functools.partial(mid_kernel, past),
        grid=(taps,),
        in_specs=[smem(), vmem(), vmem(), vmem(),
                  pl.BlockSpec((1, 3, 3, part, channels), lambda k: (k, 0, 0, 0, 0))],
        out_specs=[vmem(), vmem()],
        out_shape=[
            jax.ShapeDtypeStruct((size, frames * part), F32),
            jax.ShapeDtypeStruct((size, past * part), BF16),
        ],
        scratch_shapes=scratch,
        compiler_params=pltpu.CompilerParams(vmem_limit_bytes=room(need + 6 * latent.nbytes)),
        name="mid_conv",
    )(place, latent, halo, gain, weights)


def mid_cache_kernel(place, own, cache, halo, weights, out, seen):
    past, rows, width, channels = cache.shape
    part = weights.shape[-2]
    tap = pl.program_id(0)

    @pl.when(tap == 0)
    def _():
        out[...] = own[...]

    @pl.when(place[0] == 0)
    def _():
        @pl.when(tap == 0)
        def _():
            for f in range(past):
                for l in range(rows + 2):
                    seen[f, l] = spread(tile_row(cache, halo, f, l).astype(F32))

        for t in range(past):
            @pl.when(t + tap < past)
            def _(t=t):
                total = None
                for dy in range(3):
                    left = seen[t + tap, dy : dy + rows].reshape(rows * width, 3 * channels)
                    term = dot_nt(left, tap_rows(weights, dy))
                    total = term if total is None else total + term
                lanes = slice(t * part, (t + 1) * part)
                out[:, lanes] += total


def mid_cached(place, own, cache, halo, weights):
    past, rows, width, channels = cache.shape
    part = weights.shape[-2]
    return pl.pallas_call(
        mid_cache_kernel,
        grid=(past,),
        in_specs=[smem(), vmem(), vmem(), vmem(),
                  pl.BlockSpec((1, 3, 3, part, channels), lambda k: (k, 0, 0, 0, 0))],
        out_specs=vmem(),
        out_shape=jax.ShapeDtypeStruct(own.shape, F32),
        scratch_shapes=[pltpu.VMEM((past, rows + 2, width, 3 * channels), BF16)],
        compiler_params=pltpu.CompilerParams(
            vmem_limit_bytes=room(10 * cache.nbytes + 3 * own.nbytes + weights.nbytes)),
        cost_estimate=pl.CostEstimate(
            flops=6 * 9 * rows * width * channels * part, bytes_accessed=weights.nbytes, transcendentals=0),
        name="mid_cached",
    )(place, own, cache, halo, weights)


def attn_kernel(tile_rows, place, frame, gain, qkv, proj, out, normal, keys, values):
    count, size, channels = frame.shape
    width = size // tile_rows
    height = count * tile_rows
    rows = out.shape[0]
    step = 2
    scale = 1.0 / (math.sqrt(channels) * math.log(2.0))

    def prepare(index, carry):
        scaled = normed(frame[index].astype(F32), gain[...]).astype(BF16)
        normal[pl.ds(index * tile_rows, tile_rows)] = scaled.reshape(tile_rows, width, channels)
        both = jnp.dot(scaled, qkv[:, channels:], preferred_element_type=F32).astype(BF16)
        at = pl.ds(pl.multiple_of(index * size, 16), size)
        keys[at] = both[:, :channels]
        values[at] = both[:, channels:]
        return carry

    lax.fori_loop(0, count, prepare, 0)
    start = place[2] * tile_rows - 1
    for block in range(rows // step):
        spots = [start + block * step + i for i in range(step)]
        kept = [jnp.clip(spot, 0, height - 1) for spot in spots]
        inputs = jnp.concatenate([normal[spot] for spot in kept], axis=0)
        query = jnp.dot(inputs, qkv[:, :channels], preferred_element_type=F32).astype(BF16)
        scores = dot_nt(query, keys[...]) * scale
        powers = jnp.exp2(scores - jnp.max(scores, axis=-1, keepdims=True))
        total = jnp.sum(powers, axis=-1, keepdims=True)
        mixed = jnp.dot(powers.astype(BF16), values[...], preferred_element_type=F32) / total
        branch = jnp.dot(mixed.astype(BF16), proj[...], preferred_element_type=F32)
        for i in range(step):
            inside = (spots[i] >= 0) & (spots[i] < height)
            owner, line = kept[i] // tile_rows, kept[i] % tile_rows
            skipped = frame[owner, pl.ds(pl.multiple_of(line * width, 16), width)]
            summed = skipped.astype(F32) + branch[i * width : (i + 1) * width]
            out[block * step + i] = jnp.where(inside, summed, 0.0).astype(BF16)


def attention(place, frame, gain, qkv, proj, tile_rows):
    count, size, channels = frame.shape
    width = size // tile_rows
    pixels = count * size
    rows = tile_rows + 2
    need = 4 * frame.nbytes + 2 * width * pixels * 16 + 2 * qkv.nbytes
    return pl.pallas_call(
        functools.partial(attn_kernel, tile_rows),
        in_specs=[smem()] + [vmem()] * 4,
        out_specs=vmem(),
        out_shape=jax.ShapeDtypeStruct((rows, width, channels), BF16),
        scratch_shapes=[
            pltpu.VMEM((count * tile_rows, width, channels), BF16),
            pltpu.VMEM((pixels, channels), BF16),
            pltpu.VMEM((pixels, channels), BF16),
        ],
        compiler_params=pltpu.CompilerParams(vmem_limit_bytes=room(need)),
        name="frame_attention",
    )(place, frame, gain, qkv, proj)


def windowed(left, right):
    return jnp.concatenate([from_left(right), left, right, from_right(left)], axis=-1).astype(BF16)


def stacked(block, high):
    width, lanes = block.shape[-2:]
    return jnp.concatenate([block[dy : dy + high].reshape(high * width, lanes) for dy in range(3)], axis=-1)


def low_kernel(past, place, tile, up, gain, weights, own, passed, seen, upper, window, kept, acc):
    frames, ext, width, channels = tile.shape
    chans, _, _, part = up.shape[:4]
    low = chans * part
    rows = ext - 2
    high = 2 * rows
    phases = own.shape[1]
    line = lax.broadcasted_iota(jnp.int32, (phases, 2 * low), 0)
    spot = lax.broadcasted_iota(jnp.int32, (phases, 2 * low), 1)
    shift = place[1] * part
    picked = spot == jnp.where(line < part, line + shift, line - part + shift + low)
    select = picked.astype(F32).astype(BF16)

    for f in range(frames):
        for l in range(ext):
            seen[f, l] = spread(tile[f, l].astype(F32))
        for a in range(2):
            for b in range(2):
                lanes = slice(b * channels, (b + 2) * channels)
                span = (ext - 1) * width
                top = seen[f, : ext - 1, :, lanes].reshape(span, 2 * channels)
                bottom = seen[f, 1:, :, lanes].reshape(span, 2 * channels)
                folded = jnp.concatenate([up[c, a, b] for c in range(chans)], axis=0)
                got = dot_nt(top, folded[:, : 2 * channels]) + dot_nt(bottom, folded[:, 2 * channels :])
                for p in range(ext - 1):
                    upper[2 * p + 1 - a, b] = got[p * width : (p + 1) * width].astype(BF16)
        for j in range(high + 2):
            sides = [upper[j, b].astype(F32) for b in range(2)]
            if 1 <= j <= high:
                kept[f, j - 1] = jnp.concatenate(sides, axis=-1).astype(BF16)
            sides = [silu(normed(side, gain[...])) for side in sides]
            if j == 0:
                sides = [jnp.where(place[2] == 0, 0.0, side) for side in sides]
            if j == high + 1:
                sides = [jnp.where(place[2] == place[3] - 1, 0.0, side) for side in sides]
            window[f, j] = windowed(*sides)

    for f in range(frames):
        acc[f] = dot_nt(select, kept[f].reshape(high * width, 2 * low))
    for f in range(frames, frames + past):
        acc[f] = jnp.zeros_like(acc[f])
    for f in range(frames):
        got = dot_nt(weights[...], stacked(window[f], high))
        for tap in range(past + 1):
            acc[f + past - tap] += got[tap * phases : (tap + 1) * phases]
    for t in range(past):
        passed[t] = acc[frames + t].astype(BF16)
    for f in range(frames):
        own[f] = acc[f]


def low_stage(place, tile, up, gain, weights, taps):
    frames, ext, width, channels = tile.shape
    chans, _, _, part = up.shape[:4]
    low = chans * part
    high = 2 * (ext - 2)
    past = taps - 1
    phases = 2 * part
    scratch = [
        pltpu.VMEM((frames, ext, width, 3 * channels), BF16),
        pltpu.VMEM((high + 2, 2, width, low), BF16),
        pltpu.VMEM((frames, high + 2, width, 4 * low), BF16),
        pltpu.VMEM((frames, high, width, 2 * low), BF16),
        pltpu.VMEM((frames + past, phases, high * width), F32),
    ]
    need = 5 * tile.nbytes + up.nbytes + 2 * weights.nbytes + 12 * frames * high * width * low * 4
    return pl.pallas_call(
        functools.partial(low_kernel, past),
        in_specs=[smem()] + [vmem()] * 4,
        out_specs=[vmem(), vmem()],
        out_shape=[
            jax.ShapeDtypeStruct((frames, phases, high * width), F32),
            jax.ShapeDtypeStruct((past, phases, high * width), BF16),
        ],
        scratch_shapes=scratch,
        compiler_params=pltpu.CompilerParams(vmem_limit_bytes=room(need)),
        name="low_stage",
    )(place, tile, up, gain, weights)


def low_cache_kernel(place, own, cache, halo, weights, out, window):
    past, high, channels, columns = cache.shape
    width = columns // 2
    phases = own.shape[1]
    out[...] = own[...]

    @pl.when(place[0] == 0)
    def _():
        pixel = lax.broadcasted_iota(jnp.int32, (width, columns), 0)
        column = lax.broadcasted_iota(jnp.int32, (width, columns), 1)
        picks = [(column == 2 * pixel + b).astype(BF16) for b in range(2)]
        for f in range(past):
            for j in range(high + 2):
                if 1 <= j <= high:
                    sides = [dot_nt(pick, cache[f, j - 1]) for pick in picks]
                else:
                    rim = halo[0 if j == 0 else 1, f].astype(F32)
                    sides = [rim[:, :channels], rim[:, channels:]]
                window[j] = windowed(*sides)
            got = dot_nt(weights[: (f + 1) * phases], stacked(window[...], high))
            for tap in range(f + 1):
                out[f - tap] += got[tap * phases : (tap + 1) * phases]


def low_cached(place, own, cache, halo, weights):
    past, high, channels, columns = cache.shape
    pixels = high * columns
    return pl.pallas_call(
        low_cache_kernel,
        in_specs=[smem()] + [vmem()] * 4,
        out_specs=vmem(),
        out_shape=jax.ShapeDtypeStruct(own.shape, F32),
        scratch_shapes=[pltpu.VMEM((high + 2, columns // 2, 4 * channels), BF16)],
        compiler_params=pltpu.CompilerParams(
            vmem_limit_bytes=room(3 * own.nbytes + 2 * weights.nbytes + 16 * cache.nbytes)),
        cost_estimate=pl.CostEstimate(
            flops=6 * 9 * pixels * channels * own.shape[1] // 2, bytes_accessed=weights.nbytes, transcendentals=0),
        name="low_cached",
    )(place, own, cache, halo, weights)


def lane_windows(high, width):
    starts = [width * i // 128 * 128 for i in range(high)]
    span = max(width * i - start + width for i, start in enumerate(starts))
    span = min(-(-span // 128) * 128, high * width)
    starts = [min(start, high * width - span) for start in starts]
    return starts, span


def weaver(high, width):
    starts, span = lane_windows(high, width)
    lane = lax.broadcasted_iota(jnp.int32, (span, 2 * width), 0)
    column = lax.broadcasted_iota(jnp.int32, (span, 2 * width), 1)
    blocks = []
    for i, start in enumerate(starts):
        pixel = lane - (width * i - start)
        blocks.append([(column == 2 * pixel + b).astype(BF16) for b in range(2)])
    return jnp.stack([jnp.concatenate(pair, axis=0) for pair in blocks])


def finish_kernel(starts, own, passed, weave, out):
    frames = own.shape[0]
    half = own.shape[1] // 2
    span = weave.shape[1] // 2
    totals = []
    for f in range(frames):
        total = own[f]
        if f < passed.shape[0]:
            total = total + passed[f].astype(F32)
        totals.append(total.astype(BF16))
    for i, start in enumerate(starts):
        lanes = slice(start, start + span)
        sides = [jnp.concatenate([total[:half, lanes], total[half:, lanes]], axis=-1) for total in totals]
        woven = jnp.dot(jnp.concatenate(sides, axis=0), weave[i], preferred_element_type=F32).astype(BF16)
        for f in range(frames):
            out[f, i] = woven[f * half : (f + 1) * half]


def finish(own, passed, weave, high, width):
    frames, phases = own.shape[:2]
    starts, _ = lane_windows(high, width)
    return pl.pallas_call(
        functools.partial(finish_kernel, starts),
        in_specs=[vmem()] * 3,
        out_specs=vmem(),
        out_shape=jax.ShapeDtypeStruct((frames, high, phases // 2, 2 * width), BF16),
        compiler_params=pltpu.CompilerParams(vmem_limit_bytes=room(4 * own.nbytes + 2 * weave.nbytes)),
        name="finish",
    )(own, passed, weave)


def to_neighbour(values, only_first):
    rows, chans = lax.axis_size("rows"), lax.axis_size("chan")
    segments = 1 if only_first else lax.axis_size("segment")
    route = []
    for z in range(rows - 1):
        for x in range(segments):
            low, high = [(q * lax.axis_size("segment") + x) * chans for q in (z, z + 1)]
            route += [(low, high), (high + 1, low + 1)]
    return lax.ppermute(values, ("rows", "segment", "chan"), route)


def to_next(values):
    count = lax.axis_size("segment")
    return lax.ppermute(values, "segment", [(i, i + 1) for i in range(count - 1)])


def body(
    latent,
    cache_mid,
    cache_low,
    gain_mid,
    gain_attn,
    gain_low,
    conv_mid,
    attn_qkv,
    attn_proj,
    conv_up,
    conv_low,
):
    chan = lax.axis_index("chan")
    place = jnp.stack(
        [lax.axis_index("segment"), chan, lax.axis_index("rows"), jnp.int32(lax.axis_size("rows"))]
    ).astype(jnp.int32)
    frames, rows, width, channels = latent.shape
    part = conv_mid.shape[-1]
    taps = conv_mid.shape[0]
    past = taps - 1
    high = 2 * rows
    mid_weights = jnp.swapaxes(conv_mid, 3, 4)
    low_cache = jnp.swapaxes(cache_low, 2, 3)

    rim, cache_rim = edge_rows(place, latent, cache_mid, low_cache)
    halo = to_neighbour(rim, False)
    cache_halo = to_neighbour(cache_rim, True)
    up_part, low_weights = weight_forms(jnp.swapaxes(conv_up, 2, 3), conv_low)
    up = lax.all_gather(up_part, "chan")
    halo = lax.all_gather(halo, "chan")

    own, passed = mid_conv(place, latent, halo, gain_mid[None], mid_weights)
    arrived = to_next(passed)
    cache_halo, own = lax.optimization_barrier((cache_halo, own))
    cache_halo = lax.all_gather(cache_halo, "chan")
    own = mid_cached(place, own, cache_mid, cache_halo[:, :past], mid_weights)
    first_part = (own + jnp.pad(arrived, ((0, 0), (0, (frames - past) * part))).astype(F32)).astype(BF16)
    both = lax.all_gather(first_part, "chan")
    chans = both.shape[0]
    choices = [
        jnp.concatenate([both[c, :, f * part : (f + 1) * part] for c in range(chans)], axis=-1)
        for f in range(frames)
    ]
    mine = choices[0]
    for f in range(1, frames):
        mine = jnp.where(chan == f, choices[f], mine)
    frame = lax.all_gather(mine, "rows")

    reached = attention(place, frame, gain_attn[None], attn_qkv, attn_proj, rows)
    tile = lax.all_gather(reached, "chan")

    own_low, passed_low = low_stage(place, tile, up, gain_low[None], low_weights, taps)
    arrived_low = to_next(passed_low)
    own_low = low_cached(place, own_low, low_cache, cache_halo[:, past:], low_weights)
    out = finish(own_low, arrived_low, weaver(high, width), high, width)
    return jnp.swapaxes(out, 2, 3)


def solution(mesh):
    placed = (
        P(("groups", "segment"), "rows", None, None),
        P("groups", "rows", None, None),
        P("groups", "rows", None, None),
        P(),
        P(),
        P(),
        P(None, None, None, None, "chan"),
        P(),
        P(),
        P(None, None, None, "chan"),
        P(None, None, None, None, "chan"),
    )
    return jax.shard_map(
        body,
        mesh=mesh,
        in_specs=placed,
        out_specs=P(("groups", "segment"), "rows", None, "chan"),
        check_vma=False,
    )
```

time: 166 us -> 113 us (0.68)
  other arithmetic: 24.6 us -> 4.26 us
  local copies, waits for them, and re-layouts: 25.6 us -> 10.7 us
  blocking collectives: 37 us -> 30.8 us
  Pallas kernels: 39 us -> 33.9 us
  waiting for transfers between devices: 9.84 us -> 5.36 us
    another operation x10 -> x1, other arithmetic: 5.92 us -> 0.08 us  [body(): jnp.stack([lax.axis_index('segment'), chan, lax.axis_index('rows'), jnp.i...]
    transpose x1 -> x0, local copies, waits for them, and re-layouts: 5.37 us -> none  [low_weights(): both = both.transpose(0, 1, 3, 2, 4)]
    slice x4 -> x2, local copies, waits for them, and re-layouts: 5 us -> 0.26 us  [the longest x1 0.16 us: body(): both[c, :, f * part:(f + 1) * part]]
    ppermute x2, waiting for transfers between devices: 9.81 us -> 5.33 us  [to_next(): lax.ppermute(values, 'segment', [(i, i + 1) for i in range(count - 1)])]
    select_n x3 -> x1, other arithmetic: 4.5 us -> 0.18 us  [body(): mine = jnp.where(chan == f, choices[f], mine)]
    all_to_all x1 -> x0, blocking collectives: 4 us -> none  [body(): lax.all_to_all(first_part, 'chan', split_axis=0, concat_axis=3, tiled=True)]
    ppermute x3 -> x2, starting transfers between devices: 12.6 us -> 9.19 us  [to_neighbour(): return lax.ppermute(values, ('rows', 'segment', 'chan'), route)]
    pallas_call x3 -> x7, Pallas kernels: 35.6 us -> 32.5 us  [the longest x1 8.87 us: low_stage(): pl.pallas_call(functools.partial(low_kernel, past), in_specs=[smem()] + [...]
  transfers between devices with their start and end apart: 6 -> 5, of which waited for: 1 -> 1; matrix products, arithmetic and copies ran while one was open for 26% -> 4% of each run, Pallas kernels for 12% -> 19%
where the time goes in v1:
time: 113 us
  Pallas kernels  33.9 us (30%)
  blocking collectives  30.8 us (27%)
  starting transfers between devices  14 us (12%)
  between operations  13.7 us (12%)
  local copies, waits for them, and re-layouts  10.7 us (9%)
  waiting for transfers between devices  5.36 us (5%)
  other arithmetic  4.26 us (4%)
    all_gather x1, blocking collectives, body(): frame = lax.all_gather(mine, 'rows')  20.7 us
    unnamed x46, local copies, waits for them, and re-layouts  10.5 us
    ppermute x2, starting transfers between devices, to_neighbour(): return lax.ppermute(values, ('rows', 'segment', 'chan'), route)  9.19 us
    pallas_call x1, Pallas kernels, low_stage(): pl.pallas_call(functools.partial(low_kernel, past), in_specs=[smem()] + [...  8.87 us
    pallas_call x1, Pallas kernels, mid_conv(): pl.pallas_call(functools.partial(mid_kernel, past), grid=(taps,), in_spec...  6.51 us
    pallas_call x1, Pallas kernels, attention(): pl.pallas_call(functools.partial(attn_kernel, tile_rows), in_specs=[smem(...  6.14 us
    ppermute x2, waiting for transfers between devices, to_next(): lax.ppermute(values, 'segment', [(i, i + 1) for i in range(count - 1)])  5.33 us
    ppermute x2, starting transfers between devices, to_next(): lax.ppermute(values, 'segment', [(i, i + 1) for i in range(count - 1)])  4.79 us
  transfers between devices with their start and end apart: 5, of which 1 were waited for; matrix products, arithmetic and copies ran while one was open for 4% of the time, Pallas kernels for 19%

profile of v1, /device:TPU:0, one launch (start us, length us, event | category | flops | bytes accessed | tf_op | source)
XLA Modules:
  0.0 112.8 jit_solution(17051721936894764114)
XLA Ops:
  6.6 1.3 %copy-done.2 = bf16[2,4,320,192]{2,3,1,0:T(8,128)(2,1)S(1)} copy-done((bf16[2,4,320,192]{2,3,1,0:T(8,128)(2,1)S(1)}, bf16[2,4,320,192]{2,3,1,0:T(8,128)(2,1)}, u32[]{:S(2)}) %copy-start.2) | copy-done | bytes 983064
  7.9 1.0 copy-done.6
  8.9 1.0 copy-done.8
  10.0 1.8 %edge_rows.1 = (bf16[2,160,384]{2,1,0:T(8,128)(2,1)S(1)}, bf16[4,160,384]{2,1,0:T(8,128)(2,1)}) custom-call(s32[4]{0:T(128)S(1)} %pad_add_fusion.place, bf16[2,2,160,384]{3,2,1,0:T(8,128)(2,1)S(1)} %copy-done.6, bf16[2,2,160,384]{3,2,1,0:T(8,128)(2,1)S(1)} %copy-done.8, bf16[2,4,192,320]{3,2,1,0:T(8,128)(2,1)S(1)} %bitcast.23), custom_call_target="tpu_custom_call" | custom-call | tf_op jit(solution)/shard_map/edge_rows/pallas_call | solution.py:73
  11.8 5.6 %collective-permute-start.1 = (bf16[2,160,384]{2,1,0:T(8,128)(2,1)S(1)}, bf16[2,160,384]{2,1,0:T(8,128)(2,1)}, u32[]{:S(2)}, u32[]{:S(2)}) collective-permute-start(bf16[2,160,384]{2,1,0:T(8,128)(2,1)S(1)} %get-tuple-element.16), channel_id=1, source_target_pairs={{0,4},{5,1},{2,6},{7,3},{4,8},{9,5},{6,10},{11,7},{8,12},{13,9},{1... | collective-permute-start | bytes 737288 | tf_op jit(solution)/shard_map/ppermute | solution.py:511
  17.4 3.6 %collective-permute-start = (bf16[4,160,384]{2,1,0:T(8,128)(2,1)}, bf16[4,160,384]{2,1,0:T(8,128)(2,1)}, u32[]{:S(2)}, u32[]{:S(2)}) collective-permute-start(bf16[4,160,384]{2,1,0:T(8,128)(2,1)} %get-tuple-element.15), channel_id=1, source_target_pairs={{0,4},{5,1},{4,8},{9,5},{8,12},{13,9},{16,20},{21,17},{20,24},{25,... | collective-permute-start | bytes 1474568 | tf_op jit(solution)/shard_map/ppermute | solution.py:511
  21.0 1.4 %weight_forms.1 = (bf16[2,2,96,1536]{3,2,1,0:T(8,128)(2,1)S(1)}, bf16[576,2304]{1,0:T(8,128)(2,1)S(1)}) custom-call(bf16[3,3,96,384]{3,2,1,0:T(8,128)(2,1)S(1)} %bitcast.28, bf16[3,3,3,192,96]{4,3,2,1,0:T(8,128)(2,1)S(1)} %copy-done.10), custom_call_target="tpu_custom_call" | custom-call | tf_op jit(solution)/shard_map/weight_forms/pallas_call | solution.py:125
  22.4 1.0 copy-done.11
  23.7 0.7 add_bitcast_fusion
  24.6 0.7 add_bitcast_fusion.1
  25.3 0.8 iota_compare_fusion.2
  26.2 0.8 iota_compare_fusion
  27.0 2.4 %all-gather = bf16[4,160,384]{2,1,0:T(8,128)(2,1)S(1)} all-gather(bf16[2,160,384]{2,1,0:T(8,128)(2,1)} %collective-permute-done.1), channel_id=2, replica_groups=mesh['groups'=2,'rows'=4,'segment'=2,'chan'=2] {'chan'}, dimensions={0}, use_global_device_ids=true | all-gather | bytes 737280 | tf_op jit(solution)/shard_map/all_gather | solution.py:549
  29.4 2.5 %copy-done = bf16[3,3,3,384,192]{3,4,2,1,0:T(8,128)(2,1)S(1)} copy-done((bf16[3,3,3,384,192]{3,4,2,1,0:T(8,128)(2,1)S(1)}, bf16[3,3,3,384,192]{3,4,2,1,0:T(8,128)(2,1)}, u32[]{:S(2)}) %copy-start) | copy-done | bytes 3981336
  31.8 6.5 %mid_conv.1 = (f32[320,384]{1,0:T(8,128)S(1)}, bf16[320,384]{1,0:T(8,128)(2,1)S(1)}) custom-call(s32[4]{0:T(128)S(1)} %pad_add_fusion.place, bf16[2,2,160,384]{3,2,1,0:T(8,128)(2,1)S(1)} %copy-done.7, bf16[2,2,160,384]{3,2,1,0:T(8,128)(2,1)S(1)} %bitcast.27, f32[1,384]{1,0:T(1,128)S(1)} %broadcast_in_dim.9.gain, bf16[3,3,3,192,384]{4,3,2,1,0:T(8,128)(2,1)S(1)} %bitcast.21), custom_call_target="tpu_custom_call" | custom-call | tf_op jit(solution)/shard_map/mid_conv/pallas_call | solution.py:201
  38.4 1.4 %collective-permute-start.2 = (bf16[320,384]{1,0:T(8,128)(2,1)S(1)}, bf16[320,384]{1,0:T(8,128)(2,1)S(1)}, u32[]{:S(2)}, u32[]{:S(2)}) collective-permute-start(bf16[320,384]{1,0:T(8,128)(2,1)S(1)} %get-tuple-element.20), channel_id=1, source_target_pairs={{0,2},{1,3},{4,6},{5,7},{8,10},{9,11},{12,14},{13,15},{16,18},{17,... | collective-permute-start | bytes 737288 | tf_op jit(solution)/shard_map/ppermute | solution.py:516
  39.8 2.9 %all-gather.1 = bf16[8,160,384]{2,1,0:T(8,128)(2,1)S(1)} all-gather(bf16[4,160,384]{2,1,0:T(8,128)(2,1)} %collective-permute-done), channel_id=3, replica_groups=mesh['groups'=2,'rows'=4,'segment'=2,'chan'=2] {'chan'}, dimensions={0}, use_global_device_ids=true | all-gather | bytes 1474560 | tf_op jit(solution)/shard_map/all_gather | solution.py:554
  42.8 3.7 %mid_cached.1 = f32[320,384]{1,0:T(8,128)S(1)} custom-call(s32[4]{0:T(128)S(1)} %pad_add_fusion.place, f32[320,384]{1,0:T(8,128)S(1)} %get-tuple-element.18.own, bf16[2,2,160,384]{3,2,1,0:T(8,128)(2,1)S(1)} %copy-done.9, bf16[2,2,160,384]{3,2,1,0:T(8,128)(2,1)S(1)} %get-tuple-element.26.halo, bf16[3,3,3,192,384]{4,3,2,1,0:T(8,128)(2,1)S(1)} %bitcast.22), custom_call_target="tpu_custom_call" | custom-call | flops 1274019840 | bytes 3981312 | tf_op jit(solution)/shard_map/mid_cached/pallas_call | solution.py:249
  46.5 2.2 %all-gather.2 = bf16[640,384]{1,0:T(8,128)(2,1)S(1)} all-gather(bf16[320,384]{1,0:T(8,128)(2,1)S(1)} %add_convert_fusion.1), channel_id=4, replica_groups=mesh['groups'=2,'rows'=4,'segment'=2,'chan'=2] {'chan'}, dimensions={0}, use_global_device_ids=true | all-gather | bytes 737280 | tf_op jit(solution)/shard_map/all_gather | solution.py:557
  48.9 0.2 maximum_select_fusion
  49.0 20.7 %all_gather.40.frame = bf16[4,320,384]{2,1,0:T(8,128)(2,1)S(1)} all-gather(bf16[1,320,384]{2,1,0:T(8,128)(2,1)S(1)} %maximum_select_fusion), channel_id=1, replica_groups=mesh['groups'=2,'rows'=4,'segment'=2,'chan'=2] {'rows'}, dimensions={0}, use_global_device_ids=true | all-gather | bytes 1228800 | tf_op jit(solution)/shard_map/all_gather | solution.py:566
  69.7 6.1 %frame_attention.1 = bf16[4,160,384]{2,1,0:T(8,128)(2,1)S(1)} custom-call(s32[4]{0:T(128)S(1)} %pad_add_fusion.place, bf16[4,320,384]{2,1,0:T(8,128)(2,1)S(1)} %all_gather.40.frame, f32[1,384]{1,0:T(1,128)S(1)} %broadcast_in_dim.10.gain, bf16[384,1152]{1,0:T(8,128)(2,1)S(1)} %copy-done.12, bf16[384,384]{1,0:T(8,128)(2,1)S(1)} %copy-done.14), custom_call_target="tpu_custom_call" | custom-call | tf_op jit(solution)/shard_map/frame_attention/pallas_call | solution.py:308
  75.8 2.8 %all-gather.3 = bf16[8,160,384]{2,1,0:T(8,128)(2,1)} all-gather(bf16[4,160,384]{2,1,0:T(8,128)(2,1)S(1)} %frame_attention.1), channel_id=5, replica_groups=mesh['groups'=2,'rows'=4,'segment'=2,'chan'=2] {'chan'}, dimensions={0}, use_global_device_ids=true | all-gather | bytes 1474560 | tf_op jit(solution)/shard_map/all_gather | solution.py:569
  78.7 1.2 %copy-done.4 = bf16[8,160,384]{2,1,0:T(8,128)(2,1)S(1)} copy-done((bf16[8,160,384]{2,1,0:T(8,128)(2,1)S(1)}, bf16[8,160,384]{2,1,0:T(8,128)(2,1)}, u32[]{:S(2)}) %copy-start.4) | copy-done | bytes 983064
  79.9 1.7 %copy-done.5 = bf16[4,2,96,1536]{3,2,1,0:T(8,128)(2,1)S(1)} copy-done((bf16[4,2,96,1536]{3,2,1,0:T(8,128)(2,1)S(1)}, bf16[4,2,96,1536]{3,2,1,0:T(8,128)(2,1)}, u32[]{:S(2)}) %copy-start.5) | copy-done | bytes 2359320
  81.6 8.9 %low_stage.1 = (f32[2,192,640]{2,1,0:T(8,128)S(1)}, bf16[2,192,640]{2,1,0:T(8,128)(2,1)S(1)}) custom-call(s32[4]{0:T(128)S(1)} %pad_add_fusion.place, bf16[2,4,160,384]{3,2,1,0:T(8,128)(2,1)S(1)} %bitcast.25, bf16[2,2,2,96,1536]{4,3,2,1,0:T(8,128)(2,1)S(1)} %bitcast.26, f32[1,192]{1,0:T(1,128)S(1)} %bitcast.29, bf16[576,2304]{1,0:T(8,128)(2,1)S(1)} %get-tuple-element.22.weights), custom_call_target="tpu_custom_call" | custom-call | tf_op jit(solution)/shard_map/low_stage/pallas_call | solution.py:398
  90.4 3.4 %collective-permute-start.3 = (bf16[2,192,640]{2,1,0:T(8,128)(2,1)S(1)}, bf16[2,192,640]{2,1,0:T(8,128)(2,1)S(1)}, u32[]{:S(2)}, u32[]{:S(2)}) collective-permute-start(bf16[2,192,640]{2,1,0:T(8,128)(2,1)S(1)} %get-tuple-element.24), channel_id=1, source_target_pairs={{0,2},{1,3},{4,6},{5,7},{8,10},{9,11},{12,14},{13,15},{16,18},{17,... | collective-permute-start | bytes 1474568 | tf_op jit(solution)/shard_map/ppermute | solution.py:516
  94.1 0.3 add_convert_fusion.weave
  94.4 0.7 copy-done.3
  95.1 4.1 %low_cached.1.own = f32[2,192,640]{2,1,0:T(8,128)S(1)} custom-call(s32[4]{0:T(128)S(1)} %pad_add_fusion.place, f32[2,192,640]{2,1,0:T(8,128)S(1)} %get-tuple-element.23.own, bf16[2,4,192,320]{3,2,1,0:T(8,128)(2,1)S(1)} %bitcast.24, bf16[2,2,160,384]{3,2,1,0:T(8,128)(2,1)S(1)} %get-tuple-element.25.halo, bf16[576,2304]{1,0:T(8,128)(2,1)S(1)} %get-tuple-element.22.weights), custom_call_target="tpu_custom_call" | custom-call | flops 1274019840 | bytes 2654208 | tf_op jit(solution)/shard_map/low_cached/pallas_call | solution.py:439
  99.2 5.3 %collective-permute-done.3.passed = bf16[2,192,640]{2,1,0:T(8,128)(2,1)S(1)} collective-permute-done((bf16[2,192,640]{2,1,0:T(8,128)(2,1)S(1)}, bf16[2,192,640]{2,1,0:T(8,128)(2,1)S(1)}, u32[]{:S(2)}, u32[]{:S(2)}) %collective-permute-start.3) | collective-permute-done | bytes 491552 | tf_op jit(solution)/shard_map/ppermute | solution.py:516
  104.6 1.4 %finish.1 = bf16[2,4,96,320]{3,2,1,0:T(8,128)(2,1)} custom-call(f32[2,192,640]{2,1,0:T(8,128)S(1)} %low_cached.1.own, bf16[2,192,640]{2,1,0:T(8,128)(2,1)S(1)} %collective-permute-done.3.passed, bf16[4,512,320]{2,1,0:T(8,128)(2,1)S(1)} %add_convert_fusion.weave), custom_call_target="tpu_custom_call" | custom-call | tf_op jit(solution)/shard_map/finish/pallas_call | solution.py:493
  (62 shorter events, 1.0 us)
Async XLA Ops:
  6.5 72.1 %all-gather.7.cloned.1.call-start = ((), (), s32[]{:S(2)}) async-start(), calls=%async_computation | async-start | bytes 3538944 | tf_op jit(solution)/shard_map/all_gather | solution.py:548
  6.6 1.3 %copy-start.2 = (bf16[2,4,320,192]{2,3,1,0:T(8,128)(2,1)S(1)}, bf16[2,4,320,192]{2,3,1,0:T(8,128)(2,1)}, u32[]{:S(2)}) copy-start(bf16[2,4,320,192]{2,3,1,0:T(8,128)(2,1)} %param.13) | copy-start | bytes 2949124
  7.9 1.0 copy-start.6
  8.9 1.0 copy-start.8
  9.9 11.0 %copy-start.10 = (bf16[3,3,3,192,96]{4,3,2,1,0:T(8,128)(2,1)S(1)}, bf16[3,3,3,192,96]{4,3,2,1,0:T(8,128)(2,1)}, u32[]{:S(2)}) copy-start(bf16[3,3,3,192,96]{4,3,2,1,0:T(8,128)(2,1)} %low.1) | copy-start | bytes 2985988
  9.9 11.0 %copy-start.13 = (bf16[3,3,384,96]{2,3,1,0:T(8,128)(2,1)S(1)}, bf16[3,3,384,96]{2,3,1,0:T(8,128)(2,1)}, u32[]{:S(2)}) copy-start(bf16[3,3,384,96]{2,3,1,0:T(8,128)(2,1)} %param.20) | copy-start | bytes 1990660
  11.8 15.2 %collective-permute-start.1 = (bf16[2,160,384]{2,1,0:T(8,128)(2,1)S(1)}, bf16[2,160,384]{2,1,0:T(8,128)(2,1)}, u32[]{:S(2)}, u32[]{:S(2)}) collective-permute-start(bf16[2,160,384]{2,1,0:T(8,128)(2,1)S(1)} %get-tuple-element.16), channel_id=1, source_target_pairs={{0,4},{5,1},{2,6},{7,3},{4,8},{9,5},{6,10},{11,7},{8,12},{13,9},{1... | collective-permute-start | bytes 737288 | tf_op jit(solution)/shard_map/ppermute | solution.py:511
  17.4 22.4 %collective-permute-start = (bf16[4,160,384]{2,1,0:T(8,128)(2,1)}, bf16[4,160,384]{2,1,0:T(8,128)(2,1)}, u32[]{:S(2)}, u32[]{:S(2)}) collective-permute-start(bf16[4,160,384]{2,1,0:T(8,128)(2,1)} %get-tuple-element.15), channel_id=1, source_target_pairs={{0,4},{5,1},{4,8},{9,5},{8,12},{13,9},{16,20},{21,17},{20,24},{25,... | collective-permute-start | bytes 1474568 | tf_op jit(solution)/shard_map/ppermute | solution.py:511
  22.4 1.0 copy-start.11
  23.4 2.7 %copy-start.21 = (f32[384]{0:T(512)S(1)}, f32[384]{0:T(512)}, u32[]{:S(2)}) copy-start(f32[384]{0:T(512)} %param.14) | copy-start | bytes 4612
  23.4 2.7 %copy-start.22 = (f32[384]{0:T(512)S(1)}, f32[384]{0:T(512)}, u32[]{:S(2)}) copy-start(f32[384]{0:T(512)} %param.15) | copy-start | bytes 4612
  23.4 6.0 %copy-start.7 = (bf16[2,2,160,384]{3,2,1,0:T(8,128)(2,1)S(1)}, bf16[2,2,160,384]{3,2,1,0:T(8,128)(2,1)}, u32[]{:S(2)}) copy-start(bf16[2,2,160,384]{3,2,1,0:T(8,128)(2,1)} %latent.3) | copy-start | bytes 1474564
  29.4 2.5 %copy-start = (bf16[3,3,3,384,192]{3,4,2,1,0:T(8,128)(2,1)S(1)}, bf16[3,3,3,384,192]{3,4,2,1,0:T(8,128)(2,1)}, u32[]{:S(2)}) copy-start(bf16[3,3,3,384,192]{3,4,2,1,0:T(8,128)(2,1)} %param.17) | copy-start | bytes 11943940
  31.8 10.9 %copy-start.1 = (bf16[3,3,3,384,192]{3,4,2,1,0:T(8,128)(2,1)S(1)}, bf16[3,3,3,384,192]{3,4,2,1,0:T(8,128)(2,1)}, u32[]{:S(2)}) copy-start(bf16[3,3,3,384,192]{3,4,2,1,0:T(8,128)(2,1)} %param.17) | copy-start | bytes 11943940
  38.4 8.1 %collective-permute-start.2 = (bf16[320,384]{1,0:T(8,128)(2,1)S(1)}, bf16[320,384]{1,0:T(8,128)(2,1)S(1)}, u32[]{:S(2)}, u32[]{:S(2)}) collective-permute-start(bf16[320,384]{1,0:T(8,128)(2,1)S(1)} %get-tuple-element.20), channel_id=1, source_target_pairs={{0,2},{1,3},{4,6},{5,7},{8,10},{9,11},{12,14},{13,15},{16,18},{17,... | collective-permute-start | bytes 737288 | tf_op jit(solution)/shard_map/ppermute | solution.py:516
  39.8 3.0 %copy-start.9 = (bf16[2,2,160,384]{3,2,1,0:T(8,128)(2,1)S(1)}, bf16[2,2,160,384]{3,2,1,0:T(8,128)(2,1)}, u32[]{:S(2)}) copy-start(bf16[2,2,160,384]{3,2,1,0:T(8,128)(2,1)} %cache.3) | copy-start | bytes 1474564
  48.7 21.0 %copy-start.12 = (bf16[384,1152]{1,0:T(8,128)(2,1)S(1)}, bf16[384,1152]{1,0:T(8,128)(2,1)}, u32[]{:S(2)}) copy-start(bf16[384,1152]{1,0:T(8,128)(2,1)} %qkv.1) | copy-start | bytes 2654212
  48.7 21.0 %copy-start.14 = (bf16[384,384]{1,0:T(8,128)(2,1)S(1)}, bf16[384,384]{1,0:T(8,128)(2,1)}, u32[]{:S(2)}) copy-start(bf16[384,384]{1,0:T(8,128)(2,1)} %proj.1) | copy-start | bytes 884740
  69.7 9.0 %copy-start.15 = (f32[192]{0:T(256)S(1)}, f32[192]{0:T(256)}, u32[]{:S(2)}) copy-start(f32[192]{0:T(256)} %param.16) | copy-start | bytes 2308
  78.7 1.2 %copy-start.4 = (bf16[8,160,384]{2,1,0:T(8,128)(2,1)S(1)}, bf16[8,160,384]{2,1,0:T(8,128)(2,1)}, u32[]{:S(2)}) copy-start(bf16[8,160,384]{2,1,0:T(8,128)(2,1)} %all-gather.3) | copy-start | bytes 2949124
  79.9 1.7 %copy-start.5 = (bf16[4,2,96,1536]{3,2,1,0:T(8,128)(2,1)S(1)}, bf16[4,2,96,1536]{3,2,1,0:T(8,128)(2,1)}, u32[]{:S(2)}) copy-start(bf16[4,2,96,1536]{3,2,1,0:T(8,128)(2,1)} %all-gather.7.cloned.1.call-done) | copy-start | bytes 7077892
  81.5 12.3 %copy-start.18 = (pred[256,320]{1,0:T(8,128)(4,1)S(1)}, pred[256,320]{1,0:T(8,128)(4,1)}, u32[]{:S(2)}) copy-start(pred[256,320]{1,0:T(8,128)(4,1)} %get-tuple-element.34) | copy-start | bytes 245764
  81.5 12.4 %copy-start.19 = (pred[256,320]{1,0:T(8,128)(4,1)S(1)}, pred[256,320]{1,0:T(8,128)(4,1)}, u32[]{:S(2)}) copy-start(pred[256,320]{1,0:T(8,128)(4,1)} %get-tuple-element.31) | copy-start | bytes 245764
  81.5 12.4 %copy-start.20 = (pred[256,320]{1,0:T(8,128)(4,1)S(1)}, pred[256,320]{1,0:T(8,128)(4,1)}, u32[]{:S(2)}) copy-start(pred[256,320]{1,0:T(8,128)(4,1)} %get-tuple-element.32) | copy-start | bytes 245764
  81.5 12.5 %copy-start.16 = (pred[1,512,320]{2,1,0:T(8,128)(4,1)S(1)}, pred[1,512,320]{2,1,0:T(8,128)(4,1)}, u32[]{:S(2)}) copy-start(pred[1,512,320]{2,1,0:T(8,128)(4,1)} %add_bitcast_fusion) | copy-start | bytes 491524
  81.6 12.5 %copy-start.17 = (pred[1,512,320]{2,1,0:T(8,128)(4,1)S(1)}, pred[1,512,320]{2,1,0:T(8,128)(4,1)}, u32[]{:S(2)}) copy-start(pred[1,512,320]{2,1,0:T(8,128)(4,1)} %add_bitcast_fusion.1) | copy-start | bytes 491524
  90.4 14.1 %collective-permute-start.3 = (bf16[2,192,640]{2,1,0:T(8,128)(2,1)S(1)}, bf16[2,192,640]{2,1,0:T(8,128)(2,1)S(1)}, u32[]{:S(2)}, u32[]{:S(2)}) collective-permute-start(bf16[2,192,640]{2,1,0:T(8,128)(2,1)S(1)} %get-tuple-element.24), channel_id=1, source_target_pairs={{0,2},{1,3},{4,6},{5,7},{8,10},{9,11},{12,14},{13,15},{16,18},{17,... | collective-permute-start | bytes 1474568 | tf_op jit(solution)/shard_map/ppermute | solution.py:516
  93.9 1.3 %copy-start.3 = (bf16[2,4,320,192]{2,3,1,0:T(8,128)(2,1)S(1)}, bf16[2,4,320,192]{2,3,1,0:T(8,128)(2,1)}, u32[]{:S(2)}) copy-start(bf16[2,4,320,192]{2,3,1,0:T(8,128)(2,1)} %param.13) | copy-start | bytes 2949124
Sparse Core Ops, SparseCore 0:
  23.6 8.4 all-gather.6

commit v2 on v1

--- a/solution.py
+++ b/solution.py
@@ -10,6 +10,7 @@
 
 BF16, F32 = jnp.bfloat16, jnp.float32
 MIB = 1024 * 1024
+GATHER_PAD = 32
 NT = (((1,), (1,)), ((), ()))
 EPS = 1e-06
 
@@ -20,6 +21,10 @@
 
 def vmem():
     return pl.BlockSpec(memory_space=pltpu.VMEM)
+
+
+def hbm():
+    return pl.BlockSpec(memory_space=pltpu.HBM)
 
 
 def smem():
@@ -50,48 +55,57 @@
     return jnp.where(column == count - 1, 0.0, pltpu.roll(values, count - 1, 0))
 
 
-def rim_kernel(place, latent, cache, low, rim, cache_rim):
-    frames = latent.shape[0]
-    past, _, channels, columns = low.shape
+def edge_kernel(place, latent, cache, rim, sems):
+    frames, rows = latent.shape[:2]
+    line = jnp.where(place[1] == 0, rows - 1, 0)
+    copies = [
+        pltpu.make_async_copy(latent.at[:, line], rim.at[:frames], sems.at[0]),
+        pltpu.make_async_copy(cache.at[:, line], rim.at[frames:], sems.at[1]),
+    ]
+    for copy in copies:
+        copy.start()
+    for copy in copies:
+        copy.wait()
+
+
+def edge_rows(place, latent, cache):
+    frames, rows, width, channels = latent.shape
+    return pl.pallas_call(
+        edge_kernel,
+        in_specs=[smem(), hbm(), hbm()],
+        out_specs=vmem(),
+        out_shape=jax.ShapeDtypeStruct((frames + cache.shape[0], width, channels), BF16),
+        scratch_shapes=[pltpu.SemaphoreType.DMA((2,))],
+        compiler_params=pltpu.CompilerParams(vmem_limit_bytes=room(0)),
+        name="edge_rows",
+    )(place, latent, cache)
+
+
+def low_edge_kernel(place, low, rim, line, sem):
+    past, high, channels, columns = low.shape
     width = columns // 2
-    rim[...] = latent[:, 0]
-    cache_rim[:past] = cache[:, 0]
+    copy = pltpu.make_async_copy(low.at[:, jnp.where(place[1] == 0, high - 1, 0)], line, sem)
+    copy.start()
     pixel = lax.broadcasted_iota(jnp.int32, (width, columns), 0)
     column = lax.broadcasted_iota(jnp.int32, (width, columns), 1)
+    picks = [(column == 2 * pixel + b).astype(BF16) for b in range(2)]
+    copy.wait()
     for f in range(past):
-        sides = [dot_nt((column == 2 * pixel + b).astype(BF16), low[f, 0]) for b in range(2)]
-        cache_rim[past + f] = jnp.concatenate(sides, axis=-1).astype(BF16)
-
-
-def edge_rows(place, latent, cache, low):
-    frames, rows, width, channels = latent.shape
-    past, high, low_channels, columns = low.shape
-
-    def edge(count):
-        return lambda i, place: (0, jnp.where(place[1] == 0, count - 1, 0), 0, 0)
-
-    return pl.pallas_call(
-        rim_kernel,
-        grid_spec=pltpu.PrefetchScalarGridSpec(
-            num_scalar_prefetch=1,
-            grid=(1,),
-            in_specs=[
-                pl.BlockSpec((frames, 1, width, channels), edge(rows)),
-                pl.BlockSpec((past, 1, width, channels), edge(rows)),
-                pl.BlockSpec((past, 1, low_channels, columns), edge(high)),
-            ],
-            out_specs=[
-                pl.BlockSpec((frames, width, channels), lambda i, place: (0, 0, 0)),
-                pl.BlockSpec((2 * past, width, channels), lambda i, place: (0, 0, 0)),
-            ],
-        ),
-        out_shape=[
-            jax.ShapeDtypeStruct((frames, width, channels), BF16),
-            jax.ShapeDtypeStruct((2 * past, width, channels), BF16),
-        ],
-        compiler_params=pltpu.CompilerParams(vmem_limit_bytes=room(16 * latent.nbytes)),
-        name="edge_rows",
-    )(place, latent, cache, low)
+        sides = [dot_nt(pick, line[f]) for pick in picks]
+        rim[f] = jnp.concatenate(sides, axis=-1).astype(BF16)
+
+
+def low_edge_rows(place, low):
+    past, high, channels, columns = low.shape
+    return pl.pallas_call(
+        low_edge_kernel,
+        in_specs=[smem(), hbm()],
+        out_specs=vmem(),
+        out_shape=jax.ShapeDtypeStruct((past, columns // 2, 2 * channels), BF16),
+        scratch_shapes=[pltpu.VMEM((past, channels, columns), BF16), pltpu.SemaphoreType.DMA],
+        compiler_params=pltpu.CompilerParams(vmem_limit_bytes=room(0)),
+        name="low_edge_rows",
+    )(place, low)
 
 
 def weight_kernel(up, low, folded, turned):
@@ -139,108 +153,144 @@
     return jnp.concatenate([from_left(row), row, from_right(row)], axis=-1).astype(BF16)
 
 
-def tile_row(block, rims, f, l):
-    rows = block.shape[1]
-    if l == 0:
-        return rims[0, f]
-    if l == rows + 1:
-        return rims[1, f]
-    return block[f, l - 1]
-
-
 def tap_rows(weights, dy):
-    return jnp.concatenate([weights[0, dy, dx] for dx in range(3)], axis=-1)
-
-
-def mid_kernel(past, place, latent, halo, gain, weights, own, passed, acc, seen):
-    frames, rows, width, channels = latent.shape
-    part = weights.shape[-2]
-    size = rows * width
-    tap = pl.program_id(0)
-
-    @pl.when(tap == 0)
-    def _():
-        for f in range(frames):
-            for l in range(rows + 2):
-                row = tile_row(latent, halo, f, l).astype(F32)
-                seen[f, l] = spread(silu(normed(row, gain[...])))
-            mine = latent[f].astype(F32).reshape(size, channels)
-            kept = mine[:, :part]
-            for index in range(1, channels // part):
-                kept = jnp.where(place[1] == index, mine[:, index * part : (index + 1) * part], kept)
-            acc[f] = kept
-        for f in range(frames, frames + past):
-            acc[f] = jnp.zeros_like(acc[f])
-
-    total = None
-    for dy in range(3):
-        left = jnp.concatenate(
-            [seen[f, dy : dy + rows].reshape(size, 3 * channels) for f in range(frames)], axis=0
-        )
-        term = dot_nt(left, tap_rows(weights, dy))
-        total = term if total is None else total + term
-    for f in range(frames):
-        acc[f + past - tap] += total[f * size : (f + 1) * size]
-
-    @pl.when(tap == past)
-    def _():
-        own[...] = jnp.concatenate([acc[f] for f in range(frames)], axis=-1)
-        passed[...] = jnp.concatenate([acc[frames + t] for t in range(past)], axis=-1).astype(BF16)
-
-
-def mid_conv(place, latent, halo, gain, weights):
+    return jnp.concatenate([weights[dy, dx] for dx in range(3)], axis=-1)
+
+
+def mid_inner_kernel(place, latent, gain, weights, acc, held, seen, sems):
     frames, rows, width, channels = latent.shape
     taps, part = weights.shape[0], weights.shape[-2]
     past = taps - 1
     size = rows * width
-    scratch = [
-        pltpu.VMEM((frames + past, size, part), F32),
-        pltpu.VMEM((frames, rows + 2, width, 3 * channels), BF16),
-    ]
-    need = 4 * latent.nbytes + 2 * weights.nbytes // taps + (frames + past) * size * 3 * part * 4
-    return pl.pallas_call(
-        functools.partial(mid_kernel, past),
-        grid=(taps,),
-        in_specs=[smem(), vmem(), vmem(), vmem(),
-                  pl.BlockSpec((1, 3, 3, part, channels), lambda k: (k, 0, 0, 0, 0))],
+    copies = [pltpu.make_async_copy(weights.at[k], held.at[k], sems.at[k]) for k in range(taps)]
+    for copy in copies:
+        copy.start()
+    for f in range(frames):
+        for l in range(rows):
+            seen[f, l] = spread(silu(normed(latent[f, l].astype(F32), gain[...])))
+        mine = latent[f].astype(F32).reshape(size, channels)
+        kept = mine[:, :part]
+        for index in range(1, channels // part):
+            kept = jnp.where(place[1] == index, mine[:, index * part : (index + 1) * part], kept)
+        acc[f] = kept
+    for f in range(frames, frames + past):
+        acc[f] = jnp.zeros_like(acc[f])
+    for tap in range(taps):
+        copies[tap].wait()
+        for dy in (1, 0, 2):
+            low, high = max(0, 1 - dy), min(rows, rows + 1 - dy)
+            span = (high - low) * width
+            left = jnp.concatenate(
+                [seen[f, low + dy - 1 : high + dy - 1].reshape(span, 3 * channels) for f in range(frames)], axis=0
+            )
+            term = dot_nt(left, tap_rows(held[tap], dy))
+            for f in range(frames):
+                acc[f + past - tap, low * width : high * width] += term[f * span : (f + 1) * span]
+
+
+def mid_inner(place, latent, gain, weights):
+    frames, rows, width, channels = latent.shape
+    taps, part = weights.shape[0], weights.shape[-2]
+    size = rows * width
+    return pl.pallas_call(
+        mid_inner_kernel,
+        in_specs=[smem(), vmem(), vmem(), hbm()],
+        out_specs=vmem(),
+        out_shape=jax.ShapeDtypeStruct((frames + taps - 1, size, part), F32),
+        scratch_shapes=[
+            pltpu.VMEM(weights.shape, BF16),
+            pltpu.VMEM((frames, rows, width, 3 * channels), BF16),
+            pltpu.SemaphoreType.DMA((taps,)),
+        ],
+        compiler_params=pltpu.CompilerParams(vmem_limit_bytes=room(weights.nbytes + 10 * latent.nbytes)),
+        cost_estimate=pl.CostEstimate(
+            flops=2 * 18 * frames * size * channels * part, bytes_accessed=weights.nbytes, transcendentals=0),
+        name="mid_inner",
+    )(place, latent, gain, weights)
+
+
+def mid_rim_kernel(started, halo, gain, weights, own, passed, held, seen, acc, sems):
+    total, size, part = started.shape
+    sides, _, width, channels = halo.shape
+    taps = weights.shape[0]
+    past = taps - 1
+    frames = total - past
+    copies = []
+    for k in range(taps):
+        for side in range(2):
+            copies.append(pltpu.make_async_copy(weights.at[k, 2 * side], held.at[k, side], sems.at[2 * k + side]))
+            copies[-1].start()
+    for side in range(2):
+        for f in range(frames):
+            seen[side, f] = spread(silu(normed(halo[side, f].astype(F32), gain[...])))
+    acc[...] = started[...]
+    for tap in range(taps):
+        for side in range(2):
+            copies[2 * tap + side].wait()
+            kernel = jnp.concatenate([held[tap, side, dx] for dx in range(3)], axis=-1)
+            term = dot_nt(seen[side].reshape(frames * width, 3 * channels), kernel)
+            at = slice(0, width) if side == 0 else slice(size - width, size)
+            for f in range(frames):
+                acc[f + past - tap, at] += term[f * width : (f + 1) * width]
+    own[...] = jnp.concatenate([acc[f] for f in range(frames)], axis=-1)
+    passed[...] = jnp.concatenate([acc[frames + t] for t in range(past)], axis=-1).astype(BF16)
+
+
+def mid_rim(started, halo, gain, weights):
+    total, size, part = started.shape
+    taps = weights.shape[0]
+    past = taps - 1
+    frames = total - past
+    sides, _, width, channels = halo.shape
+    return pl.pallas_call(
+        mid_rim_kernel,
+        in_specs=[vmem(), vmem(), vmem(), hbm()],
         out_specs=[vmem(), vmem()],
         out_shape=[
             jax.ShapeDtypeStruct((size, frames * part), F32),
             jax.ShapeDtypeStruct((size, past * part), BF16),
         ],
-        scratch_shapes=scratch,
-        compiler_params=pltpu.CompilerParams(vmem_limit_bytes=room(need + 6 * latent.nbytes)),
-        name="mid_conv",
-    )(place, latent, halo, gain, weights)
-
-
-def mid_cache_kernel(place, own, cache, halo, weights, out, seen):
+        scratch_shapes=[
+            pltpu.VMEM((taps, 2) + weights.shape[2:], BF16),
+            pltpu.VMEM((2, frames, width, 3 * channels), BF16),
+            pltpu.VMEM(started.shape, F32),
+            pltpu.SemaphoreType.DMA((2 * taps,)),
+        ],
+        compiler_params=pltpu.CompilerParams(vmem_limit_bytes=room(weights.nbytes + 4 * started.nbytes)),
+        name="mid_rim",
+    )(started, halo, gain, weights)
+
+
+def mid_cache_kernel(place, own, cache, halo, weights, out, held, seen, sems):
     past, rows, width, channels = cache.shape
     part = weights.shape[-2]
-    tap = pl.program_id(0)
-
-    @pl.when(tap == 0)
-    def _():
-        out[...] = own[...]
+    frames = halo.shape[1] - past
+    out[...] = own[...]
 
     @pl.when(place[0] == 0)
     def _():
-        @pl.when(tap == 0)
-        def _():
-            for f in range(past):
-                for l in range(rows + 2):
-                    seen[f, l] = spread(tile_row(cache, halo, f, l).astype(F32))
-
-        for t in range(past):
-            @pl.when(t + tap < past)
-            def _(t=t):
-                total = None
-                for dy in range(3):
-                    left = seen[t + tap, dy : dy + rows].reshape(rows * width, 3 * channels)
-                    term = dot_nt(left, tap_rows(weights, dy))
-                    total = term if total is None else total + term
-                lanes = slice(t * part, (t + 1) * part)
-                out[:, lanes] += total
+        copies = [pltpu.make_async_copy(weights.at[k], held.at[k], sems.at[k]) for k in range(past)]
+        for copy in copies:
+            copy.start()
+        for f in range(past):
+            for l in range(rows + 2):
+                if l == 0 or l == rows + 1:
+                    row = halo[0 if l == 0 else 1, frames + f]
+                else:
+                    row = cache[f, l - 1]
+                seen[f, l] = spread(row.astype(F32))
+        for tap in range(past):
+            copies[tap].wait()
+            count = past - tap
+            total = None
+            for dy in range(3):
+                left = jnp.concatenate(
+                    [seen[t + tap, dy : dy + rows].reshape(rows * width, 3 * channels) for t in range(count)], axis=0
+                )
+                term = dot_nt(left, tap_rows(held[tap], dy))
+                total = term if total is None else total + term
+            for t in range(count):
+                out[:, t * part : (t + 1) * part] += total[t * rows * width : (t + 1) * rows * width]
 
 
 def mid_cached(place, own, cache, halo, weights):
@@ -248,14 +298,16 @@
     part = weights.shape[-2]
     return pl.pallas_call(
         mid_cache_kernel,
-        grid=(past,),
-        in_specs=[smem(), vmem(), vmem(), vmem(),
-                  pl.BlockSpec((1, 3, 3, part, channels), lambda k: (k, 0, 0, 0, 0))],
+        in_specs=[smem(), vmem(), vmem(), vmem(), hbm()],
         out_specs=vmem(),
         out_shape=jax.ShapeDtypeStruct(own.shape, F32),
-        scratch_shapes=[pltpu.VMEM((past, rows + 2, width, 3 * channels), BF16)],
+        scratch_shapes=[
+            pltpu.VMEM((past,) + weights.shape[1:], BF16),
+            pltpu.VMEM((past, rows + 2, width, 3 * channels), BF16),
+            pltpu.SemaphoreType.DMA((past,)),
+        ],
         compiler_params=pltpu.CompilerParams(
-            vmem_limit_bytes=room(10 * cache.nbytes + 3 * own.nbytes + weights.nbytes)),
+            vmem_limit_bytes=room(12 * cache.nbytes + 3 * own.nbytes + weights.nbytes)),
         cost_estimate=pl.CostEstimate(
             flops=6 * 9 * rows * width * channels * part, bytes_accessed=weights.nbytes, transcendentals=0),
         name="mid_cached",
@@ -263,15 +315,16 @@
 
 
 def attn_kernel(tile_rows, place, frame, gain, qkv, proj, out, normal, keys, values):
-    count, size, channels = frame.shape
-    width = size // tile_rows
+    count, _, channels = frame.shape
+    width = out.shape[1]
+    size = tile_rows * width
     height = count * tile_rows
     rows = out.shape[0]
     step = 2
     scale = 1.0 / (math.sqrt(channels) * math.log(2.0))
 
     def prepare(index, carry):
-        scaled = normed(frame[index].astype(F32), gain[...]).astype(BF16)
+        scaled = normed(frame[index, :size].astype(F32), gain[...]).astype(BF16)
         normal[pl.ds(index * tile_rows, tile_rows)] = scaled.reshape(tile_rows, width, channels)
         both = jnp.dot(scaled, qkv[:, channels:], preferred_element_type=F32).astype(BF16)
         at = pl.ds(pl.multiple_of(index * size, 16), size)
@@ -299,10 +352,9 @@
             out[block * step + i] = jnp.where(inside, summed, 0.0).astype(BF16)
 
 
-def attention(place, frame, gain, qkv, proj, tile_rows):
-    count, size, channels = frame.shape
-    width = size // tile_rows
-    pixels = count * size
+def attention(place, frame, gain, qkv, proj, tile_rows, width):
+    count, _, channels = frame.shape
+    pixels = count * tile_rows * width
     rows = tile_rows + 2
     need = 4 * frame.nbytes + 2 * width * pixels * 16 + 2 * qkv.nbytes
     return pl.pallas_call(
@@ -329,22 +381,24 @@
     return jnp.concatenate([block[dy : dy + high].reshape(high * width, lanes) for dy in range(3)], axis=-1)
 
 
-def low_kernel(past, place, tile, up, gain, weights, own, passed, seen, upper, window, kept, acc):
+def low_kernel(past, place, tile, up_weights, gain, weights, passed, window, kept, seen, upper, up, held, sems):
     frames, ext, width, channels = tile.shape
     chans, _, _, part = up.shape[:4]
     low = chans * part
     rows = ext - 2
     high = 2 * rows
-    phases = own.shape[1]
-    line = lax.broadcasted_iota(jnp.int32, (phases, 2 * low), 0)
-    spot = lax.broadcasted_iota(jnp.int32, (phases, 2 * low), 1)
-    shift = place[1] * part
-    picked = spot == jnp.where(line < part, line + shift, line - part + shift + low)
-    select = picked.astype(F32).astype(BF16)
-
+    phases = passed.shape[1]
+    copies = [
+        pltpu.make_async_copy(up_weights, up, sems.at[0]),
+        pltpu.make_async_copy(weights.at[: past * phases], held, sems.at[1]),
+    ]
+    for copy in copies:
+        copy.start()
     for f in range(frames):
         for l in range(ext):
             seen[f, l] = spread(tile[f, l].astype(F32))
+    copies[0].wait()
+    for f in range(frames):
         for a in range(2):
             for b in range(2):
                 lanes = slice(b * channels, (b + 2) * channels)
@@ -366,18 +420,18 @@
                 sides = [jnp.where(place[2] == place[3] - 1, 0.0, side) for side in sides]
             window[f, j] = windowed(*sides)
 
+    copies[-1].wait()
+    sums = [None] * past
     for f in range(frames):
-        acc[f] = dot_nt(select, kept[f].reshape(high * width, 2 * low))
-    for f in range(frames, frames + past):
-        acc[f] = jnp.zeros_like(acc[f])
-    for f in range(frames):
-        got = dot_nt(weights[...], stacked(window[f], high))
-        for tap in range(past + 1):
-            acc[f + past - tap] += got[tap * phases : (tap + 1) * phases]
+        count = min(f + past - frames + 1, past)
+        if count > 0:
+            got = dot_nt(held[: count * phases], stacked(window[f], high))
+            for tap in range(count):
+                t = f + past - tap - frames
+                term = got[tap * phases : (tap + 1) * phases]
+                sums[t] = term if sums[t] is None else sums[t] + term
     for t in range(past):
-        passed[t] = acc[frames + t].astype(BF16)
-    for f in range(frames):
-        own[f] = acc[f]
+        passed[t] = sums[t].astype(BF16)
 
 
 def low_stage(place, tile, up, gain, weights, taps):
@@ -387,26 +441,76 @@
     high = 2 * (ext - 2)
     past = taps - 1
     phases = 2 * part
-    scratch = [
-        pltpu.VMEM((frames, ext, width, 3 * channels), BF16),
-        pltpu.VMEM((high + 2, 2, width, low), BF16),
-        pltpu.VMEM((frames, high + 2, width, 4 * low), BF16),
-        pltpu.VMEM((frames, high, width, 2 * low), BF16),
-        pltpu.VMEM((frames + past, phases, high * width), F32),
-    ]
-    need = 5 * tile.nbytes + up.nbytes + 2 * weights.nbytes + 12 * frames * high * width * low * 4
+    need = 5 * tile.nbytes + up.nbytes + 2 * weights.nbytes + 10 * frames * high * width * low * 4
     return pl.pallas_call(
         functools.partial(low_kernel, past),
-        in_specs=[smem()] + [vmem()] * 4,
-        out_specs=[vmem(), vmem()],
+        in_specs=[smem(), vmem(), hbm(), vmem(), hbm()],
+        out_specs=[vmem()] * 3,
         out_shape=[
-            jax.ShapeDtypeStruct((frames, phases, high * width), F32),
             jax.ShapeDtypeStruct((past, phases, high * width), BF16),
-        ],
-        scratch_shapes=scratch,
+            jax.ShapeDtypeStruct((frames, high + 2, width, 4 * low), BF16),
+            jax.ShapeDtypeStruct((frames, high, width, 2 * low), BF16),
+        ],
+        scratch_shapes=[
+            pltpu.VMEM((frames, ext, width, 3 * channels), BF16),
+            pltpu.VMEM((high + 2, 2, width, low), BF16),
+            pltpu.VMEM(up.shape, BF16),
+            pltpu.VMEM((past * phases, weights.shape[1]), BF16),
+            pltpu.SemaphoreType.DMA((2,)),
+        ],
         compiler_params=pltpu.CompilerParams(vmem_limit_bytes=room(need)),
         name="low_stage",
     )(place, tile, up, gain, weights)
+
+
+def low_own_kernel(place, starts, window, kept, weights, own, weave):
+    frames, ext, width, lanes = window.shape
+    low = lanes // 4
+    high = ext - 2
+    phases = own.shape[1]
+    part = phases // 2
+    taps = weights.shape[0] // phases
+    past = taps - 1
+    line = lax.broadcasted_iota(jnp.int32, (phases, 2 * low), 0)
+    spot = lax.broadcasted_iota(jnp.int32, (phases, 2 * low), 1)
+    shift = place[1] * part
+    picked = spot == jnp.where(line < part, line + shift, line - part + shift + low)
+    select = picked.astype(F32).astype(BF16)
+    for f in range(frames):
+        own[f] = dot_nt(select, kept[f].reshape(high * width, 2 * low))
+    for f in range(frames):
+        least = max(0, f + past - frames + 1)
+        got = dot_nt(weights[least * phases :], stacked(window[f], high))
+        for tap in range(least, taps):
+            own[f + past - tap] += got[(tap - least) * phases : (tap - least + 1) * phases]
+    span = weave.shape[1] // 2
+    lane = lax.broadcasted_iota(jnp.int32, (span, 2 * width), 0)
+    column = lax.broadcasted_iota(jnp.int32, (span, 2 * width), 1)
+    for i, start in enumerate(starts):
+        for b in range(2):
+            hit = column == 2 * (lane - (width * i - start)) + b
+            weave[i, b * span : (b + 1) * span] = hit.astype(F32).astype(BF16)
+
+
+def low_own(place, window, kept, weights, taps):
+    frames, ext, width, lanes = window.shape
+    phases = weights.shape[0] // taps
+    high = ext - 2
+    starts, span = lane_windows(high, width)
+    need = 3 * window.nbytes + 2 * weights.nbytes + 3 * frames * phases * high * width * 4
+    return pl.pallas_call(
+        lambda place, *refs: low_own_kernel(place, starts, *refs),
+        in_specs=[smem()] + [vmem()] * 3,
+        out_specs=[vmem()] * 2,
+        out_shape=[
+            jax.ShapeDtypeStruct((frames, phases, high * width), F32),
+            jax.ShapeDtypeStruct((high, 2 * span, 2 * width), BF16),
+        ],
+        compiler_params=pltpu.CompilerParams(vmem_limit_bytes=room(need)),
+        cost_estimate=pl.CostEstimate(
+            flops=6 * 9 * high * width * lanes * phases // 2, bytes_accessed=weights.nbytes, transcendentals=0),
+        name="low_own",
+    )(place, window, kept, weights)
 
 
 def low_cache_kernel(place, own, cache, halo, weights, out, window):
@@ -456,17 +560,6 @@
     span = min(-(-span // 128) * 128, high * width)
     starts = [min(start, high * width - span) for start in starts]
     return starts, span
-
-
-def weaver(high, width):
-    starts, span = lane_windows(high, width)
-    lane = lax.broadcasted_iota(jnp.int32, (span, 2 * width), 0)
-    column = lax.broadcasted_iota(jnp.int32, (span, 2 * width), 1)
-    blocks = []
-    for i, start in enumerate(starts):
-        pixel = lane - (width * i - start)
-        blocks.append([(column == 2 * pixel + b).astype(BF16) for b in range(2)])
-    return jnp.stack([jnp.concatenate(pair, axis=0) for pair in blocks])
 
 
 def finish_kernel(starts, own, passed, weave, out):
@@ -541,18 +634,17 @@
     mid_weights = jnp.swapaxes(conv_mid, 3, 4)
     low_cache = jnp.swapaxes(cache_low, 2, 3)
 
-    rim, cache_rim = edge_rows(place, latent, cache_mid, low_cache)
-    halo = to_neighbour(rim, False)
-    cache_halo = to_neighbour(cache_rim, True)
+    rim = to_neighbour(edge_rows(place, latent, cache_mid), False)
+    low_rim = to_neighbour(low_edge_rows(place, low_cache), True)
+    started = mid_inner(place, latent, gain_mid[None], mid_weights)
+    halo = lax.all_gather(rim, "chan")
+    own, passed = mid_rim(started, halo, gain_mid[None], mid_weights)
+    arrived = to_next(passed)
+    own = mid_cached(place, own, cache_mid, halo, mid_weights)
+
     up_part, low_weights = weight_forms(jnp.swapaxes(conv_up, 2, 3), conv_low)
     up = lax.all_gather(up_part, "chan")
-    halo = lax.all_gather(halo, "chan")
-
-    own, passed = mid_conv(place, latent, halo, gain_mid[None], mid_weights)
-    arrived = to_next(passed)
-    cache_halo, own = lax.optimization_barrier((cache_halo, own))
-    cache_halo = lax.all_gather(cache_halo, "chan")
-    own = mid_cached(place, own, cache_mid, cache_halo[:, :past], mid_weights)
+
     first_part = (own + jnp.pad(arrived, ((0, 0), (0, (frames - past) * part))).astype(F32)).astype(BF16)
     both = lax.all_gather(first_part, "chan")
     chans = both.shape[0]
@@ -563,15 +655,17 @@
     mine = choices[0]
     for f in range(1, frames):
         mine = jnp.where(chan == f, choices[f], mine)
-    frame = lax.all_gather(mine, "rows")
-
-    reached = attention(place, frame, gain_attn[None], attn_qkv, attn_proj, rows)
+    frame = lax.all_gather(jnp.pad(mine, ((0, GATHER_PAD), (0, 0))), "rows")
+
+    reached = attention(place, frame, gain_attn[None], attn_qkv, attn_proj, rows, width)
     tile = lax.all_gather(reached, "chan")
 
-    own_low, passed_low = low_stage(place, tile, up, gain_low[None], low_weights, taps)
+    passed_low, window, kept = low_stage(place, tile, up, gain_low[None], low_weights, taps)
     arrived_low = to_next(passed_low)
-    own_low = low_cached(place, own_low, low_cache, cache_halo[:, past:], low_weights)
-    out = finish(own_low, arrived_low, weaver(high, width), high, width)
+    own_low, weave = low_own(place, window, kept, low_weights, taps)
+    low_rim, _ = lax.optimization_barrier((low_rim, passed_low))
+    own_low = low_cached(place, own_low, low_cache, lax.all_gather(low_rim, "chan"), low_weights)
+    out = finish(own_low, arrived_low, weave, high, width)
     return jnp.swapaxes(out, 2, 3)
 
 

time: 113 us -> 124 us (1.097)
  blocking collectives: 30.8 us -> 10.6 us
  waiting for transfers between devices: 5.36 us -> 20.4 us
  Pallas kernels: 33.9 us -> 45 us
  local copies, waits for them, and re-layouts: 10.7 us -> 17.7 us
  other arithmetic: 4.26 us -> 0.31 us
  starting transfers between devices: 14 us -> 15.6 us
    all_gather x3 -> x2, blocking collectives: 25.9 us -> 5.1 us  [the longest x1 2.59 us: body(): lax.all_gather(low_rim, 'chan')]
    all_gather x0 -> x1, waiting for transfers between devices: none -> 19.8 us  [body(): frame = lax.all_gather(jnp.pad(mine, ((0, GATHER_PAD), (0, 0))), 'rows')]
    pallas_call x4 -> x7, Pallas kernels: 20.9 us -> 32 us  [the longest x1 10 us: low_stage(): pl.pallas_call(functools.partial(low_kernel, past), in_specs=[smem(), vme...]
    unnamed x46 -> x38, local copies, waits for them, and re-layouts: 10.5 us -> 16.1 us
    ppermute x2, waiting for transfers between devices: 5.33 us -> 0.51 us  [to_next(): lax.ppermute(values, 'segment', [(i, i + 1) for i in range(count - 1)])]
    eq x4 -> x0, other arithmetic: 1.98 us -> none  [weaver(): blocks.append([(column == 2 * pixel + b).astype(BF16) for b in range(2)])]
    another operation x5 -> x0, other arithmetic: 1.93 us -> none  [weaver(): return jnp.stack([jnp.concatenate(pair, axis=0) for pair in blocks])]
    ppermute x2, starting transfers between devices: 4.79 us -> 6.39 us  [to_next(): lax.ppermute(values, 'segment', [(i, i + 1) for i in range(count - 1)])]
  transfers between devices with their start and end apart: 5 -> 6, of which waited for: 1 -> 3; matrix products, arithmetic and copies ran while one was open for 4% -> 1% of each run, Pallas kernels for 19% -> 30%
where the time goes in v2:
time: 124 us; the launch traced here: 123 us
  Pallas kernels  45 us (36%)
  waiting for transfers between devices  20.4 us (16%)
  local copies, waits for them, and re-layouts  17.7 us (14%)
  starting transfers between devices  15.6 us (13%)
  between operations  13.6 us (11%)
  blocking collectives  10.6 us (9%)
    all_gather x1, waiting for transfers between devices, body(): frame = lax.all_gather(jnp.pad(mine, ((0, GATHER_PAD), (0, 0))), 'rows')  19.8 us
    unnamed x38, local copies, waits for them, and re-layouts  16.1 us
    pallas_call x1, Pallas kernels, low_stage(): pl.pallas_call(functools.partial(low_kernel, past), in_specs=[smem(), vme...  10 us
    ppermute x2, starting transfers between devices, to_neighbour(): return lax.ppermute(values, ('rows', 'segment', 'chan'), route)  9.14 us
    ppermute x2, starting transfers between devices, to_next(): lax.ppermute(values, 'segment', [(i, i + 1) for i in range(count - 1)])  6.39 us
    pallas_call x1, Pallas kernels, attention(): pl.pallas_call(functools.partial(attn_kernel, tile_rows), in_specs=[smem(...  6.14 us
    pallas_call x1, Pallas kernels, mid_rim(): pl.pallas_call(mid_rim_kernel, in_specs=[vmem(), vmem(), vmem(), hbm()],...  5.8 us
    pallas_call x1, Pallas kernels, mid_inner(): pl.pallas_call(mid_inner_kernel, in_specs=[smem(), vmem(), vmem(), hbm()]...  4.93 us
  transfers between devices with their start and end apart: 6, of which 3 were waited for; matrix products, arithmetic and copies ran while one was open for 1% of the time, Pallas kernels for 30%

profile of v2, /device:TPU:0, one launch (start us, length us, event | category | flops | bytes accessed | tf_op | source)
XLA Modules:
  0.0 123.2 jit_solution(9091577418167937436)
XLA Ops:
  6.6 1.0 copy-done.7
  7.6 1.0 copy-done.14
  8.7 0.9 edge_rows.1
  9.6 5.0 %collective-permute-start = (bf16[4,160,384]{2,1,0:T(8,128)(2,1)S(1)}, bf16[4,160,384]{2,1,0:T(8,128)(2,1)S(1)}, u32[]{:S(2)}, u32[]{:S(2)}) collective-permute-start(bf16[4,160,384]{2,1,0:T(8,128)(2,1)S(1)} %edge_rows.1), channel_id=1, source_target_pairs={{0,4},{5,1},{2,6},{7,3},{4,8},{9,5},{6,10},{11,7},{8,12},{13,9},{1... | collective-permute-start | bytes 1474568 | tf_op jit(solution)/shard_map/ppermute | solution.py:604
  15.2 2.1 %copy-done = bf16[3,3,3,384,192]{3,4,2,1,0:T(8,128)(2,1)S(1)} copy-done((bf16[3,3,3,384,192]{3,4,2,1,0:T(8,128)(2,1)S(1)}, bf16[3,3,3,384,192]{3,4,2,1,0:T(8,128)(2,1)}, u32[]{:S(2)}) %copy-start) | copy-done | bytes 3981336
  17.4 1.0 copy-done.15
  18.4 4.9 %mid_inner.1.started = f32[4,320,192]{2,1,0:T(8,128)S(1)} custom-call(s32[4]{0:T(128)S(1)} %pad_add_fusion.place, bf16[2,2,160,384]{3,2,1,0:T(8,128)(2,1)S(1)} %copy-done.15, f32[1,384]{1,0:T(1,128)S(1)} %broadcast_in_dim.10.gain, bf16[3,3,3,192,384]{4,3,2,1,0:T(8,128)(2,1)S(1)} %bitcast.22), custom_call_target="tpu_custom_call" | custom-call | flops 1698693120 | bytes 3981312 | tf_op jit(solution)/shard_map/mid_inner/pallas_call | solution.py:195
  23.3 2.5 %all-gather = bf16[8,160,384]{2,1,0:T(8,128)(2,1)S(1)} all-gather(bf16[4,160,384]{2,1,0:T(8,128)(2,1)S(1)} %collective-permute-done), channel_id=2, replica_groups=mesh['groups'=2,'rows'=4,'segment'=2,'chan'=2] {'chan'}, dimensions={0}, use_global_device_ids=true | all-gather | bytes 1474560 | tf_op jit(solution)/shard_map/all_gather | solution.py:640
  25.8 5.8 %mid_rim.1 = (f32[320,384]{1,0:T(8,128)S(1)}, bf16[320,384]{1,0:T(8,128)(2,1)S(1)}) custom-call(f32[4,320,192]{2,1,0:T(8,128)S(1)} %mid_inner.1.started, bf16[2,4,160,384]{3,2,1,0:T(8,128)(2,1)S(1)} %bitcast.25, f32[1,384]{1,0:T(1,128)S(1)} %broadcast_in_dim.10.gain, bf16[3,3,3,192,384]{4,3,2,1,0:T(8,128)(2,1)S(1)} %bitcast.23), custom_call_target="tpu_custom_call" | custom-call | tf_op jit(solution)/shard_map/mid_rim/pallas_call | solution.py:245
  31.7 3.4 %collective-permute-start.1 = (bf16[320,384]{1,0:T(8,128)(2,1)S(1)}, bf16[320,384]{1,0:T(8,128)(2,1)S(1)}, u32[]{:S(2)}, u32[]{:S(2)}) collective-permute-start(bf16[320,384]{1,0:T(8,128)(2,1)S(1)} %get-tuple-element.16), channel_id=1, source_target_pairs={{0,2},{1,3},{4,6},{5,7},{8,10},{9,11},{12,14},{13,15},{16,18},{17,... | collective-permute-start | bytes 737288 | tf_op jit(solution)/shard_map/ppermute | solution.py:609
  35.1 2.1 %copy-done.2 = bf16[3,3,3,384,192]{3,4,2,1,0:T(8,128)(2,1)S(1)} copy-done((bf16[3,3,3,384,192]{3,4,2,1,0:T(8,128)(2,1)S(1)}, bf16[3,3,3,384,192]{3,4,2,1,0:T(8,128)(2,1)}, u32[]{:S(2)}) %copy-start.2) | copy-done | bytes 3981336
  37.2 4.8 %mid_cached.1 = f32[320,384]{1,0:T(8,128)S(1)} custom-call(s32[4]{0:T(128)S(1)} %pad_add_fusion.place, f32[320,384]{1,0:T(8,128)S(1)} %get-tuple-element.15.own, bf16[2,2,160,384]{3,2,1,0:T(8,128)(2,1)S(1)} %copy-done.8, bf16[2,4,160,384]{3,2,1,0:T(8,128)(2,1)S(1)} %bitcast.26, bf16[3,3,3,192,384]{4,3,2,1,0:T(8,128)(2,1)S(1)} %bitcast.24), custom_call_target="tpu_custom_call" | custom-call | flops 1274019840 | bytes 3981312 | tf_op jit(solution)/shard_map/mid_cached/pallas_call | solution.py:299
  42.1 2.2 %all-gather.1 = bf16[640,384]{1,0:T(8,128)(2,1)S(1)} all-gather(bf16[320,384]{1,0:T(8,128)(2,1)S(1)} %add_convert_fusion), channel_id=3, replica_groups=mesh['groups'=2,'rows'=4,'segment'=2,'chan'=2] {'chan'}, dimensions={0}, use_global_device_ids=true | all-gather | bytes 737280 | tf_op jit(solution)/shard_map/all_gather | solution.py:649
  45.5 1.3 %copy-done.9 = bf16[3,3,3,192,96]{4,3,2,1,0:T(8,128)(2,1)S(1)} copy-done((bf16[3,3,3,192,96]{4,3,2,1,0:T(8,128)(2,1)S(1)}, bf16[3,3,3,192,96]{4,3,2,1,0:T(8,128)(2,1)}, u32[]{:S(2)}) %copy-start.9) | copy-done | bytes 995352
  46.8 1.4 %weight_forms.1 = (bf16[2,2,96,1536]{3,2,1,0:T(8,128)(2,1)S(1)}, bf16[576,2304]{1,0:T(8,128)(2,1)S(1)}) custom-call(bf16[3,3,96,384]{3,2,1,0:T(8,128)(2,1)S(1)} %bitcast.33, bf16[3,3,3,192,96]{4,3,2,1,0:T(8,128)(2,1)S(1)} %copy-done.9), custom_call_target="tpu_custom_call" | custom-call | tf_op jit(solution)/shard_map/weight_forms/pallas_call | solution.py:139
  48.2 1.0 copy-done.10
  49.2 1.3 %copy-done.3 = bf16[2,4,320,192]{2,3,1,0:T(8,128)(2,1)S(1)} copy-done((bf16[2,4,320,192]{2,3,1,0:T(8,128)(2,1)S(1)}, bf16[2,4,320,192]{2,3,1,0:T(8,128)(2,1)}, u32[]{:S(2)}) %copy-start.3) | copy-done | bytes 983064
  50.6 1.8 %low_edge_rows.1 = bf16[2,160,384]{2,1,0:T(8,128)(2,1)} custom-call(s32[4]{0:T(128)S(1)} %pad_add_fusion.place, bf16[2,4,192,320]{3,2,1,0:T(8,128)(2,1)S(1)} %bitcast.27), custom_call_target="tpu_custom_call" | custom-call | tf_op jit(solution)/shard_map/low_edge_rows/pallas_call | solution.py:100
  52.4 4.2 %collective-permute-start.2 = (bf16[2,160,384]{2,1,0:T(8,128)(2,1)}, bf16[2,160,384]{2,1,0:T(8,128)(2,1)}, u32[]{:S(2)}, u32[]{:S(2)}) collective-permute-start(bf16[2,160,384]{2,1,0:T(8,128)(2,1)} %low_edge_rows.1), channel_id=1, source_target_pairs={{0,4},{5,1},{4,8},{9,5},{8,12},{13,9},{16,20},{21,17},{20,24},{25,... | collective-permute-start | bytes 737288 | tf_op jit(solution)/shard_map/ppermute | solution.py:604
  56.6 19.8 %all-gather.9.cloned.1.call-done = bf16[1408,384]{1,0:T(8,128)(2,1)} async-done(((bf16[352,384]{1,0:T(8,128)(2,1)}), bf16[1408,384]{1,0:T(8,128)(2,1)}) %all-gather.9.cloned.1.call-update) | async-done | bytes 1081360 | tf_op jit(solution)/shard_map/all_gather | solution.py:658
  76.3 1.2 %copy-done.11 = bf16[1408,384]{1,0:T(8,128)(2,1)S(1)} copy-done((bf16[1408,384]{1,0:T(8,128)(2,1)S(1)}, bf16[1408,384]{1,0:T(8,128)(2,1)}, u32[]{:S(2)}) %copy-start.11) | copy-done | bytes 1081368
  77.6 1.0 copy-done.16
  78.5 6.1 %frame_attention.1 = bf16[4,160,384]{2,1,0:T(8,128)(2,1)S(1)} custom-call(s32[4]{0:T(128)S(1)} %pad_add_fusion.place, bf16[4,352,384]{2,1,0:T(8,128)(2,1)S(1)} %bitcast.32, f32[1,384]{1,0:T(1,128)S(1)} %broadcast_in_dim.11.gain, bf16[384,1152]{1,0:T(8,128)(2,1)S(1)} %copy-done.12, bf16[384,384]{1,0:T(8,128)(2,1)S(1)} %copy-done.16), custom_call_target="tpu_custom_call" | custom-call | tf_op jit(solution)/shard_map/frame_attention/pallas_call | solution.py:360
  84.7 3.3 %all-gather.3 = bf16[8,160,384]{2,1,0:T(8,128)(2,1)} all-gather(bf16[4,160,384]{2,1,0:T(8,128)(2,1)S(1)} %frame_attention.1), channel_id=5, replica_groups=mesh['groups'=2,'rows'=4,'segment'=2,'chan'=2] {'chan'}, dimensions={0}, use_global_device_ids=true | all-gather | bytes 1474560 | tf_op jit(solution)/shard_map/all_gather | solution.py:661
  88.2 1.2 copy-done.5
  89.4 1.7 %copy-done.6 = bf16[4,2,96,1536]{3,2,1,0:T(8,128)(2,1)S(1)} copy-done((bf16[4,2,96,1536]{3,2,1,0:T(8,128)(2,1)S(1)}, bf16[4,2,96,1536]{3,2,1,0:T(8,128)(2,1)}, u32[]{:S(2)}) %copy-start.6) | copy-done | bytes 2359320
  91.0 10.0 %low_stage.1 = (bf16[2,192,640]{2,1,0:T(8,128)(2,1)S(1)}, bf16[2,6,160,768]{3,2,1,0:T(8,128)(2,1)S(1)}, bf16[2,4,160,384]{3,2,1,0:T(8,128)(2,1)S(1)}) custom-call(s32[4]{0:T(128)S(1)} %pad_add_fusion.place, bf16[2,4,160,384]{3,2,1,0:T(8,128)(2,1)S(1)} %bitcast.29, bf16[2,2,2,96,1536]{4,3,2,1,0:T(8,128)(2,1)S(1)} %bitcast.30, f32[1,192]{1,0:T(1,128)S(1)} %bitcast.34, ...), custom_call_target="tpu_custom_call" | custom-call | tf_op jit(solution)/shard_map/low_stage/pallas_call | solution.py:445
  101.1 3.0 %collective-permute-start.3 = (bf16[2,192,640]{2,1,0:T(8,128)(2,1)S(1)}, bf16[2,192,640]{2,1,0:T(8,128)(2,1)S(1)}, u32[]{:S(2)}, u32[]{:S(2)}) collective-permute-start(bf16[2,192,640]{2,1,0:T(8,128)(2,1)S(1)} %get-tuple-element.22), channel_id=1, source_target_pairs={{0,2},{1,3},{4,6},{5,7},{8,10},{9,11},{12,14},{13,15},{16,18},{17,... | collective-permute-start | bytes 1474568 | tf_op jit(solution)/shard_map/ppermute | solution.py:609
  104.1 2.6 %all-gather.5 = bf16[4,160,384]{2,1,0:T(8,128)(2,1)S(1)} all-gather(bf16[2,160,384]{2,1,0:T(8,128)(2,1)} %collective-permute-done.2), channel_id=7, replica_groups=mesh['groups'=2,'rows'=4,'segment'=2,'chan'=2] {'chan'}, dimensions={0}, use_global_device_ids=true | all-gather | bytes 737280 | tf_op jit(solution)/shard_map/all_gather | solution.py:667
  106.7 3.7 %low_own.1 = (f32[2,192,640]{2,1,0:T(8,128)S(1)}, bf16[4,512,320]{2,1,0:T(8,128)(2,1)S(1)}) custom-call(s32[4]{0:T(128)S(1)} %pad_add_fusion.place, bf16[2,6,160,768]{3,2,1,0:T(8,128)(2,1)S(1)} %get-tuple-element.19.refs_0_, bf16[2,4,160,384]{3,2,1,0:T(8,128)(2,1)S(1)} %get-tuple-element.20.refs_1_, bf16[576,2304]{1,0:T(8,128)(2,1)S(1)} %get-tuple-element.18.weights.refs_2_), custom_call_target="tpu_custom_call" | custom-call | flops 2548039680 | bytes 2654208 | tf_op jit(solution)/shard_map/low_own/pallas_call | solution.py:501
  110.4 4.1 %low_cached.1.own = f32[2,192,640]{2,1,0:T(8,128)S(1)} custom-call(s32[4]{0:T(128)S(1)} %pad_add_fusion.place, f32[2,192,640]{2,1,0:T(8,128)S(1)} %get-tuple-element.21.own, bf16[2,4,192,320]{3,2,1,0:T(8,128)(2,1)S(1)} %bitcast.28, bf16[2,2,160,384]{3,2,1,0:T(8,128)(2,1)S(1)} %bitcast.31, bf16[576,2304]{1,0:T(8,128)(2,1)S(1)} %get-tuple-element.18.weights.refs_2_), custom_call_target="tpu_custom_call" | custom-call | flops 1274019840 | bytes 2654208 | tf_op jit(solution)/shard_map/low_cached/pallas_call | solution.py:543
  115.0 1.4 %finish.1 = bf16[2,4,96,320]{3,2,1,0:T(8,128)(2,1)} custom-call(f32[2,192,640]{2,1,0:T(8,128)S(1)} %low_cached.1.own, bf16[2,192,640]{2,1,0:T(8,128)(2,1)S(1)} %collective-permute-done.3.passed, bf16[4,512,320]{2,1,0:T(8,128)(2,1)S(1)} %get-tuple-element.24.weave), custom_call_target="tpu_custom_call" | custom-call | tf_op jit(solution)/shard_map/finish/pallas_call | solution.py:586
  (42 shorter events, 2.7 us)
Async XLA Ops:
  6.5 69.8 %all-gather.9.cloned.1.call-start = ((), (), s32[]{:S(2)}) async-start(), calls=%async_computation | async-start | bytes 1351680 | tf_op jit(solution)/shard_map/all_gather | solution.py:658
  6.6 1.0 copy-start.7
  7.6 1.0 copy-start.14
  9.6 13.8 %collective-permute-start = (bf16[4,160,384]{2,1,0:T(8,128)(2,1)S(1)}, bf16[4,160,384]{2,1,0:T(8,128)(2,1)S(1)}, u32[]{:S(2)}, u32[]{:S(2)}) collective-permute-start(bf16[4,160,384]{2,1,0:T(8,128)(2,1)S(1)} %edge_rows.1), channel_id=1, source_target_pairs={{0,4},{5,1},{2,6},{7,3},{4,8},{9,5},{6,10},{11,7},{8,12},{13,9},{1... | collective-permute-start | bytes 1474568 | tf_op jit(solution)/shard_map/ppermute | solution.py:604
  15.2 2.1 %copy-start = (bf16[3,3,3,384,192]{3,4,2,1,0:T(8,128)(2,1)S(1)}, bf16[3,3,3,384,192]{3,4,2,1,0:T(8,128)(2,1)}, u32[]{:S(2)}) copy-start(bf16[3,3,3,384,192]{3,4,2,1,0:T(8,128)(2,1)} %param.17) | copy-start | bytes 11943940
  17.3 1.0 copy-start.15
  18.4 7.5 %copy-start.1 = (bf16[3,3,3,384,192]{3,4,2,1,0:T(8,128)(2,1)S(1)}, bf16[3,3,3,384,192]{3,4,2,1,0:T(8,128)(2,1)}, u32[]{:S(2)}) copy-start(bf16[3,3,3,384,192]{3,4,2,1,0:T(8,128)(2,1)} %param.17) | copy-start | bytes 11943940
  25.8 9.2 %copy-start.8 = (bf16[2,2,160,384]{3,2,1,0:T(8,128)(2,1)S(1)}, bf16[2,2,160,384]{3,2,1,0:T(8,128)(2,1)}, u32[]{:S(2)}) copy-start(bf16[2,2,160,384]{3,2,1,0:T(8,128)(2,1)} %cache.3) | copy-start | bytes 1474564
  31.7 10.4 %collective-permute-start.1 = (bf16[320,384]{1,0:T(8,128)(2,1)S(1)}, bf16[320,384]{1,0:T(8,128)(2,1)S(1)}, u32[]{:S(2)}, u32[]{:S(2)}) collective-permute-start(bf16[320,384]{1,0:T(8,128)(2,1)S(1)} %get-tuple-element.16), channel_id=1, source_target_pairs={{0,2},{1,3},{4,6},{5,7},{8,10},{9,11},{12,14},{13,15},{16,18},{17,... | collective-permute-start | bytes 737288 | tf_op jit(solution)/shard_map/ppermute | solution.py:609
  35.1 2.1 %copy-start.2 = (bf16[3,3,3,384,192]{3,4,2,1,0:T(8,128)(2,1)S(1)}, bf16[3,3,3,384,192]{3,4,2,1,0:T(8,128)(2,1)}, u32[]{:S(2)}) copy-start(bf16[3,3,3,384,192]{3,4,2,1,0:T(8,128)(2,1)} %param.17) | copy-start | bytes 11943940
  44.3 1.2 copy-start.13
  45.4 42.8 %all-gather.11.cloned.1.call-start = ((), (), s32[]{:S(2)}) async-start(), calls=%async_computation.1 | async-start | bytes 3538944 | tf_op jit(solution)/shard_map/all_gather | solution.py:646
  45.4 1.3 %copy-start.9 = (bf16[3,3,3,192,96]{4,3,2,1,0:T(8,128)(2,1)S(1)}, bf16[3,3,3,192,96]{4,3,2,1,0:T(8,128)(2,1)}, u32[]{:S(2)}) copy-start(bf16[3,3,3,192,96]{4,3,2,1,0:T(8,128)(2,1)} %low.1) | copy-start | bytes 2985988
  48.2 1.0 copy-start.10
  49.2 7.4 %copy-start.18 = (f32[384]{0:T(512)S(1)}, f32[384]{0:T(512)}, u32[]{:S(2)}) copy-start(f32[384]{0:T(512)} %param.15) | copy-start | bytes 4612
  49.2 27.2 %copy-start.12 = (bf16[384,1152]{1,0:T(8,128)(2,1)S(1)}, bf16[384,1152]{1,0:T(8,128)(2,1)}, u32[]{:S(2)}) copy-start(bf16[384,1152]{1,0:T(8,128)(2,1)} %qkv.1) | copy-start | bytes 2654212
  49.2 1.4 %copy-start.3 = (bf16[2,4,320,192]{2,3,1,0:T(8,128)(2,1)S(1)}, bf16[2,4,320,192]{2,3,1,0:T(8,128)(2,1)}, u32[]{:S(2)}) copy-start(bf16[2,4,320,192]{2,3,1,0:T(8,128)(2,1)} %param.13) | copy-start | bytes 2949124
  52.4 51.7 %collective-permute-start.2 = (bf16[2,160,384]{2,1,0:T(8,128)(2,1)}, bf16[2,160,384]{2,1,0:T(8,128)(2,1)}, u32[]{:S(2)}, u32[]{:S(2)}) collective-permute-start(bf16[2,160,384]{2,1,0:T(8,128)(2,1)} %low_edge_rows.1), channel_id=1, source_target_pairs={{0,4},{5,1},{4,8},{9,5},{8,12},{13,9},{16,20},{21,17},{20,24},{25,... | collective-permute-start | bytes 737288 | tf_op jit(solution)/shard_map/ppermute | solution.py:604
  76.3 1.2 %copy-start.11 = (bf16[1408,384]{1,0:T(8,128)(2,1)S(1)}, bf16[1408,384]{1,0:T(8,128)(2,1)}, u32[]{:S(2)}) copy-start(bf16[1408,384]{1,0:T(8,128)(2,1)} %all-gather.9.cloned.1.call-done) | copy-start | bytes 3244036
  77.6 1.0 copy-start.16
  78.5 9.6 %copy-start.17 = (f32[192]{0:T(256)S(1)}, f32[192]{0:T(256)}, u32[]{:S(2)}) copy-start(f32[192]{0:T(256)} %param.16) | copy-start | bytes 2308
  88.2 1.2 copy-start.5
  89.4 1.7 %copy-start.6 = (bf16[4,2,96,1536]{3,2,1,0:T(8,128)(2,1)S(1)}, bf16[4,2,96,1536]{3,2,1,0:T(8,128)(2,1)}, u32[]{:S(2)}) copy-start(bf16[4,2,96,1536]{3,2,1,0:T(8,128)(2,1)} %all-gather.11.cloned.1.call-done) | copy-start | bytes 7077892
  101.1 13.9 %collective-permute-start.3 = (bf16[2,192,640]{2,1,0:T(8,128)(2,1)S(1)}, bf16[2,192,640]{2,1,0:T(8,128)(2,1)S(1)}, u32[]{:S(2)}, u32[]{:S(2)}) collective-permute-start(bf16[2,192,640]{2,1,0:T(8,128)(2,1)S(1)} %get-tuple-element.22), channel_id=1, source_target_pairs={{0,2},{1,3},{4,6},{5,7},{8,10},{9,11},{12,14},{13,15},{16,18},{17,... | collective-permute-start | bytes 1474568 | tf_op jit(solution)/shard_map/ppermute | solution.py:609
  106.7 3.7 %copy-start.4 = (bf16[2,4,320,192]{2,3,1,0:T(8,128)(2,1)S(1)}, bf16[2,4,320,192]{2,3,1,0:T(8,128)(2,1)}, u32[]{:S(2)}) copy-start(bf16[2,4,320,192]{2,3,1,0:T(8,128)(2,1)} %param.13) | copy-start | bytes 2949124
Sparse Core Ops, SparseCore 0:
  45.5 30.7 all-gather.8
  77.9 10.2 all-gather.10

commit v3 on v2

--- a/solution.py
+++ b/solution.py
@@ -10,7 +10,6 @@
 
 BF16, F32 = jnp.bfloat16, jnp.float32
 MIB = 1024 * 1024
-GATHER_PAD = 32
 NT = (((1,), (1,)), ((), ()))
 EPS = 1e-06
 
@@ -19,6 +18,10 @@
     return min(56 * MIB, need + 6 * MIB)
 
 
+def cost(flops, moved):
+    return pl.CostEstimate(flops=int(flops), bytes_accessed=int(moved), transcendentals=0)
+
+
 def vmem():
     return pl.BlockSpec(memory_space=pltpu.VMEM)
 
@@ -37,7 +40,7 @@
 
 def normed(values, gain):
     mean = jnp.mean(values * values, axis=-1, keepdims=True)
-    return values * lax.rsqrt(mean + EPS) * gain
+    return values * lax.rsqrt(mean + EPS) * gain.reshape(1, -1)
 
 
 def silu(values):
@@ -55,12 +58,16 @@
     return jnp.where(column == count - 1, 0.0, pltpu.roll(values, count - 1, 0))
 
 
-def edge_kernel(place, latent, cache, rim, sems):
-    frames, rows = latent.shape[:2]
-    line = jnp.where(place[1] == 0, rows - 1, 0)
+def edge_kernel(place, latent, cache, low, rim, low_rim, sems):
+    frames = latent.shape[0]
+
+    def edge(source):
+        return source.at[:, jnp.where(place[1] == 0, source.shape[1] - 1, 0)]
+
     copies = [
-        pltpu.make_async_copy(latent.at[:, line], rim.at[:frames], sems.at[0]),
-        pltpu.make_async_copy(cache.at[:, line], rim.at[frames:], sems.at[1]),
+        pltpu.make_async_copy(edge(latent), rim.at[:frames], sems.at[0]),
+        pltpu.make_async_copy(edge(cache), rim.at[frames:], sems.at[1]),
+        pltpu.make_async_copy(edge(low), low_rim, sems.at[2]),
     ]
     for copy in copies:
         copy.start()
@@ -68,44 +75,21 @@
         copy.wait()
 
 
-def edge_rows(place, latent, cache):
+def edge_rows(place, latent, cache, low):
     frames, rows, width, channels = latent.shape
     return pl.pallas_call(
         edge_kernel,
-        in_specs=[smem(), hbm(), hbm()],
-        out_specs=vmem(),
-        out_shape=jax.ShapeDtypeStruct((frames + cache.shape[0], width, channels), BF16),
-        scratch_shapes=[pltpu.SemaphoreType.DMA((2,))],
-        compiler_params=pltpu.CompilerParams(vmem_limit_bytes=room(0)),
+        in_specs=[smem(), hbm(), hbm(), hbm()],
+        out_specs=[vmem(), vmem()],
+        out_shape=[
+            jax.ShapeDtypeStruct((frames + cache.shape[0], width, channels), BF16),
+            jax.ShapeDtypeStruct(low.shape[:1] + low.shape[2:], BF16),
+        ],
+        scratch_shapes=[pltpu.SemaphoreType.DMA((3,))],
+        compiler_params=pltpu.CompilerParams(vmem_limit_bytes=58 * MIB),
+        cost_estimate=cost(0, 4 * latent.nbytes),
         name="edge_rows",
-    )(place, latent, cache)
-
-
-def low_edge_kernel(place, low, rim, line, sem):
-    past, high, channels, columns = low.shape
-    width = columns // 2
-    copy = pltpu.make_async_copy(low.at[:, jnp.where(place[1] == 0, high - 1, 0)], line, sem)
-    copy.start()
-    pixel = lax.broadcasted_iota(jnp.int32, (width, columns), 0)
-    column = lax.broadcasted_iota(jnp.int32, (width, columns), 1)
-    picks = [(column == 2 * pixel + b).astype(BF16) for b in range(2)]
-    copy.wait()
-    for f in range(past):
-        sides = [dot_nt(pick, line[f]) for pick in picks]
-        rim[f] = jnp.concatenate(sides, axis=-1).astype(BF16)
-
-
-def low_edge_rows(place, low):
-    past, high, channels, columns = low.shape
-    return pl.pallas_call(
-        low_edge_kernel,
-        in_specs=[smem(), hbm()],
-        out_specs=vmem(),
-        out_shape=jax.ShapeDtypeStruct((past, columns // 2, 2 * channels), BF16),
-        scratch_shapes=[pltpu.VMEM((past, channels, columns), BF16), pltpu.SemaphoreType.DMA],
-        compiler_params=pltpu.CompilerParams(vmem_limit_bytes=room(0)),
-        name="low_edge_rows",
-    )(place, low)
+    )(place, latent, cache, low)
 
 
 def weight_kernel(up, low, folded, turned):
@@ -145,6 +129,7 @@
             jax.ShapeDtypeStruct((2 * taps * part, 12 * channels), BF16),
         ],
         compiler_params=pltpu.CompilerParams(vmem_limit_bytes=room(6 * up.nbytes + 6 * low.nbytes)),
+        cost_estimate=cost(2 * low.size * part, 4 * up.nbytes + 4 * low.nbytes),
         name="weight_forms",
     )(up, low)
 
@@ -153,18 +138,15 @@
     return jnp.concatenate([from_left(row), row, from_right(row)], axis=-1).astype(BF16)
 
 
-def tap_rows(weights, dy):
-    return jnp.concatenate([weights[dy, dx] for dx in range(3)], axis=-1)
-
-
-def mid_inner_kernel(place, latent, gain, weights, acc, held, seen, sems):
+def tap_rows(weights, tap, dy):
+    return jnp.concatenate([weights[tap, dy, dx] for dx in range(3)], axis=-1)
+
+
+def mid_inner_kernel(place, latent, gain, weights, acc, seen):
     frames, rows, width, channels = latent.shape
     taps, part = weights.shape[0], weights.shape[-2]
     past = taps - 1
     size = rows * width
-    copies = [pltpu.make_async_copy(weights.at[k], held.at[k], sems.at[k]) for k in range(taps)]
-    for copy in copies:
-        copy.start()
     for f in range(frames):
         for l in range(rows):
             seen[f, l] = spread(silu(normed(latent[f, l].astype(F32), gain[...])))
@@ -176,14 +158,13 @@
     for f in range(frames, frames + past):
         acc[f] = jnp.zeros_like(acc[f])
     for tap in range(taps):
-        copies[tap].wait()
         for dy in (1, 0, 2):
             low, high = max(0, 1 - dy), min(rows, rows + 1 - dy)
             span = (high - low) * width
             left = jnp.concatenate(
                 [seen[f, low + dy - 1 : high + dy - 1].reshape(span, 3 * channels) for f in range(frames)], axis=0
             )
-            term = dot_nt(left, tap_rows(held[tap], dy))
+            term = dot_nt(left, tap_rows(weights, tap, dy))
             for f in range(frames):
                 acc[f + past - tap, low * width : high * width] += term[f * span : (f + 1) * span]
 
@@ -194,41 +175,29 @@
     size = rows * width
     return pl.pallas_call(
         mid_inner_kernel,
-        in_specs=[smem(), vmem(), vmem(), hbm()],
+        in_specs=[smem(), vmem(), vmem(), vmem()],
         out_specs=vmem(),
         out_shape=jax.ShapeDtypeStruct((frames + taps - 1, size, part), F32),
-        scratch_shapes=[
-            pltpu.VMEM(weights.shape, BF16),
-            pltpu.VMEM((frames, rows, width, 3 * channels), BF16),
-            pltpu.SemaphoreType.DMA((taps,)),
-        ],
-        compiler_params=pltpu.CompilerParams(vmem_limit_bytes=room(weights.nbytes + 10 * latent.nbytes)),
-        cost_estimate=pl.CostEstimate(
-            flops=2 * 18 * frames * size * channels * part, bytes_accessed=weights.nbytes, transcendentals=0),
+        scratch_shapes=[pltpu.VMEM((frames, rows, width, 3 * channels), BF16)],
+        compiler_params=pltpu.CompilerParams(vmem_limit_bytes=room(10 * latent.nbytes)),
+        cost_estimate=cost(2 * 27 * frames * size * channels * part, weights.nbytes),
         name="mid_inner",
     )(place, latent, gain, weights)
 
 
-def mid_rim_kernel(started, halo, gain, weights, own, passed, held, seen, acc, sems):
+def mid_rim_kernel(started, halo, gain, weights, own, passed, seen, acc):
     total, size, part = started.shape
     sides, _, width, channels = halo.shape
     taps = weights.shape[0]
     past = taps - 1
     frames = total - past
-    copies = []
-    for k in range(taps):
-        for side in range(2):
-            copies.append(pltpu.make_async_copy(weights.at[k, 2 * side], held.at[k, side], sems.at[2 * k + side]))
-            copies[-1].start()
     for side in range(2):
         for f in range(frames):
             seen[side, f] = spread(silu(normed(halo[side, f].astype(F32), gain[...])))
     acc[...] = started[...]
     for tap in range(taps):
         for side in range(2):
-            copies[2 * tap + side].wait()
-            kernel = jnp.concatenate([held[tap, side, dx] for dx in range(3)], axis=-1)
-            term = dot_nt(seen[side].reshape(frames * width, 3 * channels), kernel)
+            term = dot_nt(seen[side].reshape(frames * width, 3 * channels), tap_rows(weights, tap, 2 * side))
             at = slice(0, width) if side == 0 else slice(size - width, size)
             for f in range(frames):
                 acc[f + past - tap, at] += term[f * width : (f + 1) * width]
@@ -244,24 +213,23 @@
     sides, _, width, channels = halo.shape
     return pl.pallas_call(
         mid_rim_kernel,
-        in_specs=[vmem(), vmem(), vmem(), hbm()],
+        in_specs=[vmem()] * 4,
         out_specs=[vmem(), vmem()],
         out_shape=[
             jax.ShapeDtypeStruct((size, frames * part), F32),
             jax.ShapeDtypeStruct((size, past * part), BF16),
         ],
         scratch_shapes=[
-            pltpu.VMEM((taps, 2) + weights.shape[2:], BF16),
             pltpu.VMEM((2, frames, width, 3 * channels), BF16),
             pltpu.VMEM(started.shape, F32),
-            pltpu.SemaphoreType.DMA((2 * taps,)),
-        ],
-        compiler_params=pltpu.CompilerParams(vmem_limit_bytes=room(weights.nbytes + 4 * started.nbytes)),
+        ],
+        compiler_params=pltpu.CompilerParams(vmem_limit_bytes=room(3 * halo.nbytes + 3 * started.nbytes)),
+        cost_estimate=cost(2 * 18 * frames * width * channels * part * taps, weights.nbytes),
         name="mid_rim",
     )(started, halo, gain, weights)
 
 
-def mid_cache_kernel(place, own, cache, halo, weights, out, held, seen, sems):
+def mid_cache_kernel(place, own, cache, halo, weights, out, seen):
     past, rows, width, channels = cache.shape
     part = weights.shape[-2]
     frames = halo.shape[1] - past
@@ -269,9 +237,6 @@
 
     @pl.when(place[0] == 0)
     def _():
-        copies = [pltpu.make_async_copy(weights.at[k], held.at[k], sems.at[k]) for k in range(past)]
-        for copy in copies:
-            copy.start()
         for f in range(past):
             for l in range(rows + 2):
                 if l == 0 or l == rows + 1:
@@ -280,14 +245,13 @@
                     row = cache[f, l - 1]
                 seen[f, l] = spread(row.astype(F32))
         for tap in range(past):
-            copies[tap].wait()
             count = past - tap
             total = None
             for dy in range(3):
                 left = jnp.concatenate(
                     [seen[t + tap, dy : dy + rows].reshape(rows * width, 3 * channels) for t in range(count)], axis=0
                 )
-                term = dot_nt(left, tap_rows(held[tap], dy))
+                term = dot_nt(left, tap_rows(weights, tap, dy))
                 total = term if total is None else total + term
             for t in range(count):
                 out[:, t * part : (t + 1) * part] += total[t * rows * width : (t + 1) * rows * width]
@@ -298,18 +262,12 @@
     part = weights.shape[-2]
     return pl.pallas_call(
         mid_cache_kernel,
-        in_specs=[smem(), vmem(), vmem(), vmem(), hbm()],
+        in_specs=[smem()] + [vmem()] * 4,
         out_specs=vmem(),
         out_shape=jax.ShapeDtypeStruct(own.shape, F32),
-        scratch_shapes=[
-            pltpu.VMEM((past,) + weights.shape[1:], BF16),
-            pltpu.VMEM((past, rows + 2, width, 3 * channels), BF16),
-            pltpu.SemaphoreType.DMA((past,)),
-        ],
-        compiler_params=pltpu.CompilerParams(
-            vmem_limit_bytes=room(12 * cache.nbytes + 3 * own.nbytes + weights.nbytes)),
-        cost_estimate=pl.CostEstimate(
-            flops=6 * 9 * rows * width * channels * part, bytes_accessed=weights.nbytes, transcendentals=0),
+        scratch_shapes=[pltpu.VMEM((past, rows + 2, width, 3 * channels), BF16)],
+        compiler_params=pltpu.CompilerParams(vmem_limit_bytes=room(12 * cache.nbytes + 2 * own.nbytes)),
+        cost_estimate=cost(6 * 9 * rows * width * channels * part, weights.nbytes),
         name="mid_cached",
     )(place, own, cache, halo, weights)
 
@@ -368,6 +326,7 @@
             pltpu.VMEM((pixels, channels), BF16),
         ],
         compiler_params=pltpu.CompilerParams(vmem_limit_bytes=room(need)),
+        cost_estimate=cost(4 * channels * (pixels * channels + rows * width * (pixels + channels)), qkv.nbytes),
         name="frame_attention",
     )(place, frame, gain, qkv, proj)
 
@@ -381,24 +340,16 @@
     return jnp.concatenate([block[dy : dy + high].reshape(high * width, lanes) for dy in range(3)], axis=-1)
 
 
-def low_kernel(past, place, tile, up_weights, gain, weights, passed, window, kept, seen, upper, up, held, sems):
+def low_kernel(past, place, tile, up, gain, weights, passed, window, kept, seen, upper):
     frames, ext, width, channels = tile.shape
     chans, _, _, part = up.shape[:4]
     low = chans * part
     rows = ext - 2
     high = 2 * rows
     phases = passed.shape[1]
-    copies = [
-        pltpu.make_async_copy(up_weights, up, sems.at[0]),
-        pltpu.make_async_copy(weights.at[: past * phases], held, sems.at[1]),
-    ]
-    for copy in copies:
-        copy.start()
     for f in range(frames):
         for l in range(ext):
             seen[f, l] = spread(tile[f, l].astype(F32))
-    copies[0].wait()
-    for f in range(frames):
         for a in range(2):
             for b in range(2):
                 lanes = slice(b * channels, (b + 2) * channels)
@@ -420,12 +371,11 @@
                 sides = [jnp.where(place[2] == place[3] - 1, 0.0, side) for side in sides]
             window[f, j] = windowed(*sides)
 
-    copies[-1].wait()
     sums = [None] * past
     for f in range(frames):
         count = min(f + past - frames + 1, past)
         if count > 0:
-            got = dot_nt(held[: count * phases], stacked(window[f], high))
+            got = dot_nt(weights[: count * phases], stacked(window[f], high))
             for tap in range(count):
                 t = f + past - tap - frames
                 term = got[tap * phases : (tap + 1) * phases]
@@ -441,10 +391,10 @@
     high = 2 * (ext - 2)
     past = taps - 1
     phases = 2 * part
-    need = 5 * tile.nbytes + up.nbytes + 2 * weights.nbytes + 10 * frames * high * width * low * 4
+    need = 4 * tile.nbytes + 10 * frames * high * width * low * 4
     return pl.pallas_call(
         functools.partial(low_kernel, past),
-        in_specs=[smem(), vmem(), hbm(), vmem(), hbm()],
+        in_specs=[smem()] + [vmem()] * 4,
         out_specs=[vmem()] * 3,
         out_shape=[
             jax.ShapeDtypeStruct((past, phases, high * width), BF16),
@@ -454,11 +404,9 @@
         scratch_shapes=[
             pltpu.VMEM((frames, ext, width, 3 * channels), BF16),
             pltpu.VMEM((high + 2, 2, width, low), BF16),
-            pltpu.VMEM(up.shape, BF16),
-            pltpu.VMEM((past * phases, weights.shape[1]), BF16),
-            pltpu.SemaphoreType.DMA((2,)),
         ],
         compiler_params=pltpu.CompilerParams(vmem_limit_bytes=room(need)),
+        cost_estimate=cost(96 * frames * high * width * channels * low // 4, up.nbytes + weights.nbytes),
         name="low_stage",
     )(place, tile, up, gain, weights)
 
@@ -497,7 +445,7 @@
     phases = weights.shape[0] // taps
     high = ext - 2
     starts, span = lane_windows(high, width)
-    need = 3 * window.nbytes + 2 * weights.nbytes + 3 * frames * phases * high * width * 4
+    need = window.nbytes + 3 * frames * phases * high * width * 4
     return pl.pallas_call(
         lambda place, *refs: low_own_kernel(place, starts, *refs),
         in_specs=[smem()] + [vmem()] * 3,
@@ -507,8 +455,7 @@
             jax.ShapeDtypeStruct((high, 2 * span, 2 * width), BF16),
         ],
         compiler_params=pltpu.CompilerParams(vmem_limit_bytes=room(need)),
-        cost_estimate=pl.CostEstimate(
-            flops=6 * 9 * high * width * lanes * phases // 2, bytes_accessed=weights.nbytes, transcendentals=0),
+        cost_estimate=cost(6 * 9 * high * width * lanes * phases // 2, weights.nbytes),
         name="low_own",
     )(place, window, kept, weights)
 
@@ -526,12 +473,8 @@
         picks = [(column == 2 * pixel + b).astype(BF16) for b in range(2)]
         for f in range(past):
             for j in range(high + 2):
-                if 1 <= j <= high:
-                    sides = [dot_nt(pick, cache[f, j - 1]) for pick in picks]
-                else:
-                    rim = halo[0 if j == 0 else 1, f].astype(F32)
-                    sides = [rim[:, :channels], rim[:, channels:]]
-                window[j] = windowed(*sides)
+                row = cache[f, j - 1] if 1 <= j <= high else halo[0 if j == 0 else 1, f]
+                window[j] = windowed(*[dot_nt(pick, row) for pick in picks])
             got = dot_nt(weights[: (f + 1) * phases], stacked(window[...], high))
             for tap in range(f + 1):
                 out[f - tap] += got[tap * phases : (tap + 1) * phases]
@@ -546,10 +489,8 @@
         out_specs=vmem(),
         out_shape=jax.ShapeDtypeStruct(own.shape, F32),
         scratch_shapes=[pltpu.VMEM((high + 2, columns // 2, 4 * channels), BF16)],
-        compiler_params=pltpu.CompilerParams(
-            vmem_limit_bytes=room(3 * own.nbytes + 2 * weights.nbytes + 16 * cache.nbytes)),
-        cost_estimate=pl.CostEstimate(
-            flops=6 * 9 * pixels * channels * own.shape[1] // 2, bytes_accessed=weights.nbytes, transcendentals=0),
+        compiler_params=pltpu.CompilerParams(vmem_limit_bytes=room(2 * own.nbytes + 16 * cache.nbytes)),
+        cost_estimate=cost(6 * 9 * pixels * channels * own.shape[1] // 2, weights.nbytes),
         name="low_cached",
     )(place, own, cache, halo, weights)
 
@@ -588,7 +529,8 @@
         in_specs=[vmem()] * 3,
         out_specs=vmem(),
         out_shape=jax.ShapeDtypeStruct((frames, high, phases // 2, 2 * width), BF16),
-        compiler_params=pltpu.CompilerParams(vmem_limit_bytes=room(4 * own.nbytes + 2 * weave.nbytes)),
+        compiler_params=pltpu.CompilerParams(vmem_limit_bytes=room(3 * own.nbytes)),
+        cost_estimate=cost(2 * own.size * weave.shape[1], own.nbytes),
         name="finish",
     )(own, passed, weave)
 
@@ -634,11 +576,12 @@
     mid_weights = jnp.swapaxes(conv_mid, 3, 4)
     low_cache = jnp.swapaxes(cache_low, 2, 3)
 
-    rim = to_neighbour(edge_rows(place, latent, cache_mid), False)
-    low_rim = to_neighbour(low_edge_rows(place, low_cache), True)
-    started = mid_inner(place, latent, gain_mid[None], mid_weights)
+    rim, low_rim = edge_rows(place, latent, cache_mid, low_cache)
+    rim = to_neighbour(rim, False)
+    low_rim = to_neighbour(low_rim, True)
+    started = mid_inner(place, latent, gain_mid, mid_weights)
     halo = lax.all_gather(rim, "chan")
-    own, passed = mid_rim(started, halo, gain_mid[None], mid_weights)
+    own, passed = mid_rim(started, halo, gain_mid, mid_weights)
     arrived = to_next(passed)
     own = mid_cached(place, own, cache_mid, halo, mid_weights)
 
@@ -655,12 +598,12 @@
     mine = choices[0]
     for f in range(1, frames):
         mine = jnp.where(chan == f, choices[f], mine)
-    frame = lax.all_gather(jnp.pad(mine, ((0, GATHER_PAD), (0, 0))), "rows")
-
-    reached = attention(place, frame, gain_attn[None], attn_qkv, attn_proj, rows, width)
+    frame = lax.all_gather(mine, "rows")
+
+    reached = attention(place, frame, gain_attn, attn_qkv, attn_proj, rows, width)
     tile = lax.all_gather(reached, "chan")
 
-    passed_low, window, kept = low_stage(place, tile, up, gain_low[None], low_weights, taps)
+    passed_low, window, kept = low_stage(place, tile, up, gain_low, low_weights, taps)
     arrived_low = to_next(passed_low)
     own_low, weave = low_own(place, window, kept, low_weights, taps)
     low_rim, _ = lax.optimization_barrier((low_rim, passed_low))

time: 124 us -> 107 us (0.86)
  waiting for transfers between devices: 20.4 us -> 0.03 us
  blocking collectives: 10.6 us -> 30.6 us
  local copies, waits for them, and re-layouts: 17.7 us -> 8.84 us
  Pallas kernels: 45 us -> 38.9 us
  starting transfers between devices: 15.6 us -> 13.5 us
    all_gather x0 -> x1, blocking collectives: none -> 20.8 us  [body(): frame = lax.all_gather(mine, 'rows')]
    all_gather x1 -> x0, waiting for transfers between devices: 19.8 us -> none  [body(): frame = lax.all_gather(jnp.pad(mine, ((0, GATHER_PAD), (0, 0))), 'rows')]
    pallas_call x6 -> x5, Pallas kernels: 28.3 us -> 20.4 us  [the longest x1 8.8 us: low_stage(): pl.pallas_call(functools.partial(low_kernel, past), in_specs=[smem()] + [...]
    unnamed x38, local copies, waits for them, and re-layouts: 16.1 us -> 8.67 us
    ppermute x2, starting transfers between devices: 6.39 us -> 5.07 us  [to_next(): lax.ppermute(values, 'segment', [(i, i + 1) for i in range(count - 1)])]
  transfers between devices with their start and end apart: 6 -> 5, of which waited for: 3 -> 0; matrix products, arithmetic and copies ran while one was open for 1% -> 0% of each run, Pallas kernels for 30% -> 33%
where the time goes in v3:
time: 107 us; the launch traced here: 106 us
  Pallas kernels  38.9 us (36%)
  blocking collectives  30.6 us (29%)
  between operations  13.7 us (13%)
  starting transfers between devices  13.5 us (13%)
  local copies, waits for them, and re-layouts  8.84 us (8%)
    all_gather x1, blocking collectives, body(): frame = lax.all_gather(mine, 'rows')  20.8 us
    pallas_call x1, Pallas kernels, low_stage(): pl.pallas_call(functools.partial(low_kernel, past), in_specs=[smem()] + [...  8.8 us
    unnamed x38, local copies, waits for them, and re-layouts  8.67 us
    ppermute x2, starting transfers between devices, to_neighbour(): return lax.ppermute(values, ('rows', 'segment', 'chan'), route)  8.43 us
    pallas_call x1, Pallas kernels, attention(): pl.pallas_call(functools.partial(attn_kernel, tile_rows), in_specs=[smem(...  6.21 us
    ppermute x2, starting transfers between devices, to_next(): lax.ppermute(values, 'segment', [(i, i + 1) for i in range(count - 1)])  5.07 us
    pallas_call x1, Pallas kernels, low_cached(): pl.pallas_call(low_cache_kernel, in_specs=[smem()] + [vmem()] * 4, out_sp...  4.76 us
    pallas_call x1, Pallas kernels, mid_inner(): pl.pallas_call(mid_inner_kernel, in_specs=[smem(), vmem(), vmem(), vmem()...  3.87 us
  transfers between devices with their start and end apart: 5, of which 0 were waited for; matrix products, arithmetic and copies ran while one was open for 0% of the time, Pallas kernels for 33%

profile of v3, /device:TPU:0, one launch (start us, length us, event | category | flops | bytes accessed | tf_op | source)
XLA Modules:
  0.0 106.3 jit_solution(4375984789966176602)
XLA Ops:
  6.5 0.6 pad_add_fusion.place
  7.2 2.8 %edge_rows.1 = (bf16[4,160,384]{2,1,0:T(8,128)(2,1)}, bf16[2,192,320]{2,1,0:T(8,128)(2,1)}) custom-call(s32[4]{0:T(128)} %pad_add_fusion.place, bf16[2,2,160,384]{3,2,1,0:T(8,128)(2,1)} %latent.3, bf16[2,2,160,384]{3,2,1,0:T(8,128)(2,1)} %cache.3, bf16[2,4,192,320]{3,2,1,0:T(8,128)(2,1)} %bitcast.12), custom_call_target="tpu_custom_call" | custom-call | bytes 1966080 | tf_op jit(solution)/shard_map/edge_rows/pallas_call | solution.py:80
  9.9 5.0 %collective-permute-start = (bf16[4,160,384]{2,1,0:T(8,128)(2,1)}, bf16[4,160,384]{2,1,0:T(8,128)(2,1)S(1)}, u32[]{:S(2)}, u32[]{:S(2)}) collective-permute-start(bf16[4,160,384]{2,1,0:T(8,128)(2,1)} %get-tuple-element.17), channel_id=1, source_target_pairs={{0,4},{5,1},{2,6},{7,3},{4,8},{9,5},{6,10},{11,7},{8,12},{13,9},{1... | collective-permute-start | bytes 1474568 | tf_op jit(solution)/shard_map/ppermute | solution.py:546
  14.9 0.0 copy-start.10
  15.0 2.4 %weight_forms.1 = (bf16[2,2,96,1536]{3,2,1,0:T(8,128)(2,1)}, bf16[576,2304]{1,0:T(8,128)(2,1)S(1)}) custom-call(bf16[3,3,96,384]{3,2,1,0:T(8,128)(2,1)S(1)} %bitcast.21, bf16[3,3,3,192,96]{4,3,2,1,0:T(8,128)(2,1)S(1)} %copy-done.7), custom_call_target="tpu_custom_call" | custom-call | flops 95551488 | bytes 6635520 | tf_op jit(solution)/shard_map/weight_forms/pallas_call | solution.py:123
  17.4 1.5 %copy-done.4 = bf16[576,2304]{1,0:T(8,128)(2,1)} copy-done((bf16[576,2304]{1,0:T(8,128)(2,1)}, bf16[576,2304]{1,0:T(8,128)(2,1)S(1)}, u32[]{:S(2)}) %copy-start.4) | copy-done | bytes 2654232
  18.9 0.0 all-gather.7.cloned.1.call-update
  18.9 0.0 copy-start.1
  18.9 2.1 %copy-done.1 = bf16[3,3,3,384,192]{3,4,2,1,0:T(8,128)(2,1)S(1)} copy-done((bf16[3,3,3,384,192]{3,4,2,1,0:T(8,128)(2,1)S(1)}, bf16[3,3,3,384,192]{3,4,2,1,0:T(8,128)(2,1)}, u32[]{:S(2)}) %copy-start.1) | copy-done | bytes 3981336
  21.1 3.9 %mid_inner.1.started = f32[4,320,192]{2,1,0:T(8,128)S(1)} custom-call(s32[4]{0:T(128)S(1)} %copy-done.11, bf16[2,2,160,384]{3,2,1,0:T(8,128)(2,1)S(1)} %copy-done.10, f32[384]{0:T(512)S(1)} %copy-done.15, bf16[3,3,3,192,384]{4,3,2,1,0:T(8,128)(2,1)S(1)} %bitcast.14), custom_call_target="tpu_custom_call" | custom-call | flops 2548039680 | bytes 3981312 | tf_op jit(solution)/shard_map/mid_inner/pallas_call | solution.py:176
  24.9 2.5 %all-gather = bf16[8,160,384]{2,1,0:T(8,128)(2,1)S(1)} all-gather(bf16[4,160,384]{2,1,0:T(8,128)(2,1)S(1)} %collective-permute-done), channel_id=2, replica_groups=mesh['groups'=2,'rows'=4,'segment'=2,'chan'=2] {'chan'}, dimensions={0}, use_global_device_ids=true | all-gather | bytes 1474560 | tf_op jit(solution)/shard_map/all_gather | solution.py:583
  27.5 2.2 %mid_rim.1 = (f32[320,384]{1,0:T(8,128)S(1)}, bf16[320,384]{1,0:T(8,128)(2,1)S(1)}) custom-call(f32[4,320,192]{2,1,0:T(8,128)S(1)} %mid_inner.1.started, bf16[2,4,160,384]{3,2,1,0:T(8,128)(2,1)S(1)} %bitcast.17, f32[384]{0:T(512)S(1)} %copy-done.15, bf16[3,3,3,192,384]{4,3,2,1,0:T(8,128)(2,1)S(1)} %bitcast.15), custom_call_target="tpu_custom_call" | custom-call | flops 2548039680 | bytes 3981312 | tf_op jit(solution)/shard_map/mid_rim/pallas_call | solution.py:214
  29.6 3.4 %collective-permute-start.1 = (bf16[320,384]{1,0:T(8,128)(2,1)S(1)}, bf16[320,384]{1,0:T(8,128)(2,1)S(1)}, u32[]{:S(2)}, u32[]{:S(2)}) collective-permute-start(bf16[320,384]{1,0:T(8,128)(2,1)S(1)} %get-tuple-element.19), channel_id=1, source_target_pairs={{0,2},{1,3},{4,6},{5,7},{8,10},{9,11},{12,14},{13,15},{16,18},{17,... | collective-permute-start | bytes 737288 | tf_op jit(solution)/shard_map/ppermute | solution.py:551
  33.1 3.5 %collective-permute-start.2 = (bf16[2,192,320]{2,1,0:T(8,128)(2,1)S(1)}, bf16[2,192,320]{2,1,0:T(8,128)(2,1)S(1)}, u32[]{:S(2)}, u32[]{:S(2)}) collective-permute-start(bf16[2,192,320]{2,1,0:T(8,128)(2,1)S(1)} %copy-done.18), channel_id=1, source_target_pairs={{0,4},{5,1},{4,8},{9,5},{8,12},{13,9},{16,20},{21,17},{20,24},{25,... | collective-permute-start | bytes 737288 | tf_op jit(solution)/shard_map/ppermute | solution.py:546
  36.6 0.0 copy-start.3
  36.6 2.1 %copy-done.3 = bf16[3,3,3,384,192]{3,4,2,1,0:T(8,128)(2,1)S(1)} copy-done((bf16[3,3,3,384,192]{3,4,2,1,0:T(8,128)(2,1)S(1)}, bf16[3,3,3,384,192]{3,4,2,1,0:T(8,128)(2,1)}, u32[]{:S(2)}) %copy-start.3) | copy-done | bytes 3981336
  38.7 2.8 %mid_cached.1 = f32[320,384]{1,0:T(8,128)S(1)} custom-call(s32[4]{0:T(128)S(1)} %copy-done.11, f32[320,384]{1,0:T(8,128)S(1)} %get-tuple-element.18.own, bf16[2,2,160,384]{3,2,1,0:T(8,128)(2,1)S(1)} %copy-done.6, bf16[2,4,160,384]{3,2,1,0:T(8,128)(2,1)S(1)} %bitcast.18, bf16[3,3,3,192,384]{4,3,2,1,0:T(8,128)(2,1)S(1)} %bitcast.16), custom_call_target="tpu_custom_call" | custom-call | flops 1274019840 | bytes 3981312 | tf_op jit(solution)/shard_map/mid_cached/pallas_call | solution.py:263
  41.5 0.1 add_convert_fusion
  41.6 2.2 %all-gather.1 = bf16[640,384]{1,0:T(8,128)(2,1)S(1)} all-gather(bf16[320,384]{1,0:T(8,128)(2,1)S(1)} %add_convert_fusion), channel_id=3, replica_groups=mesh['groups'=2,'rows'=4,'segment'=2,'chan'=2] {'chan'}, dimensions={0}, use_global_device_ids=true | all-gather | bytes 737280 | tf_op jit(solution)/shard_map/all_gather | solution.py:592
  43.7 0.2 fusion
  43.9 0.2 maximum_select_fusion
  44.1 20.8 %all_gather.38.frame = bf16[4,320,384]{2,1,0:T(8,128)(2,1)S(1)} all-gather(bf16[1,320,384]{2,1,0:T(8,128)(2,1)S(1)} %maximum_select_fusion), channel_id=1, replica_groups=mesh['groups'=2,'rows'=4,'segment'=2,'chan'=2] {'rows'}, dimensions={0}, use_global_device_ids=true | all-gather | bytes 1228800 | tf_op jit(solution)/shard_map/all_gather | solution.py:601
  64.9 6.2 %frame_attention.1 = bf16[4,160,384]{2,1,0:T(8,128)(2,1)S(1)} custom-call(s32[4]{0:T(128)S(1)} %copy-done.11, bf16[4,320,384]{2,1,0:T(8,128)(2,1)S(1)} %all_gather.38.frame, f32[384]{0:T(512)S(1)} %copy-done.16, bf16[384,1152]{1,0:T(8,128)(2,1)S(1)} %copy-done.13, bf16[384,384]{1,0:T(8,128)(2,1)S(1)} %copy-done.14), custom_call_target="tpu_custom_call" | custom-call | flops 2390753280 | bytes 884736 | tf_op jit(solution)/shard_map/frame_attention/pallas_call | solution.py:318
  71.2 2.6 %all-gather.2 = bf16[8,160,384]{2,1,0:T(8,128)(2,1)} all-gather(bf16[4,160,384]{2,1,0:T(8,128)(2,1)S(1)} %frame_attention.1), channel_id=4, replica_groups=mesh['groups'=2,'rows'=4,'segment'=2,'chan'=2] {'chan'}, dimensions={0}, use_global_device_ids=true | all-gather | bytes 1474560 | tf_op jit(solution)/shard_map/all_gather | solution.py:604
  73.8 1.2 %copy-done.8 = bf16[8,160,384]{2,1,0:T(8,128)(2,1)S(1)} copy-done((bf16[8,160,384]{2,1,0:T(8,128)(2,1)S(1)}, bf16[8,160,384]{2,1,0:T(8,128)(2,1)}, u32[]{:S(2)}) %copy-start.8) | copy-done | bytes 983064
  75.0 1.7 %copy-done.12 = bf16[4,2,96,1536]{3,2,1,0:T(8,128)(2,1)S(1)} copy-done((bf16[4,2,96,1536]{3,2,1,0:T(8,128)(2,1)S(1)}, bf16[4,2,96,1536]{3,2,1,0:T(8,128)(2,1)}, u32[]{:S(2)}) %copy-start.12) | copy-done | bytes 2359320
  76.7 8.8 %low_stage.1 = (bf16[2,192,640]{2,1,0:T(8,128)(2,1)S(1)}, bf16[2,6,160,768]{3,2,1,0:T(8,128)(2,1)S(1)}, bf16[2,4,160,384]{3,2,1,0:T(8,128)(2,1)S(1)}) custom-call(s32[4]{0:T(128)S(1)} %copy-done.11, bf16[2,4,160,384]{3,2,1,0:T(8,128)(2,1)S(1)} %bitcast.20, bf16[2,2,2,96,1536]{4,3,2,1,0:T(8,128)(2,1)S(1)} %bitcast.22, f32[192]{0:T(256)S(1)} %copy-done.17, ...), custom_call_target="tpu_custom_call" | custom-call | flops 2264924160 | bytes 5013504 | tf_op jit(solution)/shard_map/low_stage/pallas_call | solution.py:395
  85.5 1.7 %collective-permute-start.3 = (bf16[2,192,640]{2,1,0:T(8,128)(2,1)S(1)}, bf16[2,192,640]{2,1,0:T(8,128)(2,1)S(1)}, u32[]{:S(2)}, u32[]{:S(2)}) collective-permute-start(bf16[2,192,640]{2,1,0:T(8,128)(2,1)S(1)} %get-tuple-element.26), channel_id=1, source_target_pairs={{0,2},{1,3},{4,6},{5,7},{8,10},{9,11},{12,14},{13,15},{16,18},{17,... | collective-permute-start | bytes 1474568 | tf_op jit(solution)/shard_map/ppermute | solution.py:551
  87.2 2.4 %all-gather.4 = bf16[4,192,320]{2,1,0:T(8,128)(2,1)S(1)} all-gather(bf16[2,192,320]{2,1,0:T(8,128)(2,1)S(1)} %collective-permute-done.2), channel_id=6, replica_groups=mesh['groups'=2,'rows'=4,'segment'=2,'chan'=2] {'chan'}, dimensions={0}, use_global_device_ids=true | all-gather | bytes 737280 | tf_op jit(solution)/shard_map/all_gather | solution.py:610
  89.6 3.7 %low_own.1 = (f32[2,192,640]{2,1,0:T(8,128)S(1)}, bf16[4,512,320]{2,1,0:T(8,128)(2,1)S(1)}) custom-call(s32[4]{0:T(128)S(1)} %copy-done.11, bf16[2,6,160,768]{3,2,1,0:T(8,128)(2,1)S(1)} %get-tuple-element.22.refs_0_, bf16[2,4,160,384]{3,2,1,0:T(8,128)(2,1)S(1)} %get-tuple-element.23.refs_1_, bf16[576,2304]{1,0:T(8,128)(2,1)S(1)} %copy-done.5), custom_call_target="tpu_custom_call" | custom-call | flops 2548039680 | bytes 2654208 | tf_op jit(solution)/shard_map/low_own/pallas_call | solution.py:449
  93.3 4.8 %low_cached.1.own = f32[2,192,640]{2,1,0:T(8,128)S(1)} custom-call(s32[4]{0:T(128)S(1)} %copy-done.11, f32[2,192,640]{2,1,0:T(8,128)S(1)} %get-tuple-element.24.own, bf16[2,4,192,320]{3,2,1,0:T(8,128)(2,1)S(1)} %bitcast.13, bf16[2,2,192,320]{3,2,1,0:T(8,128)(2,1)S(1)} %bitcast.19, bf16[576,2304]{1,0:T(8,128)(2,1)S(1)} %copy-done.5), custom_call_target="tpu_custom_call" | custom-call | flops 1274019840 | bytes 2654208 | tf_op jit(solution)/shard_map/low_cached/pallas_call | solution.py:486
  98.1 1.4 %finish.1 = bf16[2,4,96,320]{3,2,1,0:T(8,128)(2,1)} custom-call(f32[2,192,640]{2,1,0:T(8,128)S(1)} %low_cached.1.own, bf16[2,192,640]{2,1,0:T(8,128)(2,1)S(1)} %collective-permute-done.3.passed, bf16[4,512,320]{2,1,0:T(8,128)(2,1)S(1)} %get-tuple-element.28.weave), custom_call_target="tpu_custom_call" | custom-call | flops 251658240 | bytes 983040 | tf_op jit(solution)/shard_map/finish/pallas_call | solution.py:527
  (36 shorter events, 0.1 us)
Async XLA Ops:
  6.5 8.4 %copy-start.7 = (bf16[3,3,3,192,96]{4,3,2,1,0:T(8,128)(2,1)S(1)}, bf16[3,3,3,192,96]{4,3,2,1,0:T(8,128)(2,1)}, u32[]{:S(2)}) copy-start(bf16[3,3,3,192,96]{4,3,2,1,0:T(8,128)(2,1)} %low.1) | copy-start | bytes 2985988
  6.5 8.4 %copy-start.9 = (bf16[3,3,384,96]{2,3,1,0:T(8,128)(2,1)S(1)}, bf16[3,3,384,96]{2,3,1,0:T(8,128)(2,1)}, u32[]{:S(2)}) copy-start(bf16[3,3,384,96]{2,3,1,0:T(8,128)(2,1)} %param.20) | copy-start | bytes 1990660
  6.5 67.3 %all-gather.7.cloned.1.call-start = ((), (), s32[]{:S(2)}) async-start(), calls=%async_computation | async-start | bytes 3538944 | tf_op jit(solution)/shard_map/all_gather | solution.py:589
  9.9 15.0 %collective-permute-start = (bf16[4,160,384]{2,1,0:T(8,128)(2,1)}, bf16[4,160,384]{2,1,0:T(8,128)(2,1)S(1)}, u32[]{:S(2)}, u32[]{:S(2)}) collective-permute-start(bf16[4,160,384]{2,1,0:T(8,128)(2,1)} %get-tuple-element.17), channel_id=1, source_target_pairs={{0,4},{5,1},{2,6},{7,3},{4,8},{9,5},{6,10},{11,7},{8,12},{13,9},{1... | collective-permute-start | bytes 1474568 | tf_op jit(solution)/shard_map/ppermute | solution.py:546
  14.9 4.0 %copy-start.10 = (bf16[2,2,160,384]{3,2,1,0:T(8,128)(2,1)S(1)}, bf16[2,2,160,384]{3,2,1,0:T(8,128)(2,1)}, u32[]{:S(2)}) copy-start(bf16[2,2,160,384]{3,2,1,0:T(8,128)(2,1)} %latent.3) | copy-start | bytes 1474564
  14.9 4.0 %copy-start.11 = (s32[4]{0:T(128)S(1)}, s32[4]{0:T(128)}, u32[]{:S(2)}) copy-start(s32[4]{0:T(128)} %pad_add_fusion.place) | copy-start | bytes 52
  14.9 4.0 %copy-start.15 = (f32[384]{0:T(512)S(1)}, f32[384]{0:T(512)}, u32[]{:S(2)}) copy-start(f32[384]{0:T(512)} %gain.5) | copy-start | bytes 4612
  17.4 1.5 %copy-start.4 = (bf16[576,2304]{1,0:T(8,128)(2,1)}, bf16[576,2304]{1,0:T(8,128)(2,1)S(1)}, u32[]{:S(2)}) copy-start(bf16[576,2304]{1,0:T(8,128)(2,1)S(1)} %get-tuple-element.21.weights.refs_2_) | copy-start | bytes 7962628
  18.9 2.1 %copy-start.1 = (bf16[3,3,3,384,192]{3,4,2,1,0:T(8,128)(2,1)S(1)}, bf16[3,3,3,384,192]{3,4,2,1,0:T(8,128)(2,1)}, u32[]{:S(2)}) copy-start(bf16[3,3,3,384,192]{3,4,2,1,0:T(8,128)(2,1)} %param.17) | copy-start | bytes 11943940
  21.1 6.4 %copy-start.2 = (bf16[3,3,3,384,192]{3,4,2,1,0:T(8,128)(2,1)S(1)}, bf16[3,3,3,384,192]{3,4,2,1,0:T(8,128)(2,1)}, u32[]{:S(2)}) copy-start(bf16[3,3,3,384,192]{3,4,2,1,0:T(8,128)(2,1)} %param.17) | copy-start | bytes 11943940
  27.5 5.6 %copy-start.18 = (bf16[2,192,320]{2,1,0:T(8,128)(2,1)S(1)}, bf16[2,192,320]{2,1,0:T(8,128)(2,1)}, u32[]{:S(2)}) copy-start(bf16[2,192,320]{2,1,0:T(8,128)(2,1)} %get-tuple-element.25) | copy-start | bytes 737284
  27.5 9.1 %copy-start.6 = (bf16[2,2,160,384]{3,2,1,0:T(8,128)(2,1)S(1)}, bf16[2,2,160,384]{3,2,1,0:T(8,128)(2,1)}, u32[]{:S(2)}) copy-start(bf16[2,2,160,384]{3,2,1,0:T(8,128)(2,1)} %cache.3) | copy-start | bytes 1474564
  29.6 11.8 %collective-permute-start.1 = (bf16[320,384]{1,0:T(8,128)(2,1)S(1)}, bf16[320,384]{1,0:T(8,128)(2,1)S(1)}, u32[]{:S(2)}, u32[]{:S(2)}) collective-permute-start(bf16[320,384]{1,0:T(8,128)(2,1)S(1)} %get-tuple-element.19), channel_id=1, source_target_pairs={{0,2},{1,3},{4,6},{5,7},{8,10},{9,11},{12,14},{13,15},{16,18},{17,... | collective-permute-start | bytes 737288 | tf_op jit(solution)/shard_map/ppermute | solution.py:551
  33.1 54.1 %collective-permute-start.2 = (bf16[2,192,320]{2,1,0:T(8,128)(2,1)S(1)}, bf16[2,192,320]{2,1,0:T(8,128)(2,1)S(1)}, u32[]{:S(2)}, u32[]{:S(2)}) collective-permute-start(bf16[2,192,320]{2,1,0:T(8,128)(2,1)S(1)} %copy-done.18), channel_id=1, source_target_pairs={{0,4},{5,1},{4,8},{9,5},{8,12},{13,9},{16,20},{21,17},{20,24},{25,... | collective-permute-start | bytes 737288 | tf_op jit(solution)/shard_map/ppermute | solution.py:546
  36.6 2.1 %copy-start.3 = (bf16[3,3,3,384,192]{3,4,2,1,0:T(8,128)(2,1)S(1)}, bf16[3,3,3,384,192]{3,4,2,1,0:T(8,128)(2,1)}, u32[]{:S(2)}) copy-start(bf16[3,3,3,384,192]{3,4,2,1,0:T(8,128)(2,1)} %param.17) | copy-start | bytes 11943940
  43.7 21.2 %copy-start.13 = (bf16[384,1152]{1,0:T(8,128)(2,1)S(1)}, bf16[384,1152]{1,0:T(8,128)(2,1)}, u32[]{:S(2)}) copy-start(bf16[384,1152]{1,0:T(8,128)(2,1)} %qkv.1) | copy-start | bytes 2654212
  43.7 21.2 %copy-start.14 = (bf16[384,384]{1,0:T(8,128)(2,1)S(1)}, bf16[384,384]{1,0:T(8,128)(2,1)}, u32[]{:S(2)}) copy-start(bf16[384,384]{1,0:T(8,128)(2,1)} %proj.1) | copy-start | bytes 884740
  43.7 21.2 %copy-start.16 = (f32[384]{0:T(512)S(1)}, f32[384]{0:T(512)}, u32[]{:S(2)}) copy-start(f32[384]{0:T(512)} %gain.6) | copy-start | bytes 4612
  64.9 8.9 %copy-start.5 = (bf16[576,2304]{1,0:T(8,128)(2,1)S(1)}, bf16[576,2304]{1,0:T(8,128)(2,1)}, u32[]{:S(2)}) copy-start(bf16[576,2304]{1,0:T(8,128)(2,1)} %copy-done.4) | copy-start | bytes 7962628
  64.9 8.9 %copy-start.17 = (f32[192]{0:T(256)S(1)}, f32[192]{0:T(256)}, u32[]{:S(2)}) copy-start(f32[192]{0:T(256)} %gain.7) | copy-start | bytes 2308
  73.8 1.2 %copy-start.8 = (bf16[8,160,384]{2,1,0:T(8,128)(2,1)S(1)}, bf16[8,160,384]{2,1,0:T(8,128)(2,1)}, u32[]{:S(2)}) copy-start(bf16[8,160,384]{2,1,0:T(8,128)(2,1)} %all-gather.2) | copy-start | bytes 2949124
  75.0 1.7 %copy-start.12 = (bf16[4,2,96,1536]{3,2,1,0:T(8,128)(2,1)S(1)}, bf16[4,2,96,1536]{3,2,1,0:T(8,128)(2,1)}, u32[]{:S(2)}) copy-start(bf16[4,2,96,1536]{3,2,1,0:T(8,128)(2,1)} %all-gather.7.cloned.1.call-done) | copy-start | bytes 7077892
  85.5 12.6 %collective-permute-start.3 = (bf16[2,192,640]{2,1,0:T(8,128)(2,1)S(1)}, bf16[2,192,640]{2,1,0:T(8,128)(2,1)S(1)}, u32[]{:S(2)}, u32[]{:S(2)}) collective-permute-start(bf16[2,192,640]{2,1,0:T(8,128)(2,1)S(1)} %get-tuple-element.26), channel_id=1, source_target_pairs={{0,2},{1,3},{4,6},{5,7},{8,10},{9,11},{12,14},{13,15},{16,18},{17,... | collective-permute-start | bytes 1474568 | tf_op jit(solution)/shard_map/ppermute | solution.py:551
  89.6 3.7 %copy-start = (bf16[2,4,320,192]{2,3,1,0:T(8,128)(2,1)S(1)}, bf16[2,4,320,192]{2,3,1,0:T(8,128)(2,1)}, u32[]{:S(2)}) copy-start(bf16[2,4,320,192]{2,3,1,0:T(8,128)(2,1)} %param.13) | copy-start | bytes 2949124
Sparse Core Ops, SparseCore 0:
  19.0 11.1 all-gather.6

commit v4 on v3

--- a/solution.py
+++ b/solution.py
@@ -30,10 +30,6 @@
     return pl.BlockSpec(memory_space=pltpu.HBM)
 
 
-def smem():
-    return pl.BlockSpec(memory_space=pltpu.SMEM)
-
-
 def dot_nt(left, right):
     return lax.dot_general(left, right, NT, preferred_element_type=F32)
 
@@ -58,38 +54,45 @@
     return jnp.where(column == count - 1, 0.0, pltpu.roll(values, count - 1, 0))
 
 
-def edge_kernel(place, latent, cache, low, rim, low_rim, sems):
+def edge_kernel(latent, cache, low, rim, low_rim, rows, low_rows, sems):
     frames = latent.shape[0]
+    chan = lax.axis_index("chan")
 
     def edge(source):
-        return source.at[:, jnp.where(place[1] == 0, source.shape[1] - 1, 0)]
-
-    copies = [
-        pltpu.make_async_copy(edge(latent), rim.at[:frames], sems.at[0]),
-        pltpu.make_async_copy(edge(cache), rim.at[frames:], sems.at[1]),
-        pltpu.make_async_copy(edge(low), low_rim, sems.at[2]),
+        return source.at[:, jnp.where(chan == 0, source.shape[1] - 1, 0)]
+
+    fetched = [
+        pltpu.make_async_copy(edge(latent), rows.at[:frames], sems.at[0]),
+        pltpu.make_async_copy(edge(cache), rows.at[frames:], sems.at[1]),
+        pltpu.make_async_copy(edge(low), low_rows, sems.at[2]),
     ]
-    for copy in copies:
+    for copy in fetched:
         copy.start()
-    for copy in copies:
+    for copy in fetched:
         copy.wait()
-
-
-def edge_rows(place, latent, cache, low):
+    stored = [
+        pltpu.make_async_copy(rows, rim, sems.at[3]),
+        pltpu.make_async_copy(low_rows, low_rim, sems.at[4]),
+    ]
+    for copy in stored:
+        copy.start()
+    for copy in stored:
+        copy.wait()
+
+
+def edge_rows(latent, cache, low):
     frames, rows, width, channels = latent.shape
+    shapes = [(frames + cache.shape[0], width, channels), low.shape[:1] + low.shape[2:]]
     return pl.pallas_call(
         edge_kernel,
-        in_specs=[smem(), hbm(), hbm(), hbm()],
-        out_specs=[vmem(), vmem()],
-        out_shape=[
-            jax.ShapeDtypeStruct((frames + cache.shape[0], width, channels), BF16),
-            jax.ShapeDtypeStruct(low.shape[:1] + low.shape[2:], BF16),
-        ],
-        scratch_shapes=[pltpu.SemaphoreType.DMA((3,))],
+        in_specs=[hbm()] * 3,
+        out_specs=[hbm()] * 2,
+        out_shape=[jax.ShapeDtypeStruct(shape, BF16) for shape in shapes],
+        scratch_shapes=[pltpu.VMEM(shape, BF16) for shape in shapes] + [pltpu.SemaphoreType.DMA((5,))],
         compiler_params=pltpu.CompilerParams(vmem_limit_bytes=58 * MIB),
         cost_estimate=cost(0, 4 * latent.nbytes),
         name="edge_rows",
-    )(place, latent, cache, low)
+    )(latent, cache, low)
 
 
 def weight_kernel(up, low, folded, turned):
@@ -142,52 +145,75 @@
     return jnp.concatenate([weights[tap, dy, dx] for dx in range(3)], axis=-1)
 
 
-def mid_inner_kernel(place, latent, gain, weights, acc, seen):
+def add_rows(acc, seen, weights, pairs, tap, dy, rows, width):
+    low, high = max(0, 1 - dy), min(rows, rows + 1 - dy)
+    span = (high - low) * width
+    left = jnp.concatenate([seen[f, low + dy - 1 : high + dy - 1].reshape(span, -1) for f, _ in pairs], axis=0)
+    term = dot_nt(left, tap_rows(weights, tap, dy))
+    for i, (_, t) in enumerate(pairs):
+        acc[t, low * width : high * width] += term[i * span : (i + 1) * span]
+
+
+def add_rims(acc, seen, weights, pairs, tap, side):
+    size = acc.shape[1]
+    width = seen.shape[2]
+    left = jnp.concatenate([seen[side, f] for f, _ in pairs], axis=0)
+    term = dot_nt(left, tap_rows(weights, tap, 2 * side))
+    at = slice(0, width) if side == 0 else slice(size - width, size)
+    for i, (_, t) in enumerate(pairs):
+        acc[t, at] += term[i * width : (i + 1) * width]
+
+
+def mid_inner_kernel(latent, cache, gain, weights, acc, seen, seen_cache):
     frames, rows, width, channels = latent.shape
     taps, part = weights.shape[0], weights.shape[-2]
     past = taps - 1
-    size = rows * width
+    chan = lax.axis_index("chan")
     for f in range(frames):
         for l in range(rows):
             seen[f, l] = spread(silu(normed(latent[f, l].astype(F32), gain[...])))
-        mine = latent[f].astype(F32).reshape(size, channels)
+        mine = latent[f].astype(F32).reshape(rows * width, channels)
         kept = mine[:, :part]
         for index in range(1, channels // part):
-            kept = jnp.where(place[1] == index, mine[:, index * part : (index + 1) * part], kept)
+            kept = jnp.where(chan == index, mine[:, index * part : (index + 1) * part], kept)
         acc[f] = kept
     for f in range(frames, frames + past):
         acc[f] = jnp.zeros_like(acc[f])
     for tap in range(taps):
         for dy in (1, 0, 2):
-            low, high = max(0, 1 - dy), min(rows, rows + 1 - dy)
-            span = (high - low) * width
-            left = jnp.concatenate(
-                [seen[f, low + dy - 1 : high + dy - 1].reshape(span, 3 * channels) for f in range(frames)], axis=0
-            )
-            term = dot_nt(left, tap_rows(weights, tap, dy))
-            for f in range(frames):
-                acc[f + past - tap, low * width : high * width] += term[f * span : (f + 1) * span]
-
-
-def mid_inner(place, latent, gain, weights):
+            add_rows(acc, seen, weights, [(f, f + past - tap) for f in range(frames)], tap, dy, rows, width)
+
+    @pl.when(lax.axis_index("segment") == 0)
+    def _():
+        for f in range(past):
+            for l in range(rows):
+                seen_cache[f, l] = spread(cache[f, l].astype(F32))
+        for tap in range(past):
+            for dy in (1, 0, 2):
+                add_rows(acc, seen_cache, weights, [(t + tap, t) for t in range(past - tap)], tap, dy, rows, width)
+
+
+def mid_inner(latent, cache, gain, weights):
     frames, rows, width, channels = latent.shape
     taps, part = weights.shape[0], weights.shape[-2]
     size = rows * width
     return pl.pallas_call(
         mid_inner_kernel,
-        in_specs=[smem(), vmem(), vmem(), vmem()],
+        in_specs=[vmem()] * 4,
         out_specs=vmem(),
         out_shape=jax.ShapeDtypeStruct((frames + taps - 1, size, part), F32),
-        scratch_shapes=[pltpu.VMEM((frames, rows, width, 3 * channels), BF16)],
-        compiler_params=pltpu.CompilerParams(vmem_limit_bytes=room(10 * latent.nbytes)),
+        scratch_shapes=[
+            pltpu.VMEM((frames, rows, width, 3 * channels), BF16),
+            pltpu.VMEM((taps - 1, rows, width, 3 * channels), BF16),
+        ],
+        compiler_params=pltpu.CompilerParams(vmem_limit_bytes=room(14 * latent.nbytes)),
         cost_estimate=cost(2 * 27 * frames * size * channels * part, weights.nbytes),
         name="mid_inner",
-    )(place, latent, gain, weights)
-
-
-def mid_rim_kernel(started, halo, gain, weights, own, passed, seen, acc):
+    )(latent, cache, gain, weights)
+
+
+def mid_rim_kernel(started, halo, gain, weights, own, passed, seen, seen_cache, acc):
     total, size, part = started.shape
-    sides, _, width, channels = halo.shape
     taps = weights.shape[0]
     past = taps - 1
     frames = total - past
@@ -197,10 +223,17 @@
     acc[...] = started[...]
     for tap in range(taps):
         for side in range(2):
-            term = dot_nt(seen[side].reshape(frames * width, 3 * channels), tap_rows(weights, tap, 2 * side))
-            at = slice(0, width) if side == 0 else slice(size - width, size)
-            for f in range(frames):
-                acc[f + past - tap, at] += term[f * width : (f + 1) * width]
+            add_rims(acc, seen, weights, [(f, f + past - tap) for f in range(frames)], tap, side)
+
+    @pl.when(lax.axis_index("segment") == 0)
+    def _():
+        for side in range(2):
+            for f in range(past):
+                seen_cache[side, f] = spread(halo[side, frames + f].astype(F32))
+        for tap in range(past):
+            for side in range(2):
+                add_rims(acc, seen_cache, weights, [(t + tap, t) for t in range(past - tap)], tap, side)
+
     own[...] = jnp.concatenate([acc[f] for f in range(frames)], axis=-1)
     passed[...] = jnp.concatenate([acc[frames + t] for t in range(past)], axis=-1).astype(BF16)
 
@@ -221,58 +254,16 @@
         ],
         scratch_shapes=[
             pltpu.VMEM((2, frames, width, 3 * channels), BF16),
+            pltpu.VMEM((2, past, width, 3 * channels), BF16),
             pltpu.VMEM(started.shape, F32),
         ],
-        compiler_params=pltpu.CompilerParams(vmem_limit_bytes=room(3 * halo.nbytes + 3 * started.nbytes)),
+        compiler_params=pltpu.CompilerParams(vmem_limit_bytes=room(5 * halo.nbytes + 3 * started.nbytes)),
         cost_estimate=cost(2 * 18 * frames * width * channels * part * taps, weights.nbytes),
         name="mid_rim",
     )(started, halo, gain, weights)
 
 
-def mid_cache_kernel(place, own, cache, halo, weights, out, seen):
-    past, rows, width, channels = cache.shape
-    part = weights.shape[-2]
-    frames = halo.shape[1] - past
-    out[...] = own[...]
-
-    @pl.when(place[0] == 0)
-    def _():
-        for f in range(past):
-            for l in range(rows + 2):
-                if l == 0 or l == rows + 1:
-                    row = halo[0 if l == 0 else 1, frames + f]
-                else:
-                    row = cache[f, l - 1]
-                seen[f, l] = spread(row.astype(F32))
-        for tap in range(past):
-            count = past - tap
-            total = None
-            for dy in range(3):
-                left = jnp.concatenate(
-                    [seen[t + tap, dy : dy + rows].reshape(rows * width, 3 * channels) for t in range(count)], axis=0
-                )
-                term = dot_nt(left, tap_rows(weights, tap, dy))
-                total = term if total is None else total + term
-            for t in range(count):
-                out[:, t * part : (t + 1) * part] += total[t * rows * width : (t + 1) * rows * width]
-
-
-def mid_cached(place, own, cache, halo, weights):
-    past, rows, width, channels = cache.shape
-    part = weights.shape[-2]
-    return pl.pallas_call(
-        mid_cache_kernel,
-        in_specs=[smem()] + [vmem()] * 4,
-        out_specs=vmem(),
-        out_shape=jax.ShapeDtypeStruct(own.shape, F32),
-        scratch_shapes=[pltpu.VMEM((past, rows + 2, width, 3 * channels), BF16)],
-        compiler_params=pltpu.CompilerParams(vmem_limit_bytes=room(12 * cache.nbytes + 2 * own.nbytes)),
-        cost_estimate=cost(6 * 9 * rows * width * channels * part, weights.nbytes),
-        name="mid_cached",
-    )(place, own, cache, halo, weights)
-
-
-def attn_kernel(tile_rows, place, frame, gain, qkv, proj, out, normal, keys, values):
+def attn_kernel(tile_rows, frame, gain, qkv, proj, out, normal, keys, values):
     count, _, channels = frame.shape
     width = out.shape[1]
     size = tile_rows * width
@@ -291,7 +282,7 @@
         return carry
 
     lax.fori_loop(0, count, prepare, 0)
-    start = place[2] * tile_rows - 1
+    start = lax.axis_index("rows") * tile_rows - 1
     for block in range(rows // step):
         spots = [start + block * step + i for i in range(step)]
         kept = [jnp.clip(spot, 0, height - 1) for spot in spots]
@@ -310,14 +301,14 @@
             out[block * step + i] = jnp.where(inside, summed, 0.0).astype(BF16)
 
 
-def attention(place, frame, gain, qkv, proj, tile_rows, width):
+def attention(frame, gain, qkv, proj, tile_rows, width):
     count, _, channels = frame.shape
     pixels = count * tile_rows * width
     rows = tile_rows + 2
     need = 4 * frame.nbytes + 2 * width * pixels * 16 + 2 * qkv.nbytes
     return pl.pallas_call(
         functools.partial(attn_kernel, tile_rows),
-        in_specs=[smem()] + [vmem()] * 4,
+        in_specs=[vmem()] * 4,
         out_specs=vmem(),
         out_shape=jax.ShapeDtypeStruct((rows, width, channels), BF16),
         scratch_shapes=[
@@ -328,7 +319,7 @@
         compiler_params=pltpu.CompilerParams(vmem_limit_bytes=room(need)),
         cost_estimate=cost(4 * channels * (pixels * channels + rows * width * (pixels + channels)), qkv.nbytes),
         name="frame_attention",
-    )(place, frame, gain, qkv, proj)
+    )(frame, gain, qkv, proj)
 
 
 def windowed(left, right):
@@ -340,13 +331,16 @@
     return jnp.concatenate([block[dy : dy + high].reshape(high * width, lanes) for dy in range(3)], axis=-1)
 
 
-def low_kernel(past, place, tile, up, gain, weights, passed, window, kept, seen, upper):
+def low_kernel(past, tile, mine, other, gain, weights, passed, window, kept, seen, upper, up):
     frames, ext, width, channels = tile.shape
-    chans, _, _, part = up.shape[:4]
-    low = chans * part
+    part = mine.shape[2]
+    low = up.shape[2]
     rows = ext - 2
     high = 2 * rows
     phases = passed.shape[1]
+    chan, row = lax.axis_index("chan"), lax.axis_index("rows")
+    up[:, :, pl.ds(pl.multiple_of(chan * part, 32), part)] = mine[...]
+    up[:, :, pl.ds(pl.multiple_of((1 - chan) * part, 32), part)] = other[...]
     for f in range(frames):
         for l in range(ext):
             seen[f, l] = spread(tile[f, l].astype(F32))
@@ -356,8 +350,7 @@
                 span = (ext - 1) * width
                 top = seen[f, : ext - 1, :, lanes].reshape(span, 2 * channels)
                 bottom = seen[f, 1:, :, lanes].reshape(span, 2 * channels)
-                folded = jnp.concatenate([up[c, a, b] for c in range(chans)], axis=0)
-                got = dot_nt(top, folded[:, : 2 * channels]) + dot_nt(bottom, folded[:, 2 * channels :])
+                got = dot_nt(top, up[a, b, :, : 2 * channels]) + dot_nt(bottom, up[a, b, :, 2 * channels :])
                 for p in range(ext - 1):
                     upper[2 * p + 1 - a, b] = got[p * width : (p + 1) * width].astype(BF16)
         for j in range(high + 2):
@@ -366,9 +359,9 @@
                 kept[f, j - 1] = jnp.concatenate(sides, axis=-1).astype(BF16)
             sides = [silu(normed(side, gain[...])) for side in sides]
             if j == 0:
-                sides = [jnp.where(place[2] == 0, 0.0, side) for side in sides]
+                sides = [jnp.where(row == 0, 0.0, side) for side in sides]
             if j == high + 1:
-                sides = [jnp.where(place[2] == place[3] - 1, 0.0, side) for side in sides]
+                sides = [jnp.where(row == lax.axis_size("rows") - 1, 0.0, side) for side in sides]
             window[f, j] = windowed(*sides)
 
     sums = [None] * past
@@ -384,17 +377,17 @@
         passed[t] = sums[t].astype(BF16)
 
 
-def low_stage(place, tile, up, gain, weights, taps):
+def low_stage(tile, mine, other, gain, weights, taps):
     frames, ext, width, channels = tile.shape
-    chans, _, _, part = up.shape[:4]
-    low = chans * part
+    part = mine.shape[2]
+    low = 2 * part
     high = 2 * (ext - 2)
     past = taps - 1
     phases = 2 * part
-    need = 4 * tile.nbytes + 10 * frames * high * width * low * 4
+    need = 4 * tile.nbytes + 2 * mine.nbytes + 10 * frames * high * width * low * 4
     return pl.pallas_call(
         functools.partial(low_kernel, past),
-        in_specs=[smem()] + [vmem()] * 4,
+        in_specs=[vmem()] * 5,
         out_specs=[vmem()] * 3,
         out_shape=[
             jax.ShapeDtypeStruct((past, phases, high * width), BF16),
@@ -404,14 +397,15 @@
         scratch_shapes=[
             pltpu.VMEM((frames, ext, width, 3 * channels), BF16),
             pltpu.VMEM((high + 2, 2, width, low), BF16),
+            pltpu.VMEM((2, 2, low, 4 * channels), BF16),
         ],
         compiler_params=pltpu.CompilerParams(vmem_limit_bytes=room(need)),
-        cost_estimate=cost(96 * frames * high * width * channels * low // 4, up.nbytes + weights.nbytes),
+        cost_estimate=cost(96 * frames * high * width * channels * low // 4, 2 * mine.nbytes + weights.nbytes),
         name="low_stage",
-    )(place, tile, up, gain, weights)
-
-
-def low_own_kernel(place, starts, window, kept, weights, own, weave):
+    )(tile, mine, other, gain, weights)
+
+
+def low_own_kernel(starts, window, kept, weights, own, weave):
     frames, ext, width, lanes = window.shape
     low = lanes // 4
     high = ext - 2
@@ -421,7 +415,7 @@
     past = taps - 1
     line = lax.broadcasted_iota(jnp.int32, (phases, 2 * low), 0)
     spot = lax.broadcasted_iota(jnp.int32, (phases, 2 * low), 1)
-    shift = place[1] * part
+    shift = lax.axis_index("chan") * part
     picked = spot == jnp.where(line < part, line + shift, line - part + shift + low)
     select = picked.astype(F32).astype(BF16)
     for f in range(frames):
@@ -440,15 +434,15 @@
             weave[i, b * span : (b + 1) * span] = hit.astype(F32).astype(BF16)
 
 
-def low_own(place, window, kept, weights, taps):
+def low_own(window, kept, weights, taps):
     frames, ext, width, lanes = window.shape
     phases = weights.shape[0] // taps
     high = ext - 2
     starts, span = lane_windows(high, width)
     need = window.nbytes + 3 * frames * phases * high * width * 4
     return pl.pallas_call(
-        lambda place, *refs: low_own_kernel(place, starts, *refs),
-        in_specs=[smem()] + [vmem()] * 3,
+        functools.partial(low_own_kernel, starts),
+        in_specs=[vmem()] * 3,
         out_specs=[vmem()] * 2,
         out_shape=[
             jax.ShapeDtypeStruct((frames, phases, high * width), F32),
@@ -457,16 +451,16 @@
         compiler_params=pltpu.CompilerParams(vmem_limit_bytes=room(need)),
         cost_estimate=cost(6 * 9 * high * width * lanes * phases // 2, weights.nbytes),
         name="low_own",
-    )(place, window, kept, weights)
-
-
-def low_cache_kernel(place, own, cache, halo, weights, out, window):
+    )(window, kept, weights)
+
+
+def low_cache_kernel(own, cache, halo, weights, out, window):
     past, high, channels, columns = cache.shape
     width = columns // 2
     phases = own.shape[1]
     out[...] = own[...]
 
-    @pl.when(place[0] == 0)
+    @pl.when(lax.axis_index("segment") == 0)
     def _():
         pixel = lax.broadcasted_iota(jnp.int32, (width, columns), 0)
         column = lax.broadcasted_iota(jnp.int32, (width, columns), 1)
@@ -480,19 +474,19 @@
                 out[f - tap] += got[tap * phases : (tap + 1) * phases]
 
 
-def low_cached(place, own, cache, halo, weights):
+def low_cached(own, cache, halo, weights):
     past, high, channels, columns = cache.shape
     pixels = high * columns
     return pl.pallas_call(
         low_cache_kernel,
-        in_specs=[smem()] + [vmem()] * 4,
+        in_specs=[vmem()] * 4,
         out_specs=vmem(),
         out_shape=jax.ShapeDtypeStruct(own.shape, F32),
         scratch_shapes=[pltpu.VMEM((high + 2, columns // 2, 4 * channels), BF16)],
         compiler_params=pltpu.CompilerParams(vmem_limit_bytes=room(2 * own.nbytes + 16 * cache.nbytes)),
         cost_estimate=cost(6 * 9 * pixels * channels * own.shape[1] // 2, weights.nbytes),
         name="low_cached",
-    )(place, own, cache, halo, weights)
+    )(own, cache, halo, weights)
 
 
 def lane_windows(high, width):
@@ -565,9 +559,6 @@
     conv_low,
 ):
     chan = lax.axis_index("chan")
-    place = jnp.stack(
-        [lax.axis_index("segment"), chan, lax.axis_index("rows"), jnp.int32(lax.axis_size("rows"))]
-    ).astype(jnp.int32)
     frames, rows, width, channels = latent.shape
     part = conv_mid.shape[-1]
     taps = conv_mid.shape[0]
@@ -576,17 +567,14 @@
     mid_weights = jnp.swapaxes(conv_mid, 3, 4)
     low_cache = jnp.swapaxes(cache_low, 2, 3)
 
-    rim, low_rim = edge_rows(place, latent, cache_mid, low_cache)
+    rim, low_rim = edge_rows(latent, cache_mid, low_cache)
     rim = to_neighbour(rim, False)
-    low_rim = to_neighbour(low_rim, True)
-    started = mid_inner(place, latent, gain_mid, mid_weights)
+    up_mine, low_weights = weight_forms(jnp.swapaxes(conv_up, 2, 3), conv_low)
+    up_other = lax.ppermute(up_mine, "chan", [(0, 1), (1, 0)])
+    started = mid_inner(latent, cache_mid, gain_mid, mid_weights)
     halo = lax.all_gather(rim, "chan")
     own, passed = mid_rim(started, halo, gain_mid, mid_weights)
     arrived = to_next(passed)
-    own = mid_cached(place, own, cache_mid, halo, mid_weights)
-
-    up_part, low_weights = weight_forms(jnp.swapaxes(conv_up, 2, 3), conv_low)
-    up = lax.all_gather(up_part, "chan")
 
     first_part = (own + jnp.pad(arrived, ((0, 0), (0, (frames - past) * part))).astype(F32)).astype(BF16)
     both = lax.all_gather(first_part, "chan")
@@ -600,14 +588,15 @@
         mine = jnp.where(chan == f, choices[f], mine)
     frame = lax.all_gather(mine, "rows")
 
-    reached = attention(place, frame, gain_attn, attn_qkv, attn_proj, rows, width)
+    reached = attention(frame, gain_attn, attn_qkv, attn_proj, rows, width)
     tile = lax.all_gather(reached, "chan")
 
-    passed_low, window, kept = low_stage(place, tile, up, gain_low, low_weights, taps)
+    passed_low, window, kept = low_stage(tile, up_mine, up_other, gain_low, low_weights, taps)
     arrived_low = to_next(passed_low)
-    own_low, weave = low_own(place, window, kept, low_weights, taps)
     low_rim, _ = lax.optimization_barrier((low_rim, passed_low))
-    own_low = low_cached(place, own_low, low_cache, lax.all_gather(low_rim, "chan"), low_weights)
+    low_rim = lax.all_gather(to_neighbour(low_rim, True), "chan")
+    own_low, weave = low_own(window, kept, low_weights, taps)
+    own_low = low_cached(own_low, low_cache, low_rim, low_weights)
     out = finish(own_low, arrived_low, weave, high, width)
     return jnp.swapaxes(out, 2, 3)
 

time: 107 us -> 92.2 us (0.86)
  between operations: 13.7 us -> 0.21 us
  local copies, waits for them, and re-layouts: 8.84 us -> 2.34 us
  waiting for transfers between devices: 0.03 us -> 3.45 us
  blocking collectives: 30.6 us -> 32.8 us
  Pallas kernels: 38.9 us -> 37.3 us
    unnamed x38 -> x24, local copies, waits for them, and re-layouts: 8.67 us -> 2.18 us
    pallas_call x7 -> x6, Pallas kernels: 32.9 us -> 30.3 us  [the longest x1 10 us: low_stage(): pl.pallas_call(functools.partial(low_kernel, past), in_specs=[vmem()] * 5...]
    ppermute x2, waiting for transfers between devices: 0.01 us -> 2.38 us  [to_next(): lax.ppermute(values, 'segment', [(i, i + 1) for i in range(count - 1)])]
    all_gather x1, blocking collectives: 20.8 us -> 22.9 us  [body(): frame = lax.all_gather(mine, 'rows')]
    ppermute x2, starting transfers between devices: 5.07 us -> 7.15 us  [to_next(): lax.ppermute(values, 'segment', [(i, i + 1) for i in range(count - 1)])]
  transfers between devices with their start and end apart: 5 -> 5, of which waited for: 0 -> 2; matrix products, arithmetic and copies ran while one was open for 0% -> 1% of each run, Pallas kernels for 33% -> 22%
where the time goes in v4:
time: 92.2 us; the launch traced here: 91.8 us
  Pallas kernels  37.3 us (40%)
  blocking collectives  32.8 us (36%)
  starting transfers between devices  14.5 us (16%)
  waiting for transfers between devices  3.45 us (4%)
  local copies, waits for them, and re-layouts  2.34 us (3%)
  other arithmetic  1.17 us (1%)
    all_gather x1, blocking collectives, body(): frame = lax.all_gather(mine, 'rows')  22.9 us
    pallas_call x1, Pallas kernels, low_stage(): pl.pallas_call(functools.partial(low_kernel, past), in_specs=[vmem()] * 5...  10 us
    ppermute x2, starting transfers between devices, to_neighbour(): return lax.ppermute(values, ('rows', 'segment', 'chan'), route)  7.37 us
    ppermute x2, starting transfers between devices, to_next(): lax.ppermute(values, 'segment', [(i, i + 1) for i in range(count - 1)])  7.15 us
    pallas_call x1, Pallas kernels, attention(): pl.pallas_call(functools.partial(attn_kernel, tile_rows), in_specs=[vmem(...  5.66 us
    pallas_call x1, Pallas kernels, mid_inner(): pl.pallas_call(mid_inner_kernel, in_specs=[vmem()] * 4, out_specs=vmem(),...  4.92 us
    pallas_call x1, Pallas kernels, low_cached(): pl.pallas_call(low_cache_kernel, in_specs=[vmem()] * 4, out_specs=vmem(),...  4.4 us
    pallas_call x1, Pallas kernels, mid_rim(): pl.pallas_call(mid_rim_kernel, in_specs=[vmem()] * 4, out_specs=[vmem(),...  3.2 us
  transfers between devices with their start and end apart: 5, of which 2 were waited for; matrix products, arithmetic and copies ran while one was open for 1% of the time, Pallas kernels for 22%

profile of v4, /device:TPU:0, one launch (start us, length us, event | category | flops | bytes accessed | tf_op | source)
XLA Modules:
  0.0 91.8 jit_solution(16894796754151980308)
XLA Ops:
  0.0 2.2 %edge_rows.1 = (bf16[4,160,384]{2,1,0:T(8,128)(2,1)}, bf16[2,192,320]{2,1,0:T(8,128)(2,1)}) custom-call(bf16[2,2,160,384]{3,2,1,0:T(8,128)(2,1)} %latent.3, bf16[2,2,160,384]{3,2,1,0:T(8,128)(2,1)} %cache.3, bf16[2,4,192,320]{3,2,1,0:T(8,128)(2,1)} %bitcast.8), custom_call_target="tpu_custom_call" | custom-call | bytes 1966080 | tf_op jit(solution)/shard_map/edge_rows/pallas_call | solution.py:86
  2.2 5.0 %collective-permute-start = (bf16[4,160,384]{2,1,0:T(8,128)(2,1)}, bf16[4,160,384]{2,1,0:T(8,128)(2,1)S(1)}, u32[]{:S(2)}, u32[]{:S(2)}) collective-permute-start(bf16[4,160,384]{2,1,0:T(8,128)(2,1)} %get-tuple-element.17), channel_id=1, source_target_pairs={{0,4},{5,1},{2,6},{7,3},{4,8},{9,5},{6,10},{11,7},{8,12},{13,9},{1... | collective-permute-start | bytes 1474568 | tf_op jit(solution)/shard_map/ppermute | solution.py:540
  7.2 0.0 copy-start.5
  7.2 2.1 %copy-done.5 = bf16[3,3,3,384,192]{3,4,2,1,0:T(8,128)(2,1)S(1)} copy-done((bf16[3,3,3,384,192]{3,4,2,1,0:T(8,128)(2,1)S(1)}, bf16[3,3,3,384,192]{3,4,2,1,0:T(8,128)(2,1)}, u32[]{:S(2)}) %copy-start.5) | copy-done | bytes 3981336
  9.4 4.9 %mid_inner.1.started = f32[4,320,192]{2,1,0:T(8,128)S(1)} custom-call(bf16[2,2,160,384]{3,2,1,0:T(8,128)(2,1)S(1)} %copy-done.3, bf16[2,2,160,384]{3,2,1,0:T(8,128)(2,1)S(1)} %copy-done.4, f32[384]{0:T(512)S(1)} %copy-done.8, bf16[3,3,3,192,384]{4,3,2,1,0:T(8,128)(2,1)S(1)} %bitcast.14), custom_call_target="tpu_custom_call" | custom-call | flops 2548039680 | bytes 3981312 | tf_op jit(solution)/shard_map/mid_inner/pallas_call | solution.py:200
  14.3 2.5 %all-gather = bf16[8,160,384]{2,1,0:T(8,128)(2,1)S(1)} all-gather(bf16[4,160,384]{2,1,0:T(8,128)(2,1)S(1)} %collective-permute-done), channel_id=2, replica_groups=mesh['groups'=2,'rows'=4,'segment'=2,'chan'=2] {'chan'}, dimensions={0}, use_global_device_ids=true | all-gather | bytes 1474560 | tf_op jit(solution)/shard_map/all_gather | solution.py:575
  16.8 3.2 %mid_rim.1 = (f32[320,384]{1,0:T(8,128)S(1)}, bf16[320,384]{1,0:T(8,128)(2,1)S(1)}) custom-call(f32[4,320,192]{2,1,0:T(8,128)S(1)} %mid_inner.1.started, bf16[2,4,160,384]{3,2,1,0:T(8,128)(2,1)S(1)} %bitcast.12, f32[384]{0:T(512)S(1)} %copy-done.8, bf16[3,3,3,192,384]{4,3,2,1,0:T(8,128)(2,1)S(1)} %bitcast.15), custom_call_target="tpu_custom_call" | custom-call | flops 2548039680 | bytes 3981312 | tf_op jit(solution)/shard_map/mid_rim/pallas_call | solution.py:247
  20.0 2.6 %collective-permute-start.1 = (bf16[320,384]{1,0:T(8,128)(2,1)S(1)}, bf16[320,384]{1,0:T(8,128)(2,1)}, u32[]{:S(2)}, u32[]{:S(2)}) collective-permute-start(bf16[320,384]{1,0:T(8,128)(2,1)S(1)} %get-tuple-element.19), channel_id=1, source_target_pairs={{0,2},{1,3},{4,6},{5,7},{8,10},{9,11},{12,14},{13,15},{16,18},{17,... | collective-permute-start | bytes 737288 | tf_op jit(solution)/shard_map/ppermute | solution.py:545
  22.6 2.4 %weight_forms.1 = (bf16[2,2,96,1536]{3,2,1,0:T(8,128)(2,1)}, bf16[576,2304]{1,0:T(8,128)(2,1)S(1)}) custom-call(bf16[3,3,96,384]{3,2,1,0:T(8,128)(2,1)S(1)} %bitcast.13, bf16[3,3,3,192,96]{4,3,2,1,0:T(8,128)(2,1)S(1)} %copy-done.1), custom_call_target="tpu_custom_call" | custom-call | flops 95551488 | bytes 6635520 | tf_op jit(solution)/shard_map/weight_forms/pallas_call | solution.py:126
  25.0 0.0 collective-permute-start.2
  25.0 2.4 %collective-permute-done.1 = bf16[320,384]{1,0:T(8,128)(2,1)} collective-permute-done((bf16[320,384]{1,0:T(8,128)(2,1)S(1)}, bf16[320,384]{1,0:T(8,128)(2,1)}, u32[]{:S(2)}, u32[]{:S(2)}) %collective-permute-start.1) | collective-permute-done | bytes 245792 | tf_op jit(solution)/shard_map/ppermute | solution.py:545
  27.4 1.0 %add_convert_fusion = bf16[320,384]{1,0:T(8,128)(2,1)S(1)} fusion(f32[320,384]{1,0:T(8,128)S(1)} %get-tuple-element.18, bf16[320,384]{1,0:T(8,128)(2,1)} %collective-permute-done.1), kind=kLoop, calls=%fused_computation | loop fusion | flops 368640 | bytes 983040 | tf_op jit(solution)/shard_map/convert_element_type | solution.py:579
  28.4 2.2 %all-gather.1 = bf16[640,384]{1,0:T(8,128)(2,1)S(1)} all-gather(bf16[320,384]{1,0:T(8,128)(2,1)S(1)} %add_convert_fusion), channel_id=3, replica_groups=mesh['groups'=2,'rows'=4,'segment'=2,'chan'=2] {'chan'}, dimensions={0}, use_global_device_ids=true | all-gather | bytes 737280 | tf_op jit(solution)/shard_map/all_gather | solution.py:580
  30.6 0.2 fusion
  30.7 0.0 copy-start.6
  30.8 0.0 copy-start.7
  30.8 0.0 copy-start.9
  30.8 0.2 maximum_select_fusion
  31.0 22.9 %all_gather.32.frame = bf16[4,320,384]{2,1,0:T(8,128)(2,1)S(1)} all-gather(bf16[1,320,384]{2,1,0:T(8,128)(2,1)S(1)} %maximum_select_fusion), channel_id=1, replica_groups=mesh['groups'=2,'rows'=4,'segment'=2,'chan'=2] {'rows'}, dimensions={0}, use_global_device_ids=true | all-gather | bytes 1228800 | tf_op jit(solution)/shard_map/all_gather | solution.py:589
  53.9 5.7 %frame_attention.1 = bf16[4,160,384]{2,1,0:T(8,128)(2,1)S(1)} custom-call(bf16[4,320,384]{2,1,0:T(8,128)(2,1)S(1)} %all_gather.32.frame, f32[384]{0:T(512)S(1)} %copy-done.9, bf16[384,1152]{1,0:T(8,128)(2,1)S(1)} %copy-done.6, bf16[384,384]{1,0:T(8,128)(2,1)S(1)} %copy-done.7), custom_call_target="tpu_custom_call" | custom-call | flops 2390753280 | bytes 884736 | tf_op jit(solution)/shard_map/frame_attention/pallas_call | solution.py:309
  59.6 0.0 copy-start.10
  59.6 2.7 %all-gather.2 = bf16[8,160,384]{2,1,0:T(8,128)(2,1)S(1)} all-gather(bf16[4,160,384]{2,1,0:T(8,128)(2,1)S(1)} %frame_attention.1), channel_id=4, replica_groups=mesh['groups'=2,'rows'=4,'segment'=2,'chan'=2] {'chan'}, dimensions={0}, use_global_device_ids=true | all-gather | bytes 1474560 | tf_op jit(solution)/shard_map/all_gather | solution.py:592
  62.3 0.0 collective-permute-done.2.other
  62.3 10.0 %low_stage.1 = (bf16[2,192,640]{2,1,0:T(8,128)(2,1)S(1)}, bf16[2,6,160,768]{3,2,1,0:T(8,128)(2,1)S(1)}, bf16[2,4,160,384]{3,2,1,0:T(8,128)(2,1)S(1)}) custom-call(bf16[2,4,160,384]{3,2,1,0:T(8,128)(2,1)S(1)} %bitcast.11, bf16[2,2,96,1536]{3,2,1,0:T(8,128)(2,1)} %get-tuple-element.20.mine, bf16[2,2,96,1536]{3,2,1,0:T(8,128)(2,1)} %collective-permute-done.2.other, ...), custom_call_target="tpu_custom_call" | custom-call | flops 2264924160 | bytes 5013504 | tf_op jit(solution)/shard_map/low_stage/pallas_call | solution.py:388
  72.3 4.5 %collective-permute-start.4 = (bf16[2,192,640]{2,1,0:T(8,128)(2,1)S(1)}, bf16[2,192,640]{2,1,0:T(8,128)(2,1)S(1)}, u32[]{:S(2)}, u32[]{:S(2)}) collective-permute-start(bf16[2,192,640]{2,1,0:T(8,128)(2,1)S(1)} %get-tuple-element.26), channel_id=1, source_target_pairs={{0,2},{1,3},{4,6},{5,7},{8,10},{9,11},{12,14},{13,15},{16,18},{17,... | collective-permute-start | bytes 1474568 | tf_op jit(solution)/shard_map/ppermute | solution.py:545
  76.8 2.4 %collective-permute-start.3 = (bf16[2,192,320]{2,1,0:T(8,128)(2,1)S(1)}, bf16[2,192,320]{2,1,0:T(8,128)(2,1)S(1)}, u32[]{:S(2)}, u32[]{:S(2)}) collective-permute-start(bf16[2,192,320]{2,1,0:T(8,128)(2,1)S(1)} %copy-done.11), channel_id=1, source_target_pairs={{0,4},{5,1},{4,8},{9,5},{8,12},{13,9},{16,20},{21,17},{20,24},{25,... | collective-permute-start | bytes 737288 | tf_op jit(solution)/shard_map/ppermute | solution.py:540
  79.2 0.0 copy-start
  79.2 3.1 %low_own.1 = (f32[2,192,640]{2,1,0:T(8,128)S(1)}, bf16[4,512,320]{2,1,0:T(8,128)(2,1)S(1)}) custom-call(bf16[2,6,160,768]{3,2,1,0:T(8,128)(2,1)S(1)} %get-tuple-element.22.window, bf16[2,4,160,384]{3,2,1,0:T(8,128)(2,1)S(1)} %get-tuple-element.23.kept, bf16[576,2304]{1,0:T(8,128)(2,1)S(1)} %get-tuple-element.21.weights), custom_call_target="tpu_custom_call" | custom-call | flops 2548039680 | bytes 2654208 | tf_op jit(solution)/shard_map/low_own/pallas_call | solution.py:443
  82.4 1.1 %collective-permute-done.3 = bf16[2,192,320]{2,1,0:T(8,128)(2,1)S(1)} collective-permute-done((bf16[2,192,320]{2,1,0:T(8,128)(2,1)S(1)}, bf16[2,192,320]{2,1,0:T(8,128)(2,1)S(1)}, u32[]{:S(2)}, u32[]{:S(2)}) %collective-permute-start.3) | collective-permute-done | bytes 245792 | tf_op jit(solution)/shard_map/ppermute | solution.py:540
  83.4 2.6 %all-gather.3 = bf16[4,192,320]{2,1,0:T(8,128)(2,1)S(1)} all-gather(bf16[2,192,320]{2,1,0:T(8,128)(2,1)S(1)} %collective-permute-done.3), channel_id=5, replica_groups=mesh['groups'=2,'rows'=4,'segment'=2,'chan'=2] {'chan'}, dimensions={0}, use_global_device_ids=true | all-gather | bytes 737280 | tf_op jit(solution)/shard_map/all_gather | solution.py:597
  86.0 4.4 %low_cached.1.own = f32[2,192,640]{2,1,0:T(8,128)S(1)} custom-call(f32[2,192,640]{2,1,0:T(8,128)S(1)} %get-tuple-element.24.own, bf16[2,4,192,320]{3,2,1,0:T(8,128)(2,1)S(1)} %bitcast.9, bf16[2,2,192,320]{3,2,1,0:T(8,128)(2,1)S(1)} %bitcast.10, bf16[576,2304]{1,0:T(8,128)(2,1)S(1)} %get-tuple-element.21.weights), custom_call_target="tpu_custom_call" | custom-call | flops 1274019840 | bytes 2654208 | tf_op jit(solution)/shard_map/low_cached/pallas_call | solution.py:480
  90.4 1.4 %finish.1 = bf16[2,4,96,320]{3,2,1,0:T(8,128)(2,1)} custom-call(f32[2,192,640]{2,1,0:T(8,128)S(1)} %low_cached.1.own, bf16[2,192,640]{2,1,0:T(8,128)(2,1)S(1)} %collective-permute-done.4.passed, bf16[4,512,320]{2,1,0:T(8,128)(2,1)S(1)} %get-tuple-element.28.weave), custom_call_target="tpu_custom_call" | custom-call | flops 251658240 | bytes 983040 | tf_op jit(solution)/shard_map/finish/pallas_call | solution.py:521
  (19 shorter events, 0.0 us)
Async XLA Ops:
  0.0 7.2 %copy-start.4 = (bf16[2,2,160,384]{3,2,1,0:T(8,128)(2,1)S(1)}, bf16[2,2,160,384]{3,2,1,0:T(8,128)(2,1)}, u32[]{:S(2)}) copy-start(bf16[2,2,160,384]{3,2,1,0:T(8,128)(2,1)} %cache.3) | copy-start | bytes 1474564
  0.0 7.2 %copy-start.3 = (bf16[2,2,160,384]{3,2,1,0:T(8,128)(2,1)S(1)}, bf16[2,2,160,384]{3,2,1,0:T(8,128)(2,1)}, u32[]{:S(2)}) copy-start(bf16[2,2,160,384]{3,2,1,0:T(8,128)(2,1)} %latent.3) | copy-start | bytes 1474564
  0.0 7.2 %copy-start.8 = (f32[384]{0:T(512)S(1)}, f32[384]{0:T(512)}, u32[]{:S(2)}) copy-start(f32[384]{0:T(512)} %gain.5) | copy-start | bytes 4612
  2.2 12.1 %collective-permute-start = (bf16[4,160,384]{2,1,0:T(8,128)(2,1)}, bf16[4,160,384]{2,1,0:T(8,128)(2,1)S(1)}, u32[]{:S(2)}, u32[]{:S(2)}) collective-permute-start(bf16[4,160,384]{2,1,0:T(8,128)(2,1)} %get-tuple-element.17), channel_id=1, source_target_pairs={{0,4},{5,1},{2,6},{7,3},{4,8},{9,5},{6,10},{11,7},{8,12},{13,9},{1... | collective-permute-start | bytes 1474568 | tf_op jit(solution)/shard_map/ppermute | solution.py:540
  7.2 2.1 %copy-start.5 = (bf16[3,3,3,384,192]{3,4,2,1,0:T(8,128)(2,1)S(1)}, bf16[3,3,3,384,192]{3,4,2,1,0:T(8,128)(2,1)}, u32[]{:S(2)}) copy-start(bf16[3,3,3,384,192]{3,4,2,1,0:T(8,128)(2,1)} %param.17) | copy-start | bytes 11943940
  16.8 5.8 %copy-start.1 = (bf16[3,3,3,192,96]{4,3,2,1,0:T(8,128)(2,1)S(1)}, bf16[3,3,3,192,96]{4,3,2,1,0:T(8,128)(2,1)}, u32[]{:S(2)}) copy-start(bf16[3,3,3,192,96]{4,3,2,1,0:T(8,128)(2,1)} %low.1) | copy-start | bytes 2985988
  16.8 5.8 %copy-start.2 = (bf16[3,3,384,96]{2,3,1,0:T(8,128)(2,1)S(1)}, bf16[3,3,384,96]{2,3,1,0:T(8,128)(2,1)}, u32[]{:S(2)}) copy-start(bf16[3,3,384,96]{2,3,1,0:T(8,128)(2,1)} %param.20) | copy-start | bytes 1990660
  20.0 7.4 %collective-permute-start.1 = (bf16[320,384]{1,0:T(8,128)(2,1)S(1)}, bf16[320,384]{1,0:T(8,128)(2,1)}, u32[]{:S(2)}, u32[]{:S(2)}) collective-permute-start(bf16[320,384]{1,0:T(8,128)(2,1)S(1)} %get-tuple-element.19), channel_id=1, source_target_pairs={{0,2},{1,3},{4,6},{5,7},{8,10},{9,11},{12,14},{13,15},{16,18},{17,... | collective-permute-start | bytes 737288 | tf_op jit(solution)/shard_map/ppermute | solution.py:545
  25.0 37.2 %collective-permute-start.2 = (bf16[2,2,96,1536]{3,2,1,0:T(8,128)(2,1)}, bf16[2,2,96,1536]{3,2,1,0:T(8,128)(2,1)}, u32[]{:S(2)}, u32[]{:S(2)}) collective-permute-start(bf16[2,2,96,1536]{3,2,1,0:T(8,128)(2,1)} %get-tuple-element.20.mine), channel_id=1, source_target_pairs={{0,1},{1,0},{2,3},{3,2},{4,5},{5,4},{6,7},{7,6},{8,9},{9,8},{10,11... | collective-permute-start | bytes 3538952 | tf_op jit(solution)/shard_map/ppermute | solution.py:573
  30.7 23.1 %copy-start.6 = (bf16[384,1152]{1,0:T(8,128)(2,1)S(1)}, bf16[384,1152]{1,0:T(8,128)(2,1)}, u32[]{:S(2)}) copy-start(bf16[384,1152]{1,0:T(8,128)(2,1)} %qkv.1) | copy-start | bytes 2654212
  30.8 23.1 %copy-start.7 = (bf16[384,384]{1,0:T(8,128)(2,1)S(1)}, bf16[384,384]{1,0:T(8,128)(2,1)}, u32[]{:S(2)}) copy-start(bf16[384,384]{1,0:T(8,128)(2,1)} %proj.1) | copy-start | bytes 884740
  30.8 23.1 %copy-start.9 = (f32[384]{0:T(512)S(1)}, f32[384]{0:T(512)}, u32[]{:S(2)}) copy-start(f32[384]{0:T(512)} %gain.6) | copy-start | bytes 4612
  59.6 2.7 %copy-start.10 = (f32[192]{0:T(256)S(1)}, f32[192]{0:T(256)}, u32[]{:S(2)}) copy-start(f32[192]{0:T(256)} %gain.7) | copy-start | bytes 2308
  62.3 14.6 %copy-start.11 = (bf16[2,192,320]{2,1,0:T(8,128)(2,1)S(1)}, bf16[2,192,320]{2,1,0:T(8,128)(2,1)}, u32[]{:S(2)}) copy-start(bf16[2,192,320]{2,1,0:T(8,128)(2,1)} %get-tuple-element.27) | copy-start | bytes 737284
  72.3 18.1 %collective-permute-start.4 = (bf16[2,192,640]{2,1,0:T(8,128)(2,1)S(1)}, bf16[2,192,640]{2,1,0:T(8,128)(2,1)S(1)}, u32[]{:S(2)}, u32[]{:S(2)}) collective-permute-start(bf16[2,192,640]{2,1,0:T(8,128)(2,1)S(1)} %get-tuple-element.26), channel_id=1, source_target_pairs={{0,2},{1,3},{4,6},{5,7},{8,10},{9,11},{12,14},{13,15},{16,18},{17,... | collective-permute-start | bytes 1474568 | tf_op jit(solution)/shard_map/ppermute | solution.py:545
  76.8 6.6 %collective-permute-start.3 = (bf16[2,192,320]{2,1,0:T(8,128)(2,1)S(1)}, bf16[2,192,320]{2,1,0:T(8,128)(2,1)S(1)}, u32[]{:S(2)}, u32[]{:S(2)}) collective-permute-start(bf16[2,192,320]{2,1,0:T(8,128)(2,1)S(1)} %copy-done.11), channel_id=1, source_target_pairs={{0,4},{5,1},{4,8},{9,5},{8,12},{13,9},{16,20},{21,17},{20,24},{25,... | collective-permute-start | bytes 737288 | tf_op jit(solution)/shard_map/ppermute | solution.py:540
  79.2 6.8 %copy-start = (bf16[2,4,320,192]{2,3,1,0:T(8,128)(2,1)S(1)}, bf16[2,4,320,192]{2,3,1,0:T(8,128)(2,1)}, u32[]{:S(2)}) copy-start(bf16[2,4,320,192]{2,3,1,0:T(8,128)(2,1)} %param.13) | copy-start | bytes 2949124

commit v5 on v4

--- a/solution.py
+++ b/solution.py
@@ -40,7 +40,8 @@
 
 
 def silu(values):
-    return values / (1.0 + jnp.exp(-values))
+    half = 0.5 * values
+    return half + half * jnp.tanh(half)
 
 
 def from_left(values):
@@ -89,7 +90,7 @@
         out_specs=[hbm()] * 2,
         out_shape=[jax.ShapeDtypeStruct(shape, BF16) for shape in shapes],
         scratch_shapes=[pltpu.VMEM(shape, BF16) for shape in shapes] + [pltpu.SemaphoreType.DMA((5,))],
-        compiler_params=pltpu.CompilerParams(vmem_limit_bytes=58 * MIB),
+        compiler_params=pltpu.CompilerParams(vmem_limit_bytes=room(2 * latent.nbytes)),
         cost_estimate=cost(0, 4 * latent.nbytes),
         name="edge_rows",
     )(latent, cache, low)
@@ -291,7 +292,7 @@
         scores = dot_nt(query, keys[...]) * scale
         powers = jnp.exp2(scores - jnp.max(scores, axis=-1, keepdims=True))
         total = jnp.sum(powers, axis=-1, keepdims=True)
-        mixed = jnp.dot(powers.astype(BF16), values[...], preferred_element_type=F32) / total
+        mixed = jnp.dot(powers.astype(BF16), values[...], preferred_element_type=F32) * (1.0 / total)
         branch = jnp.dot(mixed.astype(BF16), proj[...], preferred_element_type=F32)
         for i in range(step):
             inside = (spots[i] >= 0) & (spots[i] < height)
@@ -331,82 +332,120 @@
     return jnp.concatenate([block[dy : dy + high].reshape(high * width, lanes) for dy in range(3)], axis=-1)
 
 
-def low_kernel(past, tile, mine, other, gain, weights, passed, window, kept, seen, upper, up):
-    frames, ext, width, channels = tile.shape
-    part = mine.shape[2]
+def low_kernel(order, frames, past, tile, up, gain, weights, sums, window, kept, seen, upper):
+    ext, width, channels = tile.shape[1:]
     low = up.shape[2]
-    rows = ext - 2
-    high = 2 * rows
-    phases = passed.shape[1]
-    chan, row = lax.axis_index("chan"), lax.axis_index("rows")
-    up[:, :, pl.ds(pl.multiple_of(chan * part, 32), part)] = mine[...]
-    up[:, :, pl.ds(pl.multiple_of((1 - chan) * part, 32), part)] = other[...]
-    for f in range(frames):
+    high = 2 * (ext - 2)
+    phases = weights.shape[0] // (past + 1)
+    row = lax.axis_index("rows")
+    for spot, f in enumerate(order):
         for l in range(ext):
-            seen[f, l] = spread(tile[f, l].astype(F32))
+            seen[l] = spread(tile[f, l].astype(F32))
         for a in range(2):
             for b in range(2):
                 lanes = slice(b * channels, (b + 2) * channels)
                 span = (ext - 1) * width
-                top = seen[f, : ext - 1, :, lanes].reshape(span, 2 * channels)
-                bottom = seen[f, 1:, :, lanes].reshape(span, 2 * channels)
+                top = seen[: ext - 1, :, lanes].reshape(span, 2 * channels)
+                bottom = seen[1:, :, lanes].reshape(span, 2 * channels)
                 got = dot_nt(top, up[a, b, :, : 2 * channels]) + dot_nt(bottom, up[a, b, :, 2 * channels :])
                 for p in range(ext - 1):
                     upper[2 * p + 1 - a, b] = got[p * width : (p + 1) * width].astype(BF16)
         for j in range(high + 2):
             sides = [upper[j, b].astype(F32) for b in range(2)]
             if 1 <= j <= high:
-                kept[f, j - 1] = jnp.concatenate(sides, axis=-1).astype(BF16)
+                kept[spot, j - 1] = jnp.concatenate(sides, axis=-1).astype(BF16)
             sides = [silu(normed(side, gain[...])) for side in sides]
             if j == 0:
                 sides = [jnp.where(row == 0, 0.0, side) for side in sides]
             if j == high + 1:
                 sides = [jnp.where(row == lax.axis_size("rows") - 1, 0.0, side) for side in sides]
-            window[f, j] = windowed(*sides)
-
-    sums = [None] * past
-    for f in range(frames):
+            window[spot, j] = windowed(*sides)
         count = min(f + past - frames + 1, past)
         if count > 0:
-            got = dot_nt(weights[: count * phases], stacked(window[f], high))
+            got = dot_nt(weights[: count * phases], stacked(window[spot], high))
             for tap in range(count):
                 t = f + past - tap - frames
                 term = got[tap * phases : (tap + 1) * phases]
                 sums[t] = term if sums[t] is None else sums[t] + term
-    for t in range(past):
+
+
+def low_last_kernel(frames, past, tile, mine, other, gain, weights, passed, rest, window, kept, up, seen, upper):
+    part = mine.shape[2]
+    chan = lax.axis_index("chan")
+    up[:, :, pl.ds(pl.multiple_of(chan * part, 32), part)] = mine[...]
+    up[:, :, pl.ds(pl.multiple_of((1 - chan) * part, 32), part)] = other[...]
+    sums = [None] * past
+    low_kernel([frames - 1], frames, past, tile, up, gain, weights, sums, window, kept, seen, upper)
+    passed[...] = sums[-1].astype(BF16)
+    for t in range(past - 1):
+        rest[t] = sums[t]
+
+
+def low_early_kernel(frames, past, tile, up, gain, weights, rest, passed, window, kept, seen, upper):
+    sums = [rest[t] for t in range(past - 1)]
+    low_kernel(range(frames - 1), frames, past, tile, up, gain, weights, sums, window, kept, seen, upper)
+    for t in range(past - 1):
         passed[t] = sums[t].astype(BF16)
 
 
-def low_stage(tile, mine, other, gain, weights, taps):
+def low_shapes(tile, part, count):
+    frames, ext, width, channels = tile.shape
+    low, high = 2 * part, 2 * (ext - 2)
+    outs = [
+        jax.ShapeDtypeStruct((count, high + 2, width, 4 * low), BF16),
+        jax.ShapeDtypeStruct((count, high, width, 2 * low), BF16),
+    ]
+    scratch = [
+        pltpu.VMEM((ext, width, 3 * channels), BF16),
+        pltpu.VMEM((high + 2, 2, width, low), BF16),
+    ]
+    need = 3 * tile.nbytes + 10 * high * width * low * 4
+    flops = 96 * count * high * width * channels * low // 4
+    return outs, scratch, need, flops
+
+
+def low_last(tile, mine, other, gain, weights, taps):
     frames, ext, width, channels = tile.shape
     part = mine.shape[2]
-    low = 2 * part
-    high = 2 * (ext - 2)
-    past = taps - 1
-    phases = 2 * part
-    need = 4 * tile.nbytes + 2 * mine.nbytes + 10 * frames * high * width * low * 4
-    return pl.pallas_call(
-        functools.partial(low_kernel, past),
+    past, pixels = taps - 1, 2 * (ext - 2) * width
+    outs, scratch, need, flops = low_shapes(tile, part, 1)
+    return pl.pallas_call(
+        functools.partial(low_last_kernel, frames, past),
+        in_specs=[vmem()] * 5,
+        out_specs=[vmem()] * 5,
+        out_shape=[
+            jax.ShapeDtypeStruct((2 * part, pixels), BF16),
+            jax.ShapeDtypeStruct((past - 1, 2 * part, pixels), F32),
+            *outs,
+            jax.ShapeDtypeStruct((2, 2, 2 * part, 4 * channels), BF16),
+        ],
+        scratch_shapes=scratch,
+        compiler_params=pltpu.CompilerParams(vmem_limit_bytes=room(need)),
+        cost_estimate=cost(flops, weights.nbytes),
+        name="low_last",
+    )(tile, mine, other, gain, weights)
+
+
+def low_early(tile, up, gain, weights, rest):
+    frames, ext, width, channels = tile.shape
+    part = up.shape[2] // 2
+    past, pixels = rest.shape[0] + 1, rest.shape[2]
+    outs, scratch, need, flops = low_shapes(tile, part, frames - 1)
+    return pl.pallas_call(
+        functools.partial(low_early_kernel, frames, past),
         in_specs=[vmem()] * 5,
         out_specs=[vmem()] * 3,
-        out_shape=[
-            jax.ShapeDtypeStruct((past, phases, high * width), BF16),
-            jax.ShapeDtypeStruct((frames, high + 2, width, 4 * low), BF16),
-            jax.ShapeDtypeStruct((frames, high, width, 2 * low), BF16),
-        ],
-        scratch_shapes=[
-            pltpu.VMEM((frames, ext, width, 3 * channels), BF16),
-            pltpu.VMEM((high + 2, 2, width, low), BF16),
-            pltpu.VMEM((2, 2, low, 4 * channels), BF16),
-        ],
+        out_shape=[jax.ShapeDtypeStruct((past - 1, 2 * part, pixels), BF16), *outs],
+        scratch_shapes=scratch,
         compiler_params=pltpu.CompilerParams(vmem_limit_bytes=room(need)),
-        cost_estimate=cost(96 * frames * high * width * channels * low // 4, 2 * mine.nbytes + weights.nbytes),
-        name="low_stage",
-    )(tile, mine, other, gain, weights)
-
-
-def low_own_kernel(starts, window, kept, weights, own, weave):
-    frames, ext, width, lanes = window.shape
+        cost_estimate=cost(flops, weights.nbytes),
+        name="low_early",
+    )(tile, up, gain, weights, rest)
+
+
+def low_own_kernel(starts, early, last, early_kept, last_kept, weights, cached, arrived, own, weave):
+    frames = early.shape[0] + 1
+    ext, width, lanes = early.shape[1:]
     low = lanes // 4
     high = ext - 2
     phases = own.shape[1]
@@ -419,10 +458,15 @@
     picked = spot == jnp.where(line < part, line + shift, line - part + shift + low)
     select = picked.astype(F32).astype(BF16)
     for f in range(frames):
-        own[f] = dot_nt(select, kept[f].reshape(high * width, 2 * low))
+        kept = early_kept[f] if f < frames - 1 else last_kept[0]
+        total = dot_nt(select, kept.reshape(high * width, 2 * low))
+        if f < past:
+            total = total + cached[f]
+        own[f] = total + arrived[...].astype(F32) if f == past - 1 else total
     for f in range(frames):
+        window = early[f] if f < frames - 1 else last[0]
         least = max(0, f + past - frames + 1)
-        got = dot_nt(weights[least * phases :], stacked(window[f], high))
+        got = dot_nt(weights[least * phases :], stacked(window, high))
         for tap in range(least, taps):
             own[f + past - tap] += got[(tap - least) * phases : (tap - least + 1) * phases]
     span = weave.shape[1] // 2
@@ -434,15 +478,16 @@
             weave[i, b * span : (b + 1) * span] = hit.astype(F32).astype(BF16)
 
 
-def low_own(window, kept, weights, taps):
-    frames, ext, width, lanes = window.shape
+def low_own(early, last, early_kept, last_kept, weights, cached, arrived, taps):
+    frames = early.shape[0] + 1
+    ext, width, lanes = early.shape[1:]
     phases = weights.shape[0] // taps
     high = ext - 2
     starts, span = lane_windows(high, width)
-    need = window.nbytes + 3 * frames * phases * high * width * 4
+    need = frames * last.nbytes + 3 * frames * phases * high * width * 4
     return pl.pallas_call(
         functools.partial(low_own_kernel, starts),
-        in_specs=[vmem()] * 3,
+        in_specs=[vmem()] * 7,
         out_specs=[vmem()] * 2,
         out_shape=[
             jax.ShapeDtypeStruct((frames, phases, high * width), F32),
@@ -451,14 +496,14 @@
         compiler_params=pltpu.CompilerParams(vmem_limit_bytes=room(need)),
         cost_estimate=cost(6 * 9 * high * width * lanes * phases // 2, weights.nbytes),
         name="low_own",
-    )(window, kept, weights)
-
-
-def low_cache_kernel(own, cache, halo, weights, out, window):
+    )(early, last, early_kept, last_kept, weights, cached, arrived)
+
+
+def low_cache_kernel(cache, halo, weights, out, window):
     past, high, channels, columns = cache.shape
     width = columns // 2
-    phases = own.shape[1]
-    out[...] = own[...]
+    phases = out.shape[1]
+    out[...] = jnp.zeros_like(out)
 
     @pl.when(lax.axis_index("segment") == 0)
     def _():
@@ -474,19 +519,20 @@
                 out[f - tap] += got[tap * phases : (tap + 1) * phases]
 
 
-def low_cached(own, cache, halo, weights):
+def low_cached(cache, halo, weights):
     past, high, channels, columns = cache.shape
-    pixels = high * columns
+    phases = weights.shape[0] // (past + 1)
+    pixels = high * columns // 2
     return pl.pallas_call(
         low_cache_kernel,
-        in_specs=[vmem()] * 4,
+        in_specs=[vmem()] * 3,
         out_specs=vmem(),
-        out_shape=jax.ShapeDtypeStruct(own.shape, F32),
+        out_shape=jax.ShapeDtypeStruct((past, phases, pixels), F32),
         scratch_shapes=[pltpu.VMEM((high + 2, columns // 2, 4 * channels), BF16)],
-        compiler_params=pltpu.CompilerParams(vmem_limit_bytes=room(2 * own.nbytes + 16 * cache.nbytes)),
-        cost_estimate=cost(6 * 9 * pixels * channels * own.shape[1] // 2, weights.nbytes),
+        compiler_params=pltpu.CompilerParams(vmem_limit_bytes=room(18 * cache.nbytes)),
+        cost_estimate=cost(6 * 9 * pixels * channels * phases, weights.nbytes),
         name="low_cached",
-    )(own, cache, halo, weights)
+    )(cache, halo, weights)
 
 
 def lane_windows(high, width):
@@ -497,15 +543,15 @@
     return starts, span
 
 
-def finish_kernel(starts, own, passed, weave, out):
+def finish_kernel(starts, own, arrived, weave, out):
     frames = own.shape[0]
     half = own.shape[1] // 2
     span = weave.shape[1] // 2
     totals = []
     for f in range(frames):
         total = own[f]
-        if f < passed.shape[0]:
-            total = total + passed[f].astype(F32)
+        if f < arrived.shape[0]:
+            total = total + arrived[f].astype(F32)
         totals.append(total.astype(BF16))
     for i, start in enumerate(starts):
         lanes = slice(start, start + span)
@@ -515,7 +561,7 @@
             out[f, i] = woven[f * half : (f + 1) * half]
 
 
-def finish(own, passed, weave, high, width):
+def finish(own, arrived, weave, high, width):
     frames, phases = own.shape[:2]
     starts, _ = lane_windows(high, width)
     return pl.pallas_call(
@@ -526,7 +572,27 @@
         compiler_params=pltpu.CompilerParams(vmem_limit_bytes=room(3 * own.nbytes)),
         cost_estimate=cost(2 * own.size * weave.shape[1], own.nbytes),
         name="finish",
-    )(own, passed, weave)
+    )(own, arrived, weave)
+
+
+def join_kernel(own, arrived, out):
+    count = arrived.shape[1]
+    total = own[:, :count] + arrived[...].astype(F32)
+    out[:, :count] = total.astype(BF16)
+    if count < own.shape[1]:
+        out[:, count:] = own[:, count:].astype(BF16)
+
+
+def join(own, arrived):
+    return pl.pallas_call(
+        join_kernel,
+        in_specs=[vmem()] * 2,
+        out_specs=vmem(),
+        out_shape=jax.ShapeDtypeStruct(own.shape, BF16),
+        compiler_params=pltpu.CompilerParams(vmem_limit_bytes=room(2 * own.nbytes)),
+        cost_estimate=cost(own.size, 2 * own.nbytes),
+        name="join",
+    )(own, arrived)
 
 
 def to_neighbour(values, only_first):
@@ -569,14 +635,18 @@
 
     rim, low_rim = edge_rows(latent, cache_mid, low_cache)
     rim = to_neighbour(rim, False)
+    low_rim = to_neighbour(low_rim, True)
     up_mine, low_weights = weight_forms(jnp.swapaxes(conv_up, 2, 3), conv_low)
+    up_mine, tile_in = lax.optimization_barrier((up_mine, latent))
     up_other = lax.ppermute(up_mine, "chan", [(0, 1), (1, 0)])
-    started = mid_inner(latent, cache_mid, gain_mid, mid_weights)
+    started = mid_inner(tile_in, cache_mid, gain_mid, mid_weights)
     halo = lax.all_gather(rim, "chan")
     own, passed = mid_rim(started, halo, gain_mid, mid_weights)
     arrived = to_next(passed)
-
-    first_part = (own + jnp.pad(arrived, ((0, 0), (0, (frames - past) * part))).astype(F32)).astype(BF16)
+    low_rim, own = lax.optimization_barrier((low_rim, own))
+    cached = low_cached(low_cache, lax.all_gather(low_rim, "chan"), low_weights)
+    arrived, cached = lax.optimization_barrier((arrived, cached))
+    first_part = join(own, arrived)
     both = lax.all_gather(first_part, "chan")
     chans = both.shape[0]
     choices = [
@@ -591,13 +661,12 @@
     reached = attention(frame, gain_attn, attn_qkv, attn_proj, rows, width)
     tile = lax.all_gather(reached, "chan")
 
-    passed_low, window, kept = low_stage(tile, up_mine, up_other, gain_low, low_weights, taps)
-    arrived_low = to_next(passed_low)
-    low_rim, _ = lax.optimization_barrier((low_rim, passed_low))
-    low_rim = lax.all_gather(to_neighbour(low_rim, True), "chan")
-    own_low, weave = low_own(window, kept, low_weights, taps)
-    own_low = low_cached(own_low, low_cache, low_rim, low_weights)
-    out = finish(own_low, arrived_low, weave, high, width)
+    passed_last, rest, last, last_kept, up = low_last(tile, up_mine, up_other, gain_low, low_weights, taps)
+    arrived_last = to_next(passed_last)
+    passed_early, early, early_kept = low_early(tile, up, gain_low, low_weights, rest)
+    arrived_early = to_next(passed_early)
+    own_low, weave = low_own(early, last, early_kept, last_kept, low_weights, cached, arrived_last, taps)
+    out = finish(own_low, arrived_early, weave, high, width)
     return jnp.swapaxes(out, 2, 3)
 
 

time: 92.2 us -> 92.4 us (level)
  local copies, waits for them, and re-layouts: 2.34 us -> 6.93 us
  blocking collectives: 32.8 us -> 31.3 us
  other arithmetic: 1.17 us -> 0.18 us
    unnamed x24 -> x28, local copies, waits for them, and re-layouts: 2.18 us -> 6.77 us
    ppermute x2 -> x3, starting transfers between devices: 7.15 us -> 4.16 us  [to_next(): lax.ppermute(values, 'segment', [(i, i + 1) for i in range(count - 1)])]
    all_gather x1, blocking collectives: 22.9 us -> 20.6 us  [body(): frame = lax.all_gather(mine, 'rows')]
    ppermute x2, starting transfers between devices: 7.37 us -> 9.28 us  [to_neighbour(): return lax.ppermute(values, ('rows', 'segment', 'chan'), route)]
    ppermute x2, waiting for transfers between devices: 1.07 us -> 0.01 us  [to_neighbour(): return lax.ppermute(values, ('rows', 'segment', 'chan'), route)]
    convert_element_type x1 -> x0, other arithmetic: 0.99 us -> none  [body(): (own + jnp.pad(arrived, ((0, 0), (0, (frames - past) * part))).astype(F32...]
    pallas_call x2 -> x4, Pallas kernels: 14.4 us -> 13.9 us  [the longest x1 6.21 us: low_last(): pl.pallas_call(functools.partial(low_last_kernel, frames, past), in_specs...]
    ppermute x2 -> x3, waiting for transfers between devices: 2.38 us -> 2.93 us  [to_next(): lax.ppermute(values, 'segment', [(i, i + 1) for i in range(count - 1)])]
  transfers between devices with their start and end apart: 5 -> 6, of which waited for: 2 -> 2; matrix products, arithmetic and copies ran while one was open for 1% -> 0% of each run, Pallas kernels for 22% -> 30%
where the time goes in v5:
time: 92.4 us; the launch traced here: 91.9 us
  Pallas kernels  36.6 us (40%)
  blocking collectives  31.3 us (34%)
  starting transfers between devices  13.6 us (15%)
  local copies, waits for them, and re-layouts  6.93 us (7%)
  waiting for transfers between devices  2.94 us (3%)
    all_gather x1, blocking collectives, body(): frame = lax.all_gather(mine, 'rows')  20.6 us
    ppermute x2, starting transfers between devices, to_neighbour(): return lax.ppermute(values, ('rows', 'segment', 'chan'), route)  9.28 us
    unnamed x28, local copies, waits for them, and re-layouts  6.77 us
    pallas_call x1, Pallas kernels, low_last(): pl.pallas_call(functools.partial(low_last_kernel, frames, past), in_specs...  6.21 us
    pallas_call x1, Pallas kernels, attention(): pl.pallas_call(functools.partial(attn_kernel, tile_rows), in_specs=[vmem(...  5.67 us
    pallas_call x1, Pallas kernels, mid_inner(): pl.pallas_call(mid_inner_kernel, in_specs=[vmem()] * 4, out_specs=vmem(),...  4.89 us
    pallas_call x1, Pallas kernels, low_cached(): pl.pallas_call(low_cache_kernel, in_specs=[vmem()] * 3, out_specs=vmem(),...  4.19 us
    ppermute x3, starting transfers between devices, to_next(): lax.ppermute(values, 'segment', [(i, i + 1) for i in range(count - 1)])  4.16 us
  transfers between devices with their start and end apart: 6, of which 2 were waited for; matrix products, arithmetic and copies ran while one was open for 0% of the time, Pallas kernels for 30%

profile of v5, /device:TPU:0, one launch (start us, length us, event | category | flops | bytes accessed | tf_op | source)
XLA Modules:
  0.0 91.9 jit_solution(1388851212092207727)
XLA Ops:
  0.0 1.3 %copy-done = bf16[2,4,320,192]{2,3,1,0:T(8,128)(2,1)S(1)} copy-done((bf16[2,4,320,192]{2,3,1,0:T(8,128)(2,1)S(1)}, bf16[2,4,320,192]{2,3,1,0:T(8,128)(2,1)}, u32[]{:S(2)}) %copy-start) | copy-done | bytes 983064
  1.3 1.0 %copy-done.4 = bf16[2,2,160,384]{3,2,1,0:T(8,128)(2,1)S(1)} copy-done((bf16[2,2,160,384]{3,2,1,0:T(8,128)(2,1)S(1)}, bf16[2,2,160,384]{3,2,1,0:T(8,128)(2,1)}, u32[]{:S(2)}) %copy-start.4) | copy-done | bytes 491544
  2.3 1.0 %copy-done.6 = bf16[2,2,160,384]{3,2,1,0:T(8,128)(2,1)S(1)} copy-done((bf16[2,2,160,384]{3,2,1,0:T(8,128)(2,1)S(1)}, bf16[2,2,160,384]{3,2,1,0:T(8,128)(2,1)}, u32[]{:S(2)}) %copy-start.6) | copy-done | bytes 491544
  3.3 1.4 %edge_rows.1 = (bf16[4,160,384]{2,1,0:T(8,128)(2,1)S(1)}, bf16[2,192,320]{2,1,0:T(8,128)(2,1)}) custom-call(bf16[2,2,160,384]{3,2,1,0:T(8,128)(2,1)S(1)} %copy-done.4, bf16[2,2,160,384]{3,2,1,0:T(8,128)(2,1)S(1)} %copy-done.6, bf16[2,4,192,320]{3,2,1,0:T(8,128)(2,1)S(1)} %bitcast.10), custom_call_target="tpu_custom_call" | custom-call | bytes 1966080 | tf_op jit(solution)/shard_map/edge_rows/pallas_call | solution.py:87
  4.8 0.0 copy-start.5
  4.8 5.1 %collective-permute-start.1 = (bf16[4,160,384]{2,1,0:T(8,128)(2,1)S(1)}, bf16[4,160,384]{2,1,0:T(8,128)(2,1)S(1)}, u32[]{:S(2)}, u32[]{:S(2)}) collective-permute-start(bf16[4,160,384]{2,1,0:T(8,128)(2,1)S(1)} %get-tuple-element.30), channel_id=1, source_target_pairs={{0,4},{5,1},{2,6},{7,3},{4,8},{9,5},{6,10},{11,7},{8,12},{13,9},{1... | collective-permute-start | bytes 1474568 | tf_op jit(solution)/shard_map/ppermute | solution.py:606
  9.9 4.2 %collective-permute-start = (bf16[2,192,320]{2,1,0:T(8,128)(2,1)}, bf16[2,192,320]{2,1,0:T(8,128)(2,1)}, u32[]{:S(2)}, u32[]{:S(2)}) collective-permute-start(bf16[2,192,320]{2,1,0:T(8,128)(2,1)} %get-tuple-element.27), channel_id=1, source_target_pairs={{0,4},{5,1},{4,8},{9,5},{8,12},{13,9},{16,20},{21,17},{20,24},{25,... | collective-permute-start | bytes 737288 | tf_op jit(solution)/shard_map/ppermute | solution.py:606
  14.1 2.4 %weight_forms.1 = (bf16[2,2,96,1536]{3,2,1,0:T(8,128)(2,1)}, bf16[576,2304]{1,0:T(8,128)(2,1)S(1)}) custom-call(bf16[3,3,96,384]{3,2,1,0:T(8,128)(2,1)S(1)} %bitcast.14, bf16[3,3,3,192,96]{4,3,2,1,0:T(8,128)(2,1)S(1)} %copy-done.2), custom_call_target="tpu_custom_call" | custom-call | flops 95551488 | bytes 6635520 | tf_op jit(solution)/shard_map/weight_forms/pallas_call | solution.py:127
  16.5 2.1 %copy-done.9 = bf16[3,3,3,384,192]{3,4,2,1,0:T(8,128)(2,1)S(1)} copy-done((bf16[3,3,3,384,192]{3,4,2,1,0:T(8,128)(2,1)S(1)}, bf16[3,3,3,384,192]{3,4,2,1,0:T(8,128)(2,1)}, u32[]{:S(2)}) %copy-start.9) | copy-done | bytes 3981336
  18.6 4.9 %mid_inner.1.started = f32[4,320,192]{2,1,0:T(8,128)S(1)} custom-call(bf16[2,2,160,384]{3,2,1,0:T(8,128)(2,1)S(1)} %copy-done.5, bf16[2,2,160,384]{3,2,1,0:T(8,128)(2,1)S(1)} %copy-done.7, f32[384]{0:T(512)S(1)} %copy-done.12, bf16[3,3,3,192,384]{4,3,2,1,0:T(8,128)(2,1)S(1)} %bitcast.15), custom_call_target="tpu_custom_call" | custom-call | flops 2548039680 | bytes 3981312 | tf_op jit(solution)/shard_map/mid_inner/pallas_call | solution.py:201
  23.6 2.5 %all-gather = bf16[8,160,384]{2,1,0:T(8,128)(2,1)S(1)} all-gather(bf16[4,160,384]{2,1,0:T(8,128)(2,1)S(1)} %collective-permute-done.1), channel_id=2, replica_groups=mesh['groups'=2,'rows'=4,'segment'=2,'chan'=2] {'chan'}, dimensions={0}, use_global_device_ids=true | all-gather | bytes 1474560 | tf_op jit(solution)/shard_map/all_gather | solution.py:643
  26.1 3.9 %mid_rim.1 = (f32[320,384]{1,0:T(8,128)S(1)}, bf16[320,384]{1,0:T(8,128)(2,1)}) custom-call(f32[4,320,192]{2,1,0:T(8,128)S(1)} %mid_inner.1.started, bf16[2,4,160,384]{3,2,1,0:T(8,128)(2,1)S(1)} %bitcast.13, f32[384]{0:T(512)S(1)} %copy-done.12, bf16[3,3,3,192,384]{4,3,2,1,0:T(8,128)(2,1)S(1)} %bitcast.16), custom_call_target="tpu_custom_call" | custom-call | flops 2548039680 | bytes 3981312 | tf_op jit(solution)/shard_map/mid_rim/pallas_call | solution.py:248
  30.0 1.3 %collective-permute-start.2 = (bf16[320,384]{1,0:T(8,128)(2,1)}, bf16[320,384]{1,0:T(8,128)(2,1)S(1)}, u32[]{:S(2)}, u32[]{:S(2)}) collective-permute-start(bf16[320,384]{1,0:T(8,128)(2,1)} %get-tuple-element.33), channel_id=1, source_target_pairs={{0,2},{1,3},{4,6},{5,7},{8,10},{9,11},{12,14},{13,15},{16,18},{17,... | collective-permute-start | bytes 737288 | tf_op jit(solution)/shard_map/ppermute | solution.py:611
  31.3 0.2 collective-permute-start.3
  31.5 3.3 %all-gather.1 = bf16[4,192,320]{2,1,0:T(8,128)(2,1)S(1)} all-gather(bf16[2,192,320]{2,1,0:T(8,128)(2,1)} %collective-permute-done), channel_id=3, replica_groups=mesh['groups'=2,'rows'=4,'segment'=2,'chan'=2] {'chan'}, dimensions={0}, use_global_device_ids=true | all-gather | bytes 737280 | tf_op jit(solution)/shard_map/all_gather | solution.py:647
  34.8 1.3 %copy-done.1 = bf16[2,4,320,192]{2,3,1,0:T(8,128)(2,1)S(1)} copy-done((bf16[2,4,320,192]{2,3,1,0:T(8,128)(2,1)S(1)}, bf16[2,4,320,192]{2,3,1,0:T(8,128)(2,1)}, u32[]{:S(2)}) %copy-start.1) | copy-done | bytes 983064
  36.1 4.2 %low_cached.1.cached = f32[2,192,640]{2,1,0:T(8,128)S(1)} custom-call(bf16[2,4,192,320]{3,2,1,0:T(8,128)(2,1)S(1)} %bitcast.11, bf16[2,2,192,320]{3,2,1,0:T(8,128)(2,1)S(1)} %bitcast.12, bf16[576,2304]{1,0:T(8,128)(2,1)S(1)} %get-tuple-element.35.weights), custom_call_target="tpu_custom_call" | custom-call | flops 1274019840 | bytes 2654208 | tf_op jit(solution)/shard_map/low_cached/pallas_call | solution.py:526
  40.3 2.3 %all-gather.2 = bf16[640,384]{1,0:T(8,128)(2,1)S(1)} all-gather(bf16[320,384]{1,0:T(8,128)(2,1)S(1)} %join.1), channel_id=4, replica_groups=mesh['groups'=2,'rows'=4,'segment'=2,'chan'=2] {'chan'}, dimensions={0}, use_global_device_ids=true | all-gather | bytes 737280 | tf_op jit(solution)/shard_map/all_gather | solution.py:650
  42.7 0.2 fusion
  42.9 0.2 maximum_select_fusion
  43.0 20.6 %all_gather.34.frame = bf16[4,320,384]{2,1,0:T(8,128)(2,1)S(1)} all-gather(bf16[1,320,384]{2,1,0:T(8,128)(2,1)S(1)} %maximum_select_fusion), channel_id=1, replica_groups=mesh['groups'=2,'rows'=4,'segment'=2,'chan'=2] {'rows'}, dimensions={0}, use_global_device_ids=true | all-gather | bytes 1228800 | tf_op jit(solution)/shard_map/all_gather | solution.py:659
  63.7 5.7 %frame_attention.1 = bf16[4,160,384]{2,1,0:T(8,128)(2,1)S(1)} custom-call(bf16[4,320,384]{2,1,0:T(8,128)(2,1)S(1)} %all_gather.34.frame, f32[384]{0:T(512)S(1)} %copy-done.13, bf16[384,1152]{1,0:T(8,128)(2,1)S(1)} %copy-done.10, bf16[384,384]{1,0:T(8,128)(2,1)S(1)} %copy-done.11), custom_call_target="tpu_custom_call" | custom-call | flops 2390753280 | bytes 884736 | tf_op jit(solution)/shard_map/frame_attention/pallas_call | solution.py:310
  69.4 0.0 copy-start.8
  69.4 2.5 %all-gather.3 = bf16[8,160,384]{2,1,0:T(8,128)(2,1)S(1)} all-gather(bf16[4,160,384]{2,1,0:T(8,128)(2,1)S(1)} %frame_attention.1), channel_id=5, replica_groups=mesh['groups'=2,'rows'=4,'segment'=2,'chan'=2] {'chan'}, dimensions={0}, use_global_device_ids=true | all-gather | bytes 1474560 | tf_op jit(solution)/shard_map/all_gather | solution.py:662
  71.9 6.2 %low_last.1 = (bf16[192,640]{1,0:T(8,128)(2,1)S(1)}, f32[1,192,640]{2,1,0:T(8,128)S(1)}, bf16[1,6,160,768]{3,2,1,0:T(8,128)(2,1)S(1)}, bf16[1,4,160,384]{3,2,1,0:T(8,128)(2,1)S(1)}, bf16[2,2,192,1536]{3,2,1,0:T(8,128)(2,1)S(1)}) custom-call(bf16[2,4,160,384]{3,2,1,0:T(8,128)(2,1)S(1)} %bitcast.8, bf16[2,2,96,1536]{3,2,1,0:T(8,128)(2,1)} %get-tuple-element.37.mine, ...), custom_call_target="tpu_custom_call" | custom-call | flops 1132462080 | bytes 2654208 | tf_op jit(solution)/shard_map/low_last/pallas_call | solution.py:412
  78.1 1.3 %collective-permute-start.4 = (bf16[192,640]{1,0:T(8,128)(2,1)S(1)}, bf16[192,640]{1,0:T(8,128)(2,1)S(1)}, u32[]{:S(2)}, u32[]{:S(2)}) collective-permute-start(bf16[192,640]{1,0:T(8,128)(2,1)S(1)} %get-tuple-element.45), channel_id=1, source_target_pairs={{0,2},{1,3},{4,6},{5,7},{8,10},{9,11},{12,14},{13,15},{16,18},{17,... | collective-permute-start | bytes 737288 | tf_op jit(solution)/shard_map/ppermute | solution.py:611
  79.5 3.4 %low_early.1 = (bf16[1,192,640]{2,1,0:T(8,128)(2,1)S(1)}, bf16[1,6,160,768]{3,2,1,0:T(8,128)(2,1)S(1)}, bf16[1,4,160,384]{3,2,1,0:T(8,128)(2,1)S(1)}) custom-call(bf16[2,4,160,384]{3,2,1,0:T(8,128)(2,1)S(1)} %bitcast.9, bf16[2,2,192,1536]{3,2,1,0:T(8,128)(2,1)S(1)} %get-tuple-element.38.up, f32[192]{0:T(256)S(1)} %copy-done.8, ...), custom_call_target="tpu_custom_call" | custom-call | flops 1132462080 | bytes 2654208 | tf_op jit(solution)/shard_map/low_early/pallas_call | solution.py:434
  82.9 1.5 %collective-permute-start.5 = (bf16[1,192,640]{2,1,0:T(8,128)(2,1)S(1)}, bf16[1,192,640]{2,1,0:T(8,128)(2,1)S(1)}, u32[]{:S(2)}, u32[]{:S(2)}) collective-permute-start(bf16[1,192,640]{2,1,0:T(8,128)(2,1)S(1)} %get-tuple-element.47), channel_id=1, source_target_pairs={{0,2},{1,3},{4,6},{5,7},{8,10},{9,11},{12,14},{13,15},{16,18},{17,... | collective-permute-start | bytes 737288 | tf_op jit(solution)/shard_map/ppermute | solution.py:611
  84.4 1.3 %collective-permute-done.4.arrived = bf16[192,640]{1,0:T(8,128)(2,1)S(1)} collective-permute-done((bf16[192,640]{1,0:T(8,128)(2,1)S(1)}, bf16[192,640]{1,0:T(8,128)(2,1)S(1)}, u32[]{:S(2)}, u32[]{:S(2)}) %collective-permute-start.4) | collective-permute-done | bytes 245792 | tf_op jit(solution)/shard_map/ppermute | solution.py:611
  85.7 3.1 %low_own.1 = (f32[2,192,640]{2,1,0:T(8,128)S(1)}, bf16[4,512,320]{2,1,0:T(8,128)(2,1)S(1)}) custom-call(bf16[1,6,160,768]{3,2,1,0:T(8,128)(2,1)S(1)} %get-tuple-element.40.early, bf16[1,6,160,768]{3,2,1,0:T(8,128)(2,1)S(1)} %get-tuple-element.41.last, bf16[1,4,160,384]{3,2,1,0:T(8,128)(2,1)S(1)} %get-tuple-element.42.early_kept, ...), custom_call_target="tpu_custom_call" | custom-call | flops 2548039680 | bytes 2654208 | tf_op jit(solution)/shard_map/low_own/pallas_call | solution.py:488
  88.9 1.6 %collective-permute-done.5.arrived = bf16[1,192,640]{2,1,0:T(8,128)(2,1)S(1)} collective-permute-done((bf16[1,192,640]{2,1,0:T(8,128)(2,1)S(1)}, bf16[1,192,640]{2,1,0:T(8,128)(2,1)S(1)}, u32[]{:S(2)}, u32[]{:S(2)}) %collective-permute-start.5) | collective-permute-done | bytes 245792 | tf_op jit(solution)/shard_map/ppermute | solution.py:611
  90.5 1.4 %finish.1 = bf16[2,4,96,320]{3,2,1,0:T(8,128)(2,1)} custom-call(f32[2,192,640]{2,1,0:T(8,128)S(1)} %get-tuple-element.46.own, bf16[1,192,640]{2,1,0:T(8,128)(2,1)S(1)} %collective-permute-done.5.arrived, bf16[4,512,320]{2,1,0:T(8,128)(2,1)S(1)} %get-tuple-element.48.weave), custom_call_target="tpu_custom_call" | custom-call | flops 251658240 | bytes 983040 | tf_op jit(solution)/shard_map/finish/pallas_call | solution.py:567
  (26 shorter events, 0.1 us)
Async XLA Ops:
  0.0 1.3 %copy-start = (bf16[2,4,320,192]{2,3,1,0:T(8,128)(2,1)S(1)}, bf16[2,4,320,192]{2,3,1,0:T(8,128)(2,1)}, u32[]{:S(2)}) copy-start(bf16[2,4,320,192]{2,3,1,0:T(8,128)(2,1)} %param.13) | copy-start | bytes 2949124
  1.3 1.0 %copy-start.4 = (bf16[2,2,160,384]{3,2,1,0:T(8,128)(2,1)S(1)}, bf16[2,2,160,384]{3,2,1,0:T(8,128)(2,1)}, u32[]{:S(2)}) copy-start(bf16[2,2,160,384]{3,2,1,0:T(8,128)(2,1)} %latent.2) | copy-start | bytes 1474564
  2.3 1.0 %copy-start.6 = (bf16[2,2,160,384]{3,2,1,0:T(8,128)(2,1)S(1)}, bf16[2,2,160,384]{3,2,1,0:T(8,128)(2,1)}, u32[]{:S(2)}) copy-start(bf16[2,2,160,384]{3,2,1,0:T(8,128)(2,1)} %cache.3) | copy-start | bytes 1474564
  3.3 10.8 %copy-start.2 = (bf16[3,3,3,192,96]{4,3,2,1,0:T(8,128)(2,1)S(1)}, bf16[3,3,3,192,96]{4,3,2,1,0:T(8,128)(2,1)}, u32[]{:S(2)}) copy-start(bf16[3,3,3,192,96]{4,3,2,1,0:T(8,128)(2,1)} %low.1) | copy-start | bytes 2985988
  3.3 10.8 %copy-start.3 = (bf16[3,3,384,96]{2,3,1,0:T(8,128)(2,1)S(1)}, bf16[3,3,384,96]{2,3,1,0:T(8,128)(2,1)}, u32[]{:S(2)}) copy-start(bf16[3,3,384,96]{2,3,1,0:T(8,128)(2,1)} %param.20) | copy-start | bytes 1990660
  4.8 11.7 %copy-start.5 = (bf16[2,2,160,384]{3,2,1,0:T(8,128)(2,1)S(1)}, bf16[2,2,160,384]{3,2,1,0:T(8,128)(2,1)}, u32[]{:S(2)}) copy-start(bf16[2,2,160,384]{3,2,1,0:T(8,128)(2,1)} %latent.2) | copy-start | bytes 1474564
  4.8 11.7 %copy-start.7 = (bf16[2,2,160,384]{3,2,1,0:T(8,128)(2,1)S(1)}, bf16[2,2,160,384]{3,2,1,0:T(8,128)(2,1)}, u32[]{:S(2)}) copy-start(bf16[2,2,160,384]{3,2,1,0:T(8,128)(2,1)} %cache.3) | copy-start | bytes 1474564
  4.8 11.7 %copy-start.12 = (f32[384]{0:T(512)S(1)}, f32[384]{0:T(512)}, u32[]{:S(2)}) copy-start(f32[384]{0:T(512)} %gain.6) | copy-start | bytes 4612
  4.8 18.7 %collective-permute-start.1 = (bf16[4,160,384]{2,1,0:T(8,128)(2,1)S(1)}, bf16[4,160,384]{2,1,0:T(8,128)(2,1)S(1)}, u32[]{:S(2)}, u32[]{:S(2)}) collective-permute-start(bf16[4,160,384]{2,1,0:T(8,128)(2,1)S(1)} %get-tuple-element.30), channel_id=1, source_target_pairs={{0,4},{5,1},{2,6},{7,3},{4,8},{9,5},{6,10},{11,7},{8,12},{13,9},{1... | collective-permute-start | bytes 1474568 | tf_op jit(solution)/shard_map/ppermute | solution.py:606
  9.9 21.6 %collective-permute-start = (bf16[2,192,320]{2,1,0:T(8,128)(2,1)}, bf16[2,192,320]{2,1,0:T(8,128)(2,1)}, u32[]{:S(2)}, u32[]{:S(2)}) collective-permute-start(bf16[2,192,320]{2,1,0:T(8,128)(2,1)} %get-tuple-element.27), channel_id=1, source_target_pairs={{0,4},{5,1},{4,8},{9,5},{8,12},{13,9},{16,20},{21,17},{20,24},{25,... | collective-permute-start | bytes 737288 | tf_op jit(solution)/shard_map/ppermute | solution.py:606
  16.5 2.1 %copy-start.9 = (bf16[3,3,3,384,192]{3,4,2,1,0:T(8,128)(2,1)S(1)}, bf16[3,3,3,384,192]{3,4,2,1,0:T(8,128)(2,1)}, u32[]{:S(2)}) copy-start(bf16[3,3,3,384,192]{3,4,2,1,0:T(8,128)(2,1)} %param.17) | copy-start | bytes 11943940
  30.0 10.3 %collective-permute-start.2 = (bf16[320,384]{1,0:T(8,128)(2,1)}, bf16[320,384]{1,0:T(8,128)(2,1)S(1)}, u32[]{:S(2)}, u32[]{:S(2)}) collective-permute-start(bf16[320,384]{1,0:T(8,128)(2,1)} %get-tuple-element.33), channel_id=1, source_target_pairs={{0,2},{1,3},{4,6},{5,7},{8,10},{9,11},{12,14},{13,15},{16,18},{17,... | collective-permute-start | bytes 737288 | tf_op jit(solution)/shard_map/ppermute | solution.py:611
  31.3 40.6 %collective-permute-start.3 = (bf16[2,2,96,1536]{3,2,1,0:T(8,128)(2,1)}, bf16[2,2,96,1536]{3,2,1,0:T(8,128)(2,1)}, u32[]{:S(2)}, u32[]{:S(2)}) collective-permute-start(bf16[2,2,96,1536]{3,2,1,0:T(8,128)(2,1)} %get-tuple-element.37.mine), channel_id=1, source_target_pairs={{0,1},{1,0},{2,3},{3,2},{4,5},{5,4},{6,7},{7,6},{8,9},{9,8},{10,11... | collective-permute-start | bytes 3538952 | tf_op jit(solution)/shard_map/ppermute | solution.py:641
  34.8 1.3 %copy-start.1 = (bf16[2,4,320,192]{2,3,1,0:T(8,128)(2,1)S(1)}, bf16[2,4,320,192]{2,3,1,0:T(8,128)(2,1)}, u32[]{:S(2)}) copy-start(bf16[2,4,320,192]{2,3,1,0:T(8,128)(2,1)} %param.13) | copy-start | bytes 2949124
  42.7 21.0 %copy-start.10 = (bf16[384,1152]{1,0:T(8,128)(2,1)S(1)}, bf16[384,1152]{1,0:T(8,128)(2,1)}, u32[]{:S(2)}) copy-start(bf16[384,1152]{1,0:T(8,128)(2,1)} %qkv.1) | copy-start | bytes 2654212
  42.7 21.0 %copy-start.11 = (bf16[384,384]{1,0:T(8,128)(2,1)S(1)}, bf16[384,384]{1,0:T(8,128)(2,1)}, u32[]{:S(2)}) copy-start(bf16[384,384]{1,0:T(8,128)(2,1)} %proj.1) | copy-start | bytes 884740
  42.7 21.0 %copy-start.13 = (f32[384]{0:T(512)S(1)}, f32[384]{0:T(512)}, u32[]{:S(2)}) copy-start(f32[384]{0:T(512)} %gain.7) | copy-start | bytes 4612
  69.4 2.5 %copy-start.8 = (f32[192]{0:T(256)S(1)}, f32[192]{0:T(256)}, u32[]{:S(2)}) copy-start(f32[192]{0:T(256)} %gain.9) | copy-start | bytes 2308
  78.1 7.6 %collective-permute-start.4 = (bf16[192,640]{1,0:T(8,128)(2,1)S(1)}, bf16[192,640]{1,0:T(8,128)(2,1)S(1)}, u32[]{:S(2)}, u32[]{:S(2)}) collective-permute-start(bf16[192,640]{1,0:T(8,128)(2,1)S(1)} %get-tuple-element.45), channel_id=1, source_target_pairs={{0,2},{1,3},{4,6},{5,7},{8,10},{9,11},{12,14},{13,15},{16,18},{17,... | collective-permute-start | bytes 737288 | tf_op jit(solution)/shard_map/ppermute | solution.py:611
  82.9 7.6 %collective-permute-start.5 = (bf16[1,192,640]{2,1,0:T(8,128)(2,1)S(1)}, bf16[1,192,640]{2,1,0:T(8,128)(2,1)S(1)}, u32[]{:S(2)}, u32[]{:S(2)}) collective-permute-start(bf16[1,192,640]{2,1,0:T(8,128)(2,1)S(1)} %get-tuple-element.47), channel_id=1, source_target_pairs={{0,2},{1,3},{4,6},{5,7},{8,10},{9,11},{12,14},{13,15},{16,18},{17,... | collective-permute-start | bytes 737288 | tf_op jit(solution)/shard_map/ppermute | solution.py:611

commit v6 on v5

--- a/solution.py
+++ b/solution.py
@@ -90,7 +90,7 @@
         out_specs=[hbm()] * 2,
         out_shape=[jax.ShapeDtypeStruct(shape, BF16) for shape in shapes],
         scratch_shapes=[pltpu.VMEM(shape, BF16) for shape in shapes] + [pltpu.SemaphoreType.DMA((5,))],
-        compiler_params=pltpu.CompilerParams(vmem_limit_bytes=room(2 * latent.nbytes)),
+        compiler_params=pltpu.CompilerParams(vmem_limit_bytes=58 * MIB),
         cost_estimate=cost(0, 4 * latent.nbytes),
         name="edge_rows",
     )(latent, cache, low)
@@ -133,7 +133,7 @@
             jax.ShapeDtypeStruct((2 * taps * part, 12 * channels), BF16),
         ],
         compiler_params=pltpu.CompilerParams(vmem_limit_bytes=room(6 * up.nbytes + 6 * low.nbytes)),
-        cost_estimate=cost(2 * low.size * part, 4 * up.nbytes + 4 * low.nbytes),
+        cost_estimate=cost(low.size, low.nbytes // 8),
         name="weight_forms",
     )(up, low)
 
@@ -165,7 +165,7 @@
         acc[t, at] += term[i * width : (i + 1) * width]
 
 
-def mid_inner_kernel(latent, cache, gain, weights, acc, seen, seen_cache):
+def mid_inner_kernel(latent, gain, weights, acc, seen):
     frames, rows, width, channels = latent.shape
     taps, part = weights.shape[0], weights.shape[-2]
     past = taps - 1
@@ -184,36 +184,24 @@
         for dy in (1, 0, 2):
             add_rows(acc, seen, weights, [(f, f + past - tap) for f in range(frames)], tap, dy, rows, width)
 
-    @pl.when(lax.axis_index("segment") == 0)
-    def _():
-        for f in range(past):
-            for l in range(rows):
-                seen_cache[f, l] = spread(cache[f, l].astype(F32))
-        for tap in range(past):
-            for dy in (1, 0, 2):
-                add_rows(acc, seen_cache, weights, [(t + tap, t) for t in range(past - tap)], tap, dy, rows, width)
-
-
-def mid_inner(latent, cache, gain, weights):
+
+def mid_inner(latent, gain, weights):
     frames, rows, width, channels = latent.shape
     taps, part = weights.shape[0], weights.shape[-2]
     size = rows * width
     return pl.pallas_call(
         mid_inner_kernel,
-        in_specs=[vmem()] * 4,
+        in_specs=[vmem()] * 3,
         out_specs=vmem(),
         out_shape=jax.ShapeDtypeStruct((frames + taps - 1, size, part), F32),
-        scratch_shapes=[
-            pltpu.VMEM((frames, rows, width, 3 * channels), BF16),
-            pltpu.VMEM((taps - 1, rows, width, 3 * channels), BF16),
-        ],
-        compiler_params=pltpu.CompilerParams(vmem_limit_bytes=room(14 * latent.nbytes)),
+        scratch_shapes=[pltpu.VMEM((frames, rows, width, 3 * channels), BF16)],
+        compiler_params=pltpu.CompilerParams(vmem_limit_bytes=room(10 * latent.nbytes)),
         cost_estimate=cost(2 * 27 * frames * size * channels * part, weights.nbytes),
         name="mid_inner",
-    )(latent, cache, gain, weights)
-
-
-def mid_rim_kernel(started, halo, gain, weights, own, passed, seen, seen_cache, acc):
+    )(latent, gain, weights)
+
+
+def mid_rim_kernel(started, halo, gain, weights, own, passed, seen, acc):
     total, size, part = started.shape
     taps = weights.shape[0]
     past = taps - 1
@@ -226,15 +214,6 @@
         for side in range(2):
             add_rims(acc, seen, weights, [(f, f + past - tap) for f in range(frames)], tap, side)
 
-    @pl.when(lax.axis_index("segment") == 0)
-    def _():
-        for side in range(2):
-            for f in range(past):
-                seen_cache[side, f] = spread(halo[side, frames + f].astype(F32))
-        for tap in range(past):
-            for side in range(2):
-                add_rims(acc, seen_cache, weights, [(t + tap, t) for t in range(past - tap)], tap, side)
-
     own[...] = jnp.concatenate([acc[f] for f in range(frames)], axis=-1)
     passed[...] = jnp.concatenate([acc[frames + t] for t in range(past)], axis=-1).astype(BF16)
 
@@ -255,7 +234,6 @@
         ],
         scratch_shapes=[
             pltpu.VMEM((2, frames, width, 3 * channels), BF16),
-            pltpu.VMEM((2, past, width, 3 * channels), BF16),
             pltpu.VMEM(started.shape, F32),
         ],
         compiler_params=pltpu.CompilerParams(vmem_limit_bytes=room(5 * halo.nbytes + 3 * started.nbytes)),
@@ -264,63 +242,122 @@
     )(started, halo, gain, weights)
 
 
-def attn_kernel(tile_rows, frame, gain, qkv, proj, out, normal, keys, values):
-    count, _, channels = frame.shape
-    width = out.shape[1]
-    size = tile_rows * width
-    height = count * tile_rows
+def mid_cache_kernel(own, cache, halo, weights, out, seen):
+    past, rows, width, channels = cache.shape
+    part = weights.shape[-2]
+    frames = halo.shape[1] - past
+    out[...] = own[...]
+
+    @pl.when(lax.axis_index("segment") == 0)
+    def _():
+        for f in range(past):
+            for l in range(rows + 2):
+                if l == 0 or l == rows + 1:
+                    row = halo[0 if l == 0 else 1, frames + f]
+                else:
+                    row = cache[f, l - 1]
+                seen[f, l] = spread(row.astype(F32))
+        for tap in range(past):
+            count = past - tap
+            total = None
+            for dy in range(3):
+                left = jnp.concatenate(
+                    [seen[t + tap, dy : dy + rows].reshape(rows * width, 3 * channels) for t in range(count)], axis=0
+                )
+                term = dot_nt(left, tap_rows(weights, tap, dy))
+                total = term if total is None else total + term
+            for t in range(count):
+                out[:, t * part : (t + 1) * part] += total[t * rows * width : (t + 1) * rows * width]
+
+
+def mid_cached(own, cache, halo, weights):
+    past, rows, width, channels = cache.shape
+    part = weights.shape[-2]
+    return pl.pallas_call(
+        mid_cache_kernel,
+        in_specs=[vmem()] * 4,
+        out_specs=vmem(),
+        out_shape=jax.ShapeDtypeStruct(own.shape, F32),
+        scratch_shapes=[pltpu.VMEM((past, rows + 2, width, 3 * channels), BF16)],
+        compiler_params=pltpu.CompilerParams(vmem_limit_bytes=room(12 * cache.nbytes + 2 * own.nbytes)),
+        cost_estimate=cost(6 * 9 * rows * width * channels * part, weights.nbytes),
+        name="mid_cached",
+    )(own, cache, halo, weights)
+
+
+def block_kernel(gain, qkv, *refs):
+    count = len(refs) // 3
+    channels = qkv.shape[0]
+    for block, keys, values in zip(refs[:count], refs[count : 2 * count], refs[2 * count :]):
+        scaled = normed(block[...].astype(F32), gain[...]).astype(BF16)
+        both = jnp.dot(scaled, qkv[:, channels:], preferred_element_type=F32).astype(BF16)
+        keys[...] = both[:, :channels]
+        values[...] = both[:, channels:]
+
+
+def block_keys(gain, qkv, blocks):
+    count, size = len(blocks), blocks[0].size
+    outs = pl.pallas_call(
+        block_kernel,
+        in_specs=[vmem()] * (2 + count),
+        out_specs=[vmem()] * (2 * count),
+        out_shape=[jax.ShapeDtypeStruct(blocks[0].shape, BF16)] * (2 * count),
+        compiler_params=pltpu.CompilerParams(vmem_limit_bytes=room(16 * blocks[0].nbytes)),
+        cost_estimate=cost(size, blocks[0].nbytes // 4),
+        name="block_keys",
+    )(gain, qkv, *blocks)
+    return list(outs[:count]), list(outs[count:])
+
+
+def attn_kernel(count, width, gain, qkv, proj, *refs):
+    own, before, after = refs[:3]
+    given, (out, keys, values) = refs[3:-3], refs[-3:]
+    channels = qkv.shape[0]
+    size = own.shape[0]
     rows = out.shape[0]
     step = 2
     scale = 1.0 / (math.sqrt(channels) * math.log(2.0))
-
-    def prepare(index, carry):
-        scaled = normed(frame[index, :size].astype(F32), gain[...]).astype(BF16)
-        normal[pl.ds(index * tile_rows, tile_rows)] = scaled.reshape(tile_rows, width, channels)
-        both = jnp.dot(scaled, qkv[:, channels:], preferred_element_type=F32).astype(BF16)
-        at = pl.ds(pl.multiple_of(index * size, 16), size)
-        keys[at] = both[:, :channels]
-        values[at] = both[:, channels:]
-        return carry
-
-    lax.fori_loop(0, count, prepare, 0)
-    start = lax.axis_index("rows") * tile_rows - 1
+    for i in range(count):
+        keys[i * size : (i + 1) * size] = given[i][...]
+        values[i * size : (i + 1) * size] = given[count + i][...]
+    scaled = normed(after[...].astype(F32), gain[...]).astype(BF16)
+    both = jnp.dot(scaled, qkv[:, channels:], preferred_element_type=F32).astype(BF16)
+    keys[count * size :] = both[:, :channels]
+    values[count * size :] = both[:, channels:]
+    lines = [before[size - width :]] + [own[i * width : (i + 1) * width] for i in range(rows - 2)] + [after[:width]]
+    row = lax.axis_index("rows")
+    inside = [row > 0] + [None] * (rows - 2) + [row < lax.axis_size("rows") - 1]
     for block in range(rows // step):
-        spots = [start + block * step + i for i in range(step)]
-        kept = [jnp.clip(spot, 0, height - 1) for spot in spots]
-        inputs = jnp.concatenate([normal[spot] for spot in kept], axis=0)
+        skipped = jnp.concatenate(lines[block * step : (block + 1) * step], axis=0).astype(F32)
+        inputs = normed(skipped, gain[...]).astype(BF16)
         query = jnp.dot(inputs, qkv[:, :channels], preferred_element_type=F32).astype(BF16)
         scores = dot_nt(query, keys[...]) * scale
         powers = jnp.exp2(scores - jnp.max(scores, axis=-1, keepdims=True))
         total = jnp.sum(powers, axis=-1, keepdims=True)
         mixed = jnp.dot(powers.astype(BF16), values[...], preferred_element_type=F32) * (1.0 / total)
-        branch = jnp.dot(mixed.astype(BF16), proj[...], preferred_element_type=F32)
+        summed = skipped + jnp.dot(mixed.astype(BF16), proj[...], preferred_element_type=F32)
         for i in range(step):
-            inside = (spots[i] >= 0) & (spots[i] < height)
-            owner, line = kept[i] // tile_rows, kept[i] % tile_rows
-            skipped = frame[owner, pl.ds(pl.multiple_of(line * width, 16), width)]
-            summed = skipped.astype(F32) + branch[i * width : (i + 1) * width]
-            out[block * step + i] = jnp.where(inside, summed, 0.0).astype(BF16)
-
-
-def attention(frame, gain, qkv, proj, tile_rows, width):
-    count, _, channels = frame.shape
-    pixels = count * tile_rows * width
-    rows = tile_rows + 2
-    need = 4 * frame.nbytes + 2 * width * pixels * 16 + 2 * qkv.nbytes
-    return pl.pallas_call(
-        functools.partial(attn_kernel, tile_rows),
-        in_specs=[vmem()] * 4,
+            line = summed[i * width : (i + 1) * width]
+            valid = inside[block * step + i]
+            out[block * step + i] = (line if valid is None else jnp.where(valid, line, 0.0)).astype(BF16)
+
+
+def attention(own, before, after, keys, values, gain, qkv, proj, width):
+    size, channels = own.shape
+    count = len(keys)
+    pixels = (count + 1) * size
+    rows = size // width + 2
+    need = 2 * width * pixels * 16 + 12 * own.nbytes
+    return pl.pallas_call(
+        functools.partial(attn_kernel, count, width),
+        in_specs=[vmem()] * (6 + 2 * count),
         out_specs=vmem(),
         out_shape=jax.ShapeDtypeStruct((rows, width, channels), BF16),
-        scratch_shapes=[
-            pltpu.VMEM((count * tile_rows, width, channels), BF16),
-            pltpu.VMEM((pixels, channels), BF16),
-            pltpu.VMEM((pixels, channels), BF16),
-        ],
+        scratch_shapes=[pltpu.VMEM((pixels, channels), BF16), pltpu.VMEM((pixels, channels), BF16)],
         compiler_params=pltpu.CompilerParams(vmem_limit_bytes=room(need)),
-        cost_estimate=cost(4 * channels * (pixels * channels + rows * width * (pixels + channels)), qkv.nbytes),
+        cost_estimate=cost(4 * channels * rows * width * (pixels + channels), qkv.nbytes),
         name="frame_attention",
-    )(frame, gain, qkv, proj)
+    )(gain, qkv, proj, own, before, after, *keys, *values)
 
 
 def windowed(left, right):
@@ -530,7 +567,7 @@
         out_shape=jax.ShapeDtypeStruct((past, phases, pixels), F32),
         scratch_shapes=[pltpu.VMEM((high + 2, columns // 2, 4 * channels), BF16)],
         compiler_params=pltpu.CompilerParams(vmem_limit_bytes=room(18 * cache.nbytes)),
-        cost_estimate=cost(6 * 9 * pixels * channels * phases, weights.nbytes),
+        cost_estimate=cost(pixels * channels, weights.nbytes // 8),
         name="low_cached",
     )(cache, halo, weights)
 
@@ -635,17 +672,15 @@
 
     rim, low_rim = edge_rows(latent, cache_mid, low_cache)
     rim = to_neighbour(rim, False)
-    low_rim = to_neighbour(low_rim, True)
-    up_mine, low_weights = weight_forms(jnp.swapaxes(conv_up, 2, 3), conv_low)
-    up_mine, tile_in = lax.optimization_barrier((up_mine, latent))
-    up_other = lax.ppermute(up_mine, "chan", [(0, 1), (1, 0)])
-    started = mid_inner(tile_in, cache_mid, gain_mid, mid_weights)
+    started = mid_inner(latent, gain_mid, mid_weights)
     halo = lax.all_gather(rim, "chan")
     own, passed = mid_rim(started, halo, gain_mid, mid_weights)
+    passed, low_rim = lax.optimization_barrier((passed, low_rim))
     arrived = to_next(passed)
-    low_rim, own = lax.optimization_barrier((low_rim, own))
-    cached = low_cached(low_cache, lax.all_gather(low_rim, "chan"), low_weights)
-    arrived, cached = lax.optimization_barrier((arrived, cached))
+    low_halo = lax.all_gather(to_neighbour(low_rim, True), "chan")
+    own = mid_cached(own, cache_mid, halo, mid_weights)
+    up_mine, low_weights = weight_forms(jnp.swapaxes(conv_up, 2, 3), conv_low)
+    arrived, low_halo, up_mine, low_weights = lax.optimization_barrier((arrived, low_halo, up_mine, low_weights))
     first_part = join(own, arrived)
     both = lax.all_gather(first_part, "chan")
     chans = both.shape[0]
@@ -656,9 +691,18 @@
     mine = choices[0]
     for f in range(1, frames):
         mine = jnp.where(chan == f, choices[f], mine)
-    frame = lax.all_gather(mine, "rows")
-
-    reached = attention(frame, gain_attn, attn_qkv, attn_proj, rows, width)
+
+    depth = lax.axis_size("rows")
+    turns = [lax.ppermute(mine, "rows", [(i, (i + k) % depth) for i in range(depth)]) for k in range(1, depth)]
+    own_keys, own_values = block_keys(gain_attn, attn_qkv, [mine])
+    up_mine, _ = lax.optimization_barrier((up_mine, mine))
+    up_other = lax.ppermute(up_mine, "chan", [(0, 1), (1, 0)])
+    cached = low_cached(low_cache, low_halo, low_weights)
+    turns[-1], cached, low_weights = lax.optimization_barrier((turns[-1], cached, low_weights))
+    keys, values = block_keys(gain_attn, attn_qkv, turns[:-1])
+    reached = attention(
+        mine, turns[0], turns[-1], own_keys + keys, own_values + values, gain_attn, attn_qkv, attn_proj, width
+    )
     tile = lax.all_gather(reached, "chan")
 
     passed_last, rest, last, last_kept, up = low_last(tile, up_mine, up_other, gain_low, low_weights, taps)

time: 92.4 us -> 89.9 us (0.973)
  the two profiles are of different devices: /device:TPU:0 before, /device:TPU:19 now
where the time goes in v6:
time: 89.9 us; the launch traced here: 89.4 us
  waiting for transfers between devices  31.9 us (35%)
  Pallas kernels  27.7 us (31%)
  blocking collectives  11 us (12%)
  starting transfers between devices  10.6 us (12%)
  local copies, waits for them, and re-layouts  7.72 us (9%)
    ppermute x3, waiting for transfers between devices, body(): lax.ppermute(mine, 'rows', [(i, (i + k) % depth) for i in range(depth)])  21.4 us
    ppermute x3, waiting for transfers between devices, to_next(): lax.ppermute(values, 'segment', [(i, i + 1) for i in range(count - 1)])  7.97 us
    unnamed x38, local copies, waits for them, and re-layouts  7.56 us
    pallas_call x1, Pallas kernels, low_last(): pl.pallas_call(functools.partial(low_last_kernel, frames, past), in_specs...  4.63 us
    ppermute x3, starting transfers between devices, to_next(): lax.ppermute(values, 'segment', [(i, i + 1) for i in range(count - 1)])  4.08 us
    pallas_call x1, Pallas kernels, attention(): pl.pallas_call(functools.partial(attn_kernel, count, width), in_specs=[vm...  3.98 us
    all_gather x1, blocking collectives, body(): halo = lax.all_gather(rim, 'chan')  3.65 us
    ppermute x2, starting transfers between devices, to_neighbour(): return lax.ppermute(values, ('rows', 'segment', 'chan'), route)  3.61 us
  transfers between devices with their start and end apart: 9, of which 5 were waited for; matrix products, arithmetic and copies ran while one was open for 0% of the time, Pallas kernels for 19%

profile of v6, /device:TPU:19, one launch (start us, length us, event | category | flops | bytes accessed | tf_op | source)
XLA Modules:
  0.0 89.4 jit_solution(5326443132588306127)
XLA Ops:
  0.0 2.2 %edge_rows.1 = (bf16[4,160,384]{2,1,0:T(8,128)(2,1)}, bf16[2,192,320]{2,1,0:T(8,128)(2,1)}) custom-call(bf16[2,2,160,384]{3,2,1,0:T(8,128)(2,1)} %latent.3, bf16[2,2,160,384]{3,2,1,0:T(8,128)(2,1)} %cache.3, bf16[2,4,192,320]{3,2,1,0:T(8,128)(2,1)} %bitcast.18), custom_call_target="tpu_custom_call" | custom-call | bytes 1966080 | tf_op jit(solution)/shard_map/edge_rows/pallas_call | solution.py:87
  2.2 2.1 %collective-permute-start = (bf16[4,160,384]{2,1,0:T(8,128)(2,1)}, bf16[4,160,384]{2,1,0:T(8,128)(2,1)S(1)}, u32[]{:S(2)}, u32[]{:S(2)}) collective-permute-start(bf16[4,160,384]{2,1,0:T(8,128)(2,1)} %get-tuple-element.37), channel_id=1, source_target_pairs={{0,4},{5,1},{2,6},{7,3},{4,8},{9,5},{6,10},{11,7},{8,12},{13,9},{1... | collective-permute-start | bytes 1474568 | tf_op jit(solution)/shard_map/ppermute | solution.py:643
  4.3 2.1 %copy-done.1 = bf16[3,3,3,384,192]{3,4,2,1,0:T(8,128)(2,1)S(1)} copy-done((bf16[3,3,3,384,192]{3,4,2,1,0:T(8,128)(2,1)S(1)}, bf16[3,3,3,384,192]{3,4,2,1,0:T(8,128)(2,1)}, u32[]{:S(2)}) %copy-start.1) | copy-done | bytes 3981336
  6.4 3.3 %mid_inner.1.started = f32[4,320,192]{2,1,0:T(8,128)S(1)} custom-call(bf16[2,2,160,384]{3,2,1,0:T(8,128)(2,1)S(1)} %copy-done.12, f32[384]{0:T(512)S(1)} %copy-done.18, bf16[3,3,3,192,384]{4,3,2,1,0:T(8,128)(2,1)S(1)} %bitcast.20), custom_call_target="tpu_custom_call" | custom-call | flops 2548039680 | bytes 3981312 | tf_op jit(solution)/shard_map/mid_inner/pallas_call | solution.py:192
  9.7 2.6 %collective-permute-done = bf16[4,160,384]{2,1,0:T(8,128)(2,1)S(1)} collective-permute-done((bf16[4,160,384]{2,1,0:T(8,128)(2,1)}, bf16[4,160,384]{2,1,0:T(8,128)(2,1)S(1)}, u32[]{:S(2)}, u32[]{:S(2)}) %collective-permute-start) | collective-permute-done | bytes 491552 | tf_op jit(solution)/shard_map/ppermute | solution.py:643
  12.3 3.7 %all-gather = bf16[8,160,384]{2,1,0:T(8,128)(2,1)S(1)} all-gather(bf16[4,160,384]{2,1,0:T(8,128)(2,1)S(1)} %collective-permute-done), channel_id=2, replica_groups=mesh['groups'=2,'rows'=4,'segment'=2,'chan'=2] {'chan'}, dimensions={0}, use_global_device_ids=true | all-gather | bytes 1474560 | tf_op jit(solution)/shard_map/all_gather | solution.py:676
  15.9 2.8 %mid_rim.1 = (f32[320,384]{1,0:T(8,128)S(1)}, bf16[320,384]{1,0:T(8,128)(2,1)}) custom-call(f32[4,320,192]{2,1,0:T(8,128)S(1)} %mid_inner.1.started, bf16[2,4,160,384]{3,2,1,0:T(8,128)(2,1)S(1)} %bitcast.23, f32[384]{0:T(512)S(1)} %copy-done.18, bf16[3,3,3,192,384]{4,3,2,1,0:T(8,128)(2,1)S(1)} %bitcast.21), custom_call_target="tpu_custom_call" | custom-call | flops 2548039680 | bytes 3981312 | tf_op jit(solution)/shard_map/mid_rim/pallas_call | solution.py:227
  18.8 1.5 %collective-permute-start.2 = (bf16[2,192,320]{2,1,0:T(8,128)(2,1)}, bf16[2,192,320]{2,1,0:T(8,128)(2,1)}, u32[]{:S(2)}, u32[]{:S(2)}) collective-permute-start(bf16[2,192,320]{2,1,0:T(8,128)(2,1)} %get-tuple-element.42), channel_id=1, source_target_pairs={{0,4},{5,1},{4,8},{9,5},{8,12},{13,9},{16,20},{21,17},{20,24},{25,... | collective-permute-start | bytes 737288 | tf_op jit(solution)/shard_map/ppermute | solution.py:643
  20.3 1.3 %collective-permute-start.1 = (bf16[320,384]{1,0:T(8,128)(2,1)}, bf16[320,384]{1,0:T(8,128)(2,1)S(1)}, u32[]{:S(2)}, u32[]{:S(2)}) collective-permute-start(bf16[320,384]{1,0:T(8,128)(2,1)} %get-tuple-element.41), channel_id=1, source_target_pairs={{0,2},{1,3},{4,6},{5,7},{8,10},{9,11},{12,14},{13,15},{16,18},{17,... | collective-permute-start | bytes 737288 | tf_op jit(solution)/shard_map/ppermute | solution.py:648
  21.6 1.4 %weight_forms.1 = (bf16[2,2,96,1536]{3,2,1,0:T(8,128)(2,1)S(1)}, bf16[576,2304]{1,0:T(8,128)(2,1)S(1)}) custom-call(bf16[3,3,96,384]{3,2,1,0:T(8,128)(2,1)S(1)} %bitcast.26, bf16[3,3,3,192,96]{4,3,2,1,0:T(8,128)(2,1)S(1)} %copy-done.8), custom_call_target="tpu_custom_call" | custom-call | flops 497664 | bytes 124416 | tf_op jit(solution)/shard_map/weight_forms/pallas_call | solution.py:127
  23.0 1.0 %copy-done.9 = bf16[2,2,96,1536]{3,2,1,0:T(8,128)(2,1)} copy-done((bf16[2,2,96,1536]{3,2,1,0:T(8,128)(2,1)}, bf16[2,2,96,1536]{3,2,1,0:T(8,128)(2,1)S(1)}, u32[]{:S(2)}) %copy-start.9) | copy-done | bytes 1179672
  24.1 2.1 %copy-done.3 = bf16[3,3,3,384,192]{3,4,2,1,0:T(8,128)(2,1)S(1)} copy-done((bf16[3,3,3,384,192]{3,4,2,1,0:T(8,128)(2,1)S(1)}, bf16[3,3,3,384,192]{3,4,2,1,0:T(8,128)(2,1)}, u32[]{:S(2)}) %copy-start.3) | copy-done | bytes 3981336
  26.2 1.2 %copy-done.5 = bf16[8,160,384]{2,1,0:T(8,128)(2,1)S(1)} copy-done((bf16[8,160,384]{2,1,0:T(8,128)(2,1)S(1)}, bf16[8,160,384]{2,1,0:T(8,128)(2,1)}, u32[]{:S(2)}) %copy-start.5) | copy-done | bytes 983064
  27.4 1.0 %copy-done.14 = f32[320,384]{1,0:T(8,128)S(1)} copy-done((f32[320,384]{1,0:T(8,128)S(1)}, f32[320,384]{1,0:T(8,128)}, u32[]{:S(2)}) %copy-start.14) | copy-done | bytes 491544
  28.5 2.4 %all-gather.1 = bf16[4,192,320]{2,1,0:T(8,128)(2,1)S(1)} all-gather(bf16[2,192,320]{2,1,0:T(8,128)(2,1)} %collective-permute-done.2), channel_id=3, replica_groups=mesh['groups'=2,'rows'=4,'segment'=2,'chan'=2] {'chan'}, dimensions={0}, use_global_device_ids=true | all-gather | bytes 737280 | tf_op jit(solution)/shard_map/all_gather | solution.py:680
  31.0 2.3 %all-gather.2 = bf16[640,384]{1,0:T(8,128)(2,1)S(1)} all-gather(bf16[320,384]{1,0:T(8,128)(2,1)S(1)} %join.1), channel_id=4, replica_groups=mesh['groups'=2,'rows'=4,'segment'=2,'chan'=2] {'chan'}, dimensions={0}, use_global_device_ids=true | all-gather | bytes 737280 | tf_op jit(solution)/shard_map/all_gather | solution.py:685
  34.1 1.3 %collective-permute-start.3 = (bf16[320,384]{1,0:T(8,128)(2,1)S(1)}, bf16[320,384]{1,0:T(8,128)(2,1)S(1)}, u32[]{:S(2)}, u32[]{:S(2)}) collective-permute-start(bf16[320,384]{1,0:T(8,128)(2,1)S(1)} %maximum_select_fusion.refs_0_), channel_id=1, source_target_pairs={{0,4},{4,8},{8,12},{12,0},{1,5},{5,9},{9,13},{13,1},{2,6},{6,10},{... | collective-permute-start | bytes 737288 | tf_op jit(solution)/shard_map/ppermute | solution.py:696
  35.4 1.1 %collective-permute-start.4 = (bf16[320,384]{1,0:T(8,128)(2,1)S(1)}, bf16[320,384]{1,0:T(8,128)(2,1)S(1)}, u32[]{:S(2)}, u32[]{:S(2)}) collective-permute-start(bf16[320,384]{1,0:T(8,128)(2,1)S(1)} %maximum_select_fusion.refs_0_), channel_id=1, source_target_pairs={{0,12},{4,0},{8,4},{12,8},{1,13},{5,1},{9,5},{13,9},{2,14},{6,2},{... | collective-permute-start | bytes 737288 | tf_op jit(solution)/shard_map/ppermute | solution.py:696
  36.6 0.5 block_keys.2
  37.3 12.8 %collective-permute-done.5.refs_1_ = bf16[320,384]{1,0:T(8,128)(2,1)S(1)} collective-permute-done((bf16[320,384]{1,0:T(8,128)(2,1)S(1)}, bf16[320,384]{1,0:T(8,128)(2,1)S(1)}, u32[]{:S(2)}, u32[]{:S(2)}) %collective-permute-start.5) | collective-permute-done | bytes 245792 | tf_op jit(solution)/shard_map/ppermute | solution.py:696
  50.1 8.6 %collective-permute-done.3.refs_0_.refs_1_ = bf16[320,384]{1,0:T(8,128)(2,1)S(1)} collective-permute-done((bf16[320,384]{1,0:T(8,128)(2,1)S(1)}, bf16[320,384]{1,0:T(8,128)(2,1)S(1)}, u32[]{:S(2)}, u32[]{:S(2)}) %collective-permute-start.3) | collective-permute-done | bytes 245792 | tf_op jit(solution)/shard_map/ppermute | solution.py:696
  58.7 0.7 block_keys.3
  59.5 4.0 %frame_attention.1 = bf16[4,160,384]{2,1,0:T(8,128)(2,1)S(1)} custom-call(f32[384]{0:T(512)S(1)} %copy-done.15, bf16[384,1152]{1,0:T(8,128)(2,1)S(1)} %copy-done.6, bf16[384,384]{1,0:T(8,128)(2,1)S(1)} %copy-done.17, bf16[320,384]{1,0:T(8,128)(2,1)S(1)} %maximum_select_fusion.refs_0_, bf16[320,384]{1,0:T(8,128)(2,1)S(1)} %collective-permute-done.3.refs_0_.refs_1_, ...), custom_call_target="tpu_custom_call" | custom-call | flops 1635778560 | bytes 884736 | tf_op jit(solution)/shard_map/frame_attention/pallas_call | solution.py:351
  63.5 2.6 %all-gather.3 = bf16[8,160,384]{2,1,0:T(8,128)(2,1)S(1)} all-gather(bf16[4,160,384]{2,1,0:T(8,128)(2,1)S(1)} %frame_attention.1), channel_id=5, replica_groups=mesh['groups'=2,'rows'=4,'segment'=2,'chan'=2] {'chan'}, dimensions={0}, use_global_device_ids=true | all-gather | bytes 1474560 | tf_op jit(solution)/shard_map/all_gather | solution.py:706
  66.1 4.6 %low_last.1 = (bf16[192,640]{1,0:T(8,128)(2,1)S(1)}, f32[1,192,640]{2,1,0:T(8,128)S(1)}, bf16[1,6,160,768]{3,2,1,0:T(8,128)(2,1)S(1)}, bf16[1,4,160,384]{3,2,1,0:T(8,128)(2,1)S(1)}, bf16[2,2,192,1536]{3,2,1,0:T(8,128)(2,1)S(1)}) custom-call(bf16[2,4,160,384]{3,2,1,0:T(8,128)(2,1)S(1)} %bitcast.16, bf16[2,2,96,1536]{3,2,1,0:T(8,128)(2,1)S(1)} %copy-done.10, ...), custom_call_target="tpu_custom_call" | custom-call | flops 1132462080 | bytes 2654208 | tf_op jit(solution)/shard_map/low_last/pallas_call | solution.py:449
  70.7 1.5 %collective-permute-start.7 = (bf16[192,640]{1,0:T(8,128)(2,1)S(1)}, bf16[192,640]{1,0:T(8,128)(2,1)S(1)}, u32[]{:S(2)}, u32[]{:S(2)}) collective-permute-start(bf16[192,640]{1,0:T(8,128)(2,1)S(1)} %get-tuple-element.65), channel_id=1, source_target_pairs={{0,2},{1,3},{4,6},{5,7},{8,10},{9,11},{12,14},{13,15},{16,18},{17,... | collective-permute-start | bytes 737288 | tf_op jit(solution)/shard_map/ppermute | solution.py:648
  72.2 3.4 %low_early.1 = (bf16[1,192,640]{2,1,0:T(8,128)(2,1)S(1)}, bf16[1,6,160,768]{3,2,1,0:T(8,128)(2,1)S(1)}, bf16[1,4,160,384]{3,2,1,0:T(8,128)(2,1)S(1)}) custom-call(bf16[2,4,160,384]{3,2,1,0:T(8,128)(2,1)S(1)} %bitcast.17, bf16[2,2,192,1536]{3,2,1,0:T(8,128)(2,1)S(1)} %get-tuple-element.58.up, f32[192]{0:T(256)S(1)} %copy-done.16, ...), custom_call_target="tpu_custom_call" | custom-call | flops 1132462080 | bytes 2654208 | tf_op jit(solution)/shard_map/low_early/pallas_call | solution.py:471
  75.6 1.3 %collective-permute-start.8 = (bf16[1,192,640]{2,1,0:T(8,128)(2,1)S(1)}, bf16[1,192,640]{2,1,0:T(8,128)(2,1)S(1)}, u32[]{:S(2)}, u32[]{:S(2)}) collective-permute-start(bf16[1,192,640]{2,1,0:T(8,128)(2,1)S(1)} %get-tuple-element.67), channel_id=1, source_target_pairs={{0,2},{1,3},{4,6},{5,7},{8,10},{9,11},{12,14},{13,15},{16,18},{17,... | collective-permute-start | bytes 737288 | tf_op jit(solution)/shard_map/ppermute | solution.py:648
  76.9 5.6 %collective-permute-done.7.arrived = bf16[192,640]{1,0:T(8,128)(2,1)S(1)} collective-permute-done((bf16[192,640]{1,0:T(8,128)(2,1)S(1)}, bf16[192,640]{1,0:T(8,128)(2,1)S(1)}, u32[]{:S(2)}, u32[]{:S(2)}) %collective-permute-start.7) | collective-permute-done | bytes 245792 | tf_op jit(solution)/shard_map/ppermute | solution.py:648
  82.6 3.1 %low_own.1 = (f32[2,192,640]{2,1,0:T(8,128)S(1)}, bf16[4,512,320]{2,1,0:T(8,128)(2,1)S(1)}) custom-call(bf16[1,6,160,768]{3,2,1,0:T(8,128)(2,1)S(1)} %get-tuple-element.60.early, bf16[1,6,160,768]{3,2,1,0:T(8,128)(2,1)S(1)} %get-tuple-element.61.last, bf16[1,4,160,384]{3,2,1,0:T(8,128)(2,1)S(1)} %get-tuple-element.62.early_kept, ...), custom_call_target="tpu_custom_call" | custom-call | flops 2548039680 | bytes 2654208 | tf_op jit(solution)/shard_map/low_own/pallas_call | solution.py:525
  85.7 2.3 %collective-permute-done.8.arrived = bf16[1,192,640]{2,1,0:T(8,128)(2,1)S(1)} collective-permute-done((bf16[1,192,640]{2,1,0:T(8,128)(2,1)S(1)}, bf16[1,192,640]{2,1,0:T(8,128)(2,1)S(1)}, u32[]{:S(2)}, u32[]{:S(2)}) %collective-permute-start.8) | collective-permute-done | bytes 245792 | tf_op jit(solution)/shard_map/ppermute | solution.py:648
  88.0 1.4 %finish.1 = bf16[2,4,96,320]{3,2,1,0:T(8,128)(2,1)} custom-call(f32[2,192,640]{2,1,0:T(8,128)S(1)} %get-tuple-element.66.own, bf16[1,192,640]{2,1,0:T(8,128)(2,1)S(1)} %collective-permute-done.8.arrived, bf16[4,512,320]{2,1,0:T(8,128)(2,1)S(1)} %get-tuple-element.68.weave), custom_call_target="tpu_custom_call" | custom-call | flops 251658240 | bytes 983040 | tf_op jit(solution)/shard_map/finish/pallas_call | solution.py:604
  (44 shorter events, 1.2 us)
Async XLA Ops:
  0.0 4.3 %copy-start.12 = (bf16[2,2,160,384]{3,2,1,0:T(8,128)(2,1)S(1)}, bf16[2,2,160,384]{3,2,1,0:T(8,128)(2,1)}, u32[]{:S(2)}) copy-start(bf16[2,2,160,384]{3,2,1,0:T(8,128)(2,1)} %latent.3) | copy-start | bytes 1474564
  0.0 4.3 %copy-start.18 = (f32[384]{0:T(512)S(1)}, f32[384]{0:T(512)}, u32[]{:S(2)}) copy-start(f32[384]{0:T(512)} %gain.8) | copy-start | bytes 4612
  2.2 10.1 %collective-permute-start = (bf16[4,160,384]{2,1,0:T(8,128)(2,1)}, bf16[4,160,384]{2,1,0:T(8,128)(2,1)S(1)}, u32[]{:S(2)}, u32[]{:S(2)}) collective-permute-start(bf16[4,160,384]{2,1,0:T(8,128)(2,1)} %get-tuple-element.37), channel_id=1, source_target_pairs={{0,4},{5,1},{2,6},{7,3},{4,8},{9,5},{6,10},{11,7},{8,12},{13,9},{1... | collective-permute-start | bytes 1474568 | tf_op jit(solution)/shard_map/ppermute | solution.py:643
  4.3 2.1 %copy-start.1 = (bf16[3,3,3,384,192]{3,4,2,1,0:T(8,128)(2,1)S(1)}, bf16[3,3,3,384,192]{3,4,2,1,0:T(8,128)(2,1)}, u32[]{:S(2)}) copy-start(bf16[3,3,3,384,192]{3,4,2,1,0:T(8,128)(2,1)} %param.17) | copy-start | bytes 11943940
  6.4 9.5 %copy-start.2 = (bf16[3,3,3,384,192]{3,4,2,1,0:T(8,128)(2,1)S(1)}, bf16[3,3,3,384,192]{3,4,2,1,0:T(8,128)(2,1)}, u32[]{:S(2)}) copy-start(bf16[3,3,3,384,192]{3,4,2,1,0:T(8,128)(2,1)} %param.17) | copy-start | bytes 11943940
  15.9 2.8 %copy-start.4 = (bf16[8,160,384]{2,1,0:T(8,128)(2,1)}, bf16[8,160,384]{2,1,0:T(8,128)(2,1)S(1)}, u32[]{:S(2)}) copy-start(bf16[8,160,384]{2,1,0:T(8,128)(2,1)S(1)} %all-gather) | copy-start | bytes 2949124
  15.9 5.7 %copy-start.8 = (bf16[3,3,3,192,96]{4,3,2,1,0:T(8,128)(2,1)S(1)}, bf16[3,3,3,192,96]{4,3,2,1,0:T(8,128)(2,1)}, u32[]{:S(2)}) copy-start(bf16[3,3,3,192,96]{4,3,2,1,0:T(8,128)(2,1)} %low.1) | copy-start | bytes 2985988
  15.9 5.7 %copy-start.11 = (bf16[3,3,384,96]{2,3,1,0:T(8,128)(2,1)S(1)}, bf16[3,3,384,96]{2,3,1,0:T(8,128)(2,1)}, u32[]{:S(2)}) copy-start(bf16[3,3,384,96]{2,3,1,0:T(8,128)(2,1)} %param.20) | copy-start | bytes 1990660
  18.8 4.3 %copy-start.13 = (f32[320,384]{1,0:T(8,128)}, f32[320,384]{1,0:T(8,128)S(1)}, u32[]{:S(2)}) copy-start(f32[320,384]{1,0:T(8,128)S(1)} %get-tuple-element.38.own) | copy-start | bytes 1474564
  18.8 5.3 %copy-start.7 = (bf16[2,2,160,384]{3,2,1,0:T(8,128)(2,1)S(1)}, bf16[2,2,160,384]{3,2,1,0:T(8,128)(2,1)}, u32[]{:S(2)}) copy-start(bf16[2,2,160,384]{3,2,1,0:T(8,128)(2,1)} %cache.3) | copy-start | bytes 1474564
  18.8 9.7 %collective-permute-start.2 = (bf16[2,192,320]{2,1,0:T(8,128)(2,1)}, bf16[2,192,320]{2,1,0:T(8,128)(2,1)}, u32[]{:S(2)}, u32[]{:S(2)}) collective-permute-start(bf16[2,192,320]{2,1,0:T(8,128)(2,1)} %get-tuple-element.42), channel_id=1, source_target_pairs={{0,4},{5,1},{4,8},{9,5},{8,12},{13,9},{16,20},{21,17},{20,24},{25,... | collective-permute-start | bytes 737288 | tf_op jit(solution)/shard_map/ppermute | solution.py:643
  20.3 10.6 %collective-permute-start.1 = (bf16[320,384]{1,0:T(8,128)(2,1)}, bf16[320,384]{1,0:T(8,128)(2,1)S(1)}, u32[]{:S(2)}, u32[]{:S(2)}) collective-permute-start(bf16[320,384]{1,0:T(8,128)(2,1)} %get-tuple-element.41), channel_id=1, source_target_pairs={{0,2},{1,3},{4,6},{5,7},{8,10},{9,11},{12,14},{13,15},{16,18},{17,... | collective-permute-start | bytes 737288 | tf_op jit(solution)/shard_map/ppermute | solution.py:648
  23.0 1.0 %copy-start.9 = (bf16[2,2,96,1536]{3,2,1,0:T(8,128)(2,1)}, bf16[2,2,96,1536]{3,2,1,0:T(8,128)(2,1)S(1)}, u32[]{:S(2)}) copy-start(bf16[2,2,96,1536]{3,2,1,0:T(8,128)(2,1)S(1)} %get-tuple-element.56.mine) | copy-start | bytes 3538948
  24.1 2.1 %copy-start.3 = (bf16[3,3,3,384,192]{3,4,2,1,0:T(8,128)(2,1)S(1)}, bf16[3,3,3,384,192]{3,4,2,1,0:T(8,128)(2,1)}, u32[]{:S(2)}) copy-start(bf16[3,3,3,384,192]{3,4,2,1,0:T(8,128)(2,1)} %param.17) | copy-start | bytes 11943940
  26.2 1.2 %copy-start.5 = (bf16[8,160,384]{2,1,0:T(8,128)(2,1)S(1)}, bf16[8,160,384]{2,1,0:T(8,128)(2,1)}, u32[]{:S(2)}) copy-start(bf16[8,160,384]{2,1,0:T(8,128)(2,1)} %copy-done.4) | copy-start | bytes 2949124
  27.4 1.0 %copy-start.14 = (f32[320,384]{1,0:T(8,128)S(1)}, f32[320,384]{1,0:T(8,128)}, u32[]{:S(2)}) copy-start(f32[320,384]{1,0:T(8,128)} %copy-done.13) | copy-start | bytes 1474564
  31.0 2.7 %copy-start.10 = (bf16[2,2,96,1536]{3,2,1,0:T(8,128)(2,1)S(1)}, bf16[2,2,96,1536]{3,2,1,0:T(8,128)(2,1)}, u32[]{:S(2)}) copy-start(bf16[2,2,96,1536]{3,2,1,0:T(8,128)(2,1)} %copy-done.9) | copy-start | bytes 3538948
  31.0 5.6 %copy-start.6 = (bf16[384,1152]{1,0:T(8,128)(2,1)S(1)}, bf16[384,1152]{1,0:T(8,128)(2,1)}, u32[]{:S(2)}) copy-start(bf16[384,1152]{1,0:T(8,128)(2,1)} %qkv.5) | copy-start | bytes 2654212
  31.0 5.6 %copy-start.15 = (f32[384]{0:T(512)S(1)}, f32[384]{0:T(512)}, u32[]{:S(2)}) copy-start(f32[384]{0:T(512)} %gain.11) | copy-start | bytes 4612
  33.3 3.8 %copy-start = (bf16[2,4,320,192]{2,3,1,0:T(8,128)(2,1)S(1)}, bf16[2,4,320,192]{2,3,1,0:T(8,128)(2,1)}, u32[]{:S(2)}) copy-start(bf16[2,4,320,192]{2,3,1,0:T(8,128)(2,1)} %param.13) | copy-start | bytes 2949124
  33.6 32.4 %collective-permute-start.6 = (bf16[2,2,96,1536]{3,2,1,0:T(8,128)(2,1)S(1)}, bf16[2,2,96,1536]{3,2,1,0:T(8,128)(2,1)S(1)}, u32[]{:S(2)}, u32[]{:S(2)}) collective-permute-start(bf16[2,2,96,1536]{3,2,1,0:T(8,128)(2,1)S(1)} %copy-done.10), channel_id=1, source_target_pairs={{0,1},{1,0},{2,3},{3,2},{4,5},{5,4},{6,7},{7,6},{8,9},{9,8},{10,11... | collective-permute-start | bytes 3538952 | tf_op jit(solution)/shard_map/ppermute | solution.py:699
  34.1 16.0 %collective-permute-start.5 = (bf16[320,384]{1,0:T(8,128)(2,1)S(1)}, bf16[320,384]{1,0:T(8,128)(2,1)S(1)}, u32[]{:S(2)}, u32[]{:S(2)}) collective-permute-start(bf16[320,384]{1,0:T(8,128)(2,1)S(1)} %maximum_select_fusion.refs_0_), channel_id=1, source_target_pairs={{0,8},{4,12},{8,0},{12,4},{1,9},{5,13},{9,1},{13,5},{2,10},{6,14},... | collective-permute-start | bytes 737288 | tf_op jit(solution)/shard_map/ppermute | solution.py:696
  34.1 24.6 %collective-permute-start.3 = (bf16[320,384]{1,0:T(8,128)(2,1)S(1)}, bf16[320,384]{1,0:T(8,128)(2,1)S(1)}, u32[]{:S(2)}, u32[]{:S(2)}) collective-permute-start(bf16[320,384]{1,0:T(8,128)(2,1)S(1)} %maximum_select_fusion.refs_0_), channel_id=1, source_target_pairs={{0,4},{4,8},{8,12},{12,0},{1,5},{5,9},{9,13},{13,1},{2,6},{6,10},{... | collective-permute-start | bytes 737288 | tf_op jit(solution)/shard_map/ppermute | solution.py:696
  35.4 24.0 %collective-permute-start.4 = (bf16[320,384]{1,0:T(8,128)(2,1)S(1)}, bf16[320,384]{1,0:T(8,128)(2,1)S(1)}, u32[]{:S(2)}, u32[]{:S(2)}) collective-permute-start(bf16[320,384]{1,0:T(8,128)(2,1)S(1)} %maximum_select_fusion.refs_0_), channel_id=1, source_target_pairs={{0,12},{4,0},{8,4},{12,8},{1,13},{5,1},{9,5},{13,9},{2,14},{6,2},{... | collective-permute-start | bytes 737288 | tf_op jit(solution)/shard_map/ppermute | solution.py:696
  37.1 22.4 %copy-start.17 = (bf16[384,384]{1,0:T(8,128)(2,1)S(1)}, bf16[384,384]{1,0:T(8,128)(2,1)}, u32[]{:S(2)}) copy-start(bf16[384,384]{1,0:T(8,128)(2,1)} %proj.1) | copy-start | bytes 884740
  63.5 2.6 %copy-start.16 = (f32[192]{0:T(256)S(1)}, f32[192]{0:T(256)}, u32[]{:S(2)}) copy-start(f32[192]{0:T(256)} %gain.13) | copy-start | bytes 2308
  70.7 11.8 %collective-permute-start.7 = (bf16[192,640]{1,0:T(8,128)(2,1)S(1)}, bf16[192,640]{1,0:T(8,128)(2,1)S(1)}, u32[]{:S(2)}, u32[]{:S(2)}) collective-permute-start(bf16[192,640]{1,0:T(8,128)(2,1)S(1)} %get-tuple-element.65), channel_id=1, source_target_pairs={{0,2},{1,3},{4,6},{5,7},{8,10},{9,11},{12,14},{13,15},{16,18},{17,... | collective-permute-start | bytes 737288 | tf_op jit(solution)/shard_map/ppermute | solution.py:648
  75.6 12.4 %collective-permute-start.8 = (bf16[1,192,640]{2,1,0:T(8,128)(2,1)S(1)}, bf16[1,192,640]{2,1,0:T(8,128)(2,1)S(1)}, u32[]{:S(2)}, u32[]{:S(2)}) collective-permute-start(bf16[1,192,640]{2,1,0:T(8,128)(2,1)S(1)} %get-tuple-element.67), channel_id=1, source_target_pairs={{0,2},{1,3},{4,6},{5,7},{8,10},{9,11},{12,14},{13,15},{16,18},{17,... | collective-permute-start | bytes 737288 | tf_op jit(solution)/shard_map/ppermute | solution.py:648

commit v7 on v6

--- a/solution.py
+++ b/solution.py
@@ -55,41 +55,52 @@
     return jnp.where(column == count - 1, 0.0, pltpu.roll(values, count - 1, 0))
 
 
-def edge_kernel(latent, cache, low, rim, low_rim, rows, low_rows, sems):
-    frames = latent.shape[0]
+def column_picks(columns):
+    pixel = lax.broadcasted_iota(jnp.int32, (columns // 2, columns), 0)
+    column = lax.broadcasted_iota(jnp.int32, (columns // 2, columns), 1)
+    return [(column == 2 * pixel + b).astype(BF16) for b in range(2)]
+
+
+def edge_kernel(latent, cache, low, rim, cache_rim, rows, cache_rows, low_rows, sems):
+    past = cache.shape[0]
     chan = lax.axis_index("chan")
 
     def edge(source):
         return source.at[:, jnp.where(chan == 0, source.shape[1] - 1, 0)]
 
     fetched = [
-        pltpu.make_async_copy(edge(latent), rows.at[:frames], sems.at[0]),
-        pltpu.make_async_copy(edge(cache), rows.at[frames:], sems.at[1]),
-        pltpu.make_async_copy(edge(low), low_rows, sems.at[2]),
+        pltpu.make_async_copy(edge(latent), rows, sems.at[0]),
+        pltpu.make_async_copy(edge(low), low_rows, sems.at[1]),
+        pltpu.make_async_copy(edge(cache), cache_rows.at[:past], sems.at[2]),
     ]
     for copy in fetched:
         copy.start()
-    for copy in fetched:
-        copy.wait()
-    stored = [
-        pltpu.make_async_copy(rows, rim, sems.at[3]),
-        pltpu.make_async_copy(low_rows, low_rim, sems.at[4]),
-    ]
-    for copy in stored:
-        copy.start()
-    for copy in stored:
-        copy.wait()
+    picks = column_picks(low.shape[-1])
+    fetched[0].wait()
+    stored = pltpu.make_async_copy(rows, rim, sems.at[3])
+    stored.start()
+    fetched[1].wait()
+    for f in range(past):
+        sides = [dot_nt(pick, low_rows[f]) for pick in picks]
+        cache_rows[past + f] = jnp.concatenate(sides, axis=-1).astype(BF16)
+    fetched[2].wait()
+    cache_stored = pltpu.make_async_copy(cache_rows, cache_rim, sems.at[4])
+    cache_stored.start()
+    stored.wait()
+    cache_stored.wait()
 
 
 def edge_rows(latent, cache, low):
     frames, rows, width, channels = latent.shape
-    shapes = [(frames + cache.shape[0], width, channels), low.shape[:1] + low.shape[2:]]
+    past = cache.shape[0]
+    shapes = [(frames, width, channels), (2 * past, width, channels)]
+    held = shapes + [low.shape[:1] + low.shape[2:]]
     return pl.pallas_call(
         edge_kernel,
         in_specs=[hbm()] * 3,
         out_specs=[hbm()] * 2,
         out_shape=[jax.ShapeDtypeStruct(shape, BF16) for shape in shapes],
-        scratch_shapes=[pltpu.VMEM(shape, BF16) for shape in shapes] + [pltpu.SemaphoreType.DMA((5,))],
+        scratch_shapes=[pltpu.VMEM(shape, BF16) for shape in held] + [pltpu.SemaphoreType.DMA((5,))],
         compiler_params=pltpu.CompilerParams(vmem_limit_bytes=58 * MIB),
         cost_estimate=cost(0, 4 * latent.nbytes),
         name="edge_rows",
@@ -133,7 +144,7 @@
             jax.ShapeDtypeStruct((2 * taps * part, 12 * channels), BF16),
         ],
         compiler_params=pltpu.CompilerParams(vmem_limit_bytes=room(6 * up.nbytes + 6 * low.nbytes)),
-        cost_estimate=cost(low.size, low.nbytes // 8),
+        cost_estimate=cost(2 * low.size * part, 4 * up.nbytes + 4 * low.nbytes),
         name="weight_forms",
     )(up, low)
 
@@ -245,7 +256,6 @@
 def mid_cache_kernel(own, cache, halo, weights, out, seen):
     past, rows, width, channels = cache.shape
     part = weights.shape[-2]
-    frames = halo.shape[1] - past
     out[...] = own[...]
 
     @pl.when(lax.axis_index("segment") == 0)
@@ -253,7 +263,7 @@
         for f in range(past):
             for l in range(rows + 2):
                 if l == 0 or l == rows + 1:
-                    row = halo[0 if l == 0 else 1, frames + f]
+                    row = halo[0 if l == 0 else 1, f]
                 else:
                     row = cache[f, l - 1]
                 seen[f, l] = spread(row.astype(F32))
@@ -406,11 +416,27 @@
                 sums[t] = term if sums[t] is None else sums[t] + term
 
 
-def low_last_kernel(frames, past, tile, mine, other, gain, weights, passed, rest, window, kept, up, seen, upper):
+def up_kernel(mine, other, up):
     part = mine.shape[2]
     chan = lax.axis_index("chan")
     up[:, :, pl.ds(pl.multiple_of(chan * part, 32), part)] = mine[...]
     up[:, :, pl.ds(pl.multiple_of((1 - chan) * part, 32), part)] = other[...]
+
+
+def joined_up(mine, other):
+    outer, part, depth = mine.shape[:2], *mine.shape[2:]
+    return pl.pallas_call(
+        up_kernel,
+        in_specs=[vmem()] * 2,
+        out_specs=vmem(),
+        out_shape=jax.ShapeDtypeStruct(outer + (2 * part, depth), BF16),
+        compiler_params=pltpu.CompilerParams(vmem_limit_bytes=room(0)),
+        cost_estimate=cost(0, mine.nbytes // 8),
+        name="joined_up",
+    )(mine, other)
+
+
+def low_last_kernel(frames, past, tile, up, gain, weights, passed, rest, window, kept, seen, upper):
     sums = [None] * past
     low_kernel([frames - 1], frames, past, tile, up, gain, weights, sums, window, kept, seen, upper)
     passed[...] = sums[-1].astype(BF16)
@@ -441,26 +467,25 @@
     return outs, scratch, need, flops
 
 
-def low_last(tile, mine, other, gain, weights, taps):
+def low_last(tile, up, gain, weights, taps):
     frames, ext, width, channels = tile.shape
-    part = mine.shape[2]
+    part = up.shape[2] // 2
     past, pixels = taps - 1, 2 * (ext - 2) * width
     outs, scratch, need, flops = low_shapes(tile, part, 1)
     return pl.pallas_call(
         functools.partial(low_last_kernel, frames, past),
-        in_specs=[vmem()] * 5,
-        out_specs=[vmem()] * 5,
+        in_specs=[vmem()] * 4,
+        out_specs=[vmem()] * 4,
         out_shape=[
             jax.ShapeDtypeStruct((2 * part, pixels), BF16),
             jax.ShapeDtypeStruct((past - 1, 2 * part, pixels), F32),
             *outs,
-            jax.ShapeDtypeStruct((2, 2, 2 * part, 4 * channels), BF16),
         ],
         scratch_shapes=scratch,
         compiler_params=pltpu.CompilerParams(vmem_limit_bytes=room(need)),
         cost_estimate=cost(flops, weights.nbytes),
         name="low_last",
-    )(tile, mine, other, gain, weights)
+    )(tile, up, gain, weights)
 
 
 def low_early(tile, up, gain, weights, rest):
@@ -544,13 +569,15 @@
 
     @pl.when(lax.axis_index("segment") == 0)
     def _():
-        pixel = lax.broadcasted_iota(jnp.int32, (width, columns), 0)
-        column = lax.broadcasted_iota(jnp.int32, (width, columns), 1)
-        picks = [(column == 2 * pixel + b).astype(BF16) for b in range(2)]
+        picks = column_picks(columns)
         for f in range(past):
             for j in range(high + 2):
-                row = cache[f, j - 1] if 1 <= j <= high else halo[0 if j == 0 else 1, f]
-                window[j] = windowed(*[dot_nt(pick, row) for pick in picks])
+                if 1 <= j <= high:
+                    sides = [dot_nt(pick, cache[f, j - 1]) for pick in picks]
+                else:
+                    rim = halo[0 if j == 0 else 1, past + f].astype(F32)
+                    sides = [rim[:, :channels], rim[:, channels:]]
+                window[j] = windowed(*sides)
             got = dot_nt(weights[: (f + 1) * phases], stacked(window[...], high))
             for tap in range(f + 1):
                 out[f - tap] += got[tap * phases : (tap + 1) * phases]
@@ -670,17 +697,18 @@
     mid_weights = jnp.swapaxes(conv_mid, 3, 4)
     low_cache = jnp.swapaxes(cache_low, 2, 3)
 
-    rim, low_rim = edge_rows(latent, cache_mid, low_cache)
+    rim, cache_rim = edge_rows(latent, cache_mid, low_cache)
     rim = to_neighbour(rim, False)
+    cache_rim = to_neighbour(cache_rim, True)
     started = mid_inner(latent, gain_mid, mid_weights)
     halo = lax.all_gather(rim, "chan")
     own, passed = mid_rim(started, halo, gain_mid, mid_weights)
-    passed, low_rim = lax.optimization_barrier((passed, low_rim))
+    passed, cache_rim = lax.optimization_barrier((passed, cache_rim))
     arrived = to_next(passed)
-    low_halo = lax.all_gather(to_neighbour(low_rim, True), "chan")
-    own = mid_cached(own, cache_mid, halo, mid_weights)
+    cache_halo = lax.all_gather(cache_rim, "chan")
+    own = mid_cached(own, cache_mid, cache_halo, mid_weights)
     up_mine, low_weights = weight_forms(jnp.swapaxes(conv_up, 2, 3), conv_low)
-    arrived, low_halo, up_mine, low_weights = lax.optimization_barrier((arrived, low_halo, up_mine, low_weights))
+    arrived, own, up_mine, low_weights = lax.optimization_barrier((arrived, own, up_mine, low_weights))
     first_part = join(own, arrived)
     both = lax.all_gather(first_part, "chan")
     chans = both.shape[0]
@@ -697,15 +725,16 @@
     own_keys, own_values = block_keys(gain_attn, attn_qkv, [mine])
     up_mine, _ = lax.optimization_barrier((up_mine, mine))
     up_other = lax.ppermute(up_mine, "chan", [(0, 1), (1, 0)])
-    cached = low_cached(low_cache, low_halo, low_weights)
-    turns[-1], cached, low_weights = lax.optimization_barrier((turns[-1], cached, low_weights))
+    cached = low_cached(low_cache, cache_halo, low_weights)
+    up = joined_up(up_mine, up_other)
+    turns[-1], cached, low_weights, up = lax.optimization_barrier((turns[-1], cached, low_weights, up))
     keys, values = block_keys(gain_attn, attn_qkv, turns[:-1])
     reached = attention(
         mine, turns[0], turns[-1], own_keys + keys, own_values + values, gain_attn, attn_qkv, attn_proj, width
     )
     tile = lax.all_gather(reached, "chan")
 
-    passed_last, rest, last, last_kept, up = low_last(tile, up_mine, up_other, gain_low, low_weights, taps)
+    passed_last, rest, last, last_kept = low_last(tile, up, gain_low, low_weights, taps)
     arrived_last = to_next(passed_last)
     passed_early, early, early_kept = low_early(tile, up, gain_low, low_weights, rest)
     arrived_early = to_next(passed_early)

time: 89.9 us -> 84.4 us (0.939)
  the two profiles are of different devices: /device:TPU:19 before, /device:TPU:22 now
where the time goes in v7:
time: 84.4 us; the launch traced here: 84.1 us
  waiting for transfers between devices  31.4 us (37%)
  Pallas kernels  27.5 us (33%)
  starting transfers between devices  12.1 us (14%)
  blocking collectives  9.47 us (11%)
  local copies, waits for them, and re-layouts  3.1 us (4%)
    ppermute x3, waiting for transfers between devices, body(): lax.ppermute(mine, 'rows', [(i, (i + k) % depth) for i in range(depth)])  19.6 us
    ppermute x3, waiting for transfers between devices, to_next(): lax.ppermute(values, 'segment', [(i, i + 1) for i in range(count - 1)])  11.8 us
    pallas_call x1, Pallas kernels, low_last(): pl.pallas_call(functools.partial(low_last_kernel, frames, past), in_specs...  4.46 us
    ppermute x2, starting transfers between devices, to_neighbour(): return lax.ppermute(values, ('rows', 'segment', 'chan'), route)  4.31 us
    ppermute x3, starting transfers between devices, to_next(): lax.ppermute(values, 'segment', [(i, i + 1) for i in range(count - 1)])  4.23 us
    pallas_call x1, Pallas kernels, attention(): pl.pallas_call(functools.partial(attn_kernel, count, width), in_specs=[vm...  4.02 us
    pallas_call x1, Pallas kernels, low_early(): pl.pallas_call(functools.partial(low_early_kernel, frames, past), in_spec...  3.41 us
    ppermute x3, starting transfers between devices, body(): lax.ppermute(mine, 'rows', [(i, (i + k) % depth) for i in range(depth)])  3.38 us
  transfers between devices with their start and end apart: 9, of which 5 were waited for; matrix products, arithmetic and copies ran while one was open for 0% of the time, Pallas kernels for 18%

profile of v7, /device:TPU:22, one launch (start us, length us, event | category | flops | bytes accessed | tf_op | source)
XLA Modules:
  0.0 84.1 jit_solution(4504829936112540326)
XLA Ops:
  0.0 2.5 %edge_rows.1 = (bf16[2,160,384]{2,1,0:T(8,128)(2,1)}, bf16[4,160,384]{2,1,0:T(8,128)(2,1)}) custom-call(bf16[2,2,160,384]{3,2,1,0:T(8,128)(2,1)} %latent.3, bf16[2,2,160,384]{3,2,1,0:T(8,128)(2,1)} %cache.3, bf16[2,4,192,320]{3,2,1,0:T(8,128)(2,1)} %bitcast.20), custom_call_target="tpu_custom_call" | custom-call | bytes 1966080 | tf_op jit(solution)/shard_map/edge_rows/pallas_call | solution.py:98
  2.6 3.6 %collective-permute-start = (bf16[2,160,384]{2,1,0:T(8,128)(2,1)}, bf16[2,160,384]{2,1,0:T(8,128)(2,1)S(1)}, u32[]{:S(2)}, u32[]{:S(2)}) collective-permute-start(bf16[2,160,384]{2,1,0:T(8,128)(2,1)} %get-tuple-element.37), channel_id=1, source_target_pairs={{0,4},{5,1},{2,6},{7,3},{4,8},{9,5},{6,10},{11,7},{8,12},{13,9},{1... | collective-permute-start | bytes 737288 | tf_op jit(solution)/shard_map/ppermute | solution.py:670
  6.2 0.7 collective-permute-start.1
  6.9 1.4 %weight_forms.1 = (bf16[2,2,96,1536]{3,2,1,0:T(8,128)(2,1)S(1)}, bf16[576,2304]{1,0:T(8,128)(2,1)S(1)}) custom-call(bf16[3,3,96,384]{3,2,1,0:T(8,128)(2,1)S(1)} %bitcast.25, bf16[3,3,3,192,96]{4,3,2,1,0:T(8,128)(2,1)S(1)} %copy-done.5), custom_call_target="tpu_custom_call" | custom-call | flops 95551488 | bytes 6635520 | tf_op jit(solution)/shard_map/weight_forms/pallas_call | solution.py:138
  8.3 2.1 %copy-done.1 = bf16[3,3,3,384,192]{3,4,2,1,0:T(8,128)(2,1)S(1)} copy-done((bf16[3,3,3,384,192]{3,4,2,1,0:T(8,128)(2,1)S(1)}, bf16[3,3,3,384,192]{3,4,2,1,0:T(8,128)(2,1)}, u32[]{:S(2)}) %copy-start.1) | copy-done | bytes 3981336
  10.5 3.3 %mid_inner.1.started = f32[4,320,192]{2,1,0:T(8,128)S(1)} custom-call(bf16[2,2,160,384]{3,2,1,0:T(8,128)(2,1)S(1)} %copy-done.7, f32[384]{0:T(512)S(1)} %copy-done.11, bf16[3,3,3,192,384]{4,3,2,1,0:T(8,128)(2,1)S(1)} %bitcast.22), custom_call_target="tpu_custom_call" | custom-call | flops 2548039680 | bytes 3981312 | tf_op jit(solution)/shard_map/mid_inner/pallas_call | solution.py:203
  13.8 2.2 %all-gather = bf16[4,160,384]{2,1,0:T(8,128)(2,1)S(1)} all-gather(bf16[2,160,384]{2,1,0:T(8,128)(2,1)S(1)} %collective-permute-done), channel_id=2, replica_groups=mesh['groups'=2,'rows'=4,'segment'=2,'chan'=2] {'chan'}, dimensions={0}, use_global_device_ids=true | all-gather | bytes 737280 | tf_op jit(solution)/shard_map/all_gather | solution.py:704
  15.9 2.2 %mid_rim.1 = (f32[320,384]{1,0:T(8,128)S(1)}, bf16[320,384]{1,0:T(8,128)(2,1)S(1)}) custom-call(f32[4,320,192]{2,1,0:T(8,128)S(1)} %mid_inner.1.started, bf16[2,2,160,384]{3,2,1,0:T(8,128)(2,1)S(1)} %bitcast.26, f32[384]{0:T(512)S(1)} %copy-done.11, bf16[3,3,3,192,384]{4,3,2,1,0:T(8,128)(2,1)S(1)} %bitcast.23), custom_call_target="tpu_custom_call" | custom-call | flops 2548039680 | bytes 3981312 | tf_op jit(solution)/shard_map/mid_rim/pallas_call | solution.py:238
  18.1 1.4 %collective-permute-start.2 = (bf16[320,384]{1,0:T(8,128)(2,1)S(1)}, bf16[320,384]{1,0:T(8,128)(2,1)S(1)}, u32[]{:S(2)}, u32[]{:S(2)}) collective-permute-start(bf16[320,384]{1,0:T(8,128)(2,1)S(1)} %get-tuple-element.40), channel_id=1, source_target_pairs={{0,2},{1,3},{4,6},{5,7},{8,10},{9,11},{12,14},{13,15},{16,18},{17,... | collective-permute-start | bytes 737288 | tf_op jit(solution)/shard_map/ppermute | solution.py:675
  19.5 2.5 %all-gather.1 = bf16[8,160,384]{2,1,0:T(8,128)(2,1)S(1)} all-gather(bf16[4,160,384]{2,1,0:T(8,128)(2,1)S(1)} %collective-permute-done.1), channel_id=3, replica_groups=mesh['groups'=2,'rows'=4,'segment'=2,'chan'=2] {'chan'}, dimensions={0}, use_global_device_ids=true | all-gather | bytes 1474560 | tf_op jit(solution)/shard_map/all_gather | solution.py:708
  22.1 6.0 %collective-permute-done.2.arrived = bf16[320,384]{1,0:T(8,128)(2,1)S(1)} collective-permute-done((bf16[320,384]{1,0:T(8,128)(2,1)S(1)}, bf16[320,384]{1,0:T(8,128)(2,1)S(1)}, u32[]{:S(2)}, u32[]{:S(2)}) %collective-permute-start.2) | collective-permute-done | bytes 245792 | tf_op jit(solution)/shard_map/ppermute | solution.py:675
  28.2 2.3 %all-gather.2 = bf16[640,384]{1,0:T(8,128)(2,1)S(1)} all-gather(bf16[320,384]{1,0:T(8,128)(2,1)S(1)} %join.1), channel_id=4, replica_groups=mesh['groups'=2,'rows'=4,'segment'=2,'chan'=2] {'chan'}, dimensions={0}, use_global_device_ids=true | all-gather | bytes 737280 | tf_op jit(solution)/shard_map/all_gather | solution.py:713
  30.9 0.2 collective-permute-start.5
  31.1 1.4 %collective-permute-start.6 = (bf16[320,384]{1,0:T(8,128)(2,1)S(1)}, bf16[320,384]{1,0:T(8,128)(2,1)S(1)}, u32[]{:S(2)}, u32[]{:S(2)}) collective-permute-start(bf16[320,384]{1,0:T(8,128)(2,1)S(1)} %maximum_select_fusion.refs_0_), channel_id=1, source_target_pairs={{0,8},{4,12},{8,0},{12,4},{1,9},{5,13},{9,1},{13,5},{2,10},{6,14},... | collective-permute-start | bytes 737288 | tf_op jit(solution)/shard_map/ppermute | solution.py:724
  32.4 1.5 %collective-permute-start.3 = (bf16[320,384]{1,0:T(8,128)(2,1)S(1)}, bf16[320,384]{1,0:T(8,128)(2,1)S(1)}, u32[]{:S(2)}, u32[]{:S(2)}) collective-permute-start(bf16[320,384]{1,0:T(8,128)(2,1)S(1)} %maximum_select_fusion.refs_0_), channel_id=1, source_target_pairs={{0,4},{4,8},{8,12},{12,0},{1,5},{5,9},{9,13},{13,1},{2,6},{6,10},{... | collective-permute-start | bytes 737288 | tf_op jit(solution)/shard_map/ppermute | solution.py:724
  33.9 0.5 collective-permute-start.4
  34.4 0.2 low_cached.1.cached
  34.7 0.5 block_keys.2
  35.2 14.0 %collective-permute-done.6.refs_1_ = bf16[320,384]{1,0:T(8,128)(2,1)S(1)} collective-permute-done((bf16[320,384]{1,0:T(8,128)(2,1)S(1)}, bf16[320,384]{1,0:T(8,128)(2,1)S(1)}, u32[]{:S(2)}, u32[]{:S(2)}) %collective-permute-start.6) | collective-permute-done | bytes 245792 | tf_op jit(solution)/shard_map/ppermute | solution.py:724
  49.2 5.6 %collective-permute-done.3.refs_0_.refs_1_ = bf16[320,384]{1,0:T(8,128)(2,1)S(1)} collective-permute-done((bf16[320,384]{1,0:T(8,128)(2,1)S(1)}, bf16[320,384]{1,0:T(8,128)(2,1)S(1)}, u32[]{:S(2)}, u32[]{:S(2)}) %collective-permute-start.3) | collective-permute-done | bytes 245792 | tf_op jit(solution)/shard_map/ppermute | solution.py:724
  54.8 0.8 block_keys.3
  55.8 0.8 copy-done.10
  56.5 4.0 %frame_attention.1 = bf16[4,160,384]{2,1,0:T(8,128)(2,1)S(1)} custom-call(f32[384]{0:T(512)S(1)} %copy-done.8, bf16[384,1152]{1,0:T(8,128)(2,1)S(1)} %copy-done.3, bf16[384,384]{1,0:T(8,128)(2,1)S(1)} %copy-done.10, bf16[320,384]{1,0:T(8,128)(2,1)S(1)} %maximum_select_fusion.refs_0_, bf16[320,384]{1,0:T(8,128)(2,1)S(1)} %collective-permute-done.3.refs_0_.refs_1_, ...), custom_call_target="tpu_custom_call" | custom-call | flops 1635778560 | bytes 884736 | tf_op jit(solution)/shard_map/frame_attention/pallas_call | solution.py:361
  60.6 2.5 %all-gather.3 = bf16[8,160,384]{2,1,0:T(8,128)(2,1)S(1)} all-gather(bf16[4,160,384]{2,1,0:T(8,128)(2,1)S(1)} %frame_attention.1), channel_id=5, replica_groups=mesh['groups'=2,'rows'=4,'segment'=2,'chan'=2] {'chan'}, dimensions={0}, use_global_device_ids=true | all-gather | bytes 1474560 | tf_op jit(solution)/shard_map/all_gather | solution.py:735
  63.1 4.5 %low_last.1 = (bf16[192,640]{1,0:T(8,128)(2,1)S(1)}, f32[1,192,640]{2,1,0:T(8,128)S(1)}, bf16[1,6,160,768]{3,2,1,0:T(8,128)(2,1)S(1)}, bf16[1,4,160,384]{3,2,1,0:T(8,128)(2,1)S(1)}) custom-call(bf16[2,4,160,384]{3,2,1,0:T(8,128)(2,1)S(1)} %bitcast.18, bf16[2,2,192,1536]{3,2,1,0:T(8,128)(2,1)S(1)} %joined_up.1.up, f32[192]{0:T(256)S(1)} %copy-done.9, ...), custom_call_target="tpu_custom_call" | custom-call | flops 1132462080 | bytes 2654208 | tf_op jit(solution)/shard_map/low_last/pallas_call | solution.py:475
  67.6 1.5 %collective-permute-start.7 = (bf16[192,640]{1,0:T(8,128)(2,1)S(1)}, bf16[192,640]{1,0:T(8,128)(2,1)S(1)}, u32[]{:S(2)}, u32[]{:S(2)}) collective-permute-start(bf16[192,640]{1,0:T(8,128)(2,1)S(1)} %get-tuple-element.65), channel_id=1, source_target_pairs={{0,2},{1,3},{4,6},{5,7},{8,10},{9,11},{12,14},{13,15},{16,18},{17,... | collective-permute-start | bytes 737288 | tf_op jit(solution)/shard_map/ppermute | solution.py:675
  69.1 3.4 %low_early.1 = (bf16[1,192,640]{2,1,0:T(8,128)(2,1)S(1)}, bf16[1,6,160,768]{3,2,1,0:T(8,128)(2,1)S(1)}, bf16[1,4,160,384]{3,2,1,0:T(8,128)(2,1)S(1)}) custom-call(bf16[2,4,160,384]{3,2,1,0:T(8,128)(2,1)S(1)} %bitcast.19, bf16[2,2,192,1536]{3,2,1,0:T(8,128)(2,1)S(1)} %joined_up.1.up, f32[192]{0:T(256)S(1)} %copy-done.9, ...), custom_call_target="tpu_custom_call" | custom-call | flops 1132462080 | bytes 2654208 | tf_op jit(solution)/shard_map/low_early/pallas_call | solution.py:496
  72.5 1.3 %collective-permute-start.8 = (bf16[1,192,640]{2,1,0:T(8,128)(2,1)S(1)}, bf16[1,192,640]{2,1,0:T(8,128)(2,1)S(1)}, u32[]{:S(2)}, u32[]{:S(2)}) collective-permute-start(bf16[1,192,640]{2,1,0:T(8,128)(2,1)S(1)} %get-tuple-element.67), channel_id=1, source_target_pairs={{0,2},{1,3},{4,6},{5,7},{8,10},{9,11},{12,14},{13,15},{16,18},{17,... | collective-permute-start | bytes 737288 | tf_op jit(solution)/shard_map/ppermute | solution.py:675
  73.8 3.9 %collective-permute-done.7.arrived = bf16[192,640]{1,0:T(8,128)(2,1)S(1)} collective-permute-done((bf16[192,640]{1,0:T(8,128)(2,1)S(1)}, bf16[192,640]{1,0:T(8,128)(2,1)S(1)}, u32[]{:S(2)}, u32[]{:S(2)}) %collective-permute-start.7) | collective-permute-done | bytes 245792 | tf_op jit(solution)/shard_map/ppermute | solution.py:675
  77.7 3.1 %low_own.1 = (f32[2,192,640]{2,1,0:T(8,128)S(1)}, bf16[4,512,320]{2,1,0:T(8,128)(2,1)S(1)}) custom-call(bf16[1,6,160,768]{3,2,1,0:T(8,128)(2,1)S(1)} %get-tuple-element.60.early, bf16[1,6,160,768]{3,2,1,0:T(8,128)(2,1)S(1)} %get-tuple-element.61.last, bf16[1,4,160,384]{3,2,1,0:T(8,128)(2,1)S(1)} %get-tuple-element.62.early_kept, ...), custom_call_target="tpu_custom_call" | custom-call | flops 2548039680 | bytes 2654208 | tf_op jit(solution)/shard_map/low_own/pallas_call | solution.py:550
  80.8 1.9 %collective-permute-done.8.arrived = bf16[1,192,640]{2,1,0:T(8,128)(2,1)S(1)} collective-permute-done((bf16[1,192,640]{2,1,0:T(8,128)(2,1)S(1)}, bf16[1,192,640]{2,1,0:T(8,128)(2,1)S(1)}, u32[]{:S(2)}, u32[]{:S(2)}) %collective-permute-start.8) | collective-permute-done | bytes 245792 | tf_op jit(solution)/shard_map/ppermute | solution.py:675
  82.7 1.4 %finish.1 = bf16[2,4,96,320]{3,2,1,0:T(8,128)(2,1)} custom-call(f32[2,192,640]{2,1,0:T(8,128)S(1)} %get-tuple-element.66.own, bf16[1,192,640]{2,1,0:T(8,128)(2,1)S(1)} %collective-permute-done.8.arrived, bf16[4,512,320]{2,1,0:T(8,128)(2,1)S(1)} %get-tuple-element.68.weave), custom_call_target="tpu_custom_call" | custom-call | flops 251658240 | bytes 983040 | tf_op jit(solution)/shard_map/finish/pallas_call | solution.py:631
  (31 shorter events, 0.7 us)
Async XLA Ops:
  0.0 6.9 %copy-start.5 = (bf16[3,3,3,192,96]{4,3,2,1,0:T(8,128)(2,1)S(1)}, bf16[3,3,3,192,96]{4,3,2,1,0:T(8,128)(2,1)}, u32[]{:S(2)}) copy-start(bf16[3,3,3,192,96]{4,3,2,1,0:T(8,128)(2,1)} %low.1) | copy-start | bytes 2985988
  0.0 6.9 %copy-start.6 = (bf16[3,3,384,96]{2,3,1,0:T(8,128)(2,1)S(1)}, bf16[3,3,384,96]{2,3,1,0:T(8,128)(2,1)}, u32[]{:S(2)}) copy-start(bf16[3,3,384,96]{2,3,1,0:T(8,128)(2,1)} %param.20) | copy-start | bytes 1990660
  2.5 5.8 %copy-start.7 = (bf16[2,2,160,384]{3,2,1,0:T(8,128)(2,1)S(1)}, bf16[2,2,160,384]{3,2,1,0:T(8,128)(2,1)}, u32[]{:S(2)}) copy-start(bf16[2,2,160,384]{3,2,1,0:T(8,128)(2,1)} %latent.3) | copy-start | bytes 1474564
  2.5 5.8 %copy-start.11 = (f32[384]{0:T(512)S(1)}, f32[384]{0:T(512)}, u32[]{:S(2)}) copy-start(f32[384]{0:T(512)} %gain.8) | copy-start | bytes 4612
  2.6 11.2 %collective-permute-start = (bf16[2,160,384]{2,1,0:T(8,128)(2,1)}, bf16[2,160,384]{2,1,0:T(8,128)(2,1)S(1)}, u32[]{:S(2)}, u32[]{:S(2)}) collective-permute-start(bf16[2,160,384]{2,1,0:T(8,128)(2,1)} %get-tuple-element.37), channel_id=1, source_target_pairs={{0,4},{5,1},{2,6},{7,3},{4,8},{9,5},{6,10},{11,7},{8,12},{13,9},{1... | collective-permute-start | bytes 737288 | tf_op jit(solution)/shard_map/ppermute | solution.py:670
  6.2 11.9 %collective-permute-start.1 = (bf16[4,160,384]{2,1,0:T(8,128)(2,1)}, bf16[4,160,384]{2,1,0:T(8,128)(2,1)S(1)}, u32[]{:S(2)}, u32[]{:S(2)}) collective-permute-start(bf16[4,160,384]{2,1,0:T(8,128)(2,1)} %get-tuple-element.39), channel_id=1, source_target_pairs={{0,4},{5,1},{4,8},{9,5},{8,12},{13,9},{16,20},{21,17},{20,24},{25,... | collective-permute-start | bytes 1474568 | tf_op jit(solution)/shard_map/ppermute | solution.py:670
  8.3 2.1 %copy-start.1 = (bf16[3,3,3,384,192]{3,4,2,1,0:T(8,128)(2,1)S(1)}, bf16[3,3,3,384,192]{3,4,2,1,0:T(8,128)(2,1)}, u32[]{:S(2)}) copy-start(bf16[3,3,3,384,192]{3,4,2,1,0:T(8,128)(2,1)} %param.17) | copy-start | bytes 11943940
  15.9 6.1 %copy-start.2 = (bf16[3,3,3,384,192]{3,4,2,1,0:T(8,128)(2,1)S(1)}, bf16[3,3,3,384,192]{3,4,2,1,0:T(8,128)(2,1)}, u32[]{:S(2)}) copy-start(bf16[3,3,3,384,192]{3,4,2,1,0:T(8,128)(2,1)} %param.17) | copy-start | bytes 11943940
  18.1 4.0 %copy-start.4 = (bf16[2,2,160,384]{3,2,1,0:T(8,128)(2,1)S(1)}, bf16[2,2,160,384]{3,2,1,0:T(8,128)(2,1)}, u32[]{:S(2)}) copy-start(bf16[2,2,160,384]{3,2,1,0:T(8,128)(2,1)} %cache.3) | copy-start | bytes 1474564
  18.1 10.0 %collective-permute-start.2 = (bf16[320,384]{1,0:T(8,128)(2,1)S(1)}, bf16[320,384]{1,0:T(8,128)(2,1)S(1)}, u32[]{:S(2)}, u32[]{:S(2)}) collective-permute-start(bf16[320,384]{1,0:T(8,128)(2,1)S(1)} %get-tuple-element.40), channel_id=1, source_target_pairs={{0,2},{1,3},{4,6},{5,7},{8,10},{9,11},{12,14},{13,15},{16,18},{17,... | collective-permute-start | bytes 737288 | tf_op jit(solution)/shard_map/ppermute | solution.py:675
  28.2 6.3 %copy-start = (bf16[2,4,320,192]{2,3,1,0:T(8,128)(2,1)S(1)}, bf16[2,4,320,192]{2,3,1,0:T(8,128)(2,1)}, u32[]{:S(2)}) copy-start(bf16[2,4,320,192]{2,3,1,0:T(8,128)(2,1)} %param.13) | copy-start | bytes 2949124
  30.8 3.9 %copy-start.3 = (bf16[384,1152]{1,0:T(8,128)(2,1)S(1)}, bf16[384,1152]{1,0:T(8,128)(2,1)}, u32[]{:S(2)}) copy-start(bf16[384,1152]{1,0:T(8,128)(2,1)} %qkv.5) | copy-start | bytes 2654212
  30.8 3.9 %copy-start.8 = (f32[384]{0:T(512)S(1)}, f32[384]{0:T(512)}, u32[]{:S(2)}) copy-start(f32[384]{0:T(512)} %gain.11) | copy-start | bytes 4612
  30.9 24.7 %collective-permute-start.5 = (bf16[2,2,96,1536]{3,2,1,0:T(8,128)(2,1)S(1)}, bf16[2,2,96,1536]{3,2,1,0:T(8,128)(2,1)S(1)}, u32[]{:S(2)}, u32[]{:S(2)}) collective-permute-start(bf16[2,2,96,1536]{3,2,1,0:T(8,128)(2,1)S(1)} %get-tuple-element.49.mine), channel_id=1, source_target_pairs={{0,1},{1,0},{2,3},{3,2},{4,5},{5,4},{6,7},{7,6},{8,9},{9,8},{10,11... | collective-permute-start | bytes 3538952 | tf_op jit(solution)/shard_map/ppermute | solution.py:727
  31.1 18.2 %collective-permute-start.6 = (bf16[320,384]{1,0:T(8,128)(2,1)S(1)}, bf16[320,384]{1,0:T(8,128)(2,1)S(1)}, u32[]{:S(2)}, u32[]{:S(2)}) collective-permute-start(bf16[320,384]{1,0:T(8,128)(2,1)S(1)} %maximum_select_fusion.refs_0_), channel_id=1, source_target_pairs={{0,8},{4,12},{8,0},{12,4},{1,9},{5,13},{9,1},{13,5},{2,10},{6,14},... | collective-permute-start | bytes 737288 | tf_op jit(solution)/shard_map/ppermute | solution.py:724
  32.4 22.4 %collective-permute-start.3 = (bf16[320,384]{1,0:T(8,128)(2,1)S(1)}, bf16[320,384]{1,0:T(8,128)(2,1)S(1)}, u32[]{:S(2)}, u32[]{:S(2)}) collective-permute-start(bf16[320,384]{1,0:T(8,128)(2,1)S(1)} %maximum_select_fusion.refs_0_), channel_id=1, source_target_pairs={{0,4},{4,8},{8,12},{12,0},{1,5},{5,9},{9,13},{13,1},{2,6},{6,10},{... | collective-permute-start | bytes 737288 | tf_op jit(solution)/shard_map/ppermute | solution.py:724
  33.9 21.8 %collective-permute-start.4 = (bf16[320,384]{1,0:T(8,128)(2,1)S(1)}, bf16[320,384]{1,0:T(8,128)(2,1)S(1)}, u32[]{:S(2)}, u32[]{:S(2)}) collective-permute-start(bf16[320,384]{1,0:T(8,128)(2,1)S(1)} %maximum_select_fusion.refs_0_), channel_id=1, source_target_pairs={{0,12},{4,0},{8,4},{12,8},{1,13},{5,1},{9,5},{13,9},{2,14},{6,2},{... | collective-permute-start | bytes 737288 | tf_op jit(solution)/shard_map/ppermute | solution.py:724
  55.6 1.0 %copy-start.10 = (bf16[384,384]{1,0:T(8,128)(2,1)S(1)}, bf16[384,384]{1,0:T(8,128)(2,1)}, u32[]{:S(2)}) copy-start(bf16[384,384]{1,0:T(8,128)(2,1)} %proj.1) | copy-start | bytes 884740
  60.6 2.5 %copy-start.9 = (f32[192]{0:T(256)S(1)}, f32[192]{0:T(256)}, u32[]{:S(2)}) copy-start(f32[192]{0:T(256)} %gain.13) | copy-start | bytes 2308
  67.6 10.1 %collective-permute-start.7 = (bf16[192,640]{1,0:T(8,128)(2,1)S(1)}, bf16[192,640]{1,0:T(8,128)(2,1)S(1)}, u32[]{:S(2)}, u32[]{:S(2)}) collective-permute-start(bf16[192,640]{1,0:T(8,128)(2,1)S(1)} %get-tuple-element.65), channel_id=1, source_target_pairs={{0,2},{1,3},{4,6},{5,7},{8,10},{9,11},{12,14},{13,15},{16,18},{17,... | collective-permute-start | bytes 737288 | tf_op jit(solution)/shard_map/ppermute | solution.py:675
  72.5 10.2 %collective-permute-start.8 = (bf16[1,192,640]{2,1,0:T(8,128)(2,1)S(1)}, bf16[1,192,640]{2,1,0:T(8,128)(2,1)S(1)}, u32[]{:S(2)}, u32[]{:S(2)}) collective-permute-start(bf16[1,192,640]{2,1,0:T(8,128)(2,1)S(1)} %get-tuple-element.67), channel_id=1, source_target_pairs={{0,2},{1,3},{4,6},{5,7},{8,10},{9,11},{12,14},{13,15},{16,18},{17,... | collective-permute-start | bytes 737288 | tf_op jit(solution)/shard_map/ppermute | solution.py:675

commit v8 on v7

--- a/solution.py
+++ b/solution.py
@@ -319,24 +319,25 @@
     return list(outs[:count]), list(outs[count:])
 
 
-def attn_kernel(count, width, gain, qkv, proj, *refs):
-    own, before, after = refs[:3]
-    given, (out, keys, values) = refs[3:-3], refs[-3:]
+def attn_kernel(count, width, gain, qkv, proj, own, before, after, *refs):
+    given, (out, keys, values) = refs[:-3], refs[-3:]
     channels = qkv.shape[0]
     size = own.shape[0]
     rows = out.shape[0]
     step = 2
     scale = 1.0 / (math.sqrt(channels) * math.log(2.0))
+    row, depth = lax.axis_index("rows"), lax.axis_size("rows")
     for i in range(count):
         keys[i * size : (i + 1) * size] = given[i][...]
         values[i * size : (i + 1) * size] = given[count + i][...]
-    scaled = normed(after[...].astype(F32), gain[...]).astype(BF16)
-    both = jnp.dot(scaled, qkv[:, channels:], preferred_element_type=F32).astype(BF16)
-    keys[count * size :] = both[:, :channels]
-    values[count * size :] = both[:, channels:]
+    for i, block in enumerate((before, after)):
+        scaled = normed(block[...].astype(F32), gain[...]).astype(BF16)
+        both = jnp.dot(scaled, qkv[:, channels:], preferred_element_type=F32).astype(BF16)
+        at = slice((count + i) * size, (count + i + 1) * size)
+        keys[at] = both[:, :channels]
+        values[at] = both[:, channels:]
     lines = [before[size - width :]] + [own[i * width : (i + 1) * width] for i in range(rows - 2)] + [after[:width]]
-    row = lax.axis_index("rows")
-    inside = [row > 0] + [None] * (rows - 2) + [row < lax.axis_size("rows") - 1]
+    inside = [row > 0] + [None] * (rows - 2) + [row < depth - 1]
     for block in range(rows // step):
         skipped = jnp.concatenate(lines[block * step : (block + 1) * step], axis=0).astype(F32)
         inputs = normed(skipped, gain[...]).astype(BF16)
@@ -355,9 +356,9 @@
 def attention(own, before, after, keys, values, gain, qkv, proj, width):
     size, channels = own.shape
     count = len(keys)
-    pixels = (count + 1) * size
+    pixels = (count + 2) * size
     rows = size // width + 2
-    need = 2 * width * pixels * 16 + 12 * own.nbytes
+    need = 2 * width * pixels * 16 + 16 * own.nbytes
     return pl.pallas_call(
         functools.partial(attn_kernel, count, width),
         in_specs=[vmem()] * (6 + 2 * count),
@@ -699,11 +700,12 @@
 
     rim, cache_rim = edge_rows(latent, cache_mid, low_cache)
     rim = to_neighbour(rim, False)
+    started = mid_inner(latent, gain_mid, mid_weights)
+    cache_rim, started = lax.optimization_barrier((cache_rim, started))
     cache_rim = to_neighbour(cache_rim, True)
-    started = mid_inner(latent, gain_mid, mid_weights)
     halo = lax.all_gather(rim, "chan")
     own, passed = mid_rim(started, halo, gain_mid, mid_weights)
-    passed, cache_rim = lax.optimization_barrier((passed, cache_rim))
+    passed, cache_rim, conv_up, conv_low = lax.optimization_barrier((passed, cache_rim, conv_up, conv_low))
     arrived = to_next(passed)
     cache_halo = lax.all_gather(cache_rim, "chan")
     own = mid_cached(own, cache_mid, cache_halo, mid_weights)
@@ -726,9 +728,9 @@
     up_mine, _ = lax.optimization_barrier((up_mine, mine))
     up_other = lax.ppermute(up_mine, "chan", [(0, 1), (1, 0)])
     cached = low_cached(low_cache, cache_halo, low_weights)
+    keys, values = block_keys(gain_attn, attn_qkv, turns[1:-1])
     up = joined_up(up_mine, up_other)
     turns[-1], cached, low_weights, up = lax.optimization_barrier((turns[-1], cached, low_weights, up))
-    keys, values = block_keys(gain_attn, attn_qkv, turns[:-1])
     reached = attention(
         mine, turns[0], turns[-1], own_keys + keys, own_values + values, gain_attn, attn_qkv, attn_proj, width
     )

time: 84.4 us -> 84.7 us (level)
  the two profiles are of different devices: /device:TPU:22 before, /device:TPU:10 now
where the time goes in v8:
time: 84.7 us; the launch traced here: 84.4 us
  waiting for transfers between devices  31.6 us (37%)
  Pallas kernels  27.5 us (32%)
  starting transfers between devices  10.9 us (13%)
  blocking collectives  9.47 us (11%)
  local copies, waits for them, and re-layouts  4.47 us (5%)
    ppermute x3, waiting for transfers between devices, body(): lax.ppermute(mine, 'rows', [(i, (i + k) % depth) for i in range(depth)])  20.2 us
    ppermute x3, waiting for transfers between devices, to_next(): lax.ppermute(values, 'segment', [(i, i + 1) for i in range(count - 1)])  11.4 us
    pallas_call x1, Pallas kernels, low_last(): pl.pallas_call(functools.partial(low_last_kernel, frames, past), in_specs...  4.46 us
    pallas_call x1, Pallas kernels, attention(): pl.pallas_call(functools.partial(attn_kernel, count, width), in_specs=[vm...  4.35 us
    unnamed x28, local copies, waits for them, and re-layouts  4.31 us
    ppermute x3, starting transfers between devices, to_next(): lax.ppermute(values, 'segment', [(i, i + 1) for i in range(count - 1)])  4.23 us
    ppermute x2, starting transfers between devices, to_neighbour(): return lax.ppermute(values, ('rows', 'segment', 'chan'), route)  4.18 us
    pallas_call x1, Pallas kernels, low_early(): pl.pallas_call(functools.partial(low_early_kernel, frames, past), in_spec...  3.41 us
  transfers between devices with their start and end apart: 9, of which 5 were waited for; matrix products, arithmetic and copies ran while one was open for 0% of the time, Pallas kernels for 18%

profile of v8, /device:TPU:10, one launch (start us, length us, event | category | flops | bytes accessed | tf_op | source)
XLA Modules:
  0.0 84.4 jit_solution(10658504079352206684)
XLA Ops:
  0.0 2.4 %edge_rows.1 = (bf16[2,160,384]{2,1,0:T(8,128)(2,1)}, bf16[4,160,384]{2,1,0:T(8,128)(2,1)}) custom-call(bf16[2,2,160,384]{3,2,1,0:T(8,128)(2,1)} %latent.3, bf16[2,2,160,384]{3,2,1,0:T(8,128)(2,1)} %cache.3, bf16[2,4,192,320]{3,2,1,0:T(8,128)(2,1)} %bitcast.20), custom_call_target="tpu_custom_call" | custom-call | bytes 1966080 | tf_op jit(solution)/shard_map/edge_rows/pallas_call | solution.py:98
  2.4 3.5 %collective-permute-start = (bf16[2,160,384]{2,1,0:T(8,128)(2,1)}, bf16[2,160,384]{2,1,0:T(8,128)(2,1)S(1)}, u32[]{:S(2)}, u32[]{:S(2)}) collective-permute-start(bf16[2,160,384]{2,1,0:T(8,128)(2,1)} %get-tuple-element.41), channel_id=1, source_target_pairs={{0,4},{5,1},{2,6},{7,3},{4,8},{9,5},{6,10},{11,7},{8,12},{13,9},{1... | collective-permute-start | bytes 737288 | tf_op jit(solution)/shard_map/ppermute | solution.py:671
  6.0 2.1 %copy-done.1 = bf16[3,3,3,384,192]{3,4,2,1,0:T(8,128)(2,1)S(1)} copy-done((bf16[3,3,3,384,192]{3,4,2,1,0:T(8,128)(2,1)S(1)}, bf16[3,3,3,384,192]{3,4,2,1,0:T(8,128)(2,1)}, u32[]{:S(2)}) %copy-start.1) | copy-done | bytes 3981336
  8.1 3.3 %mid_inner.1.started = f32[4,320,192]{2,1,0:T(8,128)S(1)} custom-call(bf16[2,2,160,384]{3,2,1,0:T(8,128)(2,1)S(1)} %copy-done.8, f32[384]{0:T(512)S(1)} %copy-done.12, bf16[3,3,3,192,384]{4,3,2,1,0:T(8,128)(2,1)S(1)} %bitcast.22), custom_call_target="tpu_custom_call" | custom-call | flops 2548039680 | bytes 3981312 | tf_op jit(solution)/shard_map/mid_inner/pallas_call | solution.py:203
  11.4 0.7 collective-permute-start.1
  12.1 2.2 %all-gather = bf16[4,160,384]{2,1,0:T(8,128)(2,1)S(1)} all-gather(bf16[2,160,384]{2,1,0:T(8,128)(2,1)S(1)} %collective-permute-done), channel_id=2, replica_groups=mesh['groups'=2,'rows'=4,'segment'=2,'chan'=2] {'chan'}, dimensions={0}, use_global_device_ids=true | all-gather | bytes 737280 | tf_op jit(solution)/shard_map/all_gather | solution.py:706
  14.3 2.1 %copy-done.2 = bf16[3,3,3,384,192]{3,4,2,1,0:T(8,128)(2,1)S(1)} copy-done((bf16[3,3,3,384,192]{3,4,2,1,0:T(8,128)(2,1)S(1)}, bf16[3,3,3,384,192]{3,4,2,1,0:T(8,128)(2,1)}, u32[]{:S(2)}) %copy-start.2) | copy-done | bytes 3981336
  16.4 2.2 %mid_rim.1 = (f32[320,384]{1,0:T(8,128)S(1)}, bf16[320,384]{1,0:T(8,128)(2,1)S(1)}) custom-call(f32[4,320,192]{2,1,0:T(8,128)S(1)} %mid_inner.1.started, bf16[2,2,160,384]{3,2,1,0:T(8,128)(2,1)S(1)} %bitcast.26, f32[384]{0:T(512)S(1)} %copy-done.12, bf16[3,3,3,192,384]{4,3,2,1,0:T(8,128)(2,1)S(1)} %bitcast.23), custom_call_target="tpu_custom_call" | custom-call | flops 2548039680 | bytes 3981312 | tf_op jit(solution)/shard_map/mid_rim/pallas_call | solution.py:238
  18.6 1.4 %collective-permute-start.2 = (bf16[320,384]{1,0:T(8,128)(2,1)S(1)}, bf16[320,384]{1,0:T(8,128)(2,1)S(1)}, u32[]{:S(2)}, u32[]{:S(2)}) collective-permute-start(bf16[320,384]{1,0:T(8,128)(2,1)S(1)} %get-tuple-element.44), channel_id=1, source_target_pairs={{0,2},{1,3},{4,6},{5,7},{8,10},{9,11},{12,14},{13,15},{16,18},{17,... | collective-permute-start | bytes 737288 | tf_op jit(solution)/shard_map/ppermute | solution.py:676
  20.0 2.5 %all-gather.1 = bf16[8,160,384]{2,1,0:T(8,128)(2,1)S(1)} all-gather(bf16[4,160,384]{2,1,0:T(8,128)(2,1)S(1)} %collective-permute-done.1), channel_id=3, replica_groups=mesh['groups'=2,'rows'=4,'segment'=2,'chan'=2] {'chan'}, dimensions={0}, use_global_device_ids=true | all-gather | bytes 1474560 | tf_op jit(solution)/shard_map/all_gather | solution.py:710
  22.5 1.4 %weight_forms.1 = (bf16[2,2,96,1536]{3,2,1,0:T(8,128)(2,1)S(1)}, bf16[576,2304]{1,0:T(8,128)(2,1)S(1)}) custom-call(bf16[3,3,96,384]{3,2,1,0:T(8,128)(2,1)S(1)} %bitcast.25, bf16[3,3,3,192,96]{4,3,2,1,0:T(8,128)(2,1)S(1)} %copy-done.6), custom_call_target="tpu_custom_call" | custom-call | flops 95551488 | bytes 6635520 | tf_op jit(solution)/shard_map/weight_forms/pallas_call | solution.py:138
  24.0 5.6 %collective-permute-done.2.arrived = bf16[320,384]{1,0:T(8,128)(2,1)S(1)} collective-permute-done((bf16[320,384]{1,0:T(8,128)(2,1)S(1)}, bf16[320,384]{1,0:T(8,128)(2,1)S(1)}, u32[]{:S(2)}, u32[]{:S(2)}) %collective-permute-start.2) | collective-permute-done | bytes 245792 | tf_op jit(solution)/shard_map/ppermute | solution.py:676
  29.6 2.3 %all-gather.2 = bf16[640,384]{1,0:T(8,128)(2,1)S(1)} all-gather(bf16[320,384]{1,0:T(8,128)(2,1)S(1)} %join.1), channel_id=4, replica_groups=mesh['groups'=2,'rows'=4,'segment'=2,'chan'=2] {'chan'}, dimensions={0}, use_global_device_ids=true | all-gather | bytes 737280 | tf_op jit(solution)/shard_map/all_gather | solution.py:715
  32.3 0.2 collective-permute-start.5
  32.5 0.3 collective-permute-start.6
  32.8 1.8 %collective-permute-start.4 = (bf16[320,384]{1,0:T(8,128)(2,1)S(1)}, bf16[320,384]{1,0:T(8,128)(2,1)S(1)}, u32[]{:S(2)}, u32[]{:S(2)}) collective-permute-start(bf16[320,384]{1,0:T(8,128)(2,1)S(1)} %maximum_select_fusion.refs_0_.own), channel_id=1, source_target_pairs={{0,12},{4,0},{8,4},{12,8},{1,13},{5,1},{9,5},{13,9},{2,14},{6,2},{... | collective-permute-start | bytes 737288 | tf_op jit(solution)/shard_map/ppermute | solution.py:726
  34.6 0.2 collective-permute-start.3
  34.8 0.2 low_cached.1.cached
  35.1 0.5 block_keys.2
  35.6 14.1 %collective-permute-done.6.refs_0_ = bf16[320,384]{1,0:T(8,128)(2,1)S(1)} collective-permute-done((bf16[320,384]{1,0:T(8,128)(2,1)S(1)}, bf16[320,384]{1,0:T(8,128)(2,1)S(1)}, u32[]{:S(2)}, u32[]{:S(2)}) %collective-permute-start.6) | collective-permute-done | bytes 245792 | tf_op jit(solution)/shard_map/ppermute | solution.py:726
  49.7 0.5 block_keys.3
  50.3 6.1 %collective-permute-done.4.after = bf16[320,384]{1,0:T(8,128)(2,1)S(1)} collective-permute-done((bf16[320,384]{1,0:T(8,128)(2,1)S(1)}, bf16[320,384]{1,0:T(8,128)(2,1)S(1)}, u32[]{:S(2)}, u32[]{:S(2)}) %collective-permute-start.4) | collective-permute-done | bytes 245792 | tf_op jit(solution)/shard_map/ppermute | solution.py:726
  56.5 4.4 %frame_attention.1 = bf16[4,160,384]{2,1,0:T(8,128)(2,1)S(1)} custom-call(f32[384]{0:T(512)S(1)} %copy-done.9, bf16[384,1152]{1,0:T(8,128)(2,1)S(1)} %copy-done.4, bf16[384,384]{1,0:T(8,128)(2,1)S(1)} %copy-done.11, bf16[320,384]{1,0:T(8,128)(2,1)S(1)} %maximum_select_fusion.refs_0_.own, bf16[320,384]{1,0:T(8,128)(2,1)S(1)} %collective-permute-done.3.before, ...), custom_call_target="tpu_custom_call" | custom-call | flops 1635778560 | bytes 884736 | tf_op jit(solution)/shard_map/frame_attention/pallas_call | solution.py:362
  60.8 2.5 %all-gather.3 = bf16[8,160,384]{2,1,0:T(8,128)(2,1)S(1)} all-gather(bf16[4,160,384]{2,1,0:T(8,128)(2,1)S(1)} %frame_attention.1), channel_id=5, replica_groups=mesh['groups'=2,'rows'=4,'segment'=2,'chan'=2] {'chan'}, dimensions={0}, use_global_device_ids=true | all-gather | bytes 1474560 | tf_op jit(solution)/shard_map/all_gather | solution.py:737
  63.3 4.5 %low_last.1 = (bf16[192,640]{1,0:T(8,128)(2,1)S(1)}, f32[1,192,640]{2,1,0:T(8,128)S(1)}, bf16[1,6,160,768]{3,2,1,0:T(8,128)(2,1)S(1)}, bf16[1,4,160,384]{3,2,1,0:T(8,128)(2,1)S(1)}) custom-call(bf16[2,4,160,384]{3,2,1,0:T(8,128)(2,1)S(1)} %bitcast.18, bf16[2,2,192,1536]{3,2,1,0:T(8,128)(2,1)S(1)} %joined_up.1.up, f32[192]{0:T(256)S(1)} %copy-done.10, ...), custom_call_target="tpu_custom_call" | custom-call | flops 1132462080 | bytes 2654208 | tf_op jit(solution)/shard_map/low_last/pallas_call | solution.py:476
  67.8 1.5 %collective-permute-start.7 = (bf16[192,640]{1,0:T(8,128)(2,1)S(1)}, bf16[192,640]{1,0:T(8,128)(2,1)S(1)}, u32[]{:S(2)}, u32[]{:S(2)}) collective-permute-start(bf16[192,640]{1,0:T(8,128)(2,1)S(1)} %get-tuple-element.69), channel_id=1, source_target_pairs={{0,2},{1,3},{4,6},{5,7},{8,10},{9,11},{12,14},{13,15},{16,18},{17,... | collective-permute-start | bytes 737288 | tf_op jit(solution)/shard_map/ppermute | solution.py:676
  69.3 3.4 %low_early.1 = (bf16[1,192,640]{2,1,0:T(8,128)(2,1)S(1)}, bf16[1,6,160,768]{3,2,1,0:T(8,128)(2,1)S(1)}, bf16[1,4,160,384]{3,2,1,0:T(8,128)(2,1)S(1)}) custom-call(bf16[2,4,160,384]{3,2,1,0:T(8,128)(2,1)S(1)} %bitcast.19, bf16[2,2,192,1536]{3,2,1,0:T(8,128)(2,1)S(1)} %joined_up.1.up, f32[192]{0:T(256)S(1)} %copy-done.10, ...), custom_call_target="tpu_custom_call" | custom-call | flops 1132462080 | bytes 2654208 | tf_op jit(solution)/shard_map/low_early/pallas_call | solution.py:497
  72.7 1.3 %collective-permute-start.8 = (bf16[1,192,640]{2,1,0:T(8,128)(2,1)S(1)}, bf16[1,192,640]{2,1,0:T(8,128)(2,1)S(1)}, u32[]{:S(2)}, u32[]{:S(2)}) collective-permute-start(bf16[1,192,640]{2,1,0:T(8,128)(2,1)S(1)} %get-tuple-element.71), channel_id=1, source_target_pairs={{0,2},{1,3},{4,6},{5,7},{8,10},{9,11},{12,14},{13,15},{16,18},{17,... | collective-permute-start | bytes 737288 | tf_op jit(solution)/shard_map/ppermute | solution.py:676
  74.0 3.9 %collective-permute-done.7.arrived = bf16[192,640]{1,0:T(8,128)(2,1)S(1)} collective-permute-done((bf16[192,640]{1,0:T(8,128)(2,1)S(1)}, bf16[192,640]{1,0:T(8,128)(2,1)S(1)}, u32[]{:S(2)}, u32[]{:S(2)}) %collective-permute-start.7) | collective-permute-done | bytes 245792 | tf_op jit(solution)/shard_map/ppermute | solution.py:676
  78.0 3.1 %low_own.1 = (f32[2,192,640]{2,1,0:T(8,128)S(1)}, bf16[4,512,320]{2,1,0:T(8,128)(2,1)S(1)}) custom-call(bf16[1,6,160,768]{3,2,1,0:T(8,128)(2,1)S(1)} %get-tuple-element.64.early, bf16[1,6,160,768]{3,2,1,0:T(8,128)(2,1)S(1)} %get-tuple-element.65.last, bf16[1,4,160,384]{3,2,1,0:T(8,128)(2,1)S(1)} %get-tuple-element.66.early_kept, ...), custom_call_target="tpu_custom_call" | custom-call | flops 2548039680 | bytes 2654208 | tf_op jit(solution)/shard_map/low_own/pallas_call | solution.py:551
  81.1 1.9 %collective-permute-done.8.arrived = bf16[1,192,640]{2,1,0:T(8,128)(2,1)S(1)} collective-permute-done((bf16[1,192,640]{2,1,0:T(8,128)(2,1)S(1)}, bf16[1,192,640]{2,1,0:T(8,128)(2,1)S(1)}, u32[]{:S(2)}, u32[]{:S(2)}) %collective-permute-start.8) | collective-permute-done | bytes 245792 | tf_op jit(solution)/shard_map/ppermute | solution.py:676
  83.0 1.4 %finish.1 = bf16[2,4,96,320]{3,2,1,0:T(8,128)(2,1)} custom-call(f32[2,192,640]{2,1,0:T(8,128)S(1)} %get-tuple-element.70.own, bf16[1,192,640]{2,1,0:T(8,128)(2,1)S(1)} %collective-permute-done.8.arrived, bf16[4,512,320]{2,1,0:T(8,128)(2,1)S(1)} %get-tuple-element.72.weave), custom_call_target="tpu_custom_call" | custom-call | flops 251658240 | bytes 983040 | tf_op jit(solution)/shard_map/finish/pallas_call | solution.py:632
  (35 shorter events, 0.7 us)
Async XLA Ops:
  0.0 5.9 %copy-start.8 = (bf16[2,2,160,384]{3,2,1,0:T(8,128)(2,1)S(1)}, bf16[2,2,160,384]{3,2,1,0:T(8,128)(2,1)}, u32[]{:S(2)}) copy-start(bf16[2,2,160,384]{3,2,1,0:T(8,128)(2,1)} %latent.3) | copy-start | bytes 1474564
  0.0 5.9 %copy-start.12 = (f32[384]{0:T(512)S(1)}, f32[384]{0:T(512)}, u32[]{:S(2)}) copy-start(f32[384]{0:T(512)} %gain.8) | copy-start | bytes 4612
  2.4 9.6 %collective-permute-start = (bf16[2,160,384]{2,1,0:T(8,128)(2,1)}, bf16[2,160,384]{2,1,0:T(8,128)(2,1)S(1)}, u32[]{:S(2)}, u32[]{:S(2)}) collective-permute-start(bf16[2,160,384]{2,1,0:T(8,128)(2,1)} %get-tuple-element.41), channel_id=1, source_target_pairs={{0,4},{5,1},{2,6},{7,3},{4,8},{9,5},{6,10},{11,7},{8,12},{13,9},{1... | collective-permute-start | bytes 737288 | tf_op jit(solution)/shard_map/ppermute | solution.py:671
  6.0 2.1 %copy-start.1 = (bf16[3,3,3,384,192]{3,4,2,1,0:T(8,128)(2,1)S(1)}, bf16[3,3,3,384,192]{3,4,2,1,0:T(8,128)(2,1)}, u32[]{:S(2)}) copy-start(bf16[3,3,3,384,192]{3,4,2,1,0:T(8,128)(2,1)} %param.17) | copy-start | bytes 11943940
  8.1 3.3 %copy-start.13 = (bf16[4,160,384]{2,1,0:T(8,128)(2,1)S(1)}, bf16[4,160,384]{2,1,0:T(8,128)(2,1)}, u32[]{:S(2)}) copy-start(bf16[4,160,384]{2,1,0:T(8,128)(2,1)} %get-tuple-element.43) | copy-start | bytes 1474564
  11.4 7.2 %collective-permute-start.1 = (bf16[4,160,384]{2,1,0:T(8,128)(2,1)S(1)}, bf16[4,160,384]{2,1,0:T(8,128)(2,1)S(1)}, u32[]{:S(2)}, u32[]{:S(2)}) collective-permute-start(bf16[4,160,384]{2,1,0:T(8,128)(2,1)S(1)} %copy-done.13), channel_id=1, source_target_pairs={{0,4},{5,1},{4,8},{9,5},{8,12},{13,9},{16,20},{21,17},{20,24},{25,... | collective-permute-start | bytes 1474568 | tf_op jit(solution)/shard_map/ppermute | solution.py:671
  14.3 2.1 %copy-start.2 = (bf16[3,3,3,384,192]{3,4,2,1,0:T(8,128)(2,1)S(1)}, bf16[3,3,3,384,192]{3,4,2,1,0:T(8,128)(2,1)}, u32[]{:S(2)}) copy-start(bf16[3,3,3,384,192]{3,4,2,1,0:T(8,128)(2,1)} %param.17) | copy-start | bytes 11943940
  16.4 6.1 %copy-start.7 = (bf16[3,3,384,96]{2,3,1,0:T(8,128)(2,1)S(1)}, bf16[3,3,384,96]{2,3,1,0:T(8,128)(2,1)}, u32[]{:S(2)}) copy-start(bf16[3,3,384,96]{2,3,1,0:T(8,128)(2,1)} %param.20) | copy-start | bytes 1990660
  16.4 7.5 %copy-start.3 = (bf16[3,3,3,384,192]{3,4,2,1,0:T(8,128)(2,1)S(1)}, bf16[3,3,3,384,192]{3,4,2,1,0:T(8,128)(2,1)}, u32[]{:S(2)}) copy-start(bf16[3,3,3,384,192]{3,4,2,1,0:T(8,128)(2,1)} %param.17) | copy-start | bytes 11943940
  18.5 4.0 %copy-start.6 = (bf16[3,3,3,192,96]{4,3,2,1,0:T(8,128)(2,1)S(1)}, bf16[3,3,3,192,96]{4,3,2,1,0:T(8,128)(2,1)}, u32[]{:S(2)}) copy-start(bf16[3,3,3,192,96]{4,3,2,1,0:T(8,128)(2,1)} %low) | copy-start | bytes 2985988
  18.6 5.4 %copy-start.5 = (bf16[2,2,160,384]{3,2,1,0:T(8,128)(2,1)S(1)}, bf16[2,2,160,384]{3,2,1,0:T(8,128)(2,1)}, u32[]{:S(2)}) copy-start(bf16[2,2,160,384]{3,2,1,0:T(8,128)(2,1)} %cache.3) | copy-start | bytes 1474564
  18.6 11.0 %collective-permute-start.2 = (bf16[320,384]{1,0:T(8,128)(2,1)S(1)}, bf16[320,384]{1,0:T(8,128)(2,1)S(1)}, u32[]{:S(2)}, u32[]{:S(2)}) collective-permute-start(bf16[320,384]{1,0:T(8,128)(2,1)S(1)} %get-tuple-element.44), channel_id=1, source_target_pairs={{0,2},{1,3},{4,6},{5,7},{8,10},{9,11},{12,14},{13,15},{16,18},{17,... | collective-permute-start | bytes 737288 | tf_op jit(solution)/shard_map/ppermute | solution.py:676
  29.6 5.2 %copy-start = (bf16[2,4,320,192]{2,3,1,0:T(8,128)(2,1)S(1)}, bf16[2,4,320,192]{2,3,1,0:T(8,128)(2,1)}, u32[]{:S(2)}) copy-start(bf16[2,4,320,192]{2,3,1,0:T(8,128)(2,1)} %param.13) | copy-start | bytes 2949124
  32.3 2.8 %copy-start.4 = (bf16[384,1152]{1,0:T(8,128)(2,1)S(1)}, bf16[384,1152]{1,0:T(8,128)(2,1)}, u32[]{:S(2)}) copy-start(bf16[384,1152]{1,0:T(8,128)(2,1)} %qkv.5) | copy-start | bytes 2654212
  32.3 2.8 %copy-start.9 = (f32[384]{0:T(512)S(1)}, f32[384]{0:T(512)}, u32[]{:S(2)}) copy-start(f32[384]{0:T(512)} %gain.11) | copy-start | bytes 4612
  32.3 17.9 %collective-permute-start.5 = (bf16[2,2,96,1536]{3,2,1,0:T(8,128)(2,1)S(1)}, bf16[2,2,96,1536]{3,2,1,0:T(8,128)(2,1)S(1)}, u32[]{:S(2)}, u32[]{:S(2)}) collective-permute-start(bf16[2,2,96,1536]{3,2,1,0:T(8,128)(2,1)S(1)} %get-tuple-element.55.mine), channel_id=1, source_target_pairs={{0,1},{1,0},{2,3},{3,2},{4,5},{5,4},{6,7},{7,6},{8,9},{9,8},{10,11... | collective-permute-start | bytes 3538952 | tf_op jit(solution)/shard_map/ppermute | solution.py:729
  32.5 17.1 %collective-permute-start.6 = (bf16[320,384]{1,0:T(8,128)(2,1)S(1)}, bf16[320,384]{1,0:T(8,128)(2,1)S(1)}, u32[]{:S(2)}, u32[]{:S(2)}) collective-permute-start(bf16[320,384]{1,0:T(8,128)(2,1)S(1)} %maximum_select_fusion.refs_0_.own), channel_id=1, source_target_pairs={{0,8},{4,12},{8,0},{12,4},{1,9},{5,13},{9,1},{13,5},{2,10},{6,14},... | collective-permute-start | bytes 737288 | tf_op jit(solution)/shard_map/ppermute | solution.py:726
  32.8 23.7 %collective-permute-start.4 = (bf16[320,384]{1,0:T(8,128)(2,1)S(1)}, bf16[320,384]{1,0:T(8,128)(2,1)S(1)}, u32[]{:S(2)}, u32[]{:S(2)}) collective-permute-start(bf16[320,384]{1,0:T(8,128)(2,1)S(1)} %maximum_select_fusion.refs_0_.own), channel_id=1, source_target_pairs={{0,12},{4,0},{8,4},{12,8},{1,13},{5,1},{9,5},{13,9},{2,14},{6,2},{... | collective-permute-start | bytes 737288 | tf_op jit(solution)/shard_map/ppermute | solution.py:726
  34.6 21.9 %collective-permute-start.3 = (bf16[320,384]{1,0:T(8,128)(2,1)S(1)}, bf16[320,384]{1,0:T(8,128)(2,1)S(1)}, u32[]{:S(2)}, u32[]{:S(2)}) collective-permute-start(bf16[320,384]{1,0:T(8,128)(2,1)S(1)} %maximum_select_fusion.refs_0_.own), channel_id=1, source_target_pairs={{0,4},{4,8},{8,12},{12,0},{1,5},{5,9},{9,13},{13,1},{2,6},{6,10},{... | collective-permute-start | bytes 737288 | tf_op jit(solution)/shard_map/ppermute | solution.py:726
  50.2 6.3 %copy-start.11 = (bf16[384,384]{1,0:T(8,128)(2,1)S(1)}, bf16[384,384]{1,0:T(8,128)(2,1)}, u32[]{:S(2)}) copy-start(bf16[384,384]{1,0:T(8,128)(2,1)} %proj.1) | copy-start | bytes 884740
  60.8 2.5 %copy-start.10 = (f32[192]{0:T(256)S(1)}, f32[192]{0:T(256)}, u32[]{:S(2)}) copy-start(f32[192]{0:T(256)} %gain.13) | copy-start | bytes 2308
  67.8 10.1 %collective-permute-start.7 = (bf16[192,640]{1,0:T(8,128)(2,1)S(1)}, bf16[192,640]{1,0:T(8,128)(2,1)S(1)}, u32[]{:S(2)}, u32[]{:S(2)}) collective-permute-start(bf16[192,640]{1,0:T(8,128)(2,1)S(1)} %get-tuple-element.69), channel_id=1, source_target_pairs={{0,2},{1,3},{4,6},{5,7},{8,10},{9,11},{12,14},{13,15},{16,18},{17,... | collective-permute-start | bytes 737288 | tf_op jit(solution)/shard_map/ppermute | solution.py:676
  72.7 10.2 %collective-permute-start.8 = (bf16[1,192,640]{2,1,0:T(8,128)(2,1)S(1)}, bf16[1,192,640]{2,1,0:T(8,128)(2,1)S(1)}, u32[]{:S(2)}, u32[]{:S(2)}) collective-permute-start(bf16[1,192,640]{2,1,0:T(8,128)(2,1)S(1)} %get-tuple-element.71), channel_id=1, source_target_pairs={{0,2},{1,3},{4,6},{5,7},{8,10},{9,11},{12,14},{13,15},{16,18},{17,... | collective-permute-start | bytes 737288 | tf_op jit(solution)/shard_map/ppermute | solution.py:676

commit v9 on v8

--- a/solution.py
+++ b/solution.py
@@ -10,6 +10,7 @@
 
 BF16, F32 = jnp.bfloat16, jnp.float32
 MIB = 1024 * 1024
+NEAR_FLOPS = 100000
 NT = (((1,), (1,)), ((), ()))
 EPS = 1e-06
 
@@ -305,7 +306,7 @@
         values[...] = both[:, channels:]
 
 
-def block_keys(gain, qkv, blocks):
+def block_keys(gain, qkv, blocks, flops):
     count, size = len(blocks), blocks[0].size
     outs = pl.pallas_call(
         block_kernel,
@@ -313,13 +314,13 @@
         out_specs=[vmem()] * (2 * count),
         out_shape=[jax.ShapeDtypeStruct(blocks[0].shape, BF16)] * (2 * count),
         compiler_params=pltpu.CompilerParams(vmem_limit_bytes=room(16 * blocks[0].nbytes)),
-        cost_estimate=cost(size, blocks[0].nbytes // 4),
+        cost_estimate=cost(flops, blocks[0].nbytes // 4),
         name="block_keys",
     )(gain, qkv, *blocks)
     return list(outs[:count]), list(outs[count:])
 
 
-def attn_kernel(count, width, gain, qkv, proj, own, before, after, *refs):
+def attn_kernel(count, width, gain, qkv, proj, own, before, after, far_low, far_high, *refs):
     given, (out, keys, values) = refs[:-3], refs[-3:]
     channels = qkv.shape[0]
     size = own.shape[0]
@@ -330,12 +331,15 @@
     for i in range(count):
         keys[i * size : (i + 1) * size] = given[i][...]
         values[i * size : (i + 1) * size] = given[count + i][...]
-    for i, block in enumerate((before, after)):
-        scaled = normed(block[...].astype(F32), gain[...]).astype(BF16)
-        both = jnp.dot(scaled, qkv[:, channels:], preferred_element_type=F32).astype(BF16)
-        at = slice((count + i) * size, (count + i + 1) * size)
-        keys[at] = both[:, :channels]
-        values[at] = both[:, channels:]
+    for i, (block, missing) in enumerate(((far_low, row == 0), (far_high, row == depth - 1))):
+        @pl.when(missing)
+        def _(i=i, block=block):
+            scaled = normed(block[...].astype(F32), gain[...]).astype(BF16)
+            both = jnp.dot(scaled, qkv[:, channels:], preferred_element_type=F32).astype(BF16)
+            at = slice((count - 2 + i) * size, (count - 1 + i) * size)
+            keys[at] = both[:, :channels]
+            values[at] = both[:, channels:]
+
     lines = [before[size - width :]] + [own[i * width : (i + 1) * width] for i in range(rows - 2)] + [after[:width]]
     inside = [row > 0] + [None] * (rows - 2) + [row < depth - 1]
     for block in range(rows // step):
@@ -353,22 +357,22 @@
             out[block * step + i] = (line if valid is None else jnp.where(valid, line, 0.0)).astype(BF16)
 
 
-def attention(own, before, after, keys, values, gain, qkv, proj, width):
+def attention(own, ends, keys, values, gain, qkv, proj, width):
     size, channels = own.shape
     count = len(keys)
-    pixels = (count + 2) * size
+    pixels = count * size
     rows = size // width + 2
     need = 2 * width * pixels * 16 + 16 * own.nbytes
     return pl.pallas_call(
         functools.partial(attn_kernel, count, width),
-        in_specs=[vmem()] * (6 + 2 * count),
+        in_specs=[vmem()] * (8 + 2 * count),
         out_specs=vmem(),
         out_shape=jax.ShapeDtypeStruct((rows, width, channels), BF16),
         scratch_shapes=[pltpu.VMEM((pixels, channels), BF16), pltpu.VMEM((pixels, channels), BF16)],
         compiler_params=pltpu.CompilerParams(vmem_limit_bytes=room(need)),
         cost_estimate=cost(4 * channels * rows * width * (pixels + channels), qkv.nbytes),
         name="frame_attention",
-    )(gain, qkv, proj, own, before, after, *keys, *values)
+    )(gain, qkv, proj, own, *ends, *keys, *values)
 
 
 def windowed(left, right):
@@ -671,6 +675,23 @@
     return lax.ppermute(values, ("rows", "segment", "chan"), route)
 
 
+def line_blocks(mine):
+    depth = lax.axis_size("rows")
+    upper, lower = {0: mine}, {0: mine}
+    for d in (2, 1, *range(3, depth)):
+        start = 0 if d < 3 else d - 1 if d % 2 else d - 2
+        hop = d - start
+        rising = [(i - hop, i) for i in range(d, depth)]
+        falling = [(i + hop, i) for i in range(depth - d)]
+        apart = not {a for a, _ in rising} & {a for a, _ in falling} and not {b for _, b in rising} & {b for _, b in falling}
+        if apart and upper[start] is lower[start]:
+            upper[d] = lower[d] = lax.ppermute(upper[start], "rows", rising + falling)
+        else:
+            upper[d] = lax.ppermute(upper[start], "rows", rising)
+            lower[d] = lax.ppermute(lower[start], "rows", falling)
+    return upper, lower
+
+
 def to_next(values):
     count = lax.axis_size("segment")
     return lax.ppermute(values, "segment", [(i, i + 1) for i in range(count - 1)])
@@ -700,9 +721,8 @@
 
     rim, cache_rim = edge_rows(latent, cache_mid, low_cache)
     rim = to_neighbour(rim, False)
+    cache_rim = to_neighbour(cache_rim, True)
     started = mid_inner(latent, gain_mid, mid_weights)
-    cache_rim, started = lax.optimization_barrier((cache_rim, started))
-    cache_rim = to_neighbour(cache_rim, True)
     halo = lax.all_gather(rim, "chan")
     own, passed = mid_rim(started, halo, gain_mid, mid_weights)
     passed, cache_rim, conv_up, conv_low = lax.optimization_barrier((passed, cache_rim, conv_up, conv_low))
@@ -723,16 +743,26 @@
         mine = jnp.where(chan == f, choices[f], mine)
 
     depth = lax.axis_size("rows")
-    turns = [lax.ppermute(mine, "rows", [(i, (i + k) % depth) for i in range(depth)]) for k in range(1, depth)]
-    own_keys, own_values = block_keys(gain_attn, attn_qkv, [mine])
+    row = lax.axis_index("rows")
+    upper, lower = line_blocks(mine)
+    inner = []
+    for d in range(2, depth - 1):
+        same = upper[d] is lower[depth - d]
+        inner.append(upper[d] if same else jnp.where(row >= d, upper[d], lower[depth - d]))
+    own_keys, own_values = block_keys(gain_attn, attn_qkv, [mine], 1)
     up_mine, _ = lax.optimization_barrier((up_mine, mine))
     up_other = lax.ppermute(up_mine, "chan", [(0, 1), (1, 0)])
     cached = low_cached(low_cache, cache_halo, low_weights)
-    keys, values = block_keys(gain_attn, attn_qkv, turns[1:-1])
     up = joined_up(up_mine, up_other)
-    turns[-1], cached, low_weights, up = lax.optimization_barrier((turns[-1], cached, low_weights, up))
+    keys, values = block_keys(gain_attn, attn_qkv, inner, 1)
+    upper[1], cached, low_weights, up, keys[0], own_keys[0] = lax.optimization_barrier(
+        (upper[1], cached, low_weights, up, keys[0], own_keys[0])
+    )
+    near_keys, near_values = block_keys(gain_attn, attn_qkv, [upper[1], lower[1]], NEAR_FLOPS * mine.size)
+    ends = [upper[1], lower[1], lower[depth - 1], upper[depth - 1]]
     reached = attention(
-        mine, turns[0], turns[-1], own_keys + keys, own_values + values, gain_attn, attn_qkv, attn_proj, width
+        mine, ends, own_keys + keys + near_keys, own_values + values + near_values,
+        gain_attn, attn_qkv, attn_proj, width,
     )
     tile = lax.all_gather(reached, "chan")
 

time: 84.7 us -> 82.9 us (0.979)
  the two profiles are of different devices: /device:TPU:10 before, /device:TPU:0 now
where the time goes in v9:
time: 82.9 us; the launch traced here: 82.5 us
  Pallas kernels  33.9 us (41%)
  starting transfers between devices  22.2 us (27%)
  waiting for transfers between devices  14.1 us (17%)
  blocking collectives  9.47 us (11%)
  local copies, waits for them, and re-layouts  2.34 us (3%)
    ppermute x2, waiting for transfers between devices, line_blocks(): upper[d] = lower[d] = lax.ppermute(upper[start], 'rows', rising + falling)  10.6 us
    ppermute x2, starting transfers between devices, to_neighbour(): return lax.ppermute(values, ('rows', 'segment', 'chan'), route)  8.45 us
    ppermute x3, starting transfers between devices, to_next(): lax.ppermute(values, 'segment', [(i, i + 1) for i in range(count - 1)])  6.98 us
    pallas_call x1, Pallas kernels, low_last(): pl.pallas_call(functools.partial(low_last_kernel, frames, past), in_specs...  4.46 us
    pallas_call x1, Pallas kernels, attention(): pl.pallas_call(functools.partial(attn_kernel, count, width), in_specs=[vm...  4.4 us
    pallas_call x1, Pallas kernels, low_cached(): pl.pallas_call(low_cache_kernel, in_specs=[vmem()] * 3, out_specs=vmem(),...  3.74 us
    pallas_call x1, Pallas kernels, low_early(): pl.pallas_call(functools.partial(low_early_kernel, frames, past), in_spec...  3.41 us
    pallas_call x1, Pallas kernels, mid_inner(): pl.pallas_call(mid_inner_kernel, in_specs=[vmem()] * 3, out_specs=vmem(),...  3.27 us
  transfers between devices with their start and end apart: 10, of which 5 were waited for; matrix products, arithmetic and copies ran while one was open for 0% of the time, Pallas kernels for 26%

profile of v9, /device:TPU:0, one launch (start us, length us, event | category | flops | bytes accessed | tf_op | source)
XLA Modules:
  0.0 82.5 jit_solution(2762170972162369431)
XLA Ops:
  0.0 2.4 %edge_rows.1 = (bf16[2,160,384]{2,1,0:T(8,128)(2,1)}, bf16[4,160,384]{2,1,0:T(8,128)(2,1)}) custom-call(bf16[2,2,160,384]{3,2,1,0:T(8,128)(2,1)} %latent.3, bf16[2,2,160,384]{3,2,1,0:T(8,128)(2,1)} %cache.3, bf16[2,4,192,320]{3,2,1,0:T(8,128)(2,1)} %bitcast.20), custom_call_target="tpu_custom_call" | custom-call | bytes 1966080 | tf_op jit(solution)/shard_map/edge_rows/pallas_call | solution.py:99
  2.4 4.9 %collective-permute-start = (bf16[2,160,384]{2,1,0:T(8,128)(2,1)}, bf16[2,160,384]{2,1,0:T(8,128)(2,1)S(1)}, u32[]{:S(2)}, u32[]{:S(2)}) collective-permute-start(bf16[2,160,384]{2,1,0:T(8,128)(2,1)} %get-tuple-element.43), channel_id=1, source_target_pairs={{0,4},{5,1},{2,6},{7,3},{4,8},{9,5},{6,10},{11,7},{8,12},{13,9},{1... | collective-permute-start | bytes 737288 | tf_op jit(solution)/shard_map/ppermute | solution.py:675
  7.4 3.5 %collective-permute-start.1 = (bf16[4,160,384]{2,1,0:T(8,128)(2,1)}, bf16[4,160,384]{2,1,0:T(8,128)(2,1)S(1)}, u32[]{:S(2)}, u32[]{:S(2)}) collective-permute-start(bf16[4,160,384]{2,1,0:T(8,128)(2,1)} %get-tuple-element.45), channel_id=1, source_target_pairs={{0,4},{5,1},{4,8},{9,5},{8,12},{13,9},{16,20},{21,17},{20,24},{25,... | collective-permute-start | bytes 1474568 | tf_op jit(solution)/shard_map/ppermute | solution.py:675
  10.9 2.1 %copy-done.1 = bf16[3,3,3,384,192]{3,4,2,1,0:T(8,128)(2,1)S(1)} copy-done((bf16[3,3,3,384,192]{3,4,2,1,0:T(8,128)(2,1)S(1)}, bf16[3,3,3,384,192]{3,4,2,1,0:T(8,128)(2,1)}, u32[]{:S(2)}) %copy-start.1) | copy-done | bytes 3981336
  13.1 3.3 %mid_inner.1.started = f32[4,320,192]{2,1,0:T(8,128)S(1)} custom-call(bf16[2,2,160,384]{3,2,1,0:T(8,128)(2,1)S(1)} %copy-done.7, f32[384]{0:T(512)S(1)} %copy-done.11, bf16[3,3,3,192,384]{4,3,2,1,0:T(8,128)(2,1)S(1)} %bitcast.22), custom_call_target="tpu_custom_call" | custom-call | flops 2548039680 | bytes 3981312 | tf_op jit(solution)/shard_map/mid_inner/pallas_call | solution.py:204
  16.3 2.2 %all-gather = bf16[4,160,384]{2,1,0:T(8,128)(2,1)S(1)} all-gather(bf16[2,160,384]{2,1,0:T(8,128)(2,1)S(1)} %collective-permute-done), channel_id=2, replica_groups=mesh['groups'=2,'rows'=4,'segment'=2,'chan'=2] {'chan'}, dimensions={0}, use_global_device_ids=true | all-gather | bytes 737280 | tf_op jit(solution)/shard_map/all_gather | solution.py:726
  18.5 2.2 %mid_rim.1 = (f32[320,384]{1,0:T(8,128)S(1)}, bf16[320,384]{1,0:T(8,128)(2,1)S(1)}) custom-call(f32[4,320,192]{2,1,0:T(8,128)S(1)} %mid_inner.1.started, bf16[2,2,160,384]{3,2,1,0:T(8,128)(2,1)S(1)} %bitcast.26, f32[384]{0:T(512)S(1)} %copy-done.11, bf16[3,3,3,192,384]{4,3,2,1,0:T(8,128)(2,1)S(1)} %bitcast.23), custom_call_target="tpu_custom_call" | custom-call | flops 2548039680 | bytes 3981312 | tf_op jit(solution)/shard_map/mid_rim/pallas_call | solution.py:239
  20.7 1.4 %collective-permute-start.2 = (bf16[320,384]{1,0:T(8,128)(2,1)S(1)}, bf16[320,384]{1,0:T(8,128)(2,1)S(1)}, u32[]{:S(2)}, u32[]{:S(2)}) collective-permute-start(bf16[320,384]{1,0:T(8,128)(2,1)S(1)} %get-tuple-element.46), channel_id=1, source_target_pairs={{0,2},{1,3},{4,6},{5,7},{8,10},{9,11},{12,14},{13,15},{16,18},{17,... | collective-permute-start | bytes 737288 | tf_op jit(solution)/shard_map/ppermute | solution.py:697
  22.1 2.5 %all-gather.1 = bf16[8,160,384]{2,1,0:T(8,128)(2,1)S(1)} all-gather(bf16[4,160,384]{2,1,0:T(8,128)(2,1)S(1)} %collective-permute-done.1), channel_id=3, replica_groups=mesh['groups'=2,'rows'=4,'segment'=2,'chan'=2] {'chan'}, dimensions={0}, use_global_device_ids=true | all-gather | bytes 1474560 | tf_op jit(solution)/shard_map/all_gather | solution.py:730
  24.7 1.4 %weight_forms.1 = (bf16[2,2,96,1536]{3,2,1,0:T(8,128)(2,1)S(1)}, bf16[576,2304]{1,0:T(8,128)(2,1)S(1)}) custom-call(bf16[3,3,96,384]{3,2,1,0:T(8,128)(2,1)S(1)} %bitcast.25, bf16[3,3,3,192,96]{4,3,2,1,0:T(8,128)(2,1)S(1)} %copy-done.5), custom_call_target="tpu_custom_call" | custom-call | flops 95551488 | bytes 6635520 | tf_op jit(solution)/shard_map/weight_forms/pallas_call | solution.py:139
  26.1 2.2 %mid_cached.1.own = f32[320,384]{1,0:T(8,128)S(1)} custom-call(f32[320,384]{1,0:T(8,128)S(1)} %get-tuple-element.47.own, bf16[2,2,160,384]{3,2,1,0:T(8,128)(2,1)S(1)} %copy-done.4, bf16[2,4,160,384]{3,2,1,0:T(8,128)(2,1)S(1)} %bitcast.16, bf16[3,3,3,192,384]{4,3,2,1,0:T(8,128)(2,1)S(1)} %bitcast.24), custom_call_target="tpu_custom_call" | custom-call | flops 1274019840 | bytes 3981312 | tf_op jit(solution)/shard_map/mid_cached/pallas_call | solution.py:287
  28.4 2.3 %all-gather.2 = bf16[640,384]{1,0:T(8,128)(2,1)S(1)} all-gather(bf16[320,384]{1,0:T(8,128)(2,1)S(1)} %join.1), channel_id=4, replica_groups=mesh['groups'=2,'rows'=4,'segment'=2,'chan'=2] {'chan'}, dimensions={0}, use_global_device_ids=true | all-gather | bytes 737280 | tf_op jit(solution)/shard_map/all_gather | solution.py:735
  31.2 1.9 %collective-permute-start.5 = (bf16[320,384]{1,0:T(8,128)(2,1)S(1)}, bf16[320,384]{1,0:T(8,128)(2,1)S(1)}, u32[]{:S(2)}, u32[]{:S(2)}) collective-permute-start(bf16[320,384]{1,0:T(8,128)(2,1)S(1)} %maximum_select_fusion.refs_0_.own), channel_id=1, source_target_pairs={{0,8},{4,12},{8,0},{12,4},{1,9},{5,13},{9,1},{13,5},{2,10},{6,14},... | collective-permute-start | bytes 737288 | tf_op jit(solution)/shard_map/ppermute | solution.py:688
  33.1 2.1 %collective-permute-start.3 = (bf16[320,384]{1,0:T(8,128)(2,1)S(1)}, bf16[320,384]{1,0:T(8,128)(2,1)S(1)}, u32[]{:S(2)}, u32[]{:S(2)}) collective-permute-start(bf16[320,384]{1,0:T(8,128)(2,1)S(1)} %maximum_select_fusion.refs_0_.own), channel_id=1, source_target_pairs={{0,4},{4,8},{8,12},{1,5},{5,9},{9,13},{2,6},{6,10},{10,14},{3,7},{... | collective-permute-start | bytes 737288 | tf_op jit(solution)/shard_map/ppermute | solution.py:690
  35.3 1.3 %collective-permute-start.6 = (bf16[320,384]{1,0:T(8,128)(2,1)S(1)}, bf16[320,384]{1,0:T(8,128)(2,1)S(1)}, u32[]{:S(2)}, u32[]{:S(2)}) collective-permute-start(bf16[320,384]{1,0:T(8,128)(2,1)S(1)} %maximum_select_fusion.refs_0_.own), channel_id=1, source_target_pairs={{4,0},{8,4},{12,8},{5,1},{9,5},{13,9},{6,2},{10,6},{14,10},{7,3},{... | collective-permute-start | bytes 737288 | tf_op jit(solution)/shard_map/ppermute | solution.py:691
  36.6 0.5 block_keys.4
  37.1 3.7 %low_cached.1.cached = f32[2,192,640]{2,1,0:T(8,128)S(1)} custom-call(bf16[2,4,192,320]{3,2,1,0:T(8,128)(2,1)S(1)} %bitcast.21, bf16[2,4,160,384]{3,2,1,0:T(8,128)(2,1)S(1)} %bitcast.17, bf16[576,2304]{1,0:T(8,128)(2,1)S(1)} %get-tuple-element.70.weights), custom_call_target="tpu_custom_call" | custom-call | flops 122880 | bytes 331776 | tf_op jit(solution)/shard_map/low_cached/pallas_call | solution.py:595
  40.8 5.4 %collective-permute-done.5.refs_0_ = bf16[320,384]{1,0:T(8,128)(2,1)S(1)} collective-permute-done((bf16[320,384]{1,0:T(8,128)(2,1)S(1)}, bf16[320,384]{1,0:T(8,128)(2,1)S(1)}, u32[]{:S(2)}, u32[]{:S(2)}) %collective-permute-start.5) | collective-permute-done | bytes 245792 | tf_op jit(solution)/shard_map/ppermute | solution.py:688
  46.2 1.3 %collective-permute-start.7 = (bf16[320,384]{1,0:T(8,128)(2,1)S(1)}, bf16[320,384]{1,0:T(8,128)(2,1)S(1)}, u32[]{:S(2)}, u32[]{:S(2)}) collective-permute-start(bf16[320,384]{1,0:T(8,128)(2,1)S(1)} %collective-permute-done.5.refs_0_), channel_id=1, source_target_pairs={{8,12},{4,0},{9,13},{5,1},{10,14},{6,2},{11,15},{7,3},{24,28},{20,... | collective-permute-start | bytes 737288 | tf_op jit(solution)/shard_map/ppermute | solution.py:688
  48.2 0.8 collective-permute-done.6.refs_1_.after
  49.0 0.8 block_keys.5
  49.7 5.2 %collective-permute-done.7.far_low.far_high = bf16[320,384]{1,0:T(8,128)(2,1)S(1)} collective-permute-done((bf16[320,384]{1,0:T(8,128)(2,1)S(1)}, bf16[320,384]{1,0:T(8,128)(2,1)S(1)}, u32[]{:S(2)}, u32[]{:S(2)}) %collective-permute-start.7) | collective-permute-done | bytes 245792 | tf_op jit(solution)/shard_map/ppermute | solution.py:688
  55.0 4.4 %frame_attention.1 = bf16[4,160,384]{2,1,0:T(8,128)(2,1)S(1)} custom-call(f32[384]{0:T(512)S(1)} %copy-done.8, bf16[384,1152]{1,0:T(8,128)(2,1)S(1)} %copy-done.3, bf16[384,384]{1,0:T(8,128)(2,1)S(1)} %copy-done.10, bf16[320,384]{1,0:T(8,128)(2,1)S(1)} %maximum_select_fusion.refs_0_.own, bf16[320,384]{1,0:T(8,128)(2,1)S(1)} %collective-permute-done.3.refs_0_.before, ...), custom_call_target="tpu_custom_call" | custom-call | flops 1635778560 | bytes 884736 | tf_op jit(solution)/shard_map/frame_attention/pallas_call | solution.py:366
  59.4 2.5 %all-gather.3 = bf16[8,160,384]{2,1,0:T(8,128)(2,1)S(1)} all-gather(bf16[4,160,384]{2,1,0:T(8,128)(2,1)S(1)} %frame_attention.1), channel_id=5, replica_groups=mesh['groups'=2,'rows'=4,'segment'=2,'chan'=2] {'chan'}, dimensions={0}, use_global_device_ids=true | all-gather | bytes 1474560 | tf_op jit(solution)/shard_map/all_gather | solution.py:767
  61.9 4.5 %low_last.1 = (bf16[192,640]{1,0:T(8,128)(2,1)S(1)}, f32[1,192,640]{2,1,0:T(8,128)S(1)}, bf16[1,6,160,768]{3,2,1,0:T(8,128)(2,1)S(1)}, bf16[1,4,160,384]{3,2,1,0:T(8,128)(2,1)S(1)}) custom-call(bf16[2,4,160,384]{3,2,1,0:T(8,128)(2,1)S(1)} %bitcast.18, bf16[2,2,192,1536]{3,2,1,0:T(8,128)(2,1)S(1)} %joined_up.1.up, f32[192]{0:T(256)S(1)} %copy-done.9, ...), custom_call_target="tpu_custom_call" | custom-call | flops 1132462080 | bytes 2654208 | tf_op jit(solution)/shard_map/low_last/pallas_call | solution.py:480
  66.4 4.2 %collective-permute-start.8 = (bf16[192,640]{1,0:T(8,128)(2,1)S(1)}, bf16[192,640]{1,0:T(8,128)(2,1)S(1)}, u32[]{:S(2)}, u32[]{:S(2)}) collective-permute-start(bf16[192,640]{1,0:T(8,128)(2,1)S(1)} %get-tuple-element.77), channel_id=1, source_target_pairs={{0,2},{1,3},{4,6},{5,7},{8,10},{9,11},{12,14},{13,15},{16,18},{17,... | collective-permute-start | bytes 737288 | tf_op jit(solution)/shard_map/ppermute | solution.py:697
  70.6 3.4 %low_early.1 = (bf16[1,192,640]{2,1,0:T(8,128)(2,1)S(1)}, bf16[1,6,160,768]{3,2,1,0:T(8,128)(2,1)S(1)}, bf16[1,4,160,384]{3,2,1,0:T(8,128)(2,1)S(1)}) custom-call(bf16[2,4,160,384]{3,2,1,0:T(8,128)(2,1)S(1)} %bitcast.19, bf16[2,2,192,1536]{3,2,1,0:T(8,128)(2,1)S(1)} %joined_up.1.up, f32[192]{0:T(256)S(1)} %copy-done.9, ...), custom_call_target="tpu_custom_call" | custom-call | flops 1132462080 | bytes 2654208 | tf_op jit(solution)/shard_map/low_early/pallas_call | solution.py:501
  74.0 1.3 %collective-permute-start.9 = (bf16[1,192,640]{2,1,0:T(8,128)(2,1)S(1)}, bf16[1,192,640]{2,1,0:T(8,128)(2,1)S(1)}, u32[]{:S(2)}, u32[]{:S(2)}) collective-permute-start(bf16[1,192,640]{2,1,0:T(8,128)(2,1)S(1)} %get-tuple-element.79), channel_id=1, source_target_pairs={{0,2},{1,3},{4,6},{5,7},{8,10},{9,11},{12,14},{13,15},{16,18},{17,... | collective-permute-start | bytes 737288 | tf_op jit(solution)/shard_map/ppermute | solution.py:697
  75.3 0.8 collective-permute-done.8.arrived
  76.1 3.1 %low_own.1 = (f32[2,192,640]{2,1,0:T(8,128)S(1)}, bf16[4,512,320]{2,1,0:T(8,128)(2,1)S(1)}) custom-call(bf16[1,6,160,768]{3,2,1,0:T(8,128)(2,1)S(1)} %get-tuple-element.72.early, bf16[1,6,160,768]{3,2,1,0:T(8,128)(2,1)S(1)} %get-tuple-element.73.last, bf16[1,4,160,384]{3,2,1,0:T(8,128)(2,1)S(1)} %get-tuple-element.74.early_kept, ...), custom_call_target="tpu_custom_call" | custom-call | flops 2548039680 | bytes 2654208 | tf_op jit(solution)/shard_map/low_own/pallas_call | solution.py:555
  79.2 1.9 %collective-permute-done.9.arrived = bf16[1,192,640]{2,1,0:T(8,128)(2,1)S(1)} collective-permute-done((bf16[1,192,640]{2,1,0:T(8,128)(2,1)S(1)}, bf16[1,192,640]{2,1,0:T(8,128)(2,1)S(1)}, u32[]{:S(2)}, u32[]{:S(2)}) %collective-permute-start.9) | collective-permute-done | bytes 245792 | tf_op jit(solution)/shard_map/ppermute | solution.py:697
  81.1 1.4 %finish.1 = bf16[2,4,96,320]{3,2,1,0:T(8,128)(2,1)} custom-call(f32[2,192,640]{2,1,0:T(8,128)S(1)} %get-tuple-element.78.own, bf16[1,192,640]{2,1,0:T(8,128)(2,1)S(1)} %collective-permute-done.9.arrived, bf16[4,512,320]{2,1,0:T(8,128)(2,1)S(1)} %get-tuple-element.80.weave), custom_call_target="tpu_custom_call" | custom-call | flops 251658240 | bytes 983040 | tf_op jit(solution)/shard_map/finish/pallas_call | solution.py:636
  (34 shorter events, 1.3 us)
Async XLA Ops:
  0.0 10.9 %copy-start.7 = (bf16[2,2,160,384]{3,2,1,0:T(8,128)(2,1)S(1)}, bf16[2,2,160,384]{3,2,1,0:T(8,128)(2,1)}, u32[]{:S(2)}) copy-start(bf16[2,2,160,384]{3,2,1,0:T(8,128)(2,1)} %latent.3) | copy-start | bytes 1474564
  0.0 10.9 %copy-start.11 = (f32[384]{0:T(512)S(1)}, f32[384]{0:T(512)}, u32[]{:S(2)}) copy-start(f32[384]{0:T(512)} %gain.9) | copy-start | bytes 4612
  2.4 13.9 %collective-permute-start = (bf16[2,160,384]{2,1,0:T(8,128)(2,1)}, bf16[2,160,384]{2,1,0:T(8,128)(2,1)S(1)}, u32[]{:S(2)}, u32[]{:S(2)}) collective-permute-start(bf16[2,160,384]{2,1,0:T(8,128)(2,1)} %get-tuple-element.43), channel_id=1, source_target_pairs={{0,4},{5,1},{2,6},{7,3},{4,8},{9,5},{6,10},{11,7},{8,12},{13,9},{1... | collective-permute-start | bytes 737288 | tf_op jit(solution)/shard_map/ppermute | solution.py:675
  7.4 13.3 %collective-permute-start.1 = (bf16[4,160,384]{2,1,0:T(8,128)(2,1)}, bf16[4,160,384]{2,1,0:T(8,128)(2,1)S(1)}, u32[]{:S(2)}, u32[]{:S(2)}) collective-permute-start(bf16[4,160,384]{2,1,0:T(8,128)(2,1)} %get-tuple-element.45), channel_id=1, source_target_pairs={{0,4},{5,1},{4,8},{9,5},{8,12},{13,9},{16,20},{21,17},{20,24},{25,... | collective-permute-start | bytes 1474568 | tf_op jit(solution)/shard_map/ppermute | solution.py:675
  10.9 2.1 %copy-start.1 = (bf16[3,3,3,384,192]{3,4,2,1,0:T(8,128)(2,1)S(1)}, bf16[3,3,3,384,192]{3,4,2,1,0:T(8,128)(2,1)}, u32[]{:S(2)}) copy-start(bf16[3,3,3,384,192]{3,4,2,1,0:T(8,128)(2,1)} %param.17) | copy-start | bytes 11943940
  18.5 6.2 %copy-start.6 = (bf16[3,3,384,96]{2,3,1,0:T(8,128)(2,1)S(1)}, bf16[3,3,384,96]{2,3,1,0:T(8,128)(2,1)}, u32[]{:S(2)}) copy-start(bf16[3,3,384,96]{2,3,1,0:T(8,128)(2,1)} %param.20) | copy-start | bytes 1990660
  18.5 7.6 %copy-start.2 = (bf16[3,3,3,384,192]{3,4,2,1,0:T(8,128)(2,1)S(1)}, bf16[3,3,3,384,192]{3,4,2,1,0:T(8,128)(2,1)}, u32[]{:S(2)}) copy-start(bf16[3,3,3,384,192]{3,4,2,1,0:T(8,128)(2,1)} %param.17) | copy-start | bytes 11943940
  20.7 4.0 %copy-start.5 = (bf16[3,3,3,192,96]{4,3,2,1,0:T(8,128)(2,1)S(1)}, bf16[3,3,3,192,96]{4,3,2,1,0:T(8,128)(2,1)}, u32[]{:S(2)}) copy-start(bf16[3,3,3,192,96]{4,3,2,1,0:T(8,128)(2,1)} %low) | copy-start | bytes 2985988
  20.7 5.4 %copy-start.4 = (bf16[2,2,160,384]{3,2,1,0:T(8,128)(2,1)S(1)}, bf16[2,2,160,384]{3,2,1,0:T(8,128)(2,1)}, u32[]{:S(2)}) copy-start(bf16[2,2,160,384]{3,2,1,0:T(8,128)(2,1)} %cache.3) | copy-start | bytes 1474564
  20.7 7.6 %collective-permute-start.2 = (bf16[320,384]{1,0:T(8,128)(2,1)S(1)}, bf16[320,384]{1,0:T(8,128)(2,1)S(1)}, u32[]{:S(2)}, u32[]{:S(2)}) collective-permute-start(bf16[320,384]{1,0:T(8,128)(2,1)S(1)} %get-tuple-element.46), channel_id=1, source_target_pairs={{0,2},{1,3},{4,6},{5,7},{8,10},{9,11},{12,14},{13,15},{16,18},{17,... | collective-permute-start | bytes 737288 | tf_op jit(solution)/shard_map/ppermute | solution.py:697
  28.4 8.2 %copy-start.3 = (bf16[384,1152]{1,0:T(8,128)(2,1)S(1)}, bf16[384,1152]{1,0:T(8,128)(2,1)}, u32[]{:S(2)}) copy-start(bf16[384,1152]{1,0:T(8,128)(2,1)} %qkv.7) | copy-start | bytes 2654212
  28.4 8.2 %copy-start.8 = (f32[384]{0:T(512)S(1)}, f32[384]{0:T(512)}, u32[]{:S(2)}) copy-start(f32[384]{0:T(512)} %gain.13) | copy-start | bytes 4612
  30.7 6.4 %copy-start = (bf16[2,4,320,192]{2,3,1,0:T(8,128)(2,1)S(1)}, bf16[2,4,320,192]{2,3,1,0:T(8,128)(2,1)}, u32[]{:S(2)}) copy-start(bf16[2,4,320,192]{2,3,1,0:T(8,128)(2,1)} %param.13) | copy-start | bytes 2949124
  31.0 17.0 %collective-permute-start.4 = (bf16[2,2,96,1536]{3,2,1,0:T(8,128)(2,1)S(1)}, bf16[2,2,96,1536]{3,2,1,0:T(8,128)(2,1)S(1)}, u32[]{:S(2)}, u32[]{:S(2)}) collective-permute-start(bf16[2,2,96,1536]{3,2,1,0:T(8,128)(2,1)S(1)} %get-tuple-element.57.mine), channel_id=1, source_target_pairs={{0,1},{1,0},{2,3},{3,2},{4,5},{5,4},{6,7},{7,6},{8,9},{9,8},{10,11... | collective-permute-start | bytes 3538952 | tf_op jit(solution)/shard_map/ppermute | solution.py:754
  31.2 15.0 %collective-permute-start.5 = (bf16[320,384]{1,0:T(8,128)(2,1)S(1)}, bf16[320,384]{1,0:T(8,128)(2,1)S(1)}, u32[]{:S(2)}, u32[]{:S(2)}) collective-permute-start(bf16[320,384]{1,0:T(8,128)(2,1)S(1)} %maximum_select_fusion.refs_0_.own), channel_id=1, source_target_pairs={{0,8},{4,12},{8,0},{12,4},{1,9},{5,13},{9,1},{13,5},{2,10},{6,14},... | collective-permute-start | bytes 737288 | tf_op jit(solution)/shard_map/ppermute | solution.py:688
  33.1 15.1 %collective-permute-start.3 = (bf16[320,384]{1,0:T(8,128)(2,1)S(1)}, bf16[320,384]{1,0:T(8,128)(2,1)S(1)}, u32[]{:S(2)}, u32[]{:S(2)}) collective-permute-start(bf16[320,384]{1,0:T(8,128)(2,1)S(1)} %maximum_select_fusion.refs_0_.own), channel_id=1, source_target_pairs={{0,4},{4,8},{8,12},{1,5},{5,9},{9,13},{2,6},{6,10},{10,14},{3,7},{... | collective-permute-start | bytes 737288 | tf_op jit(solution)/shard_map/ppermute | solution.py:690
  35.3 13.7 %collective-permute-start.6 = (bf16[320,384]{1,0:T(8,128)(2,1)S(1)}, bf16[320,384]{1,0:T(8,128)(2,1)S(1)}, u32[]{:S(2)}, u32[]{:S(2)}) collective-permute-start(bf16[320,384]{1,0:T(8,128)(2,1)S(1)} %maximum_select_fusion.refs_0_.own), channel_id=1, source_target_pairs={{4,0},{8,4},{12,8},{5,1},{9,5},{13,9},{6,2},{10,6},{14,10},{7,3},{... | collective-permute-start | bytes 737288 | tf_op jit(solution)/shard_map/ppermute | solution.py:691
  46.2 8.7 %collective-permute-start.7 = (bf16[320,384]{1,0:T(8,128)(2,1)S(1)}, bf16[320,384]{1,0:T(8,128)(2,1)S(1)}, u32[]{:S(2)}, u32[]{:S(2)}) collective-permute-start(bf16[320,384]{1,0:T(8,128)(2,1)S(1)} %collective-permute-done.5.refs_0_), channel_id=1, source_target_pairs={{8,12},{4,0},{9,13},{5,1},{10,14},{6,2},{11,15},{7,3},{24,28},{20,... | collective-permute-start | bytes 737288 | tf_op jit(solution)/shard_map/ppermute | solution.py:688
  48.2 6.8 %copy-start.10 = (bf16[384,384]{1,0:T(8,128)(2,1)S(1)}, bf16[384,384]{1,0:T(8,128)(2,1)}, u32[]{:S(2)}) copy-start(bf16[384,384]{1,0:T(8,128)(2,1)} %proj.1) | copy-start | bytes 884740
  59.4 2.5 %copy-start.9 = (f32[192]{0:T(256)S(1)}, f32[192]{0:T(256)}, u32[]{:S(2)}) copy-start(f32[192]{0:T(256)} %gain.15) | copy-start | bytes 2308
  66.4 9.8 %collective-permute-start.8 = (bf16[192,640]{1,0:T(8,128)(2,1)S(1)}, bf16[192,640]{1,0:T(8,128)(2,1)S(1)}, u32[]{:S(2)}, u32[]{:S(2)}) collective-permute-start(bf16[192,640]{1,0:T(8,128)(2,1)S(1)} %get-tuple-element.77), channel_id=1, source_target_pairs={{0,2},{1,3},{4,6},{5,7},{8,10},{9,11},{12,14},{13,15},{16,18},{17,... | collective-permute-start | bytes 737288 | tf_op jit(solution)/shard_map/ppermute | solution.py:697
  74.0 7.1 %collective-permute-start.9 = (bf16[1,192,640]{2,1,0:T(8,128)(2,1)S(1)}, bf16[1,192,640]{2,1,0:T(8,128)(2,1)S(1)}, u32[]{:S(2)}, u32[]{:S(2)}) collective-permute-start(bf16[1,192,640]{2,1,0:T(8,128)(2,1)S(1)} %get-tuple-element.79), channel_id=1, source_target_pairs={{0,2},{1,3},{4,6},{5,7},{8,10},{9,11},{12,14},{13,15},{16,18},{17,... | collective-permute-start | bytes 737288 | tf_op jit(solution)/shard_map/ppermute | solution.py:697

commit v10 on v9

--- a/solution.py
+++ b/solution.py
@@ -10,7 +10,6 @@
 
 BF16, F32 = jnp.bfloat16, jnp.float32
 MIB = 1024 * 1024
-NEAR_FLOPS = 100000
 NT = (((1,), (1,)), ((), ()))
 EPS = 1e-06
 
@@ -306,7 +305,7 @@
         values[...] = both[:, channels:]
 
 
-def block_keys(gain, qkv, blocks, flops):
+def block_keys(gain, qkv, blocks):
     count, size = len(blocks), blocks[0].size
     outs = pl.pallas_call(
         block_kernel,
@@ -314,13 +313,13 @@
         out_specs=[vmem()] * (2 * count),
         out_shape=[jax.ShapeDtypeStruct(blocks[0].shape, BF16)] * (2 * count),
         compiler_params=pltpu.CompilerParams(vmem_limit_bytes=room(16 * blocks[0].nbytes)),
-        cost_estimate=cost(flops, blocks[0].nbytes // 4),
+        cost_estimate=cost(1, blocks[0].nbytes // 4),
         name="block_keys",
     )(gain, qkv, *blocks)
     return list(outs[:count]), list(outs[count:])
 
 
-def attn_kernel(count, width, gain, qkv, proj, own, before, after, far_low, far_high, *refs):
+def attn_kernel(count, width, gain, qkv, proj, own, partner, other, far_low, far_high, *refs):
     given, (out, keys, values) = refs[:-3], refs[-3:]
     channels = qkv.shape[0]
     size = own.shape[0]
@@ -331,19 +330,19 @@
     for i in range(count):
         keys[i * size : (i + 1) * size] = given[i][...]
         values[i * size : (i + 1) * size] = given[count + i][...]
-    for i, (block, missing) in enumerate(((far_low, row == 0), (far_high, row == depth - 1))):
-        @pl.when(missing)
-        def _(i=i, block=block):
-            scaled = normed(block[...].astype(F32), gain[...]).astype(BF16)
-            both = jnp.dot(scaled, qkv[:, channels:], preferred_element_type=F32).astype(BF16)
-            at = slice((count - 2 + i) * size, (count - 1 + i) * size)
-            keys[at] = both[:, :channels]
-            values[at] = both[:, channels:]
-
-    lines = [before[size - width :]] + [own[i * width : (i + 1) * width] for i in range(rows - 2)] + [after[:width]]
+    block = jnp.where(row == 0, far_low[...].astype(F32), other[...].astype(F32))
+    block = jnp.where(row == depth - 1, far_high[...].astype(F32), block)
+    scaled = normed(block, gain[...]).astype(BF16)
+    both = jnp.dot(scaled, qkv[:, channels:], preferred_element_type=F32).astype(BF16)
+    keys[count * size :] = both[:, :channels]
+    values[count * size :] = both[:, channels:]
+    odd = row % 2 == 1
+    before = jnp.where(odd, partner[size - width :].astype(F32), other[size - width :].astype(F32))
+    after = jnp.where(odd, other[:width].astype(F32), partner[:width].astype(F32))
+    lines = [before] + [own[i * width : (i + 1) * width].astype(F32) for i in range(rows - 2)] + [after]
     inside = [row > 0] + [None] * (rows - 2) + [row < depth - 1]
     for block in range(rows // step):
-        skipped = jnp.concatenate(lines[block * step : (block + 1) * step], axis=0).astype(F32)
+        skipped = jnp.concatenate(lines[block * step : (block + 1) * step], axis=0)
         inputs = normed(skipped, gain[...]).astype(BF16)
         query = jnp.dot(inputs, qkv[:, :channels], preferred_element_type=F32).astype(BF16)
         scores = dot_nt(query, keys[...]) * scale
@@ -360,7 +359,7 @@
 def attention(own, ends, keys, values, gain, qkv, proj, width):
     size, channels = own.shape
     count = len(keys)
-    pixels = count * size
+    pixels = (count + 1) * size
     rows = size // width + 2
     need = 2 * width * pixels * 16 + 16 * own.nbytes
     return pl.pallas_call(
@@ -678,8 +677,8 @@
 def line_blocks(mine):
     depth = lax.axis_size("rows")
     upper, lower = {0: mine}, {0: mine}
-    for d in (2, 1, *range(3, depth)):
-        start = 0 if d < 3 else d - 1 if d % 2 else d - 2
+    for d in range(2, depth):
+        start = d - 1 if d % 2 else d - 2
         hop = d - start
         rising = [(i - hop, i) for i in range(d, depth)]
         falling = [(i + hop, i) for i in range(depth - d)]
@@ -690,6 +689,11 @@
             upper[d] = lax.ppermute(upper[start], "rows", rising)
             lower[d] = lax.ppermute(lower[start], "rows", falling)
     return upper, lower
+
+
+def swapped(mine, first):
+    pairs = [(i, i + 1) for i in range(first, lax.axis_size("rows") - 1, 2)]
+    return lax.ppermute(mine, "rows", pairs + [(b, a) for a, b in pairs])
 
 
 def to_next(values):
@@ -749,20 +753,21 @@
     for d in range(2, depth - 1):
         same = upper[d] is lower[depth - d]
         inner.append(upper[d] if same else jnp.where(row >= d, upper[d], lower[depth - d]))
-    own_keys, own_values = block_keys(gain_attn, attn_qkv, [mine], 1)
+    partner = swapped(mine, 0)
+    late, _ = lax.optimization_barrier((mine, upper[2]))
+    other = swapped(late, 1)
+    own_keys, own_values = block_keys(gain_attn, attn_qkv, [mine])
     up_mine, _ = lax.optimization_barrier((up_mine, mine))
     up_other = lax.ppermute(up_mine, "chan", [(0, 1), (1, 0)])
     cached = low_cached(low_cache, cache_halo, low_weights)
     up = joined_up(up_mine, up_other)
-    keys, values = block_keys(gain_attn, attn_qkv, inner, 1)
-    upper[1], cached, low_weights, up, keys[0], own_keys[0] = lax.optimization_barrier(
-        (upper[1], cached, low_weights, up, keys[0], own_keys[0])
+    keys, values = block_keys(gain_attn, attn_qkv, inner + [partner])
+    other, cached, low_weights, up, keys[0], own_keys[0] = lax.optimization_barrier(
+        (other, cached, low_weights, up, keys[0], own_keys[0])
     )
-    near_keys, near_values = block_keys(gain_attn, attn_qkv, [upper[1], lower[1]], NEAR_FLOPS * mine.size)
-    ends = [upper[1], lower[1], lower[depth - 1], upper[depth - 1]]
+    ends = [partner, other, lower[depth - 1], upper[depth - 1]]
     reached = attention(
-        mine, ends, own_keys + keys + near_keys, own_values + values + near_values,
-        gain_attn, attn_qkv, attn_proj, width,
+        mine, ends, own_keys + keys, own_values + values, gain_attn, attn_qkv, attn_proj, width
     )
     tile = lax.all_gather(reached, "chan")
 

time: 82.9 us -> 83.2 us (level)
  waiting for transfers between devices: 14.1 us -> 17.7 us
  starting transfers between devices: 22.2 us -> 19.7 us
    ppermute x2, waiting for transfers between devices: 10.6 us -> 15 us  [line_blocks(): upper[d] = lower[d] = lax.ppermute(upper[start], 'rows', rising + falling)]
    ppermute x2, starting transfers between devices: 3.43 us -> 0.89 us  [swapped(): return lax.ppermute(mine, 'rows', pairs + [(b, a) for a, b in pairs])]
    pallas_call x3 -> x2, Pallas kernels: 1.74 us -> 1.26 us  [block_keys(): pl.pallas_call(block_kernel, in_specs=[vmem()] * (2 + count), out_specs=[...]
  transfers between devices with their start and end apart: 10 -> 10, of which waited for: 5 -> 4; matrix products, arithmetic and copies ran while one was open for 0% -> 0% of each run, Pallas kernels for 26% -> 25%
where the time goes in v10:
time: 83.2 us; the launch traced here: 82.8 us
  Pallas kernels  33.1 us (40%)
  starting transfers between devices  19.7 us (24%)
  waiting for transfers between devices  17.7 us (21%)
  blocking collectives  9.47 us (11%)
  local copies, waits for them, and re-layouts  2.34 us (3%)
    ppermute x2, waiting for transfers between devices, line_blocks(): upper[d] = lower[d] = lax.ppermute(upper[start], 'rows', rising + falling)  15 us
    ppermute x2, starting transfers between devices, to_neighbour(): return lax.ppermute(values, ('rows', 'segment', 'chan'), route)  8.45 us
    ppermute x3, starting transfers between devices, to_next(): lax.ppermute(values, 'segment', [(i, i + 1) for i in range(count - 1)])  7 us
    pallas_call x1, Pallas kernels, low_last(): pl.pallas_call(functools.partial(low_last_kernel, frames, past), in_specs...  4.45 us
    pallas_call x1, Pallas kernels, attention(): pl.pallas_call(functools.partial(attn_kernel, count, width), in_specs=[vm...  4.04 us
    pallas_call x1, Pallas kernels, low_cached(): pl.pallas_call(low_cache_kernel, in_specs=[vmem()] * 3, out_specs=vmem(),...  3.74 us
    pallas_call x1, Pallas kernels, low_early(): pl.pallas_call(functools.partial(low_early_kernel, frames, past), in_spec...  3.41 us
    pallas_call x1, Pallas kernels, mid_inner(): pl.pallas_call(mid_inner_kernel, in_specs=[vmem()] * 3, out_specs=vmem(),...  3.27 us
  transfers between devices with their start and end apart: 10, of which 4 were waited for; matrix products, arithmetic and copies ran while one was open for 0% of the time, Pallas kernels for 25%

profile of v10, /device:TPU:0, one launch (start us, length us, event | category | flops | bytes accessed | tf_op | source)
XLA Modules:
  0.0 82.8 jit_solution(7816303851954940251)
XLA Ops:
  0.0 2.4 %edge_rows.1 = (bf16[2,160,384]{2,1,0:T(8,128)(2,1)}, bf16[4,160,384]{2,1,0:T(8,128)(2,1)}) custom-call(bf16[2,2,160,384]{3,2,1,0:T(8,128)(2,1)} %latent.3, bf16[2,2,160,384]{3,2,1,0:T(8,128)(2,1)} %cache.3, bf16[2,4,192,320]{3,2,1,0:T(8,128)(2,1)} %bitcast.20), custom_call_target="tpu_custom_call" | custom-call | bytes 1966080 | tf_op jit(solution)/shard_map/edge_rows/pallas_call | solution.py:98
  2.4 4.9 %collective-permute-start = (bf16[2,160,384]{2,1,0:T(8,128)(2,1)}, bf16[2,160,384]{2,1,0:T(8,128)(2,1)S(1)}, u32[]{:S(2)}, u32[]{:S(2)}) collective-permute-start(bf16[2,160,384]{2,1,0:T(8,128)(2,1)} %get-tuple-element.42), channel_id=1, source_target_pairs={{0,4},{5,1},{2,6},{7,3},{4,8},{9,5},{6,10},{11,7},{8,12},{13,9},{1... | collective-permute-start | bytes 737288 | tf_op jit(solution)/shard_map/ppermute | solution.py:674
  7.4 3.5 %collective-permute-start.1 = (bf16[4,160,384]{2,1,0:T(8,128)(2,1)}, bf16[4,160,384]{2,1,0:T(8,128)(2,1)S(1)}, u32[]{:S(2)}, u32[]{:S(2)}) collective-permute-start(bf16[4,160,384]{2,1,0:T(8,128)(2,1)} %get-tuple-element.44), channel_id=1, source_target_pairs={{0,4},{5,1},{4,8},{9,5},{8,12},{13,9},{16,20},{21,17},{20,24},{25,... | collective-permute-start | bytes 1474568 | tf_op jit(solution)/shard_map/ppermute | solution.py:674
  10.9 2.1 %copy-done.1 = bf16[3,3,3,384,192]{3,4,2,1,0:T(8,128)(2,1)S(1)} copy-done((bf16[3,3,3,384,192]{3,4,2,1,0:T(8,128)(2,1)S(1)}, bf16[3,3,3,384,192]{3,4,2,1,0:T(8,128)(2,1)}, u32[]{:S(2)}) %copy-start.1) | copy-done | bytes 3981336
  13.1 3.3 %mid_inner.1.started = f32[4,320,192]{2,1,0:T(8,128)S(1)} custom-call(bf16[2,2,160,384]{3,2,1,0:T(8,128)(2,1)S(1)} %copy-done.7, f32[384]{0:T(512)S(1)} %copy-done.11, bf16[3,3,3,192,384]{4,3,2,1,0:T(8,128)(2,1)S(1)} %bitcast.22), custom_call_target="tpu_custom_call" | custom-call | flops 2548039680 | bytes 3981312 | tf_op jit(solution)/shard_map/mid_inner/pallas_call | solution.py:203
  16.3 2.2 %all-gather = bf16[4,160,384]{2,1,0:T(8,128)(2,1)S(1)} all-gather(bf16[2,160,384]{2,1,0:T(8,128)(2,1)S(1)} %collective-permute-done), channel_id=2, replica_groups=mesh['groups'=2,'rows'=4,'segment'=2,'chan'=2] {'chan'}, dimensions={0}, use_global_device_ids=true | all-gather | bytes 737280 | tf_op jit(solution)/shard_map/all_gather | solution.py:730
  18.5 2.2 %mid_rim.1 = (f32[320,384]{1,0:T(8,128)S(1)}, bf16[320,384]{1,0:T(8,128)(2,1)S(1)}) custom-call(f32[4,320,192]{2,1,0:T(8,128)S(1)} %mid_inner.1.started, bf16[2,2,160,384]{3,2,1,0:T(8,128)(2,1)S(1)} %bitcast.26, f32[384]{0:T(512)S(1)} %copy-done.11, bf16[3,3,3,192,384]{4,3,2,1,0:T(8,128)(2,1)S(1)} %bitcast.23), custom_call_target="tpu_custom_call" | custom-call | flops 2548039680 | bytes 3981312 | tf_op jit(solution)/shard_map/mid_rim/pallas_call | solution.py:238
  20.7 1.4 %collective-permute-start.2 = (bf16[320,384]{1,0:T(8,128)(2,1)S(1)}, bf16[320,384]{1,0:T(8,128)(2,1)S(1)}, u32[]{:S(2)}, u32[]{:S(2)}) collective-permute-start(bf16[320,384]{1,0:T(8,128)(2,1)S(1)} %get-tuple-element.45), channel_id=1, source_target_pairs={{0,2},{1,3},{4,6},{5,7},{8,10},{9,11},{12,14},{13,15},{16,18},{17,... | collective-permute-start | bytes 737288 | tf_op jit(solution)/shard_map/ppermute | solution.py:701
  22.1 2.5 %all-gather.1 = bf16[8,160,384]{2,1,0:T(8,128)(2,1)S(1)} all-gather(bf16[4,160,384]{2,1,0:T(8,128)(2,1)S(1)} %collective-permute-done.1), channel_id=3, replica_groups=mesh['groups'=2,'rows'=4,'segment'=2,'chan'=2] {'chan'}, dimensions={0}, use_global_device_ids=true | all-gather | bytes 1474560 | tf_op jit(solution)/shard_map/all_gather | solution.py:734
  24.7 1.4 %weight_forms.1 = (bf16[2,2,96,1536]{3,2,1,0:T(8,128)(2,1)S(1)}, bf16[576,2304]{1,0:T(8,128)(2,1)S(1)}) custom-call(bf16[3,3,96,384]{3,2,1,0:T(8,128)(2,1)S(1)} %bitcast.25, bf16[3,3,3,192,96]{4,3,2,1,0:T(8,128)(2,1)S(1)} %copy-done.5), custom_call_target="tpu_custom_call" | custom-call | flops 95551488 | bytes 6635520 | tf_op jit(solution)/shard_map/weight_forms/pallas_call | solution.py:138
  26.1 2.2 %mid_cached.1.own = f32[320,384]{1,0:T(8,128)S(1)} custom-call(f32[320,384]{1,0:T(8,128)S(1)} %get-tuple-element.46.own, bf16[2,2,160,384]{3,2,1,0:T(8,128)(2,1)S(1)} %copy-done.4, bf16[2,4,160,384]{3,2,1,0:T(8,128)(2,1)S(1)} %bitcast.16, bf16[3,3,3,192,384]{4,3,2,1,0:T(8,128)(2,1)S(1)} %bitcast.24), custom_call_target="tpu_custom_call" | custom-call | flops 1274019840 | bytes 3981312 | tf_op jit(solution)/shard_map/mid_cached/pallas_call | solution.py:286
  28.4 2.3 %all-gather.2 = bf16[640,384]{1,0:T(8,128)(2,1)S(1)} all-gather(bf16[320,384]{1,0:T(8,128)(2,1)S(1)} %join.1), channel_id=4, replica_groups=mesh['groups'=2,'rows'=4,'segment'=2,'chan'=2] {'chan'}, dimensions={0}, use_global_device_ids=true | all-gather | bytes 737280 | tf_op jit(solution)/shard_map/all_gather | solution.py:739
  31.0 0.2 collective-permute-start.6
  31.2 1.9 %collective-permute-start.4 = (bf16[320,384]{1,0:T(8,128)(2,1)S(1)}, bf16[320,384]{1,0:T(8,128)(2,1)S(1)}, u32[]{:S(2)}, u32[]{:S(2)}) collective-permute-start(bf16[320,384]{1,0:T(8,128)(2,1)S(1)} %maximum_select_fusion.refs_0_.own), channel_id=1, source_target_pairs={{0,8},{4,12},{8,0},{12,4},{1,9},{5,13},{9,1},{13,5},{2,10},{6,14},... | collective-permute-start | bytes 737288 | tf_op jit(solution)/shard_map/ppermute | solution.py:687
  33.1 0.2 collective-permute-start.3
  33.3 12.3 %collective-permute-done.4.refs_0_ = bf16[320,384]{1,0:T(8,128)(2,1)S(1)} collective-permute-done((bf16[320,384]{1,0:T(8,128)(2,1)S(1)}, bf16[320,384]{1,0:T(8,128)(2,1)S(1)}, u32[]{:S(2)}, u32[]{:S(2)}) %collective-permute-start.4) | collective-permute-done | bytes 245792 | tf_op jit(solution)/shard_map/ppermute | solution.py:687
  45.6 0.7 collective-permute-start.5
  46.3 1.3 %collective-permute-start.7 = (bf16[320,384]{1,0:T(8,128)(2,1)S(1)}, bf16[320,384]{1,0:T(8,128)(2,1)S(1)}, u32[]{:S(2)}, u32[]{:S(2)}) collective-permute-start(bf16[320,384]{1,0:T(8,128)(2,1)S(1)} %collective-permute-done.4.refs_0_), channel_id=1, source_target_pairs={{8,12},{4,0},{9,13},{5,1},{10,14},{6,2},{11,15},{7,3},{24,28},{20,... | collective-permute-start | bytes 737288 | tf_op jit(solution)/shard_map/ppermute | solution.py:687
  47.6 0.5 block_keys.3
  48.1 3.7 %low_cached.1.cached = f32[2,192,640]{2,1,0:T(8,128)S(1)} custom-call(bf16[2,4,192,320]{3,2,1,0:T(8,128)(2,1)S(1)} %bitcast.21, bf16[2,4,160,384]{3,2,1,0:T(8,128)(2,1)S(1)} %bitcast.17, bf16[576,2304]{1,0:T(8,128)(2,1)S(1)} %get-tuple-element.68.weights), custom_call_target="tpu_custom_call" | custom-call | flops 122880 | bytes 331776 | tf_op jit(solution)/shard_map/low_cached/pallas_call | solution.py:594
  51.9 0.8 block_keys.2
  52.9 2.7 %collective-permute-done.7.far_low.far_high = bf16[320,384]{1,0:T(8,128)(2,1)S(1)} collective-permute-done((bf16[320,384]{1,0:T(8,128)(2,1)S(1)}, bf16[320,384]{1,0:T(8,128)(2,1)S(1)}, u32[]{:S(2)}, u32[]{:S(2)}) %collective-permute-start.7) | collective-permute-done | bytes 245792 | tf_op jit(solution)/shard_map/ppermute | solution.py:687
  55.6 4.0 %frame_attention.1 = bf16[4,160,384]{2,1,0:T(8,128)(2,1)S(1)} custom-call(f32[384]{0:T(512)S(1)} %copy-done.8, bf16[384,1152]{1,0:T(8,128)(2,1)S(1)} %copy-done.3, bf16[384,384]{1,0:T(8,128)(2,1)S(1)} %copy-done.10, bf16[320,384]{1,0:T(8,128)(2,1)S(1)} %maximum_select_fusion.refs_0_.own, bf16[320,384]{1,0:T(8,128)(2,1)S(1)} %collective-permute-done.3.refs_1_.partner, ...), custom_call_target="tpu_custom_call" | custom-call | flops 1635778560 | bytes 884736 | tf_op jit(solution)/shard_map/frame_attention/pallas_call | solution.py:365
  59.7 2.5 %all-gather.3 = bf16[8,160,384]{2,1,0:T(8,128)(2,1)S(1)} all-gather(bf16[4,160,384]{2,1,0:T(8,128)(2,1)S(1)} %frame_attention.1), channel_id=5, replica_groups=mesh['groups'=2,'rows'=4,'segment'=2,'chan'=2] {'chan'}, dimensions={0}, use_global_device_ids=true | all-gather | bytes 1474560 | tf_op jit(solution)/shard_map/all_gather | solution.py:772
  62.2 4.5 %low_last.1 = (bf16[192,640]{1,0:T(8,128)(2,1)S(1)}, f32[1,192,640]{2,1,0:T(8,128)S(1)}, bf16[1,6,160,768]{3,2,1,0:T(8,128)(2,1)S(1)}, bf16[1,4,160,384]{3,2,1,0:T(8,128)(2,1)S(1)}) custom-call(bf16[2,4,160,384]{3,2,1,0:T(8,128)(2,1)S(1)} %bitcast.18, bf16[2,2,192,1536]{3,2,1,0:T(8,128)(2,1)S(1)} %joined_up.1.up, f32[192]{0:T(256)S(1)} %copy-done.9, ...), custom_call_target="tpu_custom_call" | custom-call | flops 1132462080 | bytes 2654208 | tf_op jit(solution)/shard_map/low_last/pallas_call | solution.py:479
  66.6 4.3 %collective-permute-start.8 = (bf16[192,640]{1,0:T(8,128)(2,1)S(1)}, bf16[192,640]{1,0:T(8,128)(2,1)S(1)}, u32[]{:S(2)}, u32[]{:S(2)}) collective-permute-start(bf16[192,640]{1,0:T(8,128)(2,1)S(1)} %get-tuple-element.75), channel_id=1, source_target_pairs={{0,2},{1,3},{4,6},{5,7},{8,10},{9,11},{12,14},{13,15},{16,18},{17,... | collective-permute-start | bytes 737288 | tf_op jit(solution)/shard_map/ppermute | solution.py:701
  70.9 3.4 %low_early.1 = (bf16[1,192,640]{2,1,0:T(8,128)(2,1)S(1)}, bf16[1,6,160,768]{3,2,1,0:T(8,128)(2,1)S(1)}, bf16[1,4,160,384]{3,2,1,0:T(8,128)(2,1)S(1)}) custom-call(bf16[2,4,160,384]{3,2,1,0:T(8,128)(2,1)S(1)} %bitcast.19, bf16[2,2,192,1536]{3,2,1,0:T(8,128)(2,1)S(1)} %joined_up.1.up, f32[192]{0:T(256)S(1)} %copy-done.9, ...), custom_call_target="tpu_custom_call" | custom-call | flops 1132462080 | bytes 2654208 | tf_op jit(solution)/shard_map/low_early/pallas_call | solution.py:500
  74.3 1.3 %collective-permute-start.9 = (bf16[1,192,640]{2,1,0:T(8,128)(2,1)S(1)}, bf16[1,192,640]{2,1,0:T(8,128)(2,1)S(1)}, u32[]{:S(2)}, u32[]{:S(2)}) collective-permute-start(bf16[1,192,640]{2,1,0:T(8,128)(2,1)S(1)} %get-tuple-element.77), channel_id=1, source_target_pairs={{0,2},{1,3},{4,6},{5,7},{8,10},{9,11},{12,14},{13,15},{16,18},{17,... | collective-permute-start | bytes 737288 | tf_op jit(solution)/shard_map/ppermute | solution.py:701
  75.6 0.8 collective-permute-done.8.arrived
  76.4 3.1 %low_own.1 = (f32[2,192,640]{2,1,0:T(8,128)S(1)}, bf16[4,512,320]{2,1,0:T(8,128)(2,1)S(1)}) custom-call(bf16[1,6,160,768]{3,2,1,0:T(8,128)(2,1)S(1)} %get-tuple-element.70.early, bf16[1,6,160,768]{3,2,1,0:T(8,128)(2,1)S(1)} %get-tuple-element.71.last, bf16[1,4,160,384]{3,2,1,0:T(8,128)(2,1)S(1)} %get-tuple-element.72.early_kept, ...), custom_call_target="tpu_custom_call" | custom-call | flops 2548039680 | bytes 2654208 | tf_op jit(solution)/shard_map/low_own/pallas_call | solution.py:554
  79.6 1.9 %collective-permute-done.9.arrived = bf16[1,192,640]{2,1,0:T(8,128)(2,1)S(1)} collective-permute-done((bf16[1,192,640]{2,1,0:T(8,128)(2,1)S(1)}, bf16[1,192,640]{2,1,0:T(8,128)(2,1)S(1)}, u32[]{:S(2)}, u32[]{:S(2)}) %collective-permute-start.9) | collective-permute-done | bytes 245792 | tf_op jit(solution)/shard_map/ppermute | solution.py:701
  81.4 1.4 %finish.1 = bf16[2,4,96,320]{3,2,1,0:T(8,128)(2,1)} custom-call(f32[2,192,640]{2,1,0:T(8,128)S(1)} %get-tuple-element.76.own, bf16[1,192,640]{2,1,0:T(8,128)(2,1)S(1)} %collective-permute-done.9.arrived, bf16[4,512,320]{2,1,0:T(8,128)(2,1)S(1)} %get-tuple-element.78.weave), custom_call_target="tpu_custom_call" | custom-call | flops 251658240 | bytes 983040 | tf_op jit(solution)/shard_map/finish/pallas_call | solution.py:635
  (33 shorter events, 0.6 us)
Async XLA Ops:
  0.0 10.9 %copy-start.7 = (bf16[2,2,160,384]{3,2,1,0:T(8,128)(2,1)S(1)}, bf16[2,2,160,384]{3,2,1,0:T(8,128)(2,1)}, u32[]{:S(2)}) copy-start(bf16[2,2,160,384]{3,2,1,0:T(8,128)(2,1)} %latent.3) | copy-start | bytes 1474564
  0.0 10.9 %copy-start.11 = (f32[384]{0:T(512)S(1)}, f32[384]{0:T(512)}, u32[]{:S(2)}) copy-start(f32[384]{0:T(512)} %gain.8) | copy-start | bytes 4612
  2.4 13.9 %collective-permute-start = (bf16[2,160,384]{2,1,0:T(8,128)(2,1)}, bf16[2,160,384]{2,1,0:T(8,128)(2,1)S(1)}, u32[]{:S(2)}, u32[]{:S(2)}) collective-permute-start(bf16[2,160,384]{2,1,0:T(8,128)(2,1)} %get-tuple-element.42), channel_id=1, source_target_pairs={{0,4},{5,1},{2,6},{7,3},{4,8},{9,5},{6,10},{11,7},{8,12},{13,9},{1... | collective-permute-start | bytes 737288 | tf_op jit(solution)/shard_map/ppermute | solution.py:674
  7.4 13.3 %collective-permute-start.1 = (bf16[4,160,384]{2,1,0:T(8,128)(2,1)}, bf16[4,160,384]{2,1,0:T(8,128)(2,1)S(1)}, u32[]{:S(2)}, u32[]{:S(2)}) collective-permute-start(bf16[4,160,384]{2,1,0:T(8,128)(2,1)} %get-tuple-element.44), channel_id=1, source_target_pairs={{0,4},{5,1},{4,8},{9,5},{8,12},{13,9},{16,20},{21,17},{20,24},{25,... | collective-permute-start | bytes 1474568 | tf_op jit(solution)/shard_map/ppermute | solution.py:674
  10.9 2.1 %copy-start.1 = (bf16[3,3,3,384,192]{3,4,2,1,0:T(8,128)(2,1)S(1)}, bf16[3,3,3,384,192]{3,4,2,1,0:T(8,128)(2,1)}, u32[]{:S(2)}) copy-start(bf16[3,3,3,384,192]{3,4,2,1,0:T(8,128)(2,1)} %param.17) | copy-start | bytes 11943940
  18.5 6.2 %copy-start.6 = (bf16[3,3,384,96]{2,3,1,0:T(8,128)(2,1)S(1)}, bf16[3,3,384,96]{2,3,1,0:T(8,128)(2,1)}, u32[]{:S(2)}) copy-start(bf16[3,3,384,96]{2,3,1,0:T(8,128)(2,1)} %param.20) | copy-start | bytes 1990660
  18.5 7.6 %copy-start.2 = (bf16[3,3,3,384,192]{3,4,2,1,0:T(8,128)(2,1)S(1)}, bf16[3,3,3,384,192]{3,4,2,1,0:T(8,128)(2,1)}, u32[]{:S(2)}) copy-start(bf16[3,3,3,384,192]{3,4,2,1,0:T(8,128)(2,1)} %param.17) | copy-start | bytes 11943940
  20.7 4.0 %copy-start.5 = (bf16[3,3,3,192,96]{4,3,2,1,0:T(8,128)(2,1)S(1)}, bf16[3,3,3,192,96]{4,3,2,1,0:T(8,128)(2,1)}, u32[]{:S(2)}) copy-start(bf16[3,3,3,192,96]{4,3,2,1,0:T(8,128)(2,1)} %low) | copy-start | bytes 2985988
  20.7 5.4 %copy-start.4 = (bf16[2,2,160,384]{3,2,1,0:T(8,128)(2,1)S(1)}, bf16[2,2,160,384]{3,2,1,0:T(8,128)(2,1)}, u32[]{:S(2)}) copy-start(bf16[2,2,160,384]{3,2,1,0:T(8,128)(2,1)} %cache.3) | copy-start | bytes 1474564
  20.7 7.6 %collective-permute-start.2 = (bf16[320,384]{1,0:T(8,128)(2,1)S(1)}, bf16[320,384]{1,0:T(8,128)(2,1)S(1)}, u32[]{:S(2)}, u32[]{:S(2)}) collective-permute-start(bf16[320,384]{1,0:T(8,128)(2,1)S(1)} %get-tuple-element.45), channel_id=1, source_target_pairs={{0,2},{1,3},{4,6},{5,7},{8,10},{9,11},{12,14},{13,15},{16,18},{17,... | collective-permute-start | bytes 737288 | tf_op jit(solution)/shard_map/ppermute | solution.py:701
  28.4 19.2 %copy-start.3 = (bf16[384,1152]{1,0:T(8,128)(2,1)S(1)}, bf16[384,1152]{1,0:T(8,128)(2,1)}, u32[]{:S(2)}) copy-start(bf16[384,1152]{1,0:T(8,128)(2,1)} %qkv.5) | copy-start | bytes 2654212
  28.4 19.2 %copy-start.8 = (f32[384]{0:T(512)S(1)}, f32[384]{0:T(512)}, u32[]{:S(2)}) copy-start(f32[384]{0:T(512)} %gain.11) | copy-start | bytes 4612
  30.7 17.5 %copy-start = (bf16[2,4,320,192]{2,3,1,0:T(8,128)(2,1)S(1)}, bf16[2,4,320,192]{2,3,1,0:T(8,128)(2,1)}, u32[]{:S(2)}) copy-start(bf16[2,4,320,192]{2,3,1,0:T(8,128)(2,1)} %param.13) | copy-start | bytes 2949124
  31.0 21.7 %collective-permute-start.6 = (bf16[2,2,96,1536]{3,2,1,0:T(8,128)(2,1)S(1)}, bf16[2,2,96,1536]{3,2,1,0:T(8,128)(2,1)S(1)}, u32[]{:S(2)}, u32[]{:S(2)}) collective-permute-start(bf16[2,2,96,1536]{3,2,1,0:T(8,128)(2,1)S(1)} %get-tuple-element.57.mine), channel_id=1, source_target_pairs={{0,1},{1,0},{2,3},{3,2},{4,5},{5,4},{6,7},{7,6},{8,9},{9,8},{10,11... | collective-permute-start | bytes 3538952 | tf_op jit(solution)/shard_map/ppermute | solution.py:761
  31.2 14.4 %collective-permute-start.4 = (bf16[320,384]{1,0:T(8,128)(2,1)S(1)}, bf16[320,384]{1,0:T(8,128)(2,1)S(1)}, u32[]{:S(2)}, u32[]{:S(2)}) collective-permute-start(bf16[320,384]{1,0:T(8,128)(2,1)S(1)} %maximum_select_fusion.refs_0_.own), channel_id=1, source_target_pairs={{0,8},{4,12},{8,0},{12,4},{1,9},{5,13},{9,1},{13,5},{2,10},{6,14},... | collective-permute-start | bytes 737288 | tf_op jit(solution)/shard_map/ppermute | solution.py:687
  33.1 18.8 %collective-permute-start.3 = (bf16[320,384]{1,0:T(8,128)(2,1)S(1)}, bf16[320,384]{1,0:T(8,128)(2,1)S(1)}, u32[]{:S(2)}, u32[]{:S(2)}) collective-permute-start(bf16[320,384]{1,0:T(8,128)(2,1)S(1)} %maximum_select_fusion.refs_0_.own), channel_id=1, source_target_pairs={{0,4},{8,12},{4,0},{12,8},{1,5},{9,13},{5,1},{13,9},{2,6},{10,14},... | collective-permute-start | bytes 737288 | tf_op jit(solution)/shard_map/ppermute | solution.py:696
  45.6 7.2 %collective-permute-start.5 = (bf16[320,384]{1,0:T(8,128)(2,1)S(1)}, bf16[320,384]{1,0:T(8,128)(2,1)S(1)}, u32[]{:S(2)}, u32[]{:S(2)}) collective-permute-start(bf16[320,384]{1,0:T(8,128)(2,1)S(1)} %maximum_select_fusion.refs_0_.own), channel_id=1, source_target_pairs={{4,8},{8,4},{5,9},{9,5},{6,10},{10,6},{7,11},{11,7},{20,24},{24,20... | collective-permute-start | bytes 737288 | tf_op jit(solution)/shard_map/ppermute | solution.py:696
  46.3 9.3 %collective-permute-start.7 = (bf16[320,384]{1,0:T(8,128)(2,1)S(1)}, bf16[320,384]{1,0:T(8,128)(2,1)S(1)}, u32[]{:S(2)}, u32[]{:S(2)}) collective-permute-start(bf16[320,384]{1,0:T(8,128)(2,1)S(1)} %collective-permute-done.4.refs_0_), channel_id=1, source_target_pairs={{8,12},{4,0},{9,13},{5,1},{10,14},{6,2},{11,15},{7,3},{24,28},{20,... | collective-permute-start | bytes 737288 | tf_op jit(solution)/shard_map/ppermute | solution.py:687
  52.7 2.9 %copy-start.10 = (bf16[384,384]{1,0:T(8,128)(2,1)S(1)}, bf16[384,384]{1,0:T(8,128)(2,1)}, u32[]{:S(2)}) copy-start(bf16[384,384]{1,0:T(8,128)(2,1)} %proj.1) | copy-start | bytes 884740
  59.7 2.5 %copy-start.9 = (f32[192]{0:T(256)S(1)}, f32[192]{0:T(256)}, u32[]{:S(2)}) copy-start(f32[192]{0:T(256)} %gain.13) | copy-start | bytes 2308
  66.6 9.8 %collective-permute-start.8 = (bf16[192,640]{1,0:T(8,128)(2,1)S(1)}, bf16[192,640]{1,0:T(8,128)(2,1)S(1)}, u32[]{:S(2)}, u32[]{:S(2)}) collective-permute-start(bf16[192,640]{1,0:T(8,128)(2,1)S(1)} %get-tuple-element.75), channel_id=1, source_target_pairs={{0,2},{1,3},{4,6},{5,7},{8,10},{9,11},{12,14},{13,15},{16,18},{17,... | collective-permute-start | bytes 737288 | tf_op jit(solution)/shard_map/ppermute | solution.py:701
  74.3 7.1 %collective-permute-start.9 = (bf16[1,192,640]{2,1,0:T(8,128)(2,1)S(1)}, bf16[1,192,640]{2,1,0:T(8,128)(2,1)S(1)}, u32[]{:S(2)}, u32[]{:S(2)}) collective-permute-start(bf16[1,192,640]{2,1,0:T(8,128)(2,1)S(1)} %get-tuple-element.77), channel_id=1, source_target_pairs={{0,2},{1,3},{4,6},{5,7},{8,10},{9,11},{12,14},{13,15},{16,18},{17,... | collective-permute-start | bytes 737288 | tf_op jit(solution)/shard_map/ppermute | solution.py:701

commit v11 on v8

--- a/solution.py
+++ b/solution.py
@@ -700,9 +700,8 @@
 
     rim, cache_rim = edge_rows(latent, cache_mid, low_cache)
     rim = to_neighbour(rim, False)
+    cache_rim = to_neighbour(cache_rim, True)
     started = mid_inner(latent, gain_mid, mid_weights)
-    cache_rim, started = lax.optimization_barrier((cache_rim, started))
-    cache_rim = to_neighbour(cache_rim, True)
     halo = lax.all_gather(rim, "chan")
     own, passed = mid_rim(started, halo, gain_mid, mid_weights)
     passed, cache_rim, conv_up, conv_low = lax.optimization_barrier((passed, cache_rim, conv_up, conv_low))

time: 84.7 us -> 82.5 us (0.974)
  local copies, waits for them, and re-layouts: 4.47 us -> 2.34 us
    unnamed x28 -> x24, local copies, waits for them, and re-layouts: 4.31 us -> 2.18 us
where the time goes in v11:
time: 82.5 us; the launch traced here: 82.2 us
  waiting for transfers between devices  31.5 us (38%)
  Pallas kernels  27.5 us (33%)
  starting transfers between devices  10.9 us (13%)
  blocking collectives  9.47 us (11%)
  local copies, waits for them, and re-layouts  2.34 us (3%)
    ppermute x3, waiting for transfers between devices, body(): lax.ppermute(mine, 'rows', [(i, (i + k) % depth) for i in range(depth)])  20.2 us
    ppermute x3, waiting for transfers between devices, to_next(): lax.ppermute(values, 'segment', [(i, i + 1) for i in range(count - 1)])  11.4 us
    pallas_call x1, Pallas kernels, low_last(): pl.pallas_call(functools.partial(low_last_kernel, frames, past), in_specs...  4.46 us
    pallas_call x1, Pallas kernels, attention(): pl.pallas_call(functools.partial(attn_kernel, count, width), in_specs=[vm...  4.36 us
    ppermute x3, starting transfers between devices, to_next(): lax.ppermute(values, 'segment', [(i, i + 1) for i in range(count - 1)])  4.23 us
    ppermute x2, starting transfers between devices, to_neighbour(): return lax.ppermute(values, ('rows', 'segment', 'chan'), route)  4.18 us
    pallas_call x1, Pallas kernels, low_early(): pl.pallas_call(functools.partial(low_early_kernel, frames, past), in_spec...  3.41 us
    pallas_call x1, Pallas kernels, mid_inner(): pl.pallas_call(mid_inner_kernel, in_specs=[vmem()] * 3, out_specs=vmem(),...  3.27 us
  transfers between devices with their start and end apart: 9, of which 5 were waited for; matrix products, arithmetic and copies ran while one was open for 0% of the time, Pallas kernels for 18%

profile of v11, /device:TPU:10, one launch (start us, length us, event | category | flops | bytes accessed | tf_op | source)
XLA Modules:
  0.0 82.2 jit_solution(12780554526666734301)
XLA Ops:
  0.0 2.4 %edge_rows.1 = (bf16[2,160,384]{2,1,0:T(8,128)(2,1)}, bf16[4,160,384]{2,1,0:T(8,128)(2,1)}) custom-call(bf16[2,2,160,384]{3,2,1,0:T(8,128)(2,1)} %latent.3, bf16[2,2,160,384]{3,2,1,0:T(8,128)(2,1)} %cache.3, bf16[2,4,192,320]{3,2,1,0:T(8,128)(2,1)} %bitcast.20), custom_call_target="tpu_custom_call" | custom-call | bytes 1966080 | tf_op jit(solution)/shard_map/edge_rows/pallas_call | solution.py:98
  2.4 3.5 %collective-permute-start = (bf16[2,160,384]{2,1,0:T(8,128)(2,1)}, bf16[2,160,384]{2,1,0:T(8,128)(2,1)S(1)}, u32[]{:S(2)}, u32[]{:S(2)}) collective-permute-start(bf16[2,160,384]{2,1,0:T(8,128)(2,1)} %get-tuple-element.37), channel_id=1, source_target_pairs={{0,4},{5,1},{2,6},{7,3},{4,8},{9,5},{6,10},{11,7},{8,12},{13,9},{1... | collective-permute-start | bytes 737288 | tf_op jit(solution)/shard_map/ppermute | solution.py:671
  5.9 0.7 collective-permute-start.1
  6.7 2.1 %copy-done.1 = bf16[3,3,3,384,192]{3,4,2,1,0:T(8,128)(2,1)S(1)} copy-done((bf16[3,3,3,384,192]{3,4,2,1,0:T(8,128)(2,1)S(1)}, bf16[3,3,3,384,192]{3,4,2,1,0:T(8,128)(2,1)}, u32[]{:S(2)}) %copy-start.1) | copy-done | bytes 3981336
  8.8 3.3 %mid_inner.1.started = f32[4,320,192]{2,1,0:T(8,128)S(1)} custom-call(bf16[2,2,160,384]{3,2,1,0:T(8,128)(2,1)S(1)} %copy-done.7, f32[384]{0:T(512)S(1)} %copy-done.11, bf16[3,3,3,192,384]{4,3,2,1,0:T(8,128)(2,1)S(1)} %bitcast.22), custom_call_target="tpu_custom_call" | custom-call | flops 2548039680 | bytes 3981312 | tf_op jit(solution)/shard_map/mid_inner/pallas_call | solution.py:203
  12.1 2.2 %all-gather = bf16[4,160,384]{2,1,0:T(8,128)(2,1)S(1)} all-gather(bf16[2,160,384]{2,1,0:T(8,128)(2,1)S(1)} %collective-permute-done), channel_id=2, replica_groups=mesh['groups'=2,'rows'=4,'segment'=2,'chan'=2] {'chan'}, dimensions={0}, use_global_device_ids=true | all-gather | bytes 737280 | tf_op jit(solution)/shard_map/all_gather | solution.py:705
  14.2 2.2 %mid_rim.1 = (f32[320,384]{1,0:T(8,128)S(1)}, bf16[320,384]{1,0:T(8,128)(2,1)S(1)}) custom-call(f32[4,320,192]{2,1,0:T(8,128)S(1)} %mid_inner.1.started, bf16[2,2,160,384]{3,2,1,0:T(8,128)(2,1)S(1)} %bitcast.26, f32[384]{0:T(512)S(1)} %copy-done.11, bf16[3,3,3,192,384]{4,3,2,1,0:T(8,128)(2,1)S(1)} %bitcast.23), custom_call_target="tpu_custom_call" | custom-call | flops 2548039680 | bytes 3981312 | tf_op jit(solution)/shard_map/mid_rim/pallas_call | solution.py:238
  16.4 1.4 %collective-permute-start.2 = (bf16[320,384]{1,0:T(8,128)(2,1)S(1)}, bf16[320,384]{1,0:T(8,128)(2,1)S(1)}, u32[]{:S(2)}, u32[]{:S(2)}) collective-permute-start(bf16[320,384]{1,0:T(8,128)(2,1)S(1)} %get-tuple-element.40), channel_id=1, source_target_pairs={{0,2},{1,3},{4,6},{5,7},{8,10},{9,11},{12,14},{13,15},{16,18},{17,... | collective-permute-start | bytes 737288 | tf_op jit(solution)/shard_map/ppermute | solution.py:676
  17.9 2.5 %all-gather.1 = bf16[8,160,384]{2,1,0:T(8,128)(2,1)S(1)} all-gather(bf16[4,160,384]{2,1,0:T(8,128)(2,1)S(1)} %collective-permute-done.1), channel_id=3, replica_groups=mesh['groups'=2,'rows'=4,'segment'=2,'chan'=2] {'chan'}, dimensions={0}, use_global_device_ids=true | all-gather | bytes 1474560 | tf_op jit(solution)/shard_map/all_gather | solution.py:709
  20.4 1.4 %weight_forms.1 = (bf16[2,2,96,1536]{3,2,1,0:T(8,128)(2,1)S(1)}, bf16[576,2304]{1,0:T(8,128)(2,1)S(1)}) custom-call(bf16[3,3,96,384]{3,2,1,0:T(8,128)(2,1)S(1)} %bitcast.25, bf16[3,3,3,192,96]{4,3,2,1,0:T(8,128)(2,1)S(1)} %copy-done.5), custom_call_target="tpu_custom_call" | custom-call | flops 95551488 | bytes 6635520 | tf_op jit(solution)/shard_map/weight_forms/pallas_call | solution.py:138
  21.9 5.6 %collective-permute-done.2.arrived = bf16[320,384]{1,0:T(8,128)(2,1)S(1)} collective-permute-done((bf16[320,384]{1,0:T(8,128)(2,1)S(1)}, bf16[320,384]{1,0:T(8,128)(2,1)S(1)}, u32[]{:S(2)}, u32[]{:S(2)}) %collective-permute-start.2) | collective-permute-done | bytes 245792 | tf_op jit(solution)/shard_map/ppermute | solution.py:676
  27.5 2.3 %all-gather.2 = bf16[640,384]{1,0:T(8,128)(2,1)S(1)} all-gather(bf16[320,384]{1,0:T(8,128)(2,1)S(1)} %join.1), channel_id=4, replica_groups=mesh['groups'=2,'rows'=4,'segment'=2,'chan'=2] {'chan'}, dimensions={0}, use_global_device_ids=true | all-gather | bytes 737280 | tf_op jit(solution)/shard_map/all_gather | solution.py:714
  30.0 0.2 maximum_select_fusion.refs_0_.own
  30.2 0.2 collective-permute-start.5
  30.4 0.3 collective-permute-start.6
  30.7 1.8 %collective-permute-start.4 = (bf16[320,384]{1,0:T(8,128)(2,1)S(1)}, bf16[320,384]{1,0:T(8,128)(2,1)S(1)}, u32[]{:S(2)}, u32[]{:S(2)}) collective-permute-start(bf16[320,384]{1,0:T(8,128)(2,1)S(1)} %maximum_select_fusion.refs_0_.own), channel_id=1, source_target_pairs={{0,12},{4,0},{8,4},{12,8},{1,13},{5,1},{9,5},{13,9},{2,14},{6,2},{... | collective-permute-start | bytes 737288 | tf_op jit(solution)/shard_map/ppermute | solution.py:725
  32.5 0.2 collective-permute-start.3
  32.7 0.2 low_cached.1.cached
  33.0 0.5 block_keys.2
  33.5 14.1 %collective-permute-done.6.refs_0_ = bf16[320,384]{1,0:T(8,128)(2,1)S(1)} collective-permute-done((bf16[320,384]{1,0:T(8,128)(2,1)S(1)}, bf16[320,384]{1,0:T(8,128)(2,1)S(1)}, u32[]{:S(2)}, u32[]{:S(2)}) %collective-permute-start.6) | collective-permute-done | bytes 245792 | tf_op jit(solution)/shard_map/ppermute | solution.py:725
  47.5 0.5 block_keys.3
  48.2 6.1 %collective-permute-done.4.after = bf16[320,384]{1,0:T(8,128)(2,1)S(1)} collective-permute-done((bf16[320,384]{1,0:T(8,128)(2,1)S(1)}, bf16[320,384]{1,0:T(8,128)(2,1)S(1)}, u32[]{:S(2)}, u32[]{:S(2)}) %collective-permute-start.4) | collective-permute-done | bytes 245792 | tf_op jit(solution)/shard_map/ppermute | solution.py:725
  54.3 4.4 %frame_attention.1 = bf16[4,160,384]{2,1,0:T(8,128)(2,1)S(1)} custom-call(f32[384]{0:T(512)S(1)} %copy-done.8, bf16[384,1152]{1,0:T(8,128)(2,1)S(1)} %copy-done.3, bf16[384,384]{1,0:T(8,128)(2,1)S(1)} %copy-done.10, bf16[320,384]{1,0:T(8,128)(2,1)S(1)} %maximum_select_fusion.refs_0_.own, bf16[320,384]{1,0:T(8,128)(2,1)S(1)} %collective-permute-done.3.before, ...), custom_call_target="tpu_custom_call" | custom-call | flops 1635778560 | bytes 884736 | tf_op jit(solution)/shard_map/frame_attention/pallas_call | solution.py:362
  58.7 2.5 %all-gather.3 = bf16[8,160,384]{2,1,0:T(8,128)(2,1)S(1)} all-gather(bf16[4,160,384]{2,1,0:T(8,128)(2,1)S(1)} %frame_attention.1), channel_id=5, replica_groups=mesh['groups'=2,'rows'=4,'segment'=2,'chan'=2] {'chan'}, dimensions={0}, use_global_device_ids=true | all-gather | bytes 1474560 | tf_op jit(solution)/shard_map/all_gather | solution.py:736
  61.2 4.5 %low_last.1 = (bf16[192,640]{1,0:T(8,128)(2,1)S(1)}, f32[1,192,640]{2,1,0:T(8,128)S(1)}, bf16[1,6,160,768]{3,2,1,0:T(8,128)(2,1)S(1)}, bf16[1,4,160,384]{3,2,1,0:T(8,128)(2,1)S(1)}) custom-call(bf16[2,4,160,384]{3,2,1,0:T(8,128)(2,1)S(1)} %bitcast.18, bf16[2,2,192,1536]{3,2,1,0:T(8,128)(2,1)S(1)} %joined_up.1.up, f32[192]{0:T(256)S(1)} %copy-done.9, ...), custom_call_target="tpu_custom_call" | custom-call | flops 1132462080 | bytes 2654208 | tf_op jit(solution)/shard_map/low_last/pallas_call | solution.py:476
  65.7 1.5 %collective-permute-start.7 = (bf16[192,640]{1,0:T(8,128)(2,1)S(1)}, bf16[192,640]{1,0:T(8,128)(2,1)S(1)}, u32[]{:S(2)}, u32[]{:S(2)}) collective-permute-start(bf16[192,640]{1,0:T(8,128)(2,1)S(1)} %get-tuple-element.65), channel_id=1, source_target_pairs={{0,2},{1,3},{4,6},{5,7},{8,10},{9,11},{12,14},{13,15},{16,18},{17,... | collective-permute-start | bytes 737288 | tf_op jit(solution)/shard_map/ppermute | solution.py:676
  67.2 3.4 %low_early.1 = (bf16[1,192,640]{2,1,0:T(8,128)(2,1)S(1)}, bf16[1,6,160,768]{3,2,1,0:T(8,128)(2,1)S(1)}, bf16[1,4,160,384]{3,2,1,0:T(8,128)(2,1)S(1)}) custom-call(bf16[2,4,160,384]{3,2,1,0:T(8,128)(2,1)S(1)} %bitcast.19, bf16[2,2,192,1536]{3,2,1,0:T(8,128)(2,1)S(1)} %joined_up.1.up, f32[192]{0:T(256)S(1)} %copy-done.9, ...), custom_call_target="tpu_custom_call" | custom-call | flops 1132462080 | bytes 2654208 | tf_op jit(solution)/shard_map/low_early/pallas_call | solution.py:497
  70.6 1.3 %collective-permute-start.8 = (bf16[1,192,640]{2,1,0:T(8,128)(2,1)S(1)}, bf16[1,192,640]{2,1,0:T(8,128)(2,1)S(1)}, u32[]{:S(2)}, u32[]{:S(2)}) collective-permute-start(bf16[1,192,640]{2,1,0:T(8,128)(2,1)S(1)} %get-tuple-element.67), channel_id=1, source_target_pairs={{0,2},{1,3},{4,6},{5,7},{8,10},{9,11},{12,14},{13,15},{16,18},{17,... | collective-permute-start | bytes 737288 | tf_op jit(solution)/shard_map/ppermute | solution.py:676
  71.9 3.9 %collective-permute-done.7.arrived = bf16[192,640]{1,0:T(8,128)(2,1)S(1)} collective-permute-done((bf16[192,640]{1,0:T(8,128)(2,1)S(1)}, bf16[192,640]{1,0:T(8,128)(2,1)S(1)}, u32[]{:S(2)}, u32[]{:S(2)}) %collective-permute-start.7) | collective-permute-done | bytes 245792 | tf_op jit(solution)/shard_map/ppermute | solution.py:676
  75.8 3.1 %low_own.1 = (f32[2,192,640]{2,1,0:T(8,128)S(1)}, bf16[4,512,320]{2,1,0:T(8,128)(2,1)S(1)}) custom-call(bf16[1,6,160,768]{3,2,1,0:T(8,128)(2,1)S(1)} %get-tuple-element.60.early, bf16[1,6,160,768]{3,2,1,0:T(8,128)(2,1)S(1)} %get-tuple-element.61.last, bf16[1,4,160,384]{3,2,1,0:T(8,128)(2,1)S(1)} %get-tuple-element.62.early_kept, ...), custom_call_target="tpu_custom_call" | custom-call | flops 2548039680 | bytes 2654208 | tf_op jit(solution)/shard_map/low_own/pallas_call | solution.py:551
  79.0 1.9 %collective-permute-done.8.arrived = bf16[1,192,640]{2,1,0:T(8,128)(2,1)S(1)} collective-permute-done((bf16[1,192,640]{2,1,0:T(8,128)(2,1)S(1)}, bf16[1,192,640]{2,1,0:T(8,128)(2,1)S(1)}, u32[]{:S(2)}, u32[]{:S(2)}) %collective-permute-start.8) | collective-permute-done | bytes 245792 | tf_op jit(solution)/shard_map/ppermute | solution.py:676
  80.8 1.4 %finish.1 = bf16[2,4,96,320]{3,2,1,0:T(8,128)(2,1)} custom-call(f32[2,192,640]{2,1,0:T(8,128)S(1)} %get-tuple-element.66.own, bf16[1,192,640]{2,1,0:T(8,128)(2,1)S(1)} %collective-permute-done.8.arrived, bf16[4,512,320]{2,1,0:T(8,128)(2,1)S(1)} %get-tuple-element.68.weave), custom_call_target="tpu_custom_call" | custom-call | flops 251658240 | bytes 983040 | tf_op jit(solution)/shard_map/finish/pallas_call | solution.py:632
  (31 shorter events, 0.5 us)
Async XLA Ops:
  0.0 6.6 %copy-start.7 = (bf16[2,2,160,384]{3,2,1,0:T(8,128)(2,1)S(1)}, bf16[2,2,160,384]{3,2,1,0:T(8,128)(2,1)}, u32[]{:S(2)}) copy-start(bf16[2,2,160,384]{3,2,1,0:T(8,128)(2,1)} %latent.3) | copy-start | bytes 1474564
  0.0 6.7 %copy-start.11 = (f32[384]{0:T(512)S(1)}, f32[384]{0:T(512)}, u32[]{:S(2)}) copy-start(f32[384]{0:T(512)} %gain.8) | copy-start | bytes 4612
  2.4 9.6 %collective-permute-start = (bf16[2,160,384]{2,1,0:T(8,128)(2,1)}, bf16[2,160,384]{2,1,0:T(8,128)(2,1)S(1)}, u32[]{:S(2)}, u32[]{:S(2)}) collective-permute-start(bf16[2,160,384]{2,1,0:T(8,128)(2,1)} %get-tuple-element.37), channel_id=1, source_target_pairs={{0,4},{5,1},{2,6},{7,3},{4,8},{9,5},{6,10},{11,7},{8,12},{13,9},{1... | collective-permute-start | bytes 737288 | tf_op jit(solution)/shard_map/ppermute | solution.py:671
  5.9 10.5 %collective-permute-start.1 = (bf16[4,160,384]{2,1,0:T(8,128)(2,1)}, bf16[4,160,384]{2,1,0:T(8,128)(2,1)S(1)}, u32[]{:S(2)}, u32[]{:S(2)}) collective-permute-start(bf16[4,160,384]{2,1,0:T(8,128)(2,1)} %get-tuple-element.39), channel_id=1, source_target_pairs={{0,4},{5,1},{4,8},{9,5},{8,12},{13,9},{16,20},{21,17},{20,24},{25,... | collective-permute-start | bytes 1474568 | tf_op jit(solution)/shard_map/ppermute | solution.py:671
  6.7 2.1 %copy-start.1 = (bf16[3,3,3,384,192]{3,4,2,1,0:T(8,128)(2,1)S(1)}, bf16[3,3,3,384,192]{3,4,2,1,0:T(8,128)(2,1)}, u32[]{:S(2)}) copy-start(bf16[3,3,3,384,192]{3,4,2,1,0:T(8,128)(2,1)} %param.17) | copy-start | bytes 11943940
  14.2 6.1 %copy-start.6 = (bf16[3,3,384,96]{2,3,1,0:T(8,128)(2,1)S(1)}, bf16[3,3,384,96]{2,3,1,0:T(8,128)(2,1)}, u32[]{:S(2)}) copy-start(bf16[3,3,384,96]{2,3,1,0:T(8,128)(2,1)} %param.20) | copy-start | bytes 1990660
  14.2 7.5 %copy-start.2 = (bf16[3,3,3,384,192]{3,4,2,1,0:T(8,128)(2,1)S(1)}, bf16[3,3,3,384,192]{3,4,2,1,0:T(8,128)(2,1)}, u32[]{:S(2)}) copy-start(bf16[3,3,3,384,192]{3,4,2,1,0:T(8,128)(2,1)} %param.17) | copy-start | bytes 11943940
  16.4 4.0 %copy-start.5 = (bf16[3,3,3,192,96]{4,3,2,1,0:T(8,128)(2,1)S(1)}, bf16[3,3,3,192,96]{4,3,2,1,0:T(8,128)(2,1)}, u32[]{:S(2)}) copy-start(bf16[3,3,3,192,96]{4,3,2,1,0:T(8,128)(2,1)} %low) | copy-start | bytes 2985988
  16.4 5.4 %copy-start.4 = (bf16[2,2,160,384]{3,2,1,0:T(8,128)(2,1)S(1)}, bf16[2,2,160,384]{3,2,1,0:T(8,128)(2,1)}, u32[]{:S(2)}) copy-start(bf16[2,2,160,384]{3,2,1,0:T(8,128)(2,1)} %cache.3) | copy-start | bytes 1474564
  16.4 11.0 %collective-permute-start.2 = (bf16[320,384]{1,0:T(8,128)(2,1)S(1)}, bf16[320,384]{1,0:T(8,128)(2,1)S(1)}, u32[]{:S(2)}, u32[]{:S(2)}) collective-permute-start(bf16[320,384]{1,0:T(8,128)(2,1)S(1)} %get-tuple-element.40), channel_id=1, source_target_pairs={{0,2},{1,3},{4,6},{5,7},{8,10},{9,11},{12,14},{13,15},{16,18},{17,... | collective-permute-start | bytes 737288 | tf_op jit(solution)/shard_map/ppermute | solution.py:676
  27.5 5.2 %copy-start = (bf16[2,4,320,192]{2,3,1,0:T(8,128)(2,1)S(1)}, bf16[2,4,320,192]{2,3,1,0:T(8,128)(2,1)}, u32[]{:S(2)}) copy-start(bf16[2,4,320,192]{2,3,1,0:T(8,128)(2,1)} %param.13) | copy-start | bytes 2949124
  30.1 2.8 %copy-start.3 = (bf16[384,1152]{1,0:T(8,128)(2,1)S(1)}, bf16[384,1152]{1,0:T(8,128)(2,1)}, u32[]{:S(2)}) copy-start(bf16[384,1152]{1,0:T(8,128)(2,1)} %qkv.5) | copy-start | bytes 2654212
  30.2 2.8 %copy-start.8 = (f32[384]{0:T(512)S(1)}, f32[384]{0:T(512)}, u32[]{:S(2)}) copy-start(f32[384]{0:T(512)} %gain.11) | copy-start | bytes 4612
  30.2 17.9 %collective-permute-start.5 = (bf16[2,2,96,1536]{3,2,1,0:T(8,128)(2,1)S(1)}, bf16[2,2,96,1536]{3,2,1,0:T(8,128)(2,1)S(1)}, u32[]{:S(2)}, u32[]{:S(2)}) collective-permute-start(bf16[2,2,96,1536]{3,2,1,0:T(8,128)(2,1)S(1)} %get-tuple-element.51.mine), channel_id=1, source_target_pairs={{0,1},{1,0},{2,3},{3,2},{4,5},{5,4},{6,7},{7,6},{8,9},{9,8},{10,11... | collective-permute-start | bytes 3538952 | tf_op jit(solution)/shard_map/ppermute | solution.py:728
  30.4 17.2 %collective-permute-start.6 = (bf16[320,384]{1,0:T(8,128)(2,1)S(1)}, bf16[320,384]{1,0:T(8,128)(2,1)S(1)}, u32[]{:S(2)}, u32[]{:S(2)}) collective-permute-start(bf16[320,384]{1,0:T(8,128)(2,1)S(1)} %maximum_select_fusion.refs_0_.own), channel_id=1, source_target_pairs={{0,8},{4,12},{8,0},{12,4},{1,9},{5,13},{9,1},{13,5},{2,10},{6,14},... | collective-permute-start | bytes 737288 | tf_op jit(solution)/shard_map/ppermute | solution.py:725
  30.7 23.7 %collective-permute-start.4 = (bf16[320,384]{1,0:T(8,128)(2,1)S(1)}, bf16[320,384]{1,0:T(8,128)(2,1)S(1)}, u32[]{:S(2)}, u32[]{:S(2)}) collective-permute-start(bf16[320,384]{1,0:T(8,128)(2,1)S(1)} %maximum_select_fusion.refs_0_.own), channel_id=1, source_target_pairs={{0,12},{4,0},{8,4},{12,8},{1,13},{5,1},{9,5},{13,9},{2,14},{6,2},{... | collective-permute-start | bytes 737288 | tf_op jit(solution)/shard_map/ppermute | solution.py:725
  32.5 21.9 %collective-permute-start.3 = (bf16[320,384]{1,0:T(8,128)(2,1)S(1)}, bf16[320,384]{1,0:T(8,128)(2,1)S(1)}, u32[]{:S(2)}, u32[]{:S(2)}) collective-permute-start(bf16[320,384]{1,0:T(8,128)(2,1)S(1)} %maximum_select_fusion.refs_0_.own), channel_id=1, source_target_pairs={{0,4},{4,8},{8,12},{12,0},{1,5},{5,9},{9,13},{13,1},{2,6},{6,10},{... | collective-permute-start | bytes 737288 | tf_op jit(solution)/shard_map/ppermute | solution.py:725
  48.0 6.3 %copy-start.10 = (bf16[384,384]{1,0:T(8,128)(2,1)S(1)}, bf16[384,384]{1,0:T(8,128)(2,1)}, u32[]{:S(2)}) copy-start(bf16[384,384]{1,0:T(8,128)(2,1)} %proj.1) | copy-start | bytes 884740
  58.7 2.5 %copy-start.9 = (f32[192]{0:T(256)S(1)}, f32[192]{0:T(256)}, u32[]{:S(2)}) copy-start(f32[192]{0:T(256)} %gain.13) | copy-start | bytes 2308
  65.7 10.1 %collective-permute-start.7 = (bf16[192,640]{1,0:T(8,128)(2,1)S(1)}, bf16[192,640]{1,0:T(8,128)(2,1)S(1)}, u32[]{:S(2)}, u32[]{:S(2)}) collective-permute-start(bf16[192,640]{1,0:T(8,128)(2,1)S(1)} %get-tuple-element.65), channel_id=1, source_target_pairs={{0,2},{1,3},{4,6},{5,7},{8,10},{9,11},{12,14},{13,15},{16,18},{17,... | collective-permute-start | bytes 737288 | tf_op jit(solution)/shard_map/ppermute | solution.py:676
  70.6 10.2 %collective-permute-start.8 = (bf16[1,192,640]{2,1,0:T(8,128)(2,1)S(1)}, bf16[1,192,640]{2,1,0:T(8,128)(2,1)S(1)}, u32[]{:S(2)}, u32[]{:S(2)}) collective-permute-start(bf16[1,192,640]{2,1,0:T(8,128)(2,1)S(1)} %get-tuple-element.67), channel_id=1, source_target_pairs={{0,2},{1,3},{4,6},{5,7},{8,10},{9,11},{12,14},{13,15},{16,18},{17,... | collective-permute-start | bytes 737288 | tf_op jit(solution)/shard_map/ppermute | solution.py:676

commit v12 on v11

--- a/solution.py
+++ b/solution.py
@@ -212,44 +212,44 @@
     )(latent, gain, weights)
 
 
-def mid_rim_kernel(started, halo, gain, weights, own, passed, seen, acc):
+def mid_rim_kernel(onward, started, halo, gain, weights, out, seen, acc):
     total, size, part = started.shape
     taps = weights.shape[0]
     past = taps - 1
     frames = total - past
+    targets = range(frames, total) if onward else range(frames)
     for side in range(2):
         for f in range(frames):
             seen[side, f] = spread(silu(normed(halo[side, f].astype(F32), gain[...])))
-    acc[...] = started[...]
+    for t in targets:
+        acc[t] = started[t]
     for tap in range(taps):
+        pairs = [(f, f + past - tap) for f in range(frames) if f + past - tap in targets]
         for side in range(2):
-            add_rims(acc, seen, weights, [(f, f + past - tap) for f in range(frames)], tap, side)
-
-    own[...] = jnp.concatenate([acc[f] for f in range(frames)], axis=-1)
-    passed[...] = jnp.concatenate([acc[frames + t] for t in range(past)], axis=-1).astype(BF16)
-
-
-def mid_rim(started, halo, gain, weights):
+            if pairs:
+                add_rims(acc, seen, weights, pairs, tap, side)
+    out[...] = jnp.concatenate([acc[t] for t in targets], axis=-1).astype(out.dtype)
+
+
+def mid_rim(started, halo, gain, weights, onward):
     total, size, part = started.shape
     taps = weights.shape[0]
     past = taps - 1
     frames = total - past
     sides, _, width, channels = halo.shape
-    return pl.pallas_call(
-        mid_rim_kernel,
+    shape = (size, (past if onward else frames) * part)
+    return pl.pallas_call(
+        functools.partial(mid_rim_kernel, onward),
         in_specs=[vmem()] * 4,
-        out_specs=[vmem(), vmem()],
-        out_shape=[
-            jax.ShapeDtypeStruct((size, frames * part), F32),
-            jax.ShapeDtypeStruct((size, past * part), BF16),
-        ],
+        out_specs=vmem(),
+        out_shape=jax.ShapeDtypeStruct(shape, BF16 if onward else F32),
         scratch_shapes=[
             pltpu.VMEM((2, frames, width, 3 * channels), BF16),
             pltpu.VMEM(started.shape, F32),
         ],
         compiler_params=pltpu.CompilerParams(vmem_limit_bytes=room(5 * halo.nbytes + 3 * started.nbytes)),
-        cost_estimate=cost(2 * 18 * frames * width * channels * part * taps, weights.nbytes),
-        name="mid_rim",
+        cost_estimate=cost(9 * frames * width * channels * part * taps * 2, weights.nbytes),
+        name="mid_rim_next" if onward else "mid_rim_own",
     )(started, halo, gain, weights)
 
 
@@ -703,9 +703,11 @@
     cache_rim = to_neighbour(cache_rim, True)
     started = mid_inner(latent, gain_mid, mid_weights)
     halo = lax.all_gather(rim, "chan")
-    own, passed = mid_rim(started, halo, gain_mid, mid_weights)
+    passed = mid_rim(started, halo, gain_mid, mid_weights, True)
     passed, cache_rim, conv_up, conv_low = lax.optimization_barrier((passed, cache_rim, conv_up, conv_low))
+    passed, started = lax.optimization_barrier((passed, started))
     arrived = to_next(passed)
+    own = mid_rim(started, halo, gain_mid, mid_weights, False)
     cache_halo = lax.all_gather(cache_rim, "chan")
     own = mid_cached(own, cache_mid, cache_halo, mid_weights)
     up_mine, low_weights = weight_forms(jnp.swapaxes(conv_up, 2, 3), conv_low)

time: 82.5 us -> 83.9 us (1.017)
  the two profiles are of different devices: /device:TPU:10 before, /device:TPU:18 now
where the time goes in v12:
time: 83.9 us; the launch traced here: 83.6 us
  waiting for transfers between devices  31.6 us (38%)
  Pallas kernels  28 us (33%)
  starting transfers between devices  11.7 us (14%)
  blocking collectives  9.47 us (11%)
  local copies, waits for them, and re-layouts  2.34 us (3%)
    ppermute x3, waiting for transfers between devices, body(): lax.ppermute(mine, 'rows', [(i, (i + k) % depth) for i in range(depth)])  20.5 us
    ppermute x3, waiting for transfers between devices, to_next(): lax.ppermute(values, 'segment', [(i, i + 1) for i in range(count - 1)])  11.2 us
    pallas_call x1, Pallas kernels, low_last(): pl.pallas_call(functools.partial(low_last_kernel, frames, past), in_specs...  4.46 us
    pallas_call x1, Pallas kernels, attention(): pl.pallas_call(functools.partial(attn_kernel, count, width), in_specs=[vm...  4.35 us
    ppermute x3, starting transfers between devices, to_next(): lax.ppermute(values, 'segment', [(i, i + 1) for i in range(count - 1)])  4.23 us
    ppermute x2, starting transfers between devices, to_neighbour(): return lax.ppermute(values, ('rows', 'segment', 'chan'), route)  4.17 us
    pallas_call x1, Pallas kernels, low_early(): pl.pallas_call(functools.partial(low_early_kernel, frames, past), in_spec...  3.41 us
    pallas_call x1, Pallas kernels, mid_inner(): pl.pallas_call(mid_inner_kernel, in_specs=[vmem()] * 3, out_specs=vmem(),...  3.26 us
  transfers between devices with their start and end apart: 9, of which 6 were waited for; matrix products, arithmetic and copies ran while one was open for 0% of the time, Pallas kernels for 18%

profile of v12, /device:TPU:18, one launch (start us, length us, event | category | flops | bytes accessed | tf_op | source)
XLA Modules:
  0.0 83.6 jit_solution(9425297877781196338)
XLA Ops:
  0.0 2.4 %edge_rows.1 = (bf16[2,160,384]{2,1,0:T(8,128)(2,1)}, bf16[4,160,384]{2,1,0:T(8,128)(2,1)}) custom-call(bf16[2,2,160,384]{3,2,1,0:T(8,128)(2,1)} %latent.3, bf16[2,2,160,384]{3,2,1,0:T(8,128)(2,1)} %cache.3, bf16[2,4,192,320]{3,2,1,0:T(8,128)(2,1)} %bitcast.24), custom_call_target="tpu_custom_call" | custom-call | bytes 1966080 | tf_op jit(solution)/shard_map/edge_rows/pallas_call | solution.py:98
  2.4 0.7 collective-permute-start.1
  3.1 3.5 %collective-permute-start = (bf16[2,160,384]{2,1,0:T(8,128)(2,1)}, bf16[2,160,384]{2,1,0:T(8,128)(2,1)S(1)}, u32[]{:S(2)}, u32[]{:S(2)}) collective-permute-start(bf16[2,160,384]{2,1,0:T(8,128)(2,1)} %get-tuple-element.37), channel_id=1, source_target_pairs={{0,4},{5,1},{2,6},{7,3},{4,8},{9,5},{6,10},{11,7},{8,12},{13,9},{1... | collective-permute-start | bytes 737288 | tf_op jit(solution)/shard_map/ppermute | solution.py:671
  6.7 2.1 %copy-done = bf16[3,3,3,384,192]{3,4,2,1,0:T(8,128)(2,1)S(1)} copy-done((bf16[3,3,3,384,192]{3,4,2,1,0:T(8,128)(2,1)S(1)}, bf16[3,3,3,384,192]{3,4,2,1,0:T(8,128)(2,1)}, u32[]{:S(2)}) %copy-start) | copy-done | bytes 3981336
  8.8 3.3 %mid_inner.1.started = f32[4,320,192]{2,1,0:T(8,128)S(1)} custom-call(bf16[2,2,160,384]{3,2,1,0:T(8,128)(2,1)S(1)} %copy-done.7, f32[384]{0:T(512)S(1)} %copy-done.8, bf16[3,3,3,192,384]{4,3,2,1,0:T(8,128)(2,1)S(1)} %bitcast.16), custom_call_target="tpu_custom_call" | custom-call | flops 2548039680 | bytes 3981312 | tf_op jit(solution)/shard_map/mid_inner/pallas_call | solution.py:203
  12.1 2.2 %all-gather = bf16[4,160,384]{2,1,0:T(8,128)(2,1)S(1)} all-gather(bf16[2,160,384]{2,1,0:T(8,128)(2,1)S(1)} %collective-permute-done), channel_id=2, replica_groups=mesh['groups'=2,'rows'=4,'segment'=2,'chan'=2] {'chan'}, dimensions={0}, use_global_device_ids=true | all-gather | bytes 737280 | tf_op jit(solution)/shard_map/all_gather | solution.py:705
  14.2 1.4 %mid_rim_next.1 = bf16[320,384]{1,0:T(8,128)(2,1)S(1)} custom-call(f32[4,320,192]{2,1,0:T(8,128)S(1)} %mid_inner.1.started, bf16[2,2,160,384]{3,2,1,0:T(8,128)(2,1)S(1)} %bitcast.26, f32[384]{0:T(512)S(1)} %copy-done.8, bf16[3,3,3,192,384]{4,3,2,1,0:T(8,128)(2,1)S(1)} %bitcast.17), custom_call_target="tpu_custom_call" | custom-call | flops 1274019840 | bytes 3981312 | tf_op jit(solution)/shard_map/mid_rim_next/pallas_call | solution.py:241
  15.6 1.4 %collective-permute-start.2 = (bf16[320,384]{1,0:T(8,128)(2,1)S(1)}, bf16[320,384]{1,0:T(8,128)(2,1)S(1)}, u32[]{:S(2)}, u32[]{:S(2)}) collective-permute-start(bf16[320,384]{1,0:T(8,128)(2,1)S(1)} %mid_rim_next.1), channel_id=1, source_target_pairs={{0,2},{1,3},{4,6},{5,7},{8,10},{9,11},{12,14},{13,15},{16,18},{17,... | collective-permute-start | bytes 737288 | tf_op jit(solution)/shard_map/ppermute | solution.py:676
  17.1 2.5 %all-gather.1 = bf16[8,160,384]{2,1,0:T(8,128)(2,1)S(1)} all-gather(bf16[4,160,384]{2,1,0:T(8,128)(2,1)S(1)} %collective-permute-done.1), channel_id=3, replica_groups=mesh['groups'=2,'rows'=4,'segment'=2,'chan'=2] {'chan'}, dimensions={0}, use_global_device_ids=true | all-gather | bytes 1474560 | tf_op jit(solution)/shard_map/all_gather | solution.py:711
  19.6 1.4 %weight_forms.1 = (bf16[2,2,96,1536]{3,2,1,0:T(8,128)(2,1)S(1)}, bf16[576,2304]{1,0:T(8,128)(2,1)S(1)}) custom-call(bf16[3,3,96,384]{3,2,1,0:T(8,128)(2,1)S(1)} %bitcast.28, bf16[3,3,3,192,96]{4,3,2,1,0:T(8,128)(2,1)S(1)} %copy-done.5), custom_call_target="tpu_custom_call" | custom-call | flops 95551488 | bytes 6635520 | tf_op jit(solution)/shard_map/weight_forms/pallas_call | solution.py:138
  21.0 1.3 %mid_rim_own.1.own = f32[320,384]{1,0:T(8,128)S(1)} custom-call(f32[4,320,192]{2,1,0:T(8,128)S(1)} %mid_inner.1.started, bf16[2,2,160,384]{3,2,1,0:T(8,128)(2,1)S(1)} %bitcast.27, f32[384]{0:T(512)S(1)} %copy-done.8, bf16[3,3,3,192,384]{4,3,2,1,0:T(8,128)(2,1)S(1)} %bitcast.18), custom_call_target="tpu_custom_call" | custom-call | flops 1274019840 | bytes 3981312 | tf_op jit(solution)/shard_map/mid_rim_own/pallas_call | solution.py:241
  22.4 5.4 %collective-permute-done.2.arrived = bf16[320,384]{1,0:T(8,128)(2,1)S(1)} collective-permute-done((bf16[320,384]{1,0:T(8,128)(2,1)S(1)}, bf16[320,384]{1,0:T(8,128)(2,1)S(1)}, u32[]{:S(2)}, u32[]{:S(2)}) %collective-permute-start.2) | collective-permute-done | bytes 245792 | tf_op jit(solution)/shard_map/ppermute | solution.py:676
  27.8 2.3 %all-gather.2 = bf16[640,384]{1,0:T(8,128)(2,1)S(1)} all-gather(bf16[320,384]{1,0:T(8,128)(2,1)S(1)} %join.1), channel_id=4, replica_groups=mesh['groups'=2,'rows'=4,'segment'=2,'chan'=2] {'chan'}, dimensions={0}, use_global_device_ids=true | all-gather | bytes 737280 | tf_op jit(solution)/shard_map/all_gather | solution.py:716
  30.3 0.2 maximum_select_fusion.refs_0_.own
  30.5 0.2 collective-permute-start.5
  30.7 3.1 %collective-permute-start.4 = (bf16[320,384]{1,0:T(8,128)(2,1)S(1)}, bf16[320,384]{1,0:T(8,128)(2,1)S(1)}, u32[]{:S(2)}, u32[]{:S(2)}) collective-permute-start(bf16[320,384]{1,0:T(8,128)(2,1)S(1)} %maximum_select_fusion.refs_0_.own), channel_id=1, source_target_pairs={{0,12},{4,0},{8,4},{12,8},{1,13},{5,1},{9,5},{13,9},{2,14},{6,2},{... | collective-permute-start | bytes 737288 | tf_op jit(solution)/shard_map/ppermute | solution.py:727
  33.8 0.2 low_cached.1.cached
  34.0 0.5 block_keys.2
  34.5 7.8 %collective-permute-done.6.refs_0_ = bf16[320,384]{1,0:T(8,128)(2,1)S(1)} collective-permute-done((bf16[320,384]{1,0:T(8,128)(2,1)S(1)}, bf16[320,384]{1,0:T(8,128)(2,1)S(1)}, u32[]{:S(2)}, u32[]{:S(2)}) %collective-permute-start.6) | collective-permute-done | bytes 245792 | tf_op jit(solution)/shard_map/ppermute | solution.py:727
  42.4 0.5 block_keys.3
  43.1 9.5 %collective-permute-done.4.after = bf16[320,384]{1,0:T(8,128)(2,1)S(1)} collective-permute-done((bf16[320,384]{1,0:T(8,128)(2,1)S(1)}, bf16[320,384]{1,0:T(8,128)(2,1)S(1)}, u32[]{:S(2)}, u32[]{:S(2)}) %collective-permute-start.4) | collective-permute-done | bytes 245792 | tf_op jit(solution)/shard_map/ppermute | solution.py:727
  52.6 3.1 %collective-permute-done.3.before = bf16[320,384]{1,0:T(8,128)(2,1)S(1)} collective-permute-done((bf16[320,384]{1,0:T(8,128)(2,1)S(1)}, bf16[320,384]{1,0:T(8,128)(2,1)S(1)}, u32[]{:S(2)}, u32[]{:S(2)}) %collective-permute-start.3) | collective-permute-done | bytes 245792 | tf_op jit(solution)/shard_map/ppermute | solution.py:727
  55.7 4.4 %frame_attention.1 = bf16[4,160,384]{2,1,0:T(8,128)(2,1)S(1)} custom-call(f32[384]{0:T(512)S(1)} %copy-done.9, bf16[384,1152]{1,0:T(8,128)(2,1)S(1)} %copy-done.3, bf16[384,384]{1,0:T(8,128)(2,1)S(1)} %copy-done.11, bf16[320,384]{1,0:T(8,128)(2,1)S(1)} %maximum_select_fusion.refs_0_.own, bf16[320,384]{1,0:T(8,128)(2,1)S(1)} %collective-permute-done.3.before, ...), custom_call_target="tpu_custom_call" | custom-call | flops 1635778560 | bytes 884736 | tf_op jit(solution)/shard_map/frame_attention/pallas_call | solution.py:362
  60.1 2.5 %all-gather.3 = bf16[8,160,384]{2,1,0:T(8,128)(2,1)S(1)} all-gather(bf16[4,160,384]{2,1,0:T(8,128)(2,1)S(1)} %frame_attention.1), channel_id=5, replica_groups=mesh['groups'=2,'rows'=4,'segment'=2,'chan'=2] {'chan'}, dimensions={0}, use_global_device_ids=true | all-gather | bytes 1474560 | tf_op jit(solution)/shard_map/all_gather | solution.py:738
  62.6 4.5 %low_last.1 = (bf16[192,640]{1,0:T(8,128)(2,1)S(1)}, f32[1,192,640]{2,1,0:T(8,128)S(1)}, bf16[1,6,160,768]{3,2,1,0:T(8,128)(2,1)S(1)}, bf16[1,4,160,384]{3,2,1,0:T(8,128)(2,1)S(1)}) custom-call(bf16[2,4,160,384]{3,2,1,0:T(8,128)(2,1)S(1)} %bitcast.22, bf16[2,2,192,1536]{3,2,1,0:T(8,128)(2,1)S(1)} %joined_up.1.up, f32[192]{0:T(256)S(1)} %copy-done.10, ...), custom_call_target="tpu_custom_call" | custom-call | flops 1132462080 | bytes 2654208 | tf_op jit(solution)/shard_map/low_last/pallas_call | solution.py:476
  67.0 1.5 %collective-permute-start.7 = (bf16[192,640]{1,0:T(8,128)(2,1)S(1)}, bf16[192,640]{1,0:T(8,128)(2,1)S(1)}, u32[]{:S(2)}, u32[]{:S(2)}) collective-permute-start(bf16[192,640]{1,0:T(8,128)(2,1)S(1)} %get-tuple-element.65), channel_id=1, source_target_pairs={{0,2},{1,3},{4,6},{5,7},{8,10},{9,11},{12,14},{13,15},{16,18},{17,... | collective-permute-start | bytes 737288 | tf_op jit(solution)/shard_map/ppermute | solution.py:676
  68.6 3.4 %low_early.1 = (bf16[1,192,640]{2,1,0:T(8,128)(2,1)S(1)}, bf16[1,6,160,768]{3,2,1,0:T(8,128)(2,1)S(1)}, bf16[1,4,160,384]{3,2,1,0:T(8,128)(2,1)S(1)}) custom-call(bf16[2,4,160,384]{3,2,1,0:T(8,128)(2,1)S(1)} %bitcast.23, bf16[2,2,192,1536]{3,2,1,0:T(8,128)(2,1)S(1)} %joined_up.1.up, f32[192]{0:T(256)S(1)} %copy-done.10, ...), custom_call_target="tpu_custom_call" | custom-call | flops 1132462080 | bytes 2654208 | tf_op jit(solution)/shard_map/low_early/pallas_call | solution.py:497
  72.0 1.3 %collective-permute-start.8 = (bf16[1,192,640]{2,1,0:T(8,128)(2,1)S(1)}, bf16[1,192,640]{2,1,0:T(8,128)(2,1)S(1)}, u32[]{:S(2)}, u32[]{:S(2)}) collective-permute-start(bf16[1,192,640]{2,1,0:T(8,128)(2,1)S(1)} %get-tuple-element.67), channel_id=1, source_target_pairs={{0,2},{1,3},{4,6},{5,7},{8,10},{9,11},{12,14},{13,15},{16,18},{17,... | collective-permute-start | bytes 737288 | tf_op jit(solution)/shard_map/ppermute | solution.py:676
  73.3 3.9 %collective-permute-done.7.arrived = bf16[192,640]{1,0:T(8,128)(2,1)S(1)} collective-permute-done((bf16[192,640]{1,0:T(8,128)(2,1)S(1)}, bf16[192,640]{1,0:T(8,128)(2,1)S(1)}, u32[]{:S(2)}, u32[]{:S(2)}) %collective-permute-start.7) | collective-permute-done | bytes 245792 | tf_op jit(solution)/shard_map/ppermute | solution.py:676
  77.2 3.1 %low_own.1 = (f32[2,192,640]{2,1,0:T(8,128)S(1)}, bf16[4,512,320]{2,1,0:T(8,128)(2,1)S(1)}) custom-call(bf16[1,6,160,768]{3,2,1,0:T(8,128)(2,1)S(1)} %get-tuple-element.60.early, bf16[1,6,160,768]{3,2,1,0:T(8,128)(2,1)S(1)} %get-tuple-element.61.last, bf16[1,4,160,384]{3,2,1,0:T(8,128)(2,1)S(1)} %get-tuple-element.62.early_kept, ...), custom_call_target="tpu_custom_call" | custom-call | flops 2548039680 | bytes 2654208 | tf_op jit(solution)/shard_map/low_own/pallas_call | solution.py:551
  80.3 1.9 %collective-permute-done.8.arrived = bf16[1,192,640]{2,1,0:T(8,128)(2,1)S(1)} collective-permute-done((bf16[1,192,640]{2,1,0:T(8,128)(2,1)S(1)}, bf16[1,192,640]{2,1,0:T(8,128)(2,1)S(1)}, u32[]{:S(2)}, u32[]{:S(2)}) %collective-permute-start.8) | collective-permute-done | bytes 245792 | tf_op jit(solution)/shard_map/ppermute | solution.py:676
  82.2 1.4 %finish.1 = bf16[2,4,96,320]{3,2,1,0:T(8,128)(2,1)} custom-call(f32[2,192,640]{2,1,0:T(8,128)S(1)} %get-tuple-element.66.own, bf16[1,192,640]{2,1,0:T(8,128)(2,1)S(1)} %collective-permute-done.8.arrived, bf16[4,512,320]{2,1,0:T(8,128)(2,1)S(1)} %get-tuple-element.68.weave), custom_call_target="tpu_custom_call" | custom-call | flops 251658240 | bytes 983040 | tf_op jit(solution)/shard_map/finish/pallas_call | solution.py:632
  (32 shorter events, 0.5 us)
Async XLA Ops:
  0.0 6.6 %copy-start.7 = (bf16[2,2,160,384]{3,2,1,0:T(8,128)(2,1)S(1)}, bf16[2,2,160,384]{3,2,1,0:T(8,128)(2,1)}, u32[]{:S(2)}) copy-start(bf16[2,2,160,384]{3,2,1,0:T(8,128)(2,1)} %latent.3) | copy-start | bytes 1474564
  0.0 6.7 %copy-start.8 = (f32[384]{0:T(512)S(1)}, f32[384]{0:T(512)}, u32[]{:S(2)}) copy-start(f32[384]{0:T(512)} %gain.10) | copy-start | bytes 4612
  2.4 13.2 %collective-permute-start.1 = (bf16[4,160,384]{2,1,0:T(8,128)(2,1)}, bf16[4,160,384]{2,1,0:T(8,128)(2,1)S(1)}, u32[]{:S(2)}, u32[]{:S(2)}) collective-permute-start(bf16[4,160,384]{2,1,0:T(8,128)(2,1)} %get-tuple-element.38), channel_id=1, source_target_pairs={{0,4},{5,1},{4,8},{9,5},{8,12},{13,9},{16,20},{21,17},{20,24},{25,... | collective-permute-start | bytes 1474568 | tf_op jit(solution)/shard_map/ppermute | solution.py:671
  3.1 8.9 %collective-permute-start = (bf16[2,160,384]{2,1,0:T(8,128)(2,1)}, bf16[2,160,384]{2,1,0:T(8,128)(2,1)S(1)}, u32[]{:S(2)}, u32[]{:S(2)}) collective-permute-start(bf16[2,160,384]{2,1,0:T(8,128)(2,1)} %get-tuple-element.37), channel_id=1, source_target_pairs={{0,4},{5,1},{2,6},{7,3},{4,8},{9,5},{6,10},{11,7},{8,12},{13,9},{1... | collective-permute-start | bytes 737288 | tf_op jit(solution)/shard_map/ppermute | solution.py:671
  6.7 2.1 %copy-start = (bf16[3,3,3,384,192]{3,4,2,1,0:T(8,128)(2,1)S(1)}, bf16[3,3,3,384,192]{3,4,2,1,0:T(8,128)(2,1)}, u32[]{:S(2)}) copy-start(bf16[3,3,3,384,192]{3,4,2,1,0:T(8,128)(2,1)} %param.17) | copy-start | bytes 11943940
  14.2 5.4 %copy-start.6 = (bf16[3,3,384,96]{2,3,1,0:T(8,128)(2,1)S(1)}, bf16[3,3,384,96]{2,3,1,0:T(8,128)(2,1)}, u32[]{:S(2)}) copy-start(bf16[3,3,384,96]{2,3,1,0:T(8,128)(2,1)} %param.20) | copy-start | bytes 1990660
  14.2 6.8 %copy-start.1 = (bf16[3,3,3,384,192]{3,4,2,1,0:T(8,128)(2,1)S(1)}, bf16[3,3,3,384,192]{3,4,2,1,0:T(8,128)(2,1)}, u32[]{:S(2)}) copy-start(bf16[3,3,3,384,192]{3,4,2,1,0:T(8,128)(2,1)} %param.17) | copy-start | bytes 11943940
  15.6 4.0 %copy-start.5 = (bf16[3,3,3,192,96]{4,3,2,1,0:T(8,128)(2,1)S(1)}, bf16[3,3,3,192,96]{4,3,2,1,0:T(8,128)(2,1)}, u32[]{:S(2)}) copy-start(bf16[3,3,3,192,96]{4,3,2,1,0:T(8,128)(2,1)} %low) | copy-start | bytes 2985988
  15.6 12.1 %collective-permute-start.2 = (bf16[320,384]{1,0:T(8,128)(2,1)S(1)}, bf16[320,384]{1,0:T(8,128)(2,1)S(1)}, u32[]{:S(2)}, u32[]{:S(2)}) collective-permute-start(bf16[320,384]{1,0:T(8,128)(2,1)S(1)} %mid_rim_next.1), channel_id=1, source_target_pairs={{0,2},{1,3},{4,6},{5,7},{8,10},{9,11},{12,14},{13,15},{16,18},{17,... | collective-permute-start | bytes 737288 | tf_op jit(solution)/shard_map/ppermute | solution.py:676
  21.0 1.3 %copy-start.4 = (bf16[2,2,160,384]{3,2,1,0:T(8,128)(2,1)S(1)}, bf16[2,2,160,384]{3,2,1,0:T(8,128)(2,1)}, u32[]{:S(2)}) copy-start(bf16[2,2,160,384]{3,2,1,0:T(8,128)(2,1)} %cache.3) | copy-start | bytes 1474564
  27.8 5.9 %copy-start.2 = (bf16[2,4,320,192]{2,3,1,0:T(8,128)(2,1)S(1)}, bf16[2,4,320,192]{2,3,1,0:T(8,128)(2,1)}, u32[]{:S(2)}) copy-start(bf16[2,4,320,192]{2,3,1,0:T(8,128)(2,1)} %param.13) | copy-start | bytes 2949124
  30.5 3.5 %copy-start.3 = (bf16[384,1152]{1,0:T(8,128)(2,1)S(1)}, bf16[384,1152]{1,0:T(8,128)(2,1)}, u32[]{:S(2)}) copy-start(bf16[384,1152]{1,0:T(8,128)(2,1)} %qkv.5) | copy-start | bytes 2654212
  30.5 3.5 %copy-start.9 = (f32[384]{0:T(512)S(1)}, f32[384]{0:T(512)}, u32[]{:S(2)}) copy-start(f32[384]{0:T(512)} %gain.13) | copy-start | bytes 4612
  30.5 12.4 %collective-permute-start.5 = (bf16[2,2,96,1536]{3,2,1,0:T(8,128)(2,1)S(1)}, bf16[2,2,96,1536]{3,2,1,0:T(8,128)(2,1)S(1)}, u32[]{:S(2)}, u32[]{:S(2)}) collective-permute-start(bf16[2,2,96,1536]{3,2,1,0:T(8,128)(2,1)S(1)} %get-tuple-element.51.mine), channel_id=1, source_target_pairs={{0,1},{1,0},{2,3},{3,2},{4,5},{5,4},{6,7},{7,6},{8,9},{9,8},{10,11... | collective-permute-start | bytes 3538952 | tf_op jit(solution)/shard_map/ppermute | solution.py:730
  30.7 11.7 %collective-permute-start.6 = (bf16[320,384]{1,0:T(8,128)(2,1)S(1)}, bf16[320,384]{1,0:T(8,128)(2,1)S(1)}, u32[]{:S(2)}, u32[]{:S(2)}) collective-permute-start(bf16[320,384]{1,0:T(8,128)(2,1)S(1)} %maximum_select_fusion.refs_0_.own), channel_id=1, source_target_pairs={{0,8},{4,12},{8,0},{12,4},{1,9},{5,13},{9,1},{13,5},{2,10},{6,14},... | collective-permute-start | bytes 737288 | tf_op jit(solution)/shard_map/ppermute | solution.py:727
  30.7 21.9 %collective-permute-start.4 = (bf16[320,384]{1,0:T(8,128)(2,1)S(1)}, bf16[320,384]{1,0:T(8,128)(2,1)S(1)}, u32[]{:S(2)}, u32[]{:S(2)}) collective-permute-start(bf16[320,384]{1,0:T(8,128)(2,1)S(1)} %maximum_select_fusion.refs_0_.own), channel_id=1, source_target_pairs={{0,12},{4,0},{8,4},{12,8},{1,13},{5,1},{9,5},{13,9},{2,14},{6,2},{... | collective-permute-start | bytes 737288 | tf_op jit(solution)/shard_map/ppermute | solution.py:727
  33.8 21.9 %collective-permute-start.3 = (bf16[320,384]{1,0:T(8,128)(2,1)S(1)}, bf16[320,384]{1,0:T(8,128)(2,1)S(1)}, u32[]{:S(2)}, u32[]{:S(2)}) collective-permute-start(bf16[320,384]{1,0:T(8,128)(2,1)S(1)} %maximum_select_fusion.refs_0_.own), channel_id=1, source_target_pairs={{0,4},{4,8},{8,12},{12,0},{1,5},{5,9},{9,13},{13,1},{2,6},{6,10},{... | collective-permute-start | bytes 737288 | tf_op jit(solution)/shard_map/ppermute | solution.py:727
  42.9 12.8 %copy-start.11 = (bf16[384,384]{1,0:T(8,128)(2,1)S(1)}, bf16[384,384]{1,0:T(8,128)(2,1)}, u32[]{:S(2)}) copy-start(bf16[384,384]{1,0:T(8,128)(2,1)} %proj.1) | copy-start | bytes 884740
  60.0 2.5 %copy-start.10 = (f32[192]{0:T(256)S(1)}, f32[192]{0:T(256)}, u32[]{:S(2)}) copy-start(f32[192]{0:T(256)} %gain.15) | copy-start | bytes 2308
  67.0 10.1 %collective-permute-start.7 = (bf16[192,640]{1,0:T(8,128)(2,1)S(1)}, bf16[192,640]{1,0:T(8,128)(2,1)S(1)}, u32[]{:S(2)}, u32[]{:S(2)}) collective-permute-start(bf16[192,640]{1,0:T(8,128)(2,1)S(1)} %get-tuple-element.65), channel_id=1, source_target_pairs={{0,2},{1,3},{4,6},{5,7},{8,10},{9,11},{12,14},{13,15},{16,18},{17,... | collective-permute-start | bytes 737288 | tf_op jit(solution)/shard_map/ppermute | solution.py:676
  72.0 10.2 %collective-permute-start.8 = (bf16[1,192,640]{2,1,0:T(8,128)(2,1)S(1)}, bf16[1,192,640]{2,1,0:T(8,128)(2,1)S(1)}, u32[]{:S(2)}, u32[]{:S(2)}) collective-permute-start(bf16[1,192,640]{2,1,0:T(8,128)(2,1)S(1)} %get-tuple-element.67), channel_id=1, source_target_pairs={{0,2},{1,3},{4,6},{5,7},{8,10},{9,11},{12,14},{13,15},{16,18},{17,... | collective-permute-start | bytes 737288 | tf_op jit(solution)/shard_map/ppermute | solution.py:676

commit v13 on v11

--- a/solution.py
+++ b/solution.py
@@ -39,8 +39,8 @@
     return values * lax.rsqrt(mean + EPS) * gain.reshape(1, -1)
 
 
-def silu(values):
-    half = 0.5 * values
+def normed_silu(values, gain):
+    half = normed(values, 0.5 * gain)
     return half + half * jnp.tanh(half)
 
 
@@ -183,7 +183,7 @@
     chan = lax.axis_index("chan")
     for f in range(frames):
         for l in range(rows):
-            seen[f, l] = spread(silu(normed(latent[f, l].astype(F32), gain[...])))
+            seen[f, l] = spread(normed_silu(latent[f, l].astype(F32), gain[...]))
         mine = latent[f].astype(F32).reshape(rows * width, channels)
         kept = mine[:, :part]
         for index in range(1, channels // part):
@@ -219,7 +219,7 @@
     frames = total - past
     for side in range(2):
         for f in range(frames):
-            seen[side, f] = spread(silu(normed(halo[side, f].astype(F32), gain[...])))
+            seen[side, f] = spread(normed_silu(halo[side, f].astype(F32), gain[...]))
     acc[...] = started[...]
     for tap in range(taps):
         for side in range(2):
@@ -402,7 +402,7 @@
             sides = [upper[j, b].astype(F32) for b in range(2)]
             if 1 <= j <= high:
                 kept[spot, j - 1] = jnp.concatenate(sides, axis=-1).astype(BF16)
-            sides = [silu(normed(side, gain[...])) for side in sides]
+            sides = [normed_silu(side, gain[...]) for side in sides]
             if j == 0:
                 sides = [jnp.where(row == 0, 0.0, side) for side in sides]
             if j == high + 1:

time: 82.5 us -> 82.2 us (level)
  the two profiles are of different devices: /device:TPU:10 before, /device:TPU:14 now
where the time goes in v13:
time: 82.2 us; the launch traced here: 81.9 us
  waiting for transfers between devices  31.5 us (38%)
  Pallas kernels  27.1 us (33%)
  starting transfers between devices  11 us (13%)
  blocking collectives  9.47 us (12%)
  local copies, waits for them, and re-layouts  2.34 us (3%)
    ppermute x3, waiting for transfers between devices, body(): lax.ppermute(mine, 'rows', [(i, (i + k) % depth) for i in range(depth)])  20.1 us
    ppermute x3, waiting for transfers between devices, to_next(): lax.ppermute(values, 'segment', [(i, i + 1) for i in range(count - 1)])  11.5 us
    pallas_call x1, Pallas kernels, low_last(): pl.pallas_call(functools.partial(low_last_kernel, frames, past), in_specs...  4.37 us
    pallas_call x1, Pallas kernels, attention(): pl.pallas_call(functools.partial(attn_kernel, count, width), in_specs=[vm...  4.36 us
    ppermute x3, starting transfers between devices, to_next(): lax.ppermute(values, 'segment', [(i, i + 1) for i in range(count - 1)])  4.23 us
    ppermute x2, starting transfers between devices, to_neighbour(): return lax.ppermute(values, ('rows', 'segment', 'chan'), route)  4.17 us
    pallas_call x1, Pallas kernels, low_early(): pl.pallas_call(functools.partial(low_early_kernel, frames, past), in_spec...  3.31 us
    pallas_call x1, Pallas kernels, mid_inner(): pl.pallas_call(mid_inner_kernel, in_specs=[vmem()] * 3, out_specs=vmem(),...  3.16 us
  transfers between devices with their start and end apart: 9, of which 5 were waited for; matrix products, arithmetic and copies ran while one was open for 0% of the time, Pallas kernels for 18%

profile of v13, /device:TPU:14, one launch (start us, length us, event | category | flops | bytes accessed | tf_op | source)
XLA Modules:
  0.0 81.9 jit_solution(2415899677602706416)
XLA Ops:
  0.0 2.4 %edge_rows.1 = (bf16[2,160,384]{2,1,0:T(8,128)(2,1)}, bf16[4,160,384]{2,1,0:T(8,128)(2,1)}) custom-call(bf16[2,2,160,384]{3,2,1,0:T(8,128)(2,1)} %latent.3, bf16[2,2,160,384]{3,2,1,0:T(8,128)(2,1)} %cache.3, bf16[2,4,192,320]{3,2,1,0:T(8,128)(2,1)} %bitcast.20), custom_call_target="tpu_custom_call" | custom-call | bytes 1966080 | tf_op jit(solution)/shard_map/edge_rows/pallas_call | solution.py:98
  2.4 3.5 %collective-permute-start = (bf16[2,160,384]{2,1,0:T(8,128)(2,1)}, bf16[2,160,384]{2,1,0:T(8,128)(2,1)S(1)}, u32[]{:S(2)}, u32[]{:S(2)}) collective-permute-start(bf16[2,160,384]{2,1,0:T(8,128)(2,1)} %get-tuple-element.37), channel_id=1, source_target_pairs={{0,4},{5,1},{2,6},{7,3},{4,8},{9,5},{6,10},{11,7},{8,12},{13,9},{1... | collective-permute-start | bytes 737288 | tf_op jit(solution)/shard_map/ppermute | solution.py:671
  5.9 0.7 collective-permute-start.1
  6.7 2.1 %copy-done.1 = bf16[3,3,3,384,192]{3,4,2,1,0:T(8,128)(2,1)S(1)} copy-done((bf16[3,3,3,384,192]{3,4,2,1,0:T(8,128)(2,1)S(1)}, bf16[3,3,3,384,192]{3,4,2,1,0:T(8,128)(2,1)}, u32[]{:S(2)}) %copy-start.1) | copy-done | bytes 3981336
  8.8 3.2 %mid_inner.1.started = f32[4,320,192]{2,1,0:T(8,128)S(1)} custom-call(bf16[2,2,160,384]{3,2,1,0:T(8,128)(2,1)S(1)} %copy-done.7, f32[384]{0:T(512)S(1)} %copy-done.11, bf16[3,3,3,192,384]{4,3,2,1,0:T(8,128)(2,1)S(1)} %bitcast.22), custom_call_target="tpu_custom_call" | custom-call | flops 2548039680 | bytes 3981312 | tf_op jit(solution)/shard_map/mid_inner/pallas_call | solution.py:203
  12.0 2.2 %all-gather = bf16[4,160,384]{2,1,0:T(8,128)(2,1)S(1)} all-gather(bf16[2,160,384]{2,1,0:T(8,128)(2,1)S(1)} %collective-permute-done), channel_id=2, replica_groups=mesh['groups'=2,'rows'=4,'segment'=2,'chan'=2] {'chan'}, dimensions={0}, use_global_device_ids=true | all-gather | bytes 737280 | tf_op jit(solution)/shard_map/all_gather | solution.py:705
  14.1 2.0 %mid_rim.1 = (f32[320,384]{1,0:T(8,128)S(1)}, bf16[320,384]{1,0:T(8,128)(2,1)S(1)}) custom-call(f32[4,320,192]{2,1,0:T(8,128)S(1)} %mid_inner.1.started, bf16[2,2,160,384]{3,2,1,0:T(8,128)(2,1)S(1)} %bitcast.26, f32[384]{0:T(512)S(1)} %copy-done.11, bf16[3,3,3,192,384]{4,3,2,1,0:T(8,128)(2,1)S(1)} %bitcast.23), custom_call_target="tpu_custom_call" | custom-call | flops 2548039680 | bytes 3981312 | tf_op jit(solution)/shard_map/mid_rim/pallas_call | solution.py:238
  16.2 1.4 %collective-permute-start.2 = (bf16[320,384]{1,0:T(8,128)(2,1)S(1)}, bf16[320,384]{1,0:T(8,128)(2,1)S(1)}, u32[]{:S(2)}, u32[]{:S(2)}) collective-permute-start(bf16[320,384]{1,0:T(8,128)(2,1)S(1)} %get-tuple-element.40), channel_id=1, source_target_pairs={{0,2},{1,3},{4,6},{5,7},{8,10},{9,11},{12,14},{13,15},{16,18},{17,... | collective-permute-start | bytes 737288 | tf_op jit(solution)/shard_map/ppermute | solution.py:676
  17.6 2.5 %all-gather.1 = bf16[8,160,384]{2,1,0:T(8,128)(2,1)S(1)} all-gather(bf16[4,160,384]{2,1,0:T(8,128)(2,1)S(1)} %collective-permute-done.1), channel_id=3, replica_groups=mesh['groups'=2,'rows'=4,'segment'=2,'chan'=2] {'chan'}, dimensions={0}, use_global_device_ids=true | all-gather | bytes 1474560 | tf_op jit(solution)/shard_map/all_gather | solution.py:709
  20.2 1.4 %weight_forms.1 = (bf16[2,2,96,1536]{3,2,1,0:T(8,128)(2,1)S(1)}, bf16[576,2304]{1,0:T(8,128)(2,1)S(1)}) custom-call(bf16[3,3,96,384]{3,2,1,0:T(8,128)(2,1)S(1)} %bitcast.25, bf16[3,3,3,192,96]{4,3,2,1,0:T(8,128)(2,1)S(1)} %copy-done.5), custom_call_target="tpu_custom_call" | custom-call | flops 95551488 | bytes 6635520 | tf_op jit(solution)/shard_map/weight_forms/pallas_call | solution.py:138
  21.6 5.6 %collective-permute-done.2.arrived = bf16[320,384]{1,0:T(8,128)(2,1)S(1)} collective-permute-done((bf16[320,384]{1,0:T(8,128)(2,1)S(1)}, bf16[320,384]{1,0:T(8,128)(2,1)S(1)}, u32[]{:S(2)}, u32[]{:S(2)}) %collective-permute-start.2) | collective-permute-done | bytes 245792 | tf_op jit(solution)/shard_map/ppermute | solution.py:676
  27.3 2.3 %all-gather.2 = bf16[640,384]{1,0:T(8,128)(2,1)S(1)} all-gather(bf16[320,384]{1,0:T(8,128)(2,1)S(1)} %join.1), channel_id=4, replica_groups=mesh['groups'=2,'rows'=4,'segment'=2,'chan'=2] {'chan'}, dimensions={0}, use_global_device_ids=true | all-gather | bytes 737280 | tf_op jit(solution)/shard_map/all_gather | solution.py:714
  29.7 0.2 maximum_select_fusion.refs_0_.own
  30.0 0.2 collective-permute-start.5
  30.2 0.4 collective-permute-start.6
  30.6 1.7 %collective-permute-start.4 = (bf16[320,384]{1,0:T(8,128)(2,1)S(1)}, bf16[320,384]{1,0:T(8,128)(2,1)S(1)}, u32[]{:S(2)}, u32[]{:S(2)}) collective-permute-start(bf16[320,384]{1,0:T(8,128)(2,1)S(1)} %maximum_select_fusion.refs_0_.own), channel_id=1, source_target_pairs={{0,12},{4,0},{8,4},{12,8},{1,13},{5,1},{9,5},{13,9},{2,14},{6,2},{... | collective-permute-start | bytes 737288 | tf_op jit(solution)/shard_map/ppermute | solution.py:725
  32.2 0.3 collective-permute-start.3
  32.6 0.2 low_cached.1.cached
  32.9 0.5 block_keys.2
  33.4 14.1 %collective-permute-done.6.refs_0_ = bf16[320,384]{1,0:T(8,128)(2,1)S(1)} collective-permute-done((bf16[320,384]{1,0:T(8,128)(2,1)S(1)}, bf16[320,384]{1,0:T(8,128)(2,1)S(1)}, u32[]{:S(2)}, u32[]{:S(2)}) %collective-permute-start.6) | collective-permute-done | bytes 245792 | tf_op jit(solution)/shard_map/ppermute | solution.py:725
  47.4 0.5 block_keys.3
  48.1 6.0 %collective-permute-done.4.after = bf16[320,384]{1,0:T(8,128)(2,1)S(1)} collective-permute-done((bf16[320,384]{1,0:T(8,128)(2,1)S(1)}, bf16[320,384]{1,0:T(8,128)(2,1)S(1)}, u32[]{:S(2)}, u32[]{:S(2)}) %collective-permute-start.4) | collective-permute-done | bytes 245792 | tf_op jit(solution)/shard_map/ppermute | solution.py:725
  54.1 4.4 %frame_attention.1 = bf16[4,160,384]{2,1,0:T(8,128)(2,1)S(1)} custom-call(f32[384]{0:T(512)S(1)} %copy-done.8, bf16[384,1152]{1,0:T(8,128)(2,1)S(1)} %copy-done.3, bf16[384,384]{1,0:T(8,128)(2,1)S(1)} %copy-done.10, bf16[320,384]{1,0:T(8,128)(2,1)S(1)} %maximum_select_fusion.refs_0_.own, bf16[320,384]{1,0:T(8,128)(2,1)S(1)} %collective-permute-done.3.before, ...), custom_call_target="tpu_custom_call" | custom-call | flops 1635778560 | bytes 884736 | tf_op jit(solution)/shard_map/frame_attention/pallas_call | solution.py:362
  58.5 2.5 %all-gather.3 = bf16[8,160,384]{2,1,0:T(8,128)(2,1)S(1)} all-gather(bf16[4,160,384]{2,1,0:T(8,128)(2,1)S(1)} %frame_attention.1), channel_id=5, replica_groups=mesh['groups'=2,'rows'=4,'segment'=2,'chan'=2] {'chan'}, dimensions={0}, use_global_device_ids=true | all-gather | bytes 1474560 | tf_op jit(solution)/shard_map/all_gather | solution.py:736
  61.0 4.4 %low_last.1 = (bf16[192,640]{1,0:T(8,128)(2,1)S(1)}, f32[1,192,640]{2,1,0:T(8,128)S(1)}, bf16[1,6,160,768]{3,2,1,0:T(8,128)(2,1)S(1)}, bf16[1,4,160,384]{3,2,1,0:T(8,128)(2,1)S(1)}) custom-call(bf16[2,4,160,384]{3,2,1,0:T(8,128)(2,1)S(1)} %bitcast.18, bf16[2,2,192,1536]{3,2,1,0:T(8,128)(2,1)S(1)} %joined_up.1.up, f32[192]{0:T(256)S(1)} %copy-done.9, ...), custom_call_target="tpu_custom_call" | custom-call | flops 1132462080 | bytes 2654208 | tf_op jit(solution)/shard_map/low_last/pallas_call | solution.py:476
  65.4 1.5 %collective-permute-start.7 = (bf16[192,640]{1,0:T(8,128)(2,1)S(1)}, bf16[192,640]{1,0:T(8,128)(2,1)S(1)}, u32[]{:S(2)}, u32[]{:S(2)}) collective-permute-start(bf16[192,640]{1,0:T(8,128)(2,1)S(1)} %get-tuple-element.65), channel_id=1, source_target_pairs={{0,2},{1,3},{4,6},{5,7},{8,10},{9,11},{12,14},{13,15},{16,18},{17,... | collective-permute-start | bytes 737288 | tf_op jit(solution)/shard_map/ppermute | solution.py:676
  66.9 3.3 %low_early.1 = (bf16[1,192,640]{2,1,0:T(8,128)(2,1)S(1)}, bf16[1,6,160,768]{3,2,1,0:T(8,128)(2,1)S(1)}, bf16[1,4,160,384]{3,2,1,0:T(8,128)(2,1)S(1)}) custom-call(bf16[2,4,160,384]{3,2,1,0:T(8,128)(2,1)S(1)} %bitcast.19, bf16[2,2,192,1536]{3,2,1,0:T(8,128)(2,1)S(1)} %joined_up.1.up, f32[192]{0:T(256)S(1)} %copy-done.9, ...), custom_call_target="tpu_custom_call" | custom-call | flops 1132462080 | bytes 2654208 | tf_op jit(solution)/shard_map/low_early/pallas_call | solution.py:497
  70.2 1.3 %collective-permute-start.8 = (bf16[1,192,640]{2,1,0:T(8,128)(2,1)S(1)}, bf16[1,192,640]{2,1,0:T(8,128)(2,1)S(1)}, u32[]{:S(2)}, u32[]{:S(2)}) collective-permute-start(bf16[1,192,640]{2,1,0:T(8,128)(2,1)S(1)} %get-tuple-element.67), channel_id=1, source_target_pairs={{0,2},{1,3},{4,6},{5,7},{8,10},{9,11},{12,14},{13,15},{16,18},{17,... | collective-permute-start | bytes 737288 | tf_op jit(solution)/shard_map/ppermute | solution.py:676
  71.5 4.1 %collective-permute-done.7.arrived = bf16[192,640]{1,0:T(8,128)(2,1)S(1)} collective-permute-done((bf16[192,640]{1,0:T(8,128)(2,1)S(1)}, bf16[192,640]{1,0:T(8,128)(2,1)S(1)}, u32[]{:S(2)}, u32[]{:S(2)}) %collective-permute-start.7) | collective-permute-done | bytes 245792 | tf_op jit(solution)/shard_map/ppermute | solution.py:676
  75.6 3.1 %low_own.1 = (f32[2,192,640]{2,1,0:T(8,128)S(1)}, bf16[4,512,320]{2,1,0:T(8,128)(2,1)S(1)}) custom-call(bf16[1,6,160,768]{3,2,1,0:T(8,128)(2,1)S(1)} %get-tuple-element.60.early, bf16[1,6,160,768]{3,2,1,0:T(8,128)(2,1)S(1)} %get-tuple-element.61.last, bf16[1,4,160,384]{3,2,1,0:T(8,128)(2,1)S(1)} %get-tuple-element.62.early_kept, ...), custom_call_target="tpu_custom_call" | custom-call | flops 2548039680 | bytes 2654208 | tf_op jit(solution)/shard_map/low_own/pallas_call | solution.py:551
  78.8 1.8 %collective-permute-done.8.arrived = bf16[1,192,640]{2,1,0:T(8,128)(2,1)S(1)} collective-permute-done((bf16[1,192,640]{2,1,0:T(8,128)(2,1)S(1)}, bf16[1,192,640]{2,1,0:T(8,128)(2,1)S(1)}, u32[]{:S(2)}, u32[]{:S(2)}) %collective-permute-start.8) | collective-permute-done | bytes 245792 | tf_op jit(solution)/shard_map/ppermute | solution.py:676
  80.5 1.4 %finish.1 = bf16[2,4,96,320]{3,2,1,0:T(8,128)(2,1)} custom-call(f32[2,192,640]{2,1,0:T(8,128)S(1)} %get-tuple-element.66.own, bf16[1,192,640]{2,1,0:T(8,128)(2,1)S(1)} %collective-permute-done.8.arrived, bf16[4,512,320]{2,1,0:T(8,128)(2,1)S(1)} %get-tuple-element.68.weave), custom_call_target="tpu_custom_call" | custom-call | flops 251658240 | bytes 983040 | tf_op jit(solution)/shard_map/finish/pallas_call | solution.py:632
  (31 shorter events, 0.5 us)
Async XLA Ops:
  0.0 6.6 %copy-start.7 = (bf16[2,2,160,384]{3,2,1,0:T(8,128)(2,1)S(1)}, bf16[2,2,160,384]{3,2,1,0:T(8,128)(2,1)}, u32[]{:S(2)}) copy-start(bf16[2,2,160,384]{3,2,1,0:T(8,128)(2,1)} %latent.3) | copy-start | bytes 1474564
  0.0 6.6 %copy-start.11 = (f32[384]{0:T(512)S(1)}, f32[384]{0:T(512)}, u32[]{:S(2)}) copy-start(f32[384]{0:T(512)} %gain.8) | copy-start | bytes 4612
  2.4 9.5 %collective-permute-start = (bf16[2,160,384]{2,1,0:T(8,128)(2,1)}, bf16[2,160,384]{2,1,0:T(8,128)(2,1)S(1)}, u32[]{:S(2)}, u32[]{:S(2)}) collective-permute-start(bf16[2,160,384]{2,1,0:T(8,128)(2,1)} %get-tuple-element.37), channel_id=1, source_target_pairs={{0,4},{5,1},{2,6},{7,3},{4,8},{9,5},{6,10},{11,7},{8,12},{13,9},{1... | collective-permute-start | bytes 737288 | tf_op jit(solution)/shard_map/ppermute | solution.py:671
  5.9 10.3 %collective-permute-start.1 = (bf16[4,160,384]{2,1,0:T(8,128)(2,1)}, bf16[4,160,384]{2,1,0:T(8,128)(2,1)S(1)}, u32[]{:S(2)}, u32[]{:S(2)}) collective-permute-start(bf16[4,160,384]{2,1,0:T(8,128)(2,1)} %get-tuple-element.39), channel_id=1, source_target_pairs={{0,4},{5,1},{4,8},{9,5},{8,12},{13,9},{16,20},{21,17},{20,24},{25,... | collective-permute-start | bytes 1474568 | tf_op jit(solution)/shard_map/ppermute | solution.py:671
  6.7 2.1 %copy-start.1 = (bf16[3,3,3,384,192]{3,4,2,1,0:T(8,128)(2,1)S(1)}, bf16[3,3,3,384,192]{3,4,2,1,0:T(8,128)(2,1)}, u32[]{:S(2)}) copy-start(bf16[3,3,3,384,192]{3,4,2,1,0:T(8,128)(2,1)} %param.17) | copy-start | bytes 11943940
  14.1 6.0 %copy-start.6 = (bf16[3,3,384,96]{2,3,1,0:T(8,128)(2,1)S(1)}, bf16[3,3,384,96]{2,3,1,0:T(8,128)(2,1)}, u32[]{:S(2)}) copy-start(bf16[3,3,384,96]{2,3,1,0:T(8,128)(2,1)} %param.20) | copy-start | bytes 1990660
  14.1 7.4 %copy-start.2 = (bf16[3,3,3,384,192]{3,4,2,1,0:T(8,128)(2,1)S(1)}, bf16[3,3,3,384,192]{3,4,2,1,0:T(8,128)(2,1)}, u32[]{:S(2)}) copy-start(bf16[3,3,3,384,192]{3,4,2,1,0:T(8,128)(2,1)} %param.17) | copy-start | bytes 11943940
  16.2 4.0 %copy-start.5 = (bf16[3,3,3,192,96]{4,3,2,1,0:T(8,128)(2,1)S(1)}, bf16[3,3,3,192,96]{4,3,2,1,0:T(8,128)(2,1)}, u32[]{:S(2)}) copy-start(bf16[3,3,3,192,96]{4,3,2,1,0:T(8,128)(2,1)} %low) | copy-start | bytes 2985988
  16.2 5.4 %copy-start.4 = (bf16[2,2,160,384]{3,2,1,0:T(8,128)(2,1)S(1)}, bf16[2,2,160,384]{3,2,1,0:T(8,128)(2,1)}, u32[]{:S(2)}) copy-start(bf16[2,2,160,384]{3,2,1,0:T(8,128)(2,1)} %cache.3) | copy-start | bytes 1474564
  16.2 11.0 %collective-permute-start.2 = (bf16[320,384]{1,0:T(8,128)(2,1)S(1)}, bf16[320,384]{1,0:T(8,128)(2,1)S(1)}, u32[]{:S(2)}, u32[]{:S(2)}) collective-permute-start(bf16[320,384]{1,0:T(8,128)(2,1)S(1)} %get-tuple-element.40), channel_id=1, source_target_pairs={{0,2},{1,3},{4,6},{5,7},{8,10},{9,11},{12,14},{13,15},{16,18},{17,... | collective-permute-start | bytes 737288 | tf_op jit(solution)/shard_map/ppermute | solution.py:676
  27.3 5.3 %copy-start = (bf16[2,4,320,192]{2,3,1,0:T(8,128)(2,1)S(1)}, bf16[2,4,320,192]{2,3,1,0:T(8,128)(2,1)}, u32[]{:S(2)}) copy-start(bf16[2,4,320,192]{2,3,1,0:T(8,128)(2,1)} %param.13) | copy-start | bytes 2949124
  29.9 2.9 %copy-start.3 = (bf16[384,1152]{1,0:T(8,128)(2,1)S(1)}, bf16[384,1152]{1,0:T(8,128)(2,1)}, u32[]{:S(2)}) copy-start(bf16[384,1152]{1,0:T(8,128)(2,1)} %qkv.5) | copy-start | bytes 2654212
  29.9 2.9 %copy-start.8 = (f32[384]{0:T(512)S(1)}, f32[384]{0:T(512)}, u32[]{:S(2)}) copy-start(f32[384]{0:T(512)} %gain.11) | copy-start | bytes 4612
  30.0 18.0 %collective-permute-start.5 = (bf16[2,2,96,1536]{3,2,1,0:T(8,128)(2,1)S(1)}, bf16[2,2,96,1536]{3,2,1,0:T(8,128)(2,1)S(1)}, u32[]{:S(2)}, u32[]{:S(2)}) collective-permute-start(bf16[2,2,96,1536]{3,2,1,0:T(8,128)(2,1)S(1)} %get-tuple-element.51.mine), channel_id=1, source_target_pairs={{0,1},{1,0},{2,3},{3,2},{4,5},{5,4},{6,7},{7,6},{8,9},{9,8},{10,11... | collective-permute-start | bytes 3538952 | tf_op jit(solution)/shard_map/ppermute | solution.py:728
  30.2 17.3 %collective-permute-start.6 = (bf16[320,384]{1,0:T(8,128)(2,1)S(1)}, bf16[320,384]{1,0:T(8,128)(2,1)S(1)}, u32[]{:S(2)}, u32[]{:S(2)}) collective-permute-start(bf16[320,384]{1,0:T(8,128)(2,1)S(1)} %maximum_select_fusion.refs_0_.own), channel_id=1, source_target_pairs={{0,8},{4,12},{8,0},{12,4},{1,9},{5,13},{9,1},{13,5},{2,10},{6,14},... | collective-permute-start | bytes 737288 | tf_op jit(solution)/shard_map/ppermute | solution.py:725
  30.6 23.5 %collective-permute-start.4 = (bf16[320,384]{1,0:T(8,128)(2,1)S(1)}, bf16[320,384]{1,0:T(8,128)(2,1)S(1)}, u32[]{:S(2)}, u32[]{:S(2)}) collective-permute-start(bf16[320,384]{1,0:T(8,128)(2,1)S(1)} %maximum_select_fusion.refs_0_.own), channel_id=1, source_target_pairs={{0,12},{4,0},{8,4},{12,8},{1,13},{5,1},{9,5},{13,9},{2,14},{6,2},{... | collective-permute-start | bytes 737288 | tf_op jit(solution)/shard_map/ppermute | solution.py:725
  32.2 21.9 %collective-permute-start.3 = (bf16[320,384]{1,0:T(8,128)(2,1)S(1)}, bf16[320,384]{1,0:T(8,128)(2,1)S(1)}, u32[]{:S(2)}, u32[]{:S(2)}) collective-permute-start(bf16[320,384]{1,0:T(8,128)(2,1)S(1)} %maximum_select_fusion.refs_0_.own), channel_id=1, source_target_pairs={{0,4},{4,8},{8,12},{12,0},{1,5},{5,9},{9,13},{13,1},{2,6},{6,10},{... | collective-permute-start | bytes 737288 | tf_op jit(solution)/shard_map/ppermute | solution.py:725
  47.9 6.2 %copy-start.10 = (bf16[384,384]{1,0:T(8,128)(2,1)S(1)}, bf16[384,384]{1,0:T(8,128)(2,1)}, u32[]{:S(2)}) copy-start(bf16[384,384]{1,0:T(8,128)(2,1)} %proj.1) | copy-start | bytes 884740
  58.5 2.5 %copy-start.9 = (f32[192]{0:T(256)S(1)}, f32[192]{0:T(256)}, u32[]{:S(2)}) copy-start(f32[192]{0:T(256)} %gain.13) | copy-start | bytes 2308
  65.4 10.2 %collective-permute-start.7 = (bf16[192,640]{1,0:T(8,128)(2,1)S(1)}, bf16[192,640]{1,0:T(8,128)(2,1)S(1)}, u32[]{:S(2)}, u32[]{:S(2)}) collective-permute-start(bf16[192,640]{1,0:T(8,128)(2,1)S(1)} %get-tuple-element.65), channel_id=1, source_target_pairs={{0,2},{1,3},{4,6},{5,7},{8,10},{9,11},{12,14},{13,15},{16,18},{17,... | collective-permute-start | bytes 737288 | tf_op jit(solution)/shard_map/ppermute | solution.py:676
  70.2 10.3 %collective-permute-start.8 = (bf16[1,192,640]{2,1,0:T(8,128)(2,1)S(1)}, bf16[1,192,640]{2,1,0:T(8,128)(2,1)S(1)}, u32[]{:S(2)}, u32[]{:S(2)}) collective-permute-start(bf16[1,192,640]{2,1,0:T(8,128)(2,1)S(1)} %get-tuple-element.67), channel_id=1, source_target_pairs={{0,2},{1,3},{4,6},{5,7},{8,10},{9,11},{12,14},{13,15},{16,18},{17,... | collective-permute-start | bytes 737288 | tf_op jit(solution)/shard_map/ppermute | solution.py:676
